TPU v7x, 32 devices: a whole 2x2x4 slice. The times are simulated.
32 devices in a mesh: ctx: 16 (over z, y, core), fsdp: 2 (over x).
Axes of the slice: x: 2, y: 2, z: 4, core: 2. Of those that a mesh axis runs over, the one named last changes fastest.
Arguments:
- tokens: bfloat16 [2, 6144, 2560], P('fsdp', 'ctx'), may hold values from -6 to 6
- positions: int32 [2, 6144], P('fsdp', 'ctx'), may hold values from 0 to 6142, as said below
- attn_gain: float32 [2560], P(('ctx', 'fsdp')), may hold values from 0.1 to 1.9
- query_weight: bfloat16 [2560, 2560], P(('ctx', 'fsdp')), may hold values from -0.125 to 0.125
- key_weight: bfloat16 [2560, 256], P(('ctx', 'fsdp')), may hold values from -0.125 to 0.125
- value_weight: bfloat16 [2560, 256], P(('ctx', 'fsdp')), may hold values from -0.125 to 0.125
- out_weight: bfloat16 [2560, 2560], P(None, ('ctx', 'fsdp')), may hold values from -0.5 to 0.5
- mlp_gain: float32 [2560], P(('ctx', 'fsdp')), may hold values from 0.1 to 1.9
- gate_weight: bfloat16 [2560, 7680], P(('ctx', 'fsdp')), may hold values from -0.125 to 0.125
- up_weight: bfloat16 [2560, 7680], P(('ctx', 'fsdp')), may hold values from -0.125 to 0.125
- down_weight: bfloat16 [7680, 2560], P(None, ('ctx', 'fsdp')), may hold values from -0.0625 to 0.0625
- cotangent: bfloat16 [2, 6144, 2560], P('fsdp', 'ctx'), may hold values from -6 to 6
Outputs:
- output: float32 [2, 6144, 2560], P('fsdp', 'ctx')
- grad_tokens: float32 [2, 6144, 2560], P('fsdp', 'ctx')
- grad_attn_gain: float32 [2560], P(('ctx', 'fsdp'))
- grad_query_weight: float32 [2560, 2560], P(('ctx', 'fsdp'))
- grad_key_weight: float32 [2560, 256], P(('ctx', 'fsdp'))
- grad_value_weight: float32 [2560, 256], P(('ctx', 'fsdp'))
- grad_out_weight: float32 [2560, 2560], P(None, ('ctx', 'fsdp'))
- grad_mlp_gain: float32 [2560], P(('ctx', 'fsdp'))
- grad_gate_weight: float32 [2560, 7680], P(('ctx', 'fsdp'))
- grad_up_weight: float32 [2560, 7680], P(('ctx', 'fsdp'))
- grad_down_weight: float32 [7680, 2560], P(None, ('ctx', 'fsdp'))
Inputs may be any that keep to these rules, and one draw needn't show every extreme that they name: `positions`: positions count from 0 at each document's first token and rise by one per token. In every group a first document of 1 to 383 tokens starts at token 0. In one group the first document has a single token and a second one fills the rest of the group; in every other group documents of 4096 tokens follow the first one, the last of them possibly shorter.
All inputs are finite; a program needn't handle non-finite values.
Results may differ from a plain program's by a relative error of at most 0.039.
Values may be sent and summed in bfloat16 or wider, within the bound.
No kernel may reach another device: no remote copies, remote signals or barrier semaphores. Data moves between devices by JAX's collectives and lax.ppermute only.
A program may use at most 576 MiB of HBM per device.

v0:
```python
import jax
import jax.numpy as jnp
from jax import lax
from jax.sharding import PartitionSpec as P

WINDOW = 2048


epsilon = 1e-06
blocked_score = -1e30


def from_behind(value, axis, steps):
    count = lax.axis_size(axis)
    initial, last = (max(0, -steps), min(count, count - steps))
    return lax.ppermute(value, axis, [(source, source + steps) for source in range(initial, last)])


def normalize(values, gain):
    return values * lax.rsqrt(jnp.mean(values * values, axis=-1, keepdims=True) + epsilon) * gain


def geglu(gates, upward):
    return jax.nn.gelu(gates, approximate=True) * upward


def product(left, right):
    return jnp.dot(left, right, preferred_element_type=jnp.float32)


def contract_rows(left, right):
    return lax.dot_general(
        left, right, (((0,), (0,)), ((), ())), preferred_element_type=jnp.float32
    )


def contract_cols(left, right):
    return lax.dot_general(
        left, right, (((1,), (1,)), ((), ())), preferred_element_type=jnp.float32
    )


def visible(positions, reach, window):
    device = lax.axis_index("ctx")
    count = positions.shape[0]
    queries = device * count + jnp.arange(count, dtype=jnp.int32)
    sources = (device - reach) * count + jnp.arange((reach + 1) * count, dtype=jnp.int32)
    first = (queries - positions)[:, None]
    return (
        (sources[None, :] >= first)
        & (sources[None, :] <= queries[:, None])
        & (queries[:, None] - sources[None, :] < window)
    )


def attention_scores(queries, keys, allowed, scale):
    raw = jnp.einsum("qhd,kd->hqk", queries, keys, preferred_element_type=jnp.float32) * scale
    return jnp.where(allowed[None], raw, blocked_score)


def fetch_window(stacked, reach):
    blocks = [stacked]
    current = stacked
    for offset in range(reach):
        current = from_behind(current, "ctx", 1)
        blocks.append(current)
    return jnp.concatenate(blocks[::-1], 0)


def return_window(parts, reach):
    carried = parts[reach]
    for offset in range(reach - 1, -1, -1):
        carried = (
            from_behind(carried.astype(jnp.bfloat16), "ctx", -1).astype(carried.dtype)
            + parts[offset]
        )
    return carried


def local(
    tokens,
    positions,
    attn_gain,
    query_weight,
    key_weight,
    value_weight,
    out_weight,
    mlp_gain,
    gate_weight,
    up_weight,
    down_weight,
    cotangent,
):
    count = tokens.shape[1]
    reach = (WINDOW + count - 2) // count
    head_size = key_weight.shape[1]
    scale = head_size ** (-0.5)
    gain_one, query_full, key_full, value_full, out_full = (
        lax.all_gather(attn_gain.astype(jnp.bfloat16), ("ctx", "fsdp"), axis=0, tiled=True).astype(
            attn_gain.dtype
        ),
        lax.all_gather(query_weight, ("ctx", "fsdp"), axis=0, tiled=True),
        lax.all_gather(key_weight, ("ctx", "fsdp"), axis=0, tiled=True),
        lax.all_gather(value_weight, ("ctx", "fsdp"), axis=0, tiled=True),
        lax.all_gather(out_weight, ("ctx", "fsdp"), axis=1, tiled=True),
    )
    heads = query_full.shape[1] // head_size
    inputs = tokens[0].astype(jnp.float32)
    normed_one = normalize(inputs, gain_one).astype(jnp.bfloat16)
    queries = product(normed_one, query_full).astype(jnp.bfloat16).reshape(count, heads, head_size)
    stacked = jnp.concatenate(
        [product(normed_one, key_full), product(normed_one, value_full)], 1
    ).astype(jnp.bfloat16)
    window_pair = fetch_window(stacked, reach)
    keys = window_pair[:, :head_size]
    values = window_pair[:, head_size:]
    allowed = visible(positions[0], reach, WINDOW)
    scores = attention_scores(queries, keys, allowed, scale)
    highest = jnp.max(scores, axis=-1, keepdims=True)
    expo = jnp.exp(scores - highest)
    totals = jnp.sum(expo, axis=-1, keepdims=True)
    probs = expo / totals
    log_total = highest + jnp.log(totals)
    mixed = (
        jnp.einsum(
            "hqk,kd->qhd", probs.astype(jnp.bfloat16), values, preferred_element_type=jnp.float32
        )
        .reshape(count, heads * head_size)
        .astype(jnp.bfloat16)
    )
    resid = inputs + product(mixed, out_full)
    gain_two, gate_full, up_full, down_full = (
        lax.all_gather(mlp_gain.astype(jnp.bfloat16), ("ctx", "fsdp"), axis=0, tiled=True).astype(
            mlp_gain.dtype
        ),
        lax.all_gather(gate_weight, ("ctx", "fsdp"), axis=0, tiled=True),
        lax.all_gather(up_weight, ("ctx", "fsdp"), axis=0, tiled=True),
        lax.all_gather(down_weight, ("ctx", "fsdp"), axis=1, tiled=True),
    )
    normed_two = normalize(resid, gain_two).astype(jnp.bfloat16)
    gates = product(normed_two, gate_full)
    upward = product(normed_two, up_full)
    middle = geglu(gates, upward).astype(jnp.bfloat16)
    output = resid + product(middle, down_full)
    grad_in = cotangent[0].astype(jnp.float32)
    gain_two, gate_full, up_full, down_full = (
        lax.all_gather(mlp_gain.astype(jnp.bfloat16), ("ctx", "fsdp"), axis=0, tiled=True).astype(
            mlp_gain.dtype
        ),
        lax.all_gather(gate_weight, ("ctx", "fsdp"), axis=0, tiled=True),
        lax.all_gather(up_weight, ("ctx", "fsdp"), axis=0, tiled=True),
        lax.all_gather(down_weight, ("ctx", "fsdp"), axis=1, tiled=True),
    )
    grad_final = grad_in.astype(jnp.bfloat16)
    grad_down = contract_rows(middle, grad_final)
    grad_middle = contract_cols(grad_final, down_full)
    grad_gates, grad_upward = jax.vjp(geglu, gates, upward)[1](grad_middle)
    gates_low = grad_gates.astype(jnp.bfloat16)
    upward_low = grad_upward.astype(jnp.bfloat16)
    grad_gate = contract_rows(normed_two, gates_low)
    grad_up = contract_rows(normed_two, upward_low)
    grad_normed_two = contract_cols(gates_low, gate_full) + contract_cols(upward_low, up_full)
    resid_part, grad_gain_two = jax.vjp(normalize, resid, gain_two)[1](grad_normed_two)
    mlp_sums = (
        lax.psum_scatter(grad_gain_two, ("ctx", "fsdp"), scatter_dimension=0, tiled=True),
        lax.psum_scatter(grad_gate, ("ctx", "fsdp"), scatter_dimension=0, tiled=True),
        lax.psum_scatter(grad_up, ("ctx", "fsdp"), scatter_dimension=0, tiled=True),
        lax.psum_scatter(grad_down, ("ctx", "fsdp"), scatter_dimension=1, tiled=True),
    )
    grad_resid = grad_in + resid_part
    gain_one, query_full, key_full, value_full, out_full = (
        lax.all_gather(attn_gain.astype(jnp.bfloat16), ("ctx", "fsdp"), axis=0, tiled=True).astype(
            attn_gain.dtype
        ),
        lax.all_gather(query_weight, ("ctx", "fsdp"), axis=0, tiled=True),
        lax.all_gather(key_weight, ("ctx", "fsdp"), axis=0, tiled=True),
        lax.all_gather(value_weight, ("ctx", "fsdp"), axis=0, tiled=True),
        lax.all_gather(out_weight, ("ctx", "fsdp"), axis=1, tiled=True),
    )
    grad_attn = grad_resid.astype(jnp.bfloat16)
    grad_out = contract_rows(mixed, grad_attn)
    grad_mixed = (
        contract_cols(grad_attn, out_full).astype(jnp.bfloat16).reshape(count, heads, head_size)
    )
    scores = attention_scores(queries, keys, allowed, scale)
    probs = jnp.exp(scores - log_total)
    grad_values = jnp.einsum(
        "hqk,qhd->kd", probs.astype(jnp.bfloat16), grad_mixed, preferred_element_type=jnp.float32
    )
    grad_probs = jnp.einsum("qhd,kd->hqk", grad_mixed, values, preferred_element_type=jnp.float32)
    inner = jnp.sum(probs * grad_probs, axis=-1, keepdims=True)
    grad_scores = (probs * (grad_probs - inner)).astype(jnp.bfloat16)
    grad_queries = (
        (jnp.einsum("hqk,kd->qhd", grad_scores, keys, preferred_element_type=jnp.float32) * scale)
        .reshape(count, heads * head_size)
        .astype(jnp.bfloat16)
    )
    grad_keys = (
        jnp.einsum("hqk,qhd->kd", grad_scores, queries, preferred_element_type=jnp.float32) * scale
    )
    grad_pair = jnp.concatenate([grad_keys, grad_values], 1)
    parts = [
        grad_pair[(reach - offset) * count : (reach - offset + 1) * count]
        for offset in range(reach + 1)
    ]
    own_pair = return_window(parts, reach)
    keys_low = own_pair[:, :head_size].astype(jnp.bfloat16)
    values_low = own_pair[:, head_size:].astype(jnp.bfloat16)
    grad_query = contract_rows(normed_one, grad_queries)
    grad_key = contract_rows(normed_one, keys_low)
    grad_value = contract_rows(normed_one, values_low)
    grad_normed_one = (
        contract_cols(grad_queries, query_full)
        + contract_cols(keys_low, key_full)
        + contract_cols(values_low, value_full)
    )
    input_part, grad_gain_one = jax.vjp(normalize, inputs, gain_one)[1](grad_normed_one)
    grad_tokens = (grad_resid + input_part)[None]
    attn_sums = (
        lax.psum_scatter(grad_gain_one, ("ctx", "fsdp"), scatter_dimension=0, tiled=True),
        lax.psum_scatter(grad_query, ("ctx", "fsdp"), scatter_dimension=0, tiled=True),
        lax.psum_scatter(grad_key, ("ctx", "fsdp"), scatter_dimension=0, tiled=True),
        lax.psum_scatter(grad_value, ("ctx", "fsdp"), scatter_dimension=0, tiled=True),
        lax.psum_scatter(grad_out, ("ctx", "fsdp"), scatter_dimension=1, tiled=True),
    )
    return (
        output[None],
        grad_tokens,
        attn_sums[0],
        attn_sums[1],
        attn_sums[2],
        attn_sums[3],
        attn_sums[4],
        mlp_sums[0],
        mlp_sums[1],
        mlp_sums[2],
        mlp_sums[3],
    )


def solution(mesh):
    return jax.shard_map(
        local,
        mesh=mesh,
        in_specs=(
            P("fsdp", "ctx", None),
            P("fsdp", "ctx"),
            P(("ctx", "fsdp")),
            P(("ctx", "fsdp"), None),
            P(("ctx", "fsdp"), None),
            P(("ctx", "fsdp"), None),
            P(None, ("ctx", "fsdp")),
            P(("ctx", "fsdp")),
            P(("ctx", "fsdp"), None),
            P(("ctx", "fsdp"), None),
            P(None, ("ctx", "fsdp")),
            P("fsdp", "ctx", None),
        ),
        out_specs=(
            P("fsdp", "ctx", None),
            P("fsdp", "ctx", None),
            P(("ctx", "fsdp")),
            P(("ctx", "fsdp"), None),
            P(("ctx", "fsdp"), None),
            P(("ctx", "fsdp"), None),
            P(None, ("ctx", "fsdp")),
            P(("ctx", "fsdp")),
            P(("ctx", "fsdp"), None),
            P(("ctx", "fsdp"), None),
            P(None, ("ctx", "fsdp")),
        ),
        check_vma=False,
    )
```

profile of v0, /device:TPU:0, one launch (start us, length us, event | category | flops | bytes accessed | tf_op | source)
XLA Modules:
  0.0 4716.2 jit_solution(6703056228948378183)
XLA Ops:
  12.5 42.2 all-reduce.5
  55.2 12.8 all-gather.10.cloned.1.call-done
  70.4 53.9 %all-gather.8.cloned.1.call-done = bf16[2560,256]{1,0:T(8,128)(2,1)} async-done(((bf16[80,256]{1,0:T(8,128)(2,1)}), bf16[2560,256]{1,0:T(8,128)(2,1)}) %all-gather.8.cloned.1.call-update) | async-done | bytes 1310736 | tf_op jit(solution)/shard_map/all_gather | solution.py:103
  169.1 13.0 collective-permute-start.5
  192.8 40.0 all-gather.12.cloned.1.call-done
  246.7 18.6 fusion.85
  265.3 16.5 fusion.3
  281.8 19.4 fusion.47
  301.3 32.9 all-gather.14.cloned.1.call-done
  346.2 211.5 %all-gather.18.cloned.1.call-done = bf16[2560,7680]{1,0:T(8,128)(2,1)} async-done(((bf16[80,7680]{1,0:T(8,128)(2,1)}), bf16[2560,7680]{1,0:T(8,128)(2,1)}) %all-gather.18.cloned.1.call-update) | async-done | bytes 39321616 | tf_op jit(solution)/shard_map/all_gather | solution.py:137
  557.7 23.4 fusion.87
  581.1 200.1 %all-gather.16.cloned.1.call-done = bf16[2560,7680]{1,0:T(8,128)(2,1)} async-done(((bf16[80,7680]{1,0:T(8,128)(2,1)}), bf16[2560,7680]{1,0:T(8,128)(2,1)}) %all-gather.16.cloned.1.call-update) | async-done | bytes 39321616 | tf_op jit(solution)/shard_map/all_gather | solution.py:136
  781.2 23.3 fusion.86
  804.5 200.3 %all-gather.20.cloned.1.call-done = bf16[7680,2560]{0,1:T(8,128)(2,1)} async-done(((bf16[7680,80]{0,1:T(8,128)(2,1)}), bf16[7680,2560]{0,1:T(8,128)(2,1)}) %all-gather.20.cloned.1.call-update) | async-done | bytes 39321616 | tf_op jit(solution)/shard_map/all_gather | solution.py:138
  1004.8 34.6 multiply_convert_fusion
  1039.4 23.1 fusion.88
  1062.6 28.0 multiply_reduce_fusion
  1108.0 15.8 fusion.26
  1123.8 31.3 fusion
  1155.1 33.4 fusion.2
  1254.4 14.9 fusion.49
  1295.4 32.5 fusion.41
  1329.4 32.6 fusion.91
  1362.1 32.6 fusion.90
  1407.1 25.8 fusion.23
  1440.0 49.9 %all-reduce.4 = (f32[2560]{0:T(1024)S(1)}, f32[2560]{0:T(1024)S(1)}) all-reduce(f32[2560]{0:T(1024)S(1)} %get-tuple-element.13, f32[2560]{0:T(1024)S(1)} %copy-done.30), channel_id=2, replica_groups=mesh['ctx'=16,'fsdp'=2] {'ctx','fsdp'}, use_global_device_ids=true, to_apply=%region_8.9.clone | all-reduce | flops 5120 | bytes 40960
  1497.4 40.6 reduce-scatter.12.cloned.1.call-done
  1538.0 552.1 %reduce-scatter.14.cloned.1.call-done = f32[2560,80]{0,1:T(8,128)} async-done(((f32[2560,2560]{0,1:T(8,128)}), f32[2560,80]{0,1:T(8,128)}) %reduce-scatter.14.cloned.1.call-update) | async-done | bytes 819216 | tf_op jit(solution)/shard_map/reduce_scatter | solution.py:224
  2090.1 558.6 %reduce-scatter.8.cloned.1.call-done = f32[80,2560]{1,0:T(8,128)} async-done(((f32[2560,2560]{1,0:T(8,128)}), f32[80,2560]{1,0:T(8,128)}) %reduce-scatter.8.cloned.1.call-update) | async-done | bytes 819216 | tf_op jit(solution)/shard_map/reduce_scatter | solution.py:221
  2648.7 688.7 %reduce-scatter.20.cloned.1.call-done = f32[7680,80]{0,1:T(8,128)} async-done(((f32[7680,2560]{0,1:T(8,128)}), f32[7680,80]{0,1:T(8,128)}) %reduce-scatter.20.cloned.1.call-update) | async-done | bytes 2457616 | tf_op jit(solution)/shard_map/reduce_scatter | solution.py:168
  3337.4 686.1 %reduce-scatter.18.cloned.1.call-done = f32[80,7680]{1,0:T(8,128)} async-done(((f32[2560,7680]{1,0:T(8,128)}), f32[80,7680]{1,0:T(8,128)}) %reduce-scatter.18.cloned.1.call-update) | async-done | bytes 2457616 | tf_op jit(solution)/shard_map/reduce_scatter | solution.py:167
  4023.4 686.0 %reduce-scatter.16.cloned.1.call-done = f32[80,7680]{1,0:T(8,128)} async-done(((f32[2560,7680]{1,0:T(8,128)}), f32[80,7680]{1,0:T(8,128)}) %reduce-scatter.16.cloned.1.call-update) | async-done | bytes 2457616 | tf_op jit(solution)/shard_map/reduce_scatter | solution.py:166
  (177 shorter events, 226.6 us)
Async XLA Ops:
  7.2 60.9 %all-gather.10.cloned.1.call-start = ((), (), s32[]{:S(2)}) async-start(), calls=%async_computation.8 | async-start | bytes 1351680 | tf_op jit(solution)/shard_map/all_gather | solution.py:104
  7.9 116.4 %all-gather.8.cloned.1.call-start = ((), (), s32[]{:S(2)}) async-start(), calls=%async_computation.7 | async-start | bytes 1351680 | tf_op jit(solution)/shard_map/all_gather | solution.py:103
  8.7 224.1 %all-gather.12.cloned.1.call-start = ((), (), s32[]{:S(2)}) async-start(), calls=%async_computation.9 | async-start | bytes 13516800 | tf_op jit(solution)/shard_map/all_gather | solution.py:102
  9.4 324.8 %all-gather.14.cloned.1.call-start = ((), (), s32[]{:S(2)}) async-start(), calls=%async_computation.10 | async-start | bytes 13516800 | tf_op jit(solution)/shard_map/all_gather | solution.py:105
  10.0 547.7 %all-gather.18.cloned.1.call-start = ((), (), s32[]{:S(2)}) async-start(), calls=%async_computation.12 | async-start | bytes 40550400 | tf_op jit(solution)/shard_map/all_gather | solution.py:137
  10.6 770.6 %all-gather.16.cloned.1.call-start = ((), (), s32[]{:S(2)}) async-start(), calls=%async_computation.11 | async-start | bytes 40550400 | tf_op jit(solution)/shard_map/all_gather | solution.py:136
  11.2 993.6 %all-gather.20.cloned.1.call-start = ((), (), s32[]{:S(2)}) async-start(), calls=%async_computation.13 | async-start | bytes 40550400 | tf_op jit(solution)/shard_map/all_gather | solution.py:138
  11.9 1485.5 %reduce-scatter.10.cloned.1.call-start = ((), (), s32[]{:S(2)}) async-start(), calls=%async_computation.15 | async-start | bytes 2703360 | tf_op jit(solution)/shard_map/reduce_scatter | solution.py:222
  54.7 178.0 %copy-start.16 = (f32[2560]{0:T(1024)}, f32[2560]{0:T(1024)S(1)}, u32[]{:S(2)}) copy-start(f32[2560]{0:T(1024)S(1)} %convert_element_type.127) | copy-start | bytes 30724
  55.2 71.4 %copy-start.28 = (f32[384]{0:T(512)}, f32[384]{0:T(512)S(1)}, u32[]{:S(2)}) copy-start(f32[384]{0:T(512)S(1)} %fusion.31) | copy-start | bytes 4612
  55.2 177.6 %copy-start.25 = (f32[384]{0:T(512)}, f32[384]{0:T(512)S(1)}, u32[]{:S(2)}) copy-start(f32[384]{0:T(512)S(1)} %fusion.77) | copy-start | bytes 4612
  70.4 97.8 %copy-start.33 = (s32[1,384]{1,0:T(1,128)S(1)}, s32[1,384]{1,0:T(1,128)}, u32[]{:S(2)}) copy-start(s32[1,384]{1,0:T(1,128)} %param.13) | copy-start | bytes 4612
  126.7 3.5 collective-permute-start
  130.2 7.9 collective-permute-start.1
  138.2 9.1 collective-permute-start.2
  148.0 9.2 collective-permute-start.3
  157.2 11.9 collective-permute-start.4
  169.1 14.6 collective-permute-start.5
  343.9 237.2 %copy-start.31 = (f32[384]{0:T(512)}, f32[384]{0:T(512)S(1)}, u32[]{:S(2)}) copy-start(f32[384]{0:T(512)S(1)} %get-tuple-element.24) | copy-start | bytes 4612
  346.2 434.9 %copy-start.5 = (bf16[384,2560]{1,0:T(8,128)(2,1)}, bf16[384,2560]{1,0:T(8,128)(2,1)S(1)}, u32[]{:S(2)}) copy-start(bf16[384,2560]{1,0:T(8,128)(2,1)S(1)} %multiply_convert_fusion.3) | copy-start | bytes 5898244
  1199.6 3.6 collective-permute-start.6
  1203.3 8.8 collective-permute-start.7
  1212.2 9.1 collective-permute-start.8
  1221.3 9.1 collective-permute-start.9
  1230.5 9.1 collective-permute-start.10
  1239.7 9.4 collective-permute-start.11
  1251.8 286.3 %reduce-scatter.12.cloned.1.call-start = ((), (), s32[]{:S(2)}) async-start(), calls=%async_computation.16 | async-start | bytes 2703360 | tf_op jit(solution)/shard_map/reduce_scatter | solution.py:223
  1254.4 835.8 %reduce-scatter.14.cloned.1.call-start = ((), (), s32[]{:S(2)}) async-start(), calls=%async_computation.17 | async-start | bytes 27033600 | tf_op jit(solution)/shard_map/reduce_scatter | solution.py:224
  1269.3 1379.4 %reduce-scatter.8.cloned.1.call-start = ((), (), s32[]{:S(2)}) async-start(), calls=%async_computation.14 | async-start | bytes 27033600 | tf_op jit(solution)/shard_map/reduce_scatter | solution.py:221
  1293.9 2043.5 %reduce-scatter.20.cloned.1.call-start = ((), (), s32[]{:S(2)}) async-start(), calls=%async_computation.20 | async-start | bytes 81100800 | tf_op jit(solution)/shard_map/reduce_scatter | solution.py:168
  1327.9 2695.5 %reduce-scatter.18.cloned.1.call-start = ((), (), s32[]{:S(2)}) async-start(), calls=%async_computation.19 | async-start | bytes 81100800 | tf_op jit(solution)/shard_map/reduce_scatter | solution.py:167
  1362.1 3347.3 %reduce-scatter.16.cloned.1.call-start = ((), (), s32[]{:S(2)}) async-start(), calls=%async_computation.18 | async-start | bytes 81100800 | tf_op jit(solution)/shard_map/reduce_scatter | solution.py:166
  (30 other events, 381.1 us)
Sparse Core Ops, SparseCore 0:
  10.9 57.1 all-gather.9
  70.9 53.3 all-gather.7
  127.2 105.5 all-gather.11
  235.5 98.6 all-gather.13
  337.0 220.6 all-gather.17
  560.5 220.6 all-gather.15
  784.1 220.6 all-gather.19
  1251.9 148.1 reduce-scatter.9
  1402.9 135.0 reduce-scatter.11
  1540.8 549.3 reduce-scatter.13
  2093.0 555.6 reduce-scatter.7
  2655.6 681.7 reduce-scatter.19
  3344.4 679.0 reduce-scatter.17
  4030.3 679.0 reduce-scatter.15
where the time goes:
time: 4720 us
  waiting for transfers between devices  4010 us (85%)
  matrix products  446 us (9%)
  blocking collectives  92.1 us (2%)
  other arithmetic  65.5 us (1%)
  starting transfers between devices  58.1 us (1%)
    reduce_scatter x1, waiting for transfers between devices, local(): lax.psum_scatter(grad_down, ('ctx', 'fsdp'), scatter_dimension=1, tiled=T...  689 us
    reduce_scatter x1, waiting for transfers between devices, local(): lax.psum_scatter(grad_up, ('ctx', 'fsdp'), scatter_dimension=0, tiled=True)  686 us
    reduce_scatter x1, waiting for transfers between devices, local(): lax.psum_scatter(grad_gate, ('ctx', 'fsdp'), scatter_dimension=0, tiled=T...  686 us
    reduce_scatter x1, waiting for transfers between devices, local(): lax.psum_scatter(grad_query, ('ctx', 'fsdp'), scatter_dimension=0, tiled=...  559 us
    reduce_scatter x1, waiting for transfers between devices, local(): lax.psum_scatter(grad_out, ('ctx', 'fsdp'), scatter_dimension=1, tiled=True)  552 us
    all_gather x1, waiting for transfers between devices, local(): lax.all_gather(up_weight, ('ctx', 'fsdp'), axis=0, tiled=True)  211 us
    all_gather x1, waiting for transfers between devices, local(): lax.all_gather(down_weight, ('ctx', 'fsdp'), axis=1, tiled=True)  200 us
    all_gather x1, waiting for transfers between devices, local(): lax.all_gather(gate_weight, ('ctx', 'fsdp'), axis=0, tiled=True)  200 us
  transfers between devices with their start and end apart: 26, of which 24 were waited for; matrix products, arithmetic and copies ran while one was open for 7% of the time, Pallas kernels for 0%

commit v1 on v0

v1 whole, which is shorter than its diff:
```python
import functools

import jax
import jax.numpy as jnp
from jax import lax
from jax.experimental import pallas as pl
from jax.experimental.pallas import tpu as pltpu
from jax.sharding import Mesh, PartitionSpec as P

WINDOW = 2048
SUB = 128
epsilon = 1e-06
blocked_score = -1e30
PLANE = ("y", "c", "x")
low = jnp.bfloat16
f32 = jnp.float32


def dot(left, right, contract, kind=f32):
    return lax.dot_general(
        left, right, ((contract[:1], contract[1:]), ((), ())), preferred_element_type=f32
    ).astype(kind)


def swap(value, axis):
    return lax.ppermute(value, axis, [(0, 1), (1, 0)])


def plane_gather(own):
    half = own.shape[0] // 2
    by_x = swap(own, "x")
    by_y = swap(own, "y")
    own_c = swap(own, "c")
    diag_top = swap(by_y[:half], "x")
    diag_bottom = swap(by_x[half:], "y")
    by_x_c = swap(by_x, "c")
    by_y_c = swap(by_y, "c")
    diag = jnp.concatenate([diag_top, diag_bottom], 0)
    diag_c = swap(diag, "c")
    return [own, by_x, own_c, by_x_c, by_y, diag, by_y_c, diag_c]


def plane_scatter(parts):
    half = parts[0].shape[0] // 2

    def chip(r):
        return parts[r].astype(f32) + swap(parts[r + 2].astype(low), "c").astype(f32)

    diag = chip(5).astype(low)
    diag_x = swap(diag[:half], "x").astype(f32)
    diag_y = swap(diag[half:], "y").astype(f32)
    to_x, to_y = chip(1), chip(4)
    x_top = swap(to_x[:half].astype(low), "x").astype(f32)
    y_bottom = swap(to_y[half:].astype(low), "y").astype(f32)
    mine = chip(0)
    x_bottom = swap((to_x[half:] + diag_y).astype(low), "x").astype(f32)
    y_top = swap((to_y[:half] + diag_x).astype(low), "y").astype(f32)
    return jnp.concatenate(
        [mine[:half] + x_top + y_top, mine[half:] + x_bottom + y_bottom], 0
    )


def plane_index():
    return (lax.axis_index("y") * 2 + lax.axis_index("c")) * 2 + lax.axis_index("x")


def gather_rows(shard):
    column = lax.all_gather(shard, "z", axis=0, tiled=False)
    blocks = plane_gather(column)
    here = plane_index()
    planes, rows, wide = column.shape
    whole = jnp.zeros((planes, 8, rows, wide), shard.dtype)
    for r, block in enumerate(blocks):
        whole = lax.dynamic_update_slice(whole, block[:, None], (0, here ^ r, 0, 0))
    return whole.reshape(planes * 8 * rows, wide)


def scatter_rows(partial):
    planes = lax.axis_size("z")
    wide = partial.shape[1]
    rows = partial.shape[0] // (planes * 8)
    blocks = partial.reshape(planes, 8, rows, wide)
    here = plane_index()
    parts = [
        lax.dynamic_slice(blocks, (0, here ^ r, 0, 0), (planes, 1, rows, wide))[:, 0]
        for r in range(8)
    ]
    column = plane_scatter(parts).astype(low).reshape(planes * rows, wide)
    return lax.psum_scatter(column, "z", scatter_dimension=0, tiled=True).astype(f32)


def columns_of_plane(shard):
    rows, wide = shard.shape
    split = jnp.swapaxes(shard.reshape(rows, 8, wide // 8), 0, 1)
    return lax.all_to_all(split, PLANE, split_axis=0, concat_axis=0, tiled=True)


def window_blocks(pair, chips):
    count = lax.axis_size("z") * lax.axis_size("y")
    same = [
        lax.ppermute(pair, ("z", "y"), [(i, i + d) for i in range(count - d)])
        for d in range(chips, 0, -1)
    ] + [pair]
    same = jnp.stack(same)
    other = swap(same, "c")
    first = lax.axis_index("c") == 0
    return jnp.stack(
        [jnp.where(first, same, other), jnp.where(first, other, same)], 1
    ).reshape((chips + 1) * 2 * pair.shape[0], pair.shape[1])


def return_blocks(grads, chips, rows):
    count = lax.axis_size("z") * lax.axis_size("y")
    both = grads.reshape(chips + 1, 2, rows, grads.shape[1])
    first = lax.axis_index("c") == 0
    mine = jnp.where(first, both[:, 0], both[:, 1])
    theirs = jnp.where(first, both[:, 1], both[:, 0])
    mine = mine + swap(theirs.astype(low), "c").astype(f32)
    total = mine[chips]
    for d in range(chips, 0, -1):
        total = total + lax.ppermute(
            mine[chips - d].astype(low), ("z", "y"), [(i + d, i) for i in range(count - d)]
        ).astype(f32)
    return total


def two_heads(block, size):
    return jnp.concatenate([block[:, :size], block[:, size:]], 0)


def side_by_side(rows, size):
    half = rows.shape[0] // 2
    return jnp.concatenate([rows[:half], rows[half:]], 1)


def write_bias(bias, places, span, block):
    key = lax.broadcasted_iota(jnp.int32, (span, SUB), 0) - WINDOW
    query = lax.broadcasted_iota(jnp.int32, (span, SUB), 1)
    age = query - key
    seen = (age <= places) & (age >= 0) & (age < WINDOW)
    value = jnp.where(seen, 0.0, blocked_score).astype(f32)
    bias[:, :SUB] = value
    bias[:, SUB:] = value


def attend_kernel(size, scale, span, base, offset, places, queries, pairs, values_t, mixed, logs, bias):
    block = pl.program_id(0)
    start = pl.multiple_of(offset[0] + base + block * SUB, SUB)

    @pl.when(pl.program_id(1) == 0)
    def _():
        write_bias(bias, places[...], span, block)

    query = two_heads(queries[...], size)
    keys = pairs[pl.ds(start, span), :size]
    scores = dot(keys, query, (1, 1)) * scale + bias[...]
    highest = jnp.max(scores, axis=0, keepdims=True)
    expo = jnp.exp(scores - highest)
    total = jnp.sum(expo, axis=0, keepdims=True)
    flat = dot(values_t[:, pl.ds(start, span)], expo.astype(low), (1, 0)) / total
    mixed[...] = side_by_side(flat.T, size).astype(low)
    logs[0] = highest + jnp.log(total)


def attend_back_kernel(
    size, scale, span, base, offset, places, queries, grads, logs, pairs, keys_t, grad_queries, grad_pairs, bias
):
    block = pl.program_id(0)
    start = pl.multiple_of(offset[0] + base + block * SUB, SUB)

    @pl.when((block == 0) & (pl.program_id(1) == 0))
    def _():
        grad_pairs[...] = jnp.zeros_like(grad_pairs)

    @pl.when(pl.program_id(1) == 0)
    def _():
        write_bias(bias, places[...], span, block)

    query = two_heads(queries[...], size)
    grad = two_heads(grads[...], size)
    keys = pairs[pl.ds(start, span), :size]
    values = pairs[pl.ds(start, span), size:]
    probs = jnp.exp(dot(keys, query, (1, 1)) * scale + bias[...] - logs[0])
    grad_pairs[pl.ds(start, span), size:] += dot(probs.astype(low), grad, (1, 0))
    grad_probs = dot(values, grad, (1, 1))
    inner = jnp.sum(probs * grad_probs, axis=0, keepdims=True)
    grad_scores = (probs * (grad_probs - inner)).astype(low)
    grad_pairs[pl.ds(start, span), :size] += dot(grad_scores, query, (1, 0)) * scale
    flat = dot(keys_t[:, pl.ds(start, span)], grad_scores, (1, 0)) * scale
    grad_queries[...] = side_by_side(flat.T, size).astype(low)


def attend(queries, pairs, places, size, base):
    count, wide = queries.shape
    grid = (count // SUB, wide // (2 * size))
    span = WINDOW + SUB
    offset = (lax.axis_index("c") * count).astype(jnp.int32)[None]
    whole = lambda shape: pl.BlockSpec(shape, lambda s, h, o: (0, 0))
    return pl.pallas_call(
        functools.partial(attend_kernel, size, size**-0.5, span, base),
        out_shape=(
            jax.ShapeDtypeStruct((count, wide), low),
            jax.ShapeDtypeStruct((grid[0] * grid[1], 1, 2 * SUB), f32),
        ),
        grid_spec=pltpu.PrefetchScalarGridSpec(
            num_scalar_prefetch=1,
            grid=grid,
            in_specs=[
                pl.BlockSpec((1, SUB), lambda s, h, o: (0, s)),
                pl.BlockSpec((SUB, 2 * size), lambda s, h, o: (s, h)),
                whole(pairs.shape),
                whole((size, pairs.shape[0])),
            ],
            out_specs=[
                pl.BlockSpec((SUB, 2 * size), lambda s, h, o: (s, h)),
                pl.BlockSpec((1, 1, 2 * SUB), lambda s, h, o: (s * grid[1] + h, 0, 0)),
            ],
            scratch_shapes=[pltpu.VMEM((span, 2 * SUB), f32)],
        ),
        compiler_params=pltpu.CompilerParams(vmem_limit_bytes=48 << 20),
        cost_estimate=pl.CostEstimate(
            flops=4 * count * wide * span, bytes_accessed=8 << 20, transcendentals=count * span * wide // size
        ),
    )(offset, places, queries, pairs, pairs[:, size:].T)


def attend_back(queries, grads, logs, pairs, places, size, base):
    count, wide = queries.shape
    grid = (count // SUB, wide // (2 * size))
    span = WINDOW + SUB
    offset = (lax.axis_index("c") * count).astype(jnp.int32)[None]
    whole = lambda shape: pl.BlockSpec(shape, lambda s, h, o: (0, 0))
    tile = pl.BlockSpec((SUB, 2 * size), lambda s, h, o: (s, h))
    return pl.pallas_call(
        functools.partial(attend_back_kernel, size, size**-0.5, span, base),
        out_shape=(
            jax.ShapeDtypeStruct((count, wide), low),
            jax.ShapeDtypeStruct(pairs.shape, f32),
        ),
        grid_spec=pltpu.PrefetchScalarGridSpec(
            num_scalar_prefetch=1,
            grid=grid,
            in_specs=[
                pl.BlockSpec((1, SUB), lambda s, h, o: (0, s)),
                tile,
                tile,
                pl.BlockSpec((1, 1, 2 * SUB), lambda s, h, o: (s * grid[1] + h, 0, 0)),
                whole(pairs.shape),
                whole((size, pairs.shape[0])),
            ],
            out_specs=[tile, whole(pairs.shape)],
            scratch_shapes=[pltpu.VMEM((span, 2 * SUB), f32)],
        ),
        compiler_params=pltpu.CompilerParams(vmem_limit_bytes=56 << 20),
        cost_estimate=pl.CostEstimate(
            flops=10 * count * wide * span, bytes_accessed=16 << 20, transcendentals=count * span * wide // size
        ),
    )(offset, places, queries, grads, logs, pairs, pairs[:, :size].T)


def unit_of(values):
    scale = lax.rsqrt(jnp.mean(values * values, axis=-1, keepdims=True) + epsilon)
    return scale, (values * scale).astype(low)


def unit_back(grad, values, scale):
    unit = values * scale
    return scale * (grad - unit * jnp.mean(grad * unit, axis=-1, keepdims=True))


def geglu(gates, upward):
    return jax.nn.gelu(gates, approximate=True) * upward


def local(
    tokens,
    positions,
    attn_gain,
    query_weight,
    key_weight,
    value_weight,
    out_weight,
    mlp_gain,
    gate_weight,
    up_weight,
    down_weight,
    cotangent,
):
    count = tokens.shape[1]
    size = key_weight.shape[1]
    wide = query_weight.shape[1]
    reach = (WINDOW + count - 2) // count
    chips = (reach + 1) // 2
    base = 2 * chips * count - WINDOW
    gain_one = attn_gain[:, None]
    gain_two = mlp_gain[:, None]

    qkv_shard = (
        jnp.concatenate([query_weight, key_weight, value_weight], 1).astype(f32) * gain_one
    ).astype(low)
    qkv_full = gather_rows(qkv_shard)
    out_full = gather_rows(out_weight.T)
    mlp_shards = (
        (gate_weight.astype(f32) * gain_two).astype(low),
        (up_weight.astype(f32) * gain_two).astype(low),
        down_weight.T,
    )
    gate_full, up_full, down_full = [
        lax.all_gather(
            columns_of_plane(shard).reshape(-1, shard.shape[1] // 8), "z", axis=0, tiled=True
        )
        for shard in mlp_shards
    ]

    inputs = tokens[0].astype(f32)
    scale_one, unit_one = unit_of(inputs)
    qkv = dot(unit_one, qkv_full, (1, 0), low)
    queries = qkv[:, :wide]
    pairs = window_blocks(qkv[:, wide:], chips)
    mixed, logs = attend(queries, pairs, positions, size, base)
    resid = inputs + dot(mixed, out_full, (1, 1))

    scale_two, unit_two = unit_of(resid)
    units = jnp.concatenate(plane_gather(unit_two), 0)
    grad_final = jnp.concatenate(plane_gather(cotangent[0]), 0)
    gates = dot(units, gate_full, (1, 0))
    upward = dot(units, up_full, (1, 0))
    middle = geglu(gates, upward).astype(low)
    finals = dot(middle, down_full, (1, 1), low).reshape(8, count, -1)
    output = resid + plane_scatter([finals[r] for r in range(8)])

    grad_down = dot(grad_final, middle, (0, 0), low)
    grad_middle = dot(grad_final, down_full, (1, 0))
    grad_gates, grad_upward = jax.vjp(geglu, gates, upward)[1](grad_middle)
    grad_gates = grad_gates.astype(low)
    grad_upward = grad_upward.astype(low)
    grad_gate = dot(units, grad_gates, (0, 0), low)
    grad_up = dot(units, grad_upward, (0, 0), low)
    grad_units = (dot(grad_gates, gate_full, (1, 1)) + dot(grad_upward, up_full, (1, 1))).astype(low)
    grad_units = grad_units.reshape(8, count, -1)
    grad_unit_two = plane_scatter([grad_units[r] for r in range(8)])
    grad_resid = cotangent[0].astype(f32) + unit_back(grad_unit_two, resid, scale_two)

    def to_shard(partial):
        column = lax.psum_scatter(partial, "z", scatter_dimension=0, tiled=True)
        rows = column.shape[0] // 8
        split = lax.all_to_all(
            column.reshape(8, rows, -1), PLANE, split_axis=0, concat_axis=0, tiled=True
        )
        return jnp.swapaxes(split, 0, 1).reshape(rows, -1).astype(f32)

    down_sum, gate_sum, up_sum = to_shard(grad_down), to_shard(grad_gate), to_shard(grad_up)
    grad_mlp_gain = jnp.sum(
        gate_weight.astype(f32) * gate_sum + up_weight.astype(f32) * up_sum, axis=1
    )

    grad_attn = grad_resid.astype(low)
    out_sum = scatter_rows(dot(grad_attn, mixed, (0, 0), low))
    grad_mixed = dot(grad_attn, out_full, (1, 0), low)
    grad_queries, grad_pairs = attend_back(queries, grad_mixed, logs, pairs, positions, size, base)
    grad_pair = return_blocks(grad_pairs, chips, count).astype(low)
    grad_qkv = jnp.concatenate([grad_queries, grad_pair], 1)
    qkv_sum = scatter_rows(dot(unit_one, grad_qkv, (0, 0), low))
    grad_unit_one = dot(grad_qkv, qkv_full, (1, 1))
    grad_tokens = grad_resid + unit_back(grad_unit_one, inputs, scale_one)
    query_sum = qkv_sum[:, :wide]
    key_sum = qkv_sum[:, wide : wide + size]
    value_sum = qkv_sum[:, wide + size :]
    grad_attn_gain = (
        jnp.sum(query_weight.astype(f32) * query_sum, axis=1)
        + jnp.sum(key_weight.astype(f32) * key_sum, axis=1)
        + jnp.sum(value_weight.astype(f32) * value_sum, axis=1)
    )
    return (
        output[None],
        grad_tokens[None],
        grad_attn_gain,
        query_sum * gain_one,
        key_sum * gain_one,
        value_sum * gain_one,
        out_sum.T,
        grad_mlp_gain,
        gate_sum * gain_two,
        up_sum * gain_two,
        down_sum.T,
    )


def solution(mesh):
    ctx, fsdp = mesh.shape["ctx"], mesh.shape["fsdp"]
    fine = Mesh(mesh.devices.reshape(ctx // 4, 2, 2, fsdp), ("z", "y", "c", "x"))
    rows = ("z", "y", "c")
    every = ("z", "y", "c", "x")
    return jax.shard_map(
        local,
        mesh=fine,
        in_specs=(
            P("x", rows, None),
            P("x", rows),
            P(every),
            P(every, None),
            P(every, None),
            P(every, None),
            P(None, every),
            P(every),
            P(every, None),
            P(every, None),
            P(None, every),
            P("x", rows, None),
        ),
        out_specs=(
            P("x", rows, None),
            P("x", rows, None),
            P(every),
            P(every, None),
            P(every, None),
            P(every, None),
            P(None, every),
            P(every),
            P(every, None),
            P(every, None),
            P(None, every),
        ),
        check_vma=False,
    )
```

time: 4720 us -> 1300 us (0.28)
  waiting for transfers between devices: 4010 us -> 455 us
  local copies, waits for them, and re-layouts: 25.4 us -> 205 us
  matrix products: 446 us -> 279 us
  Pallas kernels: 0 us -> 79.6 us
  blocking collectives: 92.1 us -> 43.7 us
    reduce_scatter x7 -> x5, waiting for transfers between devices: 3210 us -> 0.03 us  [the longest x2 0.02 us: scatter_rows(): lax.psum_scatter(column, 'z', scatter_dimension=0, tiled=True).astype(f32)]
    all_gather x7 -> x5, waiting for transfers between devices: 752 us -> 0.01 us  [the longest x3 0.01 us: local(): lax.all_gather(columns_of_plane(shard).reshape(-1, shard.shape[1] // 8),...]
    ppermute x12 -> x80, waiting for transfers between devices: 46.5 us -> 391 us  [the longest x74 312 us: swap(): return lax.ppermute(value, axis, [(0, 1), (1, 0)])]
    dot_general x27 -> x15, matrix products: 446 us -> 279 us  [dot(): lax.dot_general(left, right, ((contract[:1], contract[1:]), ((), ())), pr...]
    unnamed x2 -> x0, blocking collectives: 92.1 us -> none
    pallas_call x0 -> x2, Pallas kernels: none -> 79.6 us  [the longest x1 47.6 us: attend_back(): pl.pallas_call(functools.partial(attend_back_kernel, size, size ** (-0.5)...]
    all_to_all x0 -> x4, waiting for transfers between devices: none -> 63.4 us  [the longest x1 45.6 us: columns_of_plane(): return lax.all_to_all(split, PLANE, split_axis=0, concat_axis=0, tiled=True)]
  transfers between devices with their start and end apart: 26 -> 94, of which waited for: 24 -> 31; matrix products, arithmetic and copies ran while one was open for 7% -> 40% of each run, Pallas kernels for 0% -> 6%
where the time goes in v1:
time: 1300 us; the launch traced here: 1280 us
  waiting for transfers between devices  455 us (35%)
  matrix products  279 us (21%)
  local copies, waits for them, and re-layouts  205 us (16%)
  other arithmetic  106 us (8%)
  starting transfers between devices  98.4 us (8%)
  Pallas kernels  79.6 us (6%)
  blocking collectives  43.7 us (3%)
  between operations  15.5 us (1%)
    ppermute x74, waiting for transfers between devices, swap(): return lax.ppermute(value, axis, [(0, 1), (1, 0)])  312 us
    dot_general x15, matrix products, dot(): lax.dot_general(left, right, ((contract[:1], contract[1:]), ((), ())), pr...  279 us
    ppermute x3, waiting for transfers between devices, return_blocks(): lax.ppermute(mine[chips - d].astype(low), ('z', 'y'), [(i + d, i) for i i...  68.1 us
    ppermute x74, starting transfers between devices, swap(): return lax.ppermute(value, axis, [(0, 1), (1, 0)])  66.3 us
    unnamed x116, local copies, waits for them, and re-layouts  61 us
    pallas_call x1, Pallas kernels, attend_back(): pl.pallas_call(functools.partial(attend_back_kernel, size, size ** (-0.5)...  47.6 us
    all_to_all x1, waiting for transfers between devices, columns_of_plane(): return lax.all_to_all(split, PLANE, split_axis=0, concat_axis=0, tiled=True)  45.6 us
    all_to_all x2, blocking collectives, columns_of_plane(): return lax.all_to_all(split, PLANE, split_axis=0, concat_axis=0, tiled=True)  43.7 us
  transfers between devices with their start and end apart: 94, of which 31 were waited for; matrix products, arithmetic and copies ran while one was open for 40% of the time, Pallas kernels for 6%

profile of v1, /device:TPU:0, one launch (start us, length us, event | category | flops | bytes accessed | tf_op | source)
XLA Modules:
  0.0 1282.6 jit_solution(5553507081546580808)
XLA Ops:
  16.6 22.8 %all_to_all.30 = bf16[8,80,960]{2,1,0:T(8,128)(2,1)} all-to-all(bf16[8,80,960]{2,1,0:T(8,128)(2,1)S(1)} %bitcast.277), channel_id=1, replica_groups=mesh['z'=4,'y'=2,'c'=2,'x'=2] {'y','c','x'}, dimensions={0} | all-to-all | bytes 2457600 | tf_op jit(solution)/shard_map/all_to_all | solution.py:95
  41.8 20.9 %all_to_all.31 = bf16[8,80,960]{2,1,0:T(8,128)(2,1)} all-to-all(bf16[8,80,960]{2,1,0:T(8,128)(2,1)S(1)} %bitcast.278), channel_id=1, replica_groups=mesh['z'=4,'y'=2,'c'=2,'x'=2] {'y','c','x'}, dimensions={0} | all-to-all | bytes 2457600 | tf_op jit(solution)/shard_map/all_to_all | solution.py:95
  78.3 45.6 %all-to-all-done.2 = bf16[8,80,960]{2,1,0:T(8,128)(2,1)S(1)} async-done(((bf16[8,80,960]{2,1,0:T(8,128)(2,1)}), bf16[8,80,960]{2,1,0:T(8,128)(2,1)S(1)}, u32[]{:S(2)}, u32[]{:S(2)}) %all-to-all-start.2) | async-done | bytes 1228832 | tf_op jit(solution)/shard_map/all_to_all | solution.py:95
  169.7 48.7 %collective-permute-done.16 = bf16[2,80,2560]{2,1,0:T(8,128)(2,1)S(1)} collective-permute-done((bf16[2,80,2560]{2,1,0:T(8,128)(2,1)S(1)}, bf16[2,80,2560]{2,1,0:T(8,128)(2,1)S(1)}, u32[]{:S(2)}, u32[]{:S(2)}) %collective-permute-start.16) | collective-permute-done | bytes 819232 | tf_op jit(solution)/shard_map/ppermute | solution.py:26
  229.3 15.4 %collective-permute-done.4 = bf16[2,80,3072]{2,1,0:T(8,128)(2,1)S(1)} collective-permute-done((bf16[2,80,3072]{2,1,0:T(8,128)(2,1)S(1)}, bf16[2,80,3072]{2,1,0:T(8,128)(2,1)S(1)}, u32[]{:S(2)}, u32[]{:S(2)}) %collective-permute-start.4) | collective-permute-done | bytes 983072 | tf_op jit(solution)/shard_map/ppermute | solution.py:26
  337.7 32.0 %shard_map.203 = (bf16[384,2560]{1,0:T(8,128)(2,1)S(1)}, f32[15,1,256]{2,1,0:T(1,128)S(1)}) custom-call(s32[1]{0:T(128)} %bitcast.1.offset, s32[1,384]{1,0:T(1,128)S(1)} %copy-done.1, bf16[384,2560]{1,0:T(8,128)(2,1)S(1)} %slice.307.queries, bf16[3072,512]{1,0:T(8,128)(2,1)} %copy.106.pairs, bf16[256,3072]{1,0:T(8,128)(2,1)S(1)} %get-tuple-element.71.values_t), custom_call_target="tpu_custom_call" | custom-call | flops 8556380160 | bytes 8388608 | tf_op jit(solution)/shard_map/pallas_call | solution.py:199
  406.2 28.4 %collective-permute-done.23 = bf16[384,2560]{1,0:T(8,128)(2,1)S(1)} collective-permute-done((bf16[384,2560]{1,0:T(8,128)(2,1)S(1)}, bf16[384,2560]{1,0:T(8,128)(2,1)S(1)}, u32[]{:S(2)}, u32[]{:S(2)}) %collective-permute-start.23) | collective-permute-done | bytes 1966112 | tf_op jit(solution)/shard_map/ppermute | solution.py:26
  443.6 14.5 %collective-permute-done.24 = bf16[192,2560]{1,0:T(8,128)(2,1)S(1)} collective-permute-done((bf16[192,2560]{1,0:T(8,128)(2,1)S(1)}, bf16[192,2560]{1,0:T(8,128)(2,1)S(1)}, u32[]{:S(2)}, u32[]{:S(2)}) %collective-permute-start.24) | collective-permute-done | bytes 983072 | tf_op jit(solution)/shard_map/ppermute | solution.py:26
  468.2 22.2 %fusion.71 = f32[3072,960]{0,1:T(8,128)} fusion(bf16[3072,2560]{1,0:T(8,128)(2,1)} %constant_dynamic-update-slice_fusion.4, bf16[2560,960]{1,0:T(8,128)(2,1)} %all-gather.11.cloned.1.call-done), kind=kOutput, calls=%fused_computation.222 | convolution fusion | flops 15099494400 | bytes 32440320 | tf_op jit(solution)/shard_map/dot_general | solution.py:20
  490.5 21.8 %fusion.70 = f32[3072,960]{0,1:T(8,128)} fusion(bf16[3072,2560]{1,0:T(8,128)(2,1)} %constant_dynamic-update-slice_fusion.4, bf16[2560,960]{1,0:T(8,128)(2,1)} %all-gather.9.cloned.1.call-done), kind=kOutput, calls=%fused_computation.221 | convolution fusion | flops 15099494400 | bytes 32440320 | tf_op jit(solution)/shard_map/dot_general | solution.py:20
  512.3 33.5 %multiply_convert_fusion = (bf16[3072,960]{0,1:T(8,128)(2,1)}, bf16[3072,960]{0,1:T(8,128)(2,1)}, bf16[3072,960]{0,1:T(8,128)(2,1)}) fusion(f32[3072,960]{0,1:T(8,128)} %fusion.70, f32[3072,960]{0,1:T(8,128)} %fusion.71, bf16[3072,2560]{1,0:T(8,128)(2,1)} %constant_dynamic-update-slice_fusion.13, bf16[2560,960]{1,0:T(8,128)(2,1)} %all-gather.13.cloned.1.call-done), kind=kOutput, calls=%fused_computation.13 | convolution fusion | flops 15176171520 | bytes 61931520 | tf_op jit(solution)/shard_map/dot_general | solution.py:20
  545.7 22.0 %convolution_convert_fusion.3 = bf16[2560,960]{0,1:T(8,128)(2,1)} fusion(bf16[3072,960]{0,1:T(8,128)(2,1)} %get-tuple-element.27, bf16[3072,2560]{1,0:T(8,128)(2,1)} %constant_dynamic-update-slice_fusion.13), kind=kOutput, calls=%fused_computation.16 | convolution fusion | flops 15101952000 | bytes 26542080 | tf_op jit(solution)/shard_map/dot_general | solution.py:20
  575.9 24.0 %fusion.72 = f32[3072,2560]{1,0:T(8,128)} fusion(bf16[3072,960]{0,1:T(8,128)(2,1)} %get-tuple-element.26, bf16[2560,960]{1,0:T(8,128)(2,1)} %all-gather.9.cloned.1.call-done), kind=kOutput, calls=%fused_computation.223 | convolution fusion | flops 15099494400 | bytes 42270720 | tf_op jit(solution)/shard_map/dot_general | solution.py:20
  599.9 27.8 %add_convert_fusion = bf16[3072,2560]{1,0:T(8,128)(2,1)} fusion(f32[3072,2560]{1,0:T(8,128)} %fusion.72, bf16[3072,960]{0,1:T(8,128)(2,1)} %get-tuple-element.25, bf16[2560,960]{1,0:T(8,128)(2,1)} %all-gather.11.cloned.1.call-done), kind=kOutput, calls=%fused_computation | convolution fusion | flops 15115223040 | bytes 57999360 | tf_op jit(solution)/shard_map/dot_general | solution.py:20
  634.8 22.7 %convolution_convert_fusion.4 = bf16[2560,960]{0,1:T(8,128)(2,1)} fusion(bf16[3072,960]{0,1:T(8,128)(2,1)} %get-tuple-element.25, bf16[3072,2560]{1,0:T(8,128)(2,1)} %constant_dynamic-update-slice_fusion.4), kind=kOutput, calls=%fused_computation.17 | convolution fusion | flops 15101952000 | bytes 26542080 | tf_op jit(solution)/shard_map/dot_general | solution.py:20
  657.4 20.2 %convolution_convert_fusion.2 = bf16[3072,2560]{1,0:T(8,128)(2,1)} fusion(bf16[3072,960]{0,1:T(8,128)(2,1)S(1)} %bitcast.299, bf16[2560,960]{1,0:T(8,128)(2,1)S(1)} %bitcast.295), kind=kOutput, calls=%fused_computation.3 | convolution fusion | flops 15107358720 | bytes 26542080 | tf_op jit(solution)/shard_map/dot_general | solution.py:20
  733.2 15.8 %collective-permute-done.33 = bf16[192,2560]{1,0:T(8,128)(2,1)S(1)} collective-permute-done((bf16[192,2560]{1,0:T(8,128)(2,1)S(1)}, bf16[192,2560]{1,0:T(8,128)(2,1)S(1)}, u32[]{:S(2)}, u32[]{:S(2)}) %collective-permute-start.33) | collective-permute-done | bytes 983072 | tf_op jit(solution)/shard_map/ppermute | solution.py:26
  751.5 18.5 %collective-permute-done.48 = bf16[192,2560]{1,0:T(8,128)(2,1)S(1)} collective-permute-done((bf16[192,2560]{1,0:T(8,128)(2,1)S(1)}, bf16[192,2560]{1,0:T(8,128)(2,1)S(1)}, u32[]{:S(2)}, u32[]{:S(2)}) %collective-permute-start.48) | collective-permute-done | bytes 983072 | tf_op jit(solution)/shard_map/ppermute | solution.py:26
  772.1 18.9 %collective-permute-done.52 = bf16[192,2560]{1,0:T(8,128)(2,1)S(1)} collective-permute-done((bf16[192,2560]{1,0:T(8,128)(2,1)S(1)}, bf16[192,2560]{1,0:T(8,128)(2,1)S(1)}, u32[]{:S(2)}, u32[]{:S(2)}) %collective-permute-start.52) | collective-permute-done | bytes 983072 | tf_op jit(solution)/shard_map/ppermute | solution.py:26
  795.6 16.5 %collective-permute-done.30 = bf16[192,2560]{1,0:T(8,128)(2,1)S(1)} collective-permute-done((bf16[192,2560]{1,0:T(8,128)(2,1)S(1)}, bf16[192,2560]{1,0:T(8,128)(2,1)S(1)}, u32[]{:S(2)}, u32[]{:S(2)}) %collective-permute-start.30) | collective-permute-done | bytes 983072 | tf_op jit(solution)/shard_map/ppermute | solution.py:26
  812.2 20.9 %collective-permute-done.34 = bf16[192,2560]{1,0:T(8,128)(2,1)S(1)} collective-permute-done((bf16[192,2560]{1,0:T(8,128)(2,1)S(1)}, bf16[192,2560]{1,0:T(8,128)(2,1)S(1)}, u32[]{:S(2)}, u32[]{:S(2)}) %collective-permute-start.34) | collective-permute-done | bytes 983072 | tf_op jit(solution)/shard_map/ppermute | solution.py:26
  848.9 47.6 %shard_map.204 = (bf16[384,2560]{1,0:T(8,128)(2,1)}, f32[3072,512]{1,0:T(8,128)}) custom-call(s32[1]{0:T(128)} %bitcast.1.offset, s32[1,384]{1,0:T(1,128)} %places.3, bf16[384,2560]{1,0:T(8,128)(2,1)} %copy-done, bf16[384,2560]{1,0:T(8,128)(2,1)} %convolution_convert_fusion.6.grads, f32[15,1,256]{2,1,0:T(1,128)} %copy-done.4, ...), custom_call_target="tpu_custom_call" | custom-call | flops 21390950400 | bytes 16777216 | tf_op jit(solution)/shard_map/pallas_call | solution.py:234
  917.8 20.8 %convolution_convert_fusion.5 = bf16[2560,960]{0,1:T(8,128)(2,1)} fusion(bf16[3072,960]{0,1:T(8,128)(2,1)S(1)} %bitcast.297, bf16[3072,2560]{1,0:T(8,128)(2,1)} %constant_dynamic-update-slice_fusion.4), kind=kOutput, calls=%fused_computation.18 | convolution fusion | flops 15101952000 | bytes 26542080 | tf_op jit(solution)/shard_map/dot_general | solution.py:20
  970.4 44.8 %collective-permute-done.57 = bf16[384,512]{1,0:T(8,128)(2,1)S(1)} collective-permute-done((bf16[384,512]{1,0:T(8,128)(2,1)}, bf16[384,512]{1,0:T(8,128)(2,1)S(1)}, u32[]{:S(2)}, u32[]{:S(2)}) %collective-permute-start.57) | collective-permute-done | bytes 393248 | tf_op jit(solution)/shard_map/ppermute | solution.py:121
  1015.2 23.3 %collective-permute-done.58 = bf16[384,512]{1,0:T(8,128)(2,1)} collective-permute-done((bf16[384,512]{1,0:T(8,128)(2,1)}, bf16[384,512]{1,0:T(8,128)(2,1)}, u32[]{:S(2)}, u32[]{:S(2)}) %collective-permute-start.58) | collective-permute-done | bytes 393248 | tf_op jit(solution)/shard_map/ppermute | solution.py:121
  1040.3 11.8 convolution_convert_fusion.1
  1065.0 15.5 %collective-permute-done.77 = bf16[2,80,2560]{2,1,0:T(8,128)(2,1)S(1)} collective-permute-done((bf16[2,80,2560]{2,1,0:T(8,128)(2,1)S(1)}, bf16[2,80,2560]{2,1,0:T(8,128)(2,1)S(1)}, u32[]{:S(2)}, u32[]{:S(2)}) %collective-permute-start.77) | collective-permute-done | bytes 819232 | tf_op jit(solution)/shard_map/ppermute | solution.py:26
  1085.6 12.7 fusion.21
  1104.8 13.3 %collective-permute-done.76 = bf16[2,80,2560]{2,1,0:T(8,128)(2,1)} collective-permute-done((bf16[2,80,2560]{2,1,0:T(8,128)(2,1)}, bf16[2,80,2560]{2,1,0:T(8,128)(2,1)}, u32[]{:S(2)}, u32[]{:S(2)}) %collective-permute-start.76) | collective-permute-done | bytes 819232 | tf_op jit(solution)/shard_map/ppermute | solution.py:26
  1155.0 15.9 %collective-permute-done.69 = bf16[2,80,3072]{2,1,0:T(8,128)(2,1)S(1)} collective-permute-done((bf16[2,80,3072]{2,1,0:T(8,128)(2,1)}, bf16[2,80,3072]{2,1,0:T(8,128)(2,1)S(1)}, u32[]{:S(2)}, u32[]{:S(2)}) %collective-permute-start.69) | collective-permute-done | bytes 983072 | tf_op jit(solution)/shard_map/ppermute | solution.py:26
  1170.9 26.8 %collective-permute-done.66 = bf16[2,80,3072]{2,1,0:T(8,128)(2,1)} collective-permute-done((bf16[2,80,3072]{2,1,0:T(8,128)(2,1)}, bf16[2,80,3072]{2,1,0:T(8,128)(2,1)}, u32[]{:S(2)}, u32[]{:S(2)}) %collective-permute-start.66) | collective-permute-done | bytes 983072 | tf_op jit(solution)/shard_map/ppermute | solution.py:26
  1203.5 12.1 fusion.13
  (416 shorter events, 509.4 us)
Async XLA Ops:
  7.2 67.8 %all-gather.15.cloned.1.call-start = ((), (), s32[]{:S(2)}) async-start(), calls=%async_computation.17 | async-start | bytes 2048000 | tf_op jit(solution)/shard_map/all_gather | solution.py:68
  7.9 133.7 %all-gather.7.cloned.1.call-start = ((), (), s32[]{:S(2)}) async-start(), calls=%async_computation.11 | async-start | bytes 2457600 | tf_op jit(solution)/shard_map/all_gather | solution.py:68
  10.0 458.2 %all-gather.11.cloned.1.call-start = ((), (), s32[]{:S(2)}) async-start(), calls=%async_computation.13 | async-start | bytes 6553600 | tf_op jit(solution)/shard_map/all_gather | solution.py:309
  39.4 451.1 %all-gather.9.cloned.1.call-start = ((), (), s32[]{:S(2)}) async-start(), calls=%async_computation.12 | async-start | bytes 6553600 | tf_op jit(solution)/shard_map/all_gather | solution.py:309
  62.8 62.4 %collective-permute-start.38 = (bf16[384,2560]{1,0:T(8,128)(2,1)}, bf16[384,2560]{1,0:T(8,128)(2,1)}, u32[]{:S(2)}, u32[]{:S(2)}) collective-permute-start(bf16[384,2560]{1,0:T(8,128)(2,1)} %bitcast.52), channel_id=1, source_target_pairs={{0,1},{1,0},{2,3},{3,2},{4,5},{5,4},{6,7},{7,6},{8,9},{9,8},{10,11... | collective-permute-start | bytes 5898248 | tf_op jit(solution)/shard_map/ppermute | solution.py:26
  63.9 63.5 %collective-permute-start.41 = (bf16[384,2560]{1,0:T(8,128)(2,1)}, bf16[384,2560]{1,0:T(8,128)(2,1)}, u32[]{:S(2)}, u32[]{:S(2)}) collective-permute-start(bf16[384,2560]{1,0:T(8,128)(2,1)} %bitcast.52), channel_id=1, source_target_pairs={{0,4},{4,0},{1,5},{5,1},{2,6},{6,2},{3,7},{7,3},{8,12},{12,8},{9,1... | collective-permute-start | bytes 5898248 | tf_op jit(solution)/shard_map/ppermute | solution.py:26
  71.4 440.8 %all-gather.13.cloned.1.call-start = ((), (), s32[]{:S(2)}) async-start(), calls=%async_computation.14 | async-start | bytes 6553600 | tf_op jit(solution)/shard_map/all_gather | solution.py:309
  74.9 86.3 %collective-permute-start.12 = (bf16[4,80,2560]{2,1,0:T(8,128)(2,1)}, bf16[4,80,2560]{2,1,0:T(8,128)(2,1)}, u32[]{:S(2)}, u32[]{:S(2)}) collective-permute-start(bf16[4,80,2560]{2,1,0:T(8,128)(2,1)} %bitcast.29), channel_id=1, source_target_pairs={{0,1},{1,0},{2,3},{3,2},{4,5},{5,4},{6,7},{7,6},{8,9},{9,8},{10,11... | collective-permute-start | bytes 4915208 | tf_op jit(solution)/shard_map/ppermute | solution.py:26
  76.8 82.3 %collective-permute-start.15 = (bf16[4,80,2560]{2,1,0:T(8,128)(2,1)}, bf16[4,80,2560]{2,1,0:T(8,128)(2,1)}, u32[]{:S(2)}, u32[]{:S(2)}) collective-permute-start(bf16[4,80,2560]{2,1,0:T(8,128)(2,1)} %bitcast.29), channel_id=1, source_target_pairs={{0,4},{4,0},{1,5},{5,1},{2,6},{6,2},{3,7},{7,3},{8,12},{12,8},{9,1... | collective-permute-start | bytes 4915208 | tf_op jit(solution)/shard_map/ppermute | solution.py:26
  125.0 1026.4 %reduce-scatter.20.cloned.1.call-start = ((), (), s32[]{:S(2)}) async-start(), calls=%async_computation.20 | async-start | bytes 6553600 | tf_op jit(solution)/shard_map/reduce_scatter | solution.py:345
  141.6 77.5 %collective-permute-start.3 = (bf16[4,80,3072]{2,1,0:T(8,128)(2,1)}, bf16[4,80,3072]{2,1,0:T(8,128)(2,1)}, u32[]{:S(2)}, u32[]{:S(2)}) collective-permute-start(bf16[4,80,3072]{2,1,0:T(8,128)(2,1)} %all-gather.7.cloned.1.call-done), channel_id=1, source_target_pairs={{0,4},{4,0},{1,5},{5,1},{2,6},{6,2},{3,7},{7,3},{8,12},{12,8},{9,1... | collective-permute-start | bytes 5898248 | tf_op jit(solution)/shard_map/ppermute | solution.py:26
  142.1 81.6 %collective-permute-start.1 = (bf16[4,80,3072]{2,1,0:T(8,128)(2,1)}, bf16[4,80,3072]{2,1,0:T(8,128)(2,1)}, u32[]{:S(2)}, u32[]{:S(2)}) collective-permute-start(bf16[4,80,3072]{2,1,0:T(8,128)(2,1)} %all-gather.7.cloned.1.call-done), channel_id=1, source_target_pairs={{0,2},{2,0},{1,3},{3,1},{4,6},{6,4},{5,7},{7,5},{8,10},{10,8},{9,1... | collective-permute-start | bytes 5898248 | tf_op jit(solution)/shard_map/ppermute | solution.py:26
  159.1 61.4 %collective-permute-start = (bf16[4,80,3072]{2,1,0:T(8,128)(2,1)S(1)}, bf16[4,80,3072]{2,1,0:T(8,128)(2,1)S(1)}, u32[]{:S(2)}, u32[]{:S(2)}) collective-permute-start(bf16[4,80,3072]{2,1,0:T(8,128)(2,1)S(1)} %copy-done.22), channel_id=1, source_target_pairs={{0,1},{1,0},{2,3},{3,2},{4,5},{5,4},{6,7},{7,6},{8,9},{9,8},{10,11... | collective-permute-start | bytes 5898248 | tf_op jit(solution)/shard_map/ppermute | solution.py:26
  218.4 175.0 %collective-permute-start.39 = (bf16[384,2560]{1,0:T(8,128)(2,1)}, bf16[384,2560]{1,0:T(8,128)(2,1)}, u32[]{:S(2)}, u32[]{:S(2)}) collective-permute-start(bf16[384,2560]{1,0:T(8,128)(2,1)} %bitcast.52), channel_id=1, source_target_pairs={{0,2},{2,0},{1,3},{3,1},{4,6},{6,4},{5,7},{7,5},{8,10},{10,8},{9,1... | collective-permute-start | bytes 5898248 | tf_op jit(solution)/shard_map/ppermute | solution.py:26
  219.1 86.6 %collective-permute-start.18 = (bf16[4,80,2560]{2,1,0:T(8,128)(2,1)}, bf16[4,80,2560]{2,1,0:T(8,128)(2,1)S(1)}, u32[]{:S(2)}, u32[]{:S(2)}) collective-permute-start(bf16[4,80,2560]{2,1,0:T(8,128)(2,1)} %collective-permute-done.15), channel_id=1, source_target_pairs={{0,2},{2,0},{1,3},{3,1},{4,6},{6,4},{5,7},{7,5},{8,10},{10,8},{9,1... | collective-permute-start | bytes 4915208 | tf_op jit(solution)/shard_map/ppermute | solution.py:26
  284.9 96.7 %collective-permute-start.43 = (bf16[192,2560]{1,0:T(8,128)(2,1)}, bf16[192,2560]{1,0:T(8,128)(2,1)S(1)}, u32[]{:S(2)}, u32[]{:S(2)}) collective-permute-start(bf16[192,2560]{1,0:T(8,128)(2,1)} %slice.331), channel_id=1, source_target_pairs={{0,4},{4,0},{1,5},{5,1},{2,6},{6,2},{3,7},{7,3},{8,12},{12,8},{9,1... | collective-permute-start | bytes 2949128 | tf_op jit(solution)/shard_map/ppermute | solution.py:26
  305.7 85.8 %collective-permute-start.42 = (bf16[192,2560]{1,0:T(8,128)(2,1)}, bf16[192,2560]{1,0:T(8,128)(2,1)}, u32[]{:S(2)}, u32[]{:S(2)}) collective-permute-start(bf16[192,2560]{1,0:T(8,128)(2,1)} %slice.330), channel_id=1, source_target_pairs={{0,1},{1,0},{2,3},{3,2},{4,5},{5,4},{6,7},{7,6},{8,9},{9,8},{10,11... | collective-permute-start | bytes 2949128 | tf_op jit(solution)/shard_map/ppermute | solution.py:26
  308.7 87.8 %collective-permute-start.40 = (bf16[384,2560]{1,0:T(8,128)(2,1)}, bf16[384,2560]{1,0:T(8,128)(2,1)}, u32[]{:S(2)}, u32[]{:S(2)}) collective-permute-start(bf16[384,2560]{1,0:T(8,128)(2,1)} %collective-permute-done.38), channel_id=1, source_target_pairs={{0,2},{2,0},{1,3},{3,1},{4,6},{6,4},{5,7},{7,5},{8,10},{10,8},{9,1... | collective-permute-start | bytes 5898248 | tf_op jit(solution)/shard_map/ppermute | solution.py:26
  310.3 126.9 %collective-permute-start.44 = (bf16[384,2560]{1,0:T(8,128)(2,1)}, bf16[384,2560]{1,0:T(8,128)(2,1)}, u32[]{:S(2)}, u32[]{:S(2)}) collective-permute-start(bf16[384,2560]{1,0:T(8,128)(2,1)} %collective-permute-done.41), channel_id=1, source_target_pairs={{0,2},{2,0},{1,3},{3,1},{4,6},{6,4},{5,7},{7,5},{8,10},{10,8},{9,1... | collective-permute-start | bytes 5898248 | tf_op jit(solution)/shard_map/ppermute | solution.py:26
  575.8 639.8 %reduce-scatter.18.cloned.1.call-start = ((), (), s32[]{:S(2)}) async-start(), calls=%async_computation.19 | async-start | bytes 6553600 | tf_op jit(solution)/shard_map/reduce_scatter | solution.py:345
  633.3 58.4 %collective-permute-start.50 = (bf16[384,2560]{1,0:T(8,128)(2,1)}, bf16[384,2560]{1,0:T(8,128)(2,1)}, u32[]{:S(2)}, u32[]{:S(2)}) collective-permute-start(bf16[384,2560]{1,0:T(8,128)(2,1)} %get-tuple-element.40), channel_id=1, source_target_pairs={{0,2},{2,0},{1,3},{3,1},{4,6},{6,4},{5,7},{7,5},{8,10},{10,8},{9,1... | collective-permute-start | bytes 5898248 | tf_op jit(solution)/shard_map/ppermute | solution.py:26
  691.7 534.3 %reduce-scatter.16.cloned.1.call-start = ((), (), s32[]{:S(2)}) async-start(), calls=%async_computation.18 | async-start | bytes 6553600 | tf_op jit(solution)/shard_map/reduce_scatter | solution.py:345
  729.5 61.5 %collective-permute-start.52 = (bf16[192,2560]{1,0:T(8,128)(2,1)S(1)}, bf16[192,2560]{1,0:T(8,128)(2,1)S(1)}, u32[]{:S(2)}, u32[]{:S(2)}) collective-permute-start(bf16[192,2560]{1,0:T(8,128)(2,1)S(1)} %fusion.38), channel_id=1, source_target_pairs={{0,4},{4,0},{1,5},{5,1},{2,6},{6,2},{3,7},{7,3},{8,12},{12,8},{9,1... | collective-permute-start | bytes 2949128 | tf_op jit(solution)/shard_map/ppermute | solution.py:26
  749.2 62.9 %collective-permute-start.30 = (bf16[192,2560]{1,0:T(8,128)(2,1)S(1)}, bf16[192,2560]{1,0:T(8,128)(2,1)S(1)}, u32[]{:S(2)}, u32[]{:S(2)}) collective-permute-start(bf16[192,2560]{1,0:T(8,128)(2,1)S(1)} %slice.486), channel_id=1, source_target_pairs={{0,1},{1,0},{2,3},{3,2},{4,5},{5,4},{6,7},{7,6},{8,9},{9,8},{10,11... | collective-permute-start | bytes 2949128 | tf_op jit(solution)/shard_map/ppermute | solution.py:26
  770.0 63.0 %collective-permute-start.34 = (bf16[192,2560]{1,0:T(8,128)(2,1)S(1)}, bf16[192,2560]{1,0:T(8,128)(2,1)S(1)}, u32[]{:S(2)}, u32[]{:S(2)}) collective-permute-start(bf16[192,2560]{1,0:T(8,128)(2,1)S(1)} %fusion.42), channel_id=1, source_target_pairs={{0,4},{4,0},{1,5},{5,1},{2,6},{6,2},{3,7},{7,3},{8,12},{12,8},{9,1... | collective-permute-start | bytes 2949128 | tf_op jit(solution)/shard_map/ppermute | solution.py:26
  946.5 295.4 %reduce-scatter.14.cloned.1.call-start = ((), (), s32[]{:S(2)}) async-start(), calls=%async_computation.16 | async-start | bytes 2048000 | tf_op jit(solution)/shard_map/reduce_scatter | solution.py:89
  953.5 61.7 %collective-permute-start.57 = (bf16[384,512]{1,0:T(8,128)(2,1)}, bf16[384,512]{1,0:T(8,128)(2,1)S(1)}, u32[]{:S(2)}, u32[]{:S(2)}) collective-permute-start(bf16[384,512]{1,0:T(8,128)(2,1)} %get-tuple-element.87), channel_id=1, source_target_pairs={{12,0},{16,4},{20,8},{24,12},{28,16},{13,1},{17,5},{21,9},{25,13},... | collective-permute-start | bytes 1179656 | tf_op jit(solution)/shard_map/ppermute | solution.py:121
  954.8 60.4 %collective-permute-start.59 = (bf16[384,512]{1,0:T(8,128)(2,1)}, bf16[384,512]{1,0:T(8,128)(2,1)}, u32[]{:S(2)}, u32[]{:S(2)}) collective-permute-start(bf16[384,512]{1,0:T(8,128)(2,1)} %get-tuple-element.88), channel_id=1, source_target_pairs={{4,0},{8,4},{12,8},{16,12},{20,16},{24,20},{28,24},{5,1},{9,5},{13... | collective-permute-start | bytes 1179656 | tf_op jit(solution)/shard_map/ppermute | solution.py:121
  956.1 82.4 %collective-permute-start.58 = (bf16[384,512]{1,0:T(8,128)(2,1)}, bf16[384,512]{1,0:T(8,128)(2,1)}, u32[]{:S(2)}, u32[]{:S(2)}) collective-permute-start(bf16[384,512]{1,0:T(8,128)(2,1)} %get-tuple-element.89), channel_id=1, source_target_pairs={{8,0},{12,4},{16,8},{20,12},{24,16},{28,20},{9,1},{13,5},{17,9},{2... | collective-permute-start | bytes 1179656 | tf_op jit(solution)/shard_map/ppermute | solution.py:121
  968.9 88.4 %collective-permute-start.75 = (bf16[2,80,2560]{2,1,0:T(8,128)(2,1)}, bf16[2,80,2560]{2,1,0:T(8,128)(2,1)S(1)}, u32[]{:S(2)}, u32[]{:S(2)}) collective-permute-start(bf16[2,80,2560]{2,1,0:T(8,128)(2,1)} %get-tuple-element.85), channel_id=1, source_target_pairs={{0,1},{1,0},{2,3},{3,2},{4,5},{5,4},{6,7},{7,6},{8,9},{9,8},{10,11... | collective-permute-start | bytes 2457608 | tf_op jit(solution)/shard_map/ppermute | solution.py:26
  1151.4 64.2 %all-to-all-start.5 = ((bf16[8,80,960]{2,1,0:T(8,128)(2,1)}), bf16[8,80,960]{2,1,0:T(8,128)(2,1)S(1)}, u32[]{:S(2)}, u32[]{:S(2)}) async-start(bf16[8,80,960]{2,1,0:T(8,128)(2,1)} %bitcast.287), calls=%async_computation.7 | async-start | bytes 2621440 | tf_op jit(solution)/shard_map/all_to_all | solution.py:347
  1155.0 116.9 %reduce-scatter.12.cloned.1.call-start = ((), (), s32[]{:S(2)}) async-start(), calls=%async_computation.15 | async-start | bytes 2457600 | tf_op jit(solution)/shard_map/reduce_scatter | solution.py:89
  (110 other events, 2959.9 us)
Sparse Core Ops, SparseCore 0:
  9.6 40.8 all-gather.14
  52.6 42.4 all-gather.6
  96.6 96.8 all-gather.10
  195.0 102.4 all-gather.8
  299.5 102.7 all-gather.12
  575.9 129.0 reduce-scatter.19
  707.3 111.6 reduce-scatter.17
  946.6 152.0 reduce-scatter.15
  1126.7 42.5 reduce-scatter.13
  1202.9 47.4 reduce-scatter.11

commit v2 on v1

v2 whole, which is shorter than its diff:
```python
import functools

import jax
import jax.numpy as jnp
from jax import lax
from jax.experimental import pallas as pl
from jax.experimental.pallas import tpu as pltpu
from jax.sharding import Mesh, PartitionSpec as P

WINDOW = 2048
SUB = 128
TILE = 512
epsilon = 1e-06
blocked_score = -1e30
PLANE = ("y", "c", "x")
low = jnp.bfloat16
f32 = jnp.float32


def dot(left, right, contract, kind=f32):
    return lax.dot_general(
        left, right, ((contract[:1], contract[1:]), ((), ())), preferred_element_type=f32
    ).astype(kind)


def swap(value, axis):
    return lax.ppermute(value, axis, [(0, 1), (1, 0)])


def plane_gather(own):
    half = own.shape[0] // 2
    by_x = swap(own, "x")
    by_y = swap(own, "y")
    own_c = swap(own, "c")
    diag_top = swap(by_y[:half], "x")
    diag_bottom = swap(by_x[half:], "y")
    by_x_c = swap(by_x, "c")
    by_y_c = swap(by_y, "c")
    diag = jnp.concatenate([diag_top, diag_bottom], 0)
    diag_c = swap(diag, "c")
    return [own, by_x, own_c, by_x_c, by_y, diag, by_y_c, diag_c]


def plane_scatter(parts):
    half = parts[0].shape[0] // 2

    def chip(r):
        return parts[r].astype(f32) + swap(parts[r + 2].astype(low), "c").astype(f32)

    diag = chip(5).astype(low)
    diag_x = swap(diag[:half], "x").astype(f32)
    diag_y = swap(diag[half:], "y").astype(f32)
    to_x, to_y = chip(1), chip(4)
    x_top = swap(to_x[:half].astype(low), "x").astype(f32)
    y_bottom = swap(to_y[half:].astype(low), "y").astype(f32)
    mine = chip(0)
    x_bottom = swap((to_x[half:] + diag_y).astype(low), "x").astype(f32)
    y_top = swap((to_y[:half] + diag_x).astype(low), "y").astype(f32)
    return jnp.concatenate(
        [mine[:half] + x_top + y_top, mine[half:] + x_bottom + y_bottom], 0
    )


def plane_index():
    return (lax.axis_index("y") * 2 + lax.axis_index("c")) * 2 + lax.axis_index("x")


def scatter_rows(partial):
    planes = lax.axis_size("z")
    wide = partial.shape[1]
    rows = partial.shape[0] // (planes * 8)
    blocks = partial.reshape(planes, 8, rows, wide)
    here = plane_index()
    parts = [
        lax.dynamic_slice(blocks, (0, here ^ r, 0, 0), (planes, 1, rows, wide))[:, 0]
        for r in range(8)
    ]
    return plane_scatter(parts).astype(low).reshape(planes * rows, wide)


def after(value, *earlier):
    return lax.optimization_barrier((value,) + earlier)[0]


def window_blocks(pair, chips):
    count = lax.axis_size("z") * lax.axis_size("y")
    same = [
        lax.ppermute(pair, ("z", "y"), [(i, i + d) for i in range(count - d)])
        for d in range(chips, 0, -1)
    ] + [pair]
    return same + [swap(block, "c") for block in same]


def return_blocks(mine, theirs, chips):
    count = lax.axis_size("z") * lax.axis_size("y")
    mine = mine + swap(theirs, "c").astype(f32)
    total = mine[chips]
    for d in range(chips, 0, -1):
        total = total + lax.ppermute(
            mine[chips - d].astype(low), ("z", "y"), [(i + d, i) for i in range(count - d)]
        ).astype(f32)
    return total


def two_heads(block, size):
    return jnp.concatenate([block[:, :size], block[:, size:]], 0)


def side_by_side(rows, size):
    half = rows.shape[0] // 2
    return jnp.concatenate([rows[:half], rows[half:]], 1)


def write_bias(bias, places, span, block):
    key = lax.broadcasted_iota(jnp.int32, (span, SUB), 0) - WINDOW
    query = lax.broadcasted_iota(jnp.int32, (span, SUB), 1)
    age = query - key
    seen = (age <= places) & (age >= 0) & (age < WINDOW)
    value = jnp.where(seen, 0.0, blocked_score).astype(f32)
    bias[:, :SUB] = value
    bias[:, SUB:] = value


def lay_window(core, blocks, window, turned, columns):
    count = blocks[0].shape[0]
    half = len(blocks) // 2
    for i in range(half):
        for which, block in ((core, blocks[i]), (1 - core, blocks[half + i])):
            at = pl.multiple_of((2 * i + which) * count, SUB)
            window[pl.ds(at, count), :] = block[...]
            turned[:, pl.ds(at, count)] = block[:, columns].T


def attend_kernel(size, scale, span, base, core, places, queries, *rest):
    blocks, (mixed, logs, bias, window, turned) = rest[:-5], rest[-5:]
    block = pl.program_id(0)
    count = blocks[0].shape[0]
    start = pl.multiple_of(core[0] * count + base + block * SUB, SUB)

    @pl.when((block == 0) & (pl.program_id(1) == 0))
    def _():
        lay_window(core[0], blocks, window, turned, slice(size, 2 * size))

    @pl.when(pl.program_id(1) == 0)
    def _():
        write_bias(bias, places[...], span, block)

    query = two_heads(queries[...], size)
    keys = window[pl.ds(start, span), :size]
    scores = dot(keys, query, (1, 1)) * scale + bias[...]
    highest = jnp.max(scores, axis=0, keepdims=True)
    expo = jnp.exp(scores - highest)
    total = jnp.sum(expo, axis=0, keepdims=True)
    flat = dot(turned[:, pl.ds(start, span)], expo.astype(low), (1, 0)) / total
    mixed[...] = side_by_side(flat.T, size).astype(low)
    logs[0] = highest + jnp.log(total)


def attend_back_kernel(size, scale, span, base, core, places, queries, grads, logs, *rest):
    blocks, (grad_queries, mine, theirs, bias, window, turned, total) = rest[:-7], rest[-7:]
    block = pl.program_id(0)
    count = blocks[0].shape[0]
    start = pl.multiple_of(core[0] * count + base + block * SUB, SUB)

    @pl.when((block == 0) & (pl.program_id(1) == 0))
    def _():
        lay_window(core[0], blocks, window, turned, slice(0, size))
        total[...] = jnp.zeros_like(total)

    @pl.when(pl.program_id(1) == 0)
    def _():
        write_bias(bias, places[...], span, block)

    query = two_heads(queries[...], size)
    grad = two_heads(grads[...], size)
    keys = window[pl.ds(start, span), :size]
    values = window[pl.ds(start, span), size:]
    probs = jnp.exp(dot(keys, query, (1, 1)) * scale + bias[...] - logs[0])
    total[pl.ds(start, span), size:] += dot(probs.astype(low), grad, (1, 0))
    grad_probs = dot(values, grad, (1, 1))
    inner = jnp.sum(probs * grad_probs, axis=0, keepdims=True)
    grad_scores = (probs * (grad_probs - inner)).astype(low)
    total[pl.ds(start, span), :size] += dot(grad_scores, query, (1, 0)) * scale
    flat = dot(turned[:, pl.ds(start, span)], grad_scores, (1, 0)) * scale
    grad_queries[...] = side_by_side(flat.T, size).astype(low)

    @pl.when((block == pl.num_programs(0) - 1) & (pl.program_id(1) == pl.num_programs(1) - 1))
    def _():
        for i in range(len(blocks) // 2):
            at = pl.multiple_of((2 * i + core[0]) * count, SUB)
            mine[i] = total[pl.ds(at, count), :]
            at = pl.multiple_of((2 * i + 1 - core[0]) * count, SUB)
            theirs[i] = total[pl.ds(at, count), :].astype(low)


def attend(queries, blocks, places, size, base):
    count, wide = queries.shape
    grid = (count // SUB, wide // (2 * size))
    span = WINDOW + SUB
    rows = len(blocks) * count
    core = lax.axis_index("c").astype(jnp.int32)[None]
    tile = pl.BlockSpec((SUB, 2 * size), lambda s, h, o: (s, h))
    return pl.pallas_call(
        functools.partial(attend_kernel, size, size**-0.5, span, base),
        out_shape=(
            jax.ShapeDtypeStruct((count, wide), low),
            jax.ShapeDtypeStruct((grid[0] * grid[1], 1, 2 * SUB), f32),
        ),
        grid_spec=pltpu.PrefetchScalarGridSpec(
            num_scalar_prefetch=1,
            grid=grid,
            in_specs=[pl.BlockSpec((1, SUB), lambda s, h, o: (0, s)), tile]
            + [pl.BlockSpec(block.shape, lambda s, h, o: (0, 0)) for block in blocks],
            out_specs=[tile, pl.BlockSpec((1, 1, 2 * SUB), lambda s, h, o: (s * grid[1] + h, 0, 0))],
            scratch_shapes=[
                pltpu.VMEM((span, 2 * SUB), f32),
                pltpu.VMEM((rows, 2 * size), low),
                pltpu.VMEM((size, rows), low),
            ],
        ),
        compiler_params=pltpu.CompilerParams(vmem_limit_bytes=56 << 20),
        cost_estimate=pl.CostEstimate(
            flops=4 * count * wide * span, bytes_accessed=8 << 20, transcendentals=count * span * wide // size
        ),
    )(core, places, queries, *blocks)


def attend_back(queries, grads, logs, blocks, places, size, base):
    count, wide = queries.shape
    grid = (count // SUB, wide // (2 * size))
    span = WINDOW + SUB
    rows = len(blocks) * count
    half = len(blocks) // 2
    core = lax.axis_index("c").astype(jnp.int32)[None]
    tile = pl.BlockSpec((SUB, 2 * size), lambda s, h, o: (s, h))
    whole = pl.BlockSpec((half, count, 2 * size), lambda s, h, o: (0, 0, 0))
    return pl.pallas_call(
        functools.partial(attend_back_kernel, size, size**-0.5, span, base),
        out_shape=(
            jax.ShapeDtypeStruct((count, wide), low),
            jax.ShapeDtypeStruct((half, count, 2 * size), f32),
            jax.ShapeDtypeStruct((half, count, 2 * size), low),
        ),
        grid_spec=pltpu.PrefetchScalarGridSpec(
            num_scalar_prefetch=1,
            grid=grid,
            in_specs=[
                pl.BlockSpec((1, SUB), lambda s, h, o: (0, s)),
                tile,
                tile,
                pl.BlockSpec((1, 1, 2 * SUB), lambda s, h, o: (s * grid[1] + h, 0, 0)),
            ]
            + [pl.BlockSpec(block.shape, lambda s, h, o: (0, 0)) for block in blocks],
            out_specs=[tile, whole, whole],
            scratch_shapes=[
                pltpu.VMEM((span, 2 * SUB), f32),
                pltpu.VMEM((rows, 2 * size), low),
                pltpu.VMEM((size, rows), low),
                pltpu.VMEM((rows, 2 * size), f32),
            ],
        ),
        compiler_params=pltpu.CompilerParams(vmem_limit_bytes=60 << 20),
        cost_estimate=pl.CostEstimate(
            flops=10 * count * wide * span, bytes_accessed=16 << 20, transcendentals=count * span * wide // size
        ),
    )(core, places, queries, grads, logs, *blocks)


def lay_rows(slots, blocks, full):
    planes, rows, _ = blocks[0].shape
    for r in range(8):
        for plane in range(planes):
            at = pl.multiple_of((plane * 8 + slots[r]) * rows, 16)
            full[pl.ds(at, rows), :] = blocks[r][plane]


def apply_kernel(slots, left, *rest):
    blocks, (out, full) = rest[:8], rest[8:]
    lay_rows(slots, blocks, full)
    out[...] = dot(left[...], full[...], (1, 0), low)


def apply_turned_kernel(slots, left, start, *rest):
    blocks, (out, full) = rest[:8], rest[8:]
    lay_rows(slots, blocks, full)

    @pl.when(pl.program_id(0) == 0)
    def _():
        out[...] = start[...]

    out[...] += dot(left[...], full[...], (1, 1))


def whole_rows(blocks):
    planes, rows, wide = blocks[0].shape
    here = plane_index()
    whole = jnp.zeros((planes, 8, rows, wide), blocks[0].dtype)
    for r, block in enumerate(blocks):
        whole = lax.dynamic_update_slice(whole, block[:, None], (0, here ^ r, 0, 0))
    return whole.reshape(planes * 8 * rows, wide)


def apply_rows(left, blocks, start=None):
    planes, rows, wide = blocks[0].shape
    if rows % 16 or wide % TILE:
        whole = whole_rows(blocks)
        if start is None:
            return dot(left, whole, (1, 0), low)
        return start + dot(left, whole, (1, 1))
    count, deep = left.shape[0], planes * 8 * rows
    slots = (plane_index() ^ jnp.arange(8)).astype(jnp.int32)
    pieces = [pl.BlockSpec((planes, rows, TILE), lambda n, s: (0, 0, n))] * 8
    whole = pl.BlockSpec((count, deep), lambda n, s: (0, 0))
    part = pl.BlockSpec((count, TILE), lambda n, s: (0, n))
    if start is None:
        kernel, given, specs, result = apply_kernel, [left], [whole], part
        shape = jax.ShapeDtypeStruct((count, wide), low)
    else:
        kernel, given, specs, result = apply_turned_kernel, [left, start], [part, whole], whole
        shape = jax.ShapeDtypeStruct((count, deep), f32)
    return pl.pallas_call(
        kernel,
        out_shape=shape,
        grid_spec=pltpu.PrefetchScalarGridSpec(
            num_scalar_prefetch=1,
            grid=(wide // TILE,),
            in_specs=specs + pieces,
            out_specs=result,
            scratch_shapes=[pltpu.VMEM((deep, TILE), low)],
        ),
        compiler_params=pltpu.CompilerParams(vmem_limit_bytes=48 << 20),
        cost_estimate=pl.CostEstimate(
            flops=2 * count * deep * wide, bytes_accessed=2 * deep * wide + 8 * count * deep, transcendentals=0
        ),
    )(slots, *given, *blocks)


def mlp_kernel(part, units, grads, weights, *rest):
    before, (out, grad_units, hidden) = rest[:-3], rest[-3:]
    both = dot(units[...], weights[:, : 2 * part], (1, 0))
    gates, upward = both[:, :part], both[:, part:]
    grad_middle = dot(grads[...], weights[:, 2 * part :], (1, 0))
    slope = 0.7978845608028654
    square = gates * gates
    bend = jnp.tanh(slope * gates * (1.0 + 0.044715 * square))
    half = 0.5 * (1.0 + bend)
    gelu = gates * half
    grad_gelu = half + 0.5 * gates * (1.0 - bend * bend) * (slope * (1.0 + 3 * 0.044715 * square))
    hidden[:, :part] = (grad_middle * upward * grad_gelu).astype(low)
    hidden[:, part : 2 * part] = (grad_middle * gelu).astype(low)
    hidden[:, 2 * part :] = (gelu * upward).astype(low)
    value = dot(hidden[:, 2 * part :], weights[:, 2 * part :], (1, 1))
    if before:
        value = value + before[0][...].astype(f32)
    out[...] = value.astype(low)
    value = dot(hidden[:, : 2 * part], weights[:, : 2 * part], (1, 1))
    if before:
        value = value + before[1][...].astype(f32)
    grad_units[...] = value.astype(low)


def mlp(units, grads, weights, before, rows):
    count, wide = units.shape
    deep = weights.shape[1]
    tile = pl.BlockSpec((rows, wide), lambda i: (i, 0))
    return pl.pallas_call(
        functools.partial(mlp_kernel, deep // 3),
        out_shape=(
            jax.ShapeDtypeStruct((count, wide), low),
            jax.ShapeDtypeStruct((count, wide), low),
            jax.ShapeDtypeStruct((count, deep), low),
        ),
        grid=(count // rows,),
        in_specs=[tile, tile, pl.BlockSpec(weights.shape, lambda i: (0, 0), pipeline_mode=pl.Buffered(1))]
        + [tile] * len(before),
        out_specs=[tile, tile, pl.BlockSpec((rows, deep), lambda i: (i, 0))],
        compiler_params=pltpu.CompilerParams(vmem_limit_bytes=60 << 20),
        cost_estimate=pl.CostEstimate(
            flops=4 * count * wide * deep,
            bytes_accessed=2 * (wide * deep + count * (4 * wide + deep)),
            transcendentals=count * deep // 3,
        ),
    )(units, grads, weights, *before)


def mlp_grads_kernel(units_a, units_b, grads_a, grads_b, hidden_a, hidden_b, out, turned):
    piece = pl.program_id(1)
    count = units_a.shape[0]

    @pl.when(piece == 0)
    def _():
        turned[:, :count] = units_a[...].T
        turned[:, count:] = units_b[...].T

    @pl.when(piece == 2)
    def _():
        turned[:, :count] = grads_a[...].T
        turned[:, count:] = grads_b[...].T

    out[...] = (
        dot(turned[:, :count], hidden_a[...], (1, 0)) + dot(turned[:, count:], hidden_b[...], (1, 0))
    ).astype(low)


def mlp_grads(units, grads, hidden):
    count, wide = units[0].shape
    deep = hidden[0].shape[1]
    part = deep // 3
    rows = 512
    left = pl.BlockSpec((count, rows), lambda d, f: (0, d))
    right = pl.BlockSpec((count, part), lambda d, f: (0, f))
    return pl.pallas_call(
        mlp_grads_kernel,
        out_shape=jax.ShapeDtypeStruct((wide, deep), low),
        grid=(wide // rows, 3),
        in_specs=[left] * 4 + [right] * 2,
        out_specs=pl.BlockSpec((rows, part), lambda d, f: (d, f)),
        scratch_shapes=[pltpu.VMEM((rows, 2 * count), low)],
        compiler_params=pltpu.CompilerParams(vmem_limit_bytes=56 << 20),
        cost_estimate=pl.CostEstimate(
            flops=4 * count * wide * deep,
            bytes_accessed=8 * count * wide + 20 * count * deep + 2 * wide * deep,
            transcendentals=0,
        ),
    )(*units, *grads, *hidden)


def shares(columns):
    tiles = -(-columns // 128)
    few, more = divmod(tiles, 8)
    sizes = [128 * (few + (p < more)) for p in range(8)]
    return [(sum(sizes[:p]), size) for p, size in enumerate(sizes)], 128 * (few + (more > 0))


def unit_of(values):
    scale = lax.rsqrt(jnp.mean(values * values, axis=-1, keepdims=True) + epsilon)
    return scale, (values * scale).astype(low)


def unit_back(grad, values, scale):
    unit = values * scale
    return scale * (grad - unit * jnp.mean(grad * unit, axis=-1, keepdims=True))


def local(
    tokens,
    positions,
    attn_gain,
    query_weight,
    key_weight,
    value_weight,
    out_weight,
    mlp_gain,
    gate_weight,
    up_weight,
    down_weight,
    cotangent,
):
    count = tokens.shape[1]
    size = key_weight.shape[1]
    wide = query_weight.shape[1]
    reach = (WINDOW + count - 2) // count
    chips = (reach + 1) // 2
    base = 2 * chips * count - WINDOW
    gain_one = attn_gain[:, None]
    gain_two = mlp_gain[:, None]

    qkv_shard = (
        jnp.concatenate([query_weight, key_weight, value_weight], 1).astype(f32) * gain_one
    ).astype(low)
    qkv_column = lax.all_gather(qkv_shard, "z", axis=0, tiled=False)
    out_column = lax.all_gather(after(out_weight.T, qkv_column), "z", axis=0, tiled=False)

    spans, share = shares(gate_weight.shape[1])
    parts = 2 if share % 256 == 0 else 1
    part = share // parts
    mlp_shards = (
        (gate_weight.astype(f32) * gain_two).astype(low),
        (up_weight.astype(f32) * gain_two).astype(low),
        down_weight.T,
    )
    split = [
        jnp.stack([jnp.pad(shard[:, at : at + n], ((0, 0), (0, share - n))) for at, n in spans])
        for shard in mlp_shards
    ]
    mlp_columns = [
        lax.all_to_all(
            jnp.concatenate([whole[:, :, k * part : (k + 1) * part] for whole in split], 2),
            PLANE,
            split_axis=0,
            concat_axis=0,
            tiled=True,
        ).reshape(-1, 3 * part)
        for k in range(parts)
    ]
    mlp_full = []
    earlier = out_column
    for column in mlp_columns:
        earlier = lax.all_gather(after(column, earlier), "z", axis=0, tiled=True)
        mlp_full.append(earlier)

    qkv_blocks = plane_gather(qkv_column)
    inputs = tokens[0].astype(f32)
    scale_one, unit_one = unit_of(inputs)
    qkv = apply_rows(unit_one, qkv_blocks)
    out_blocks = plane_gather(after(out_column, qkv_blocks[7]))
    queries = qkv[:, :wide]
    pairs = window_blocks(qkv[:, wide:], chips)
    mixed, logs = attend(queries, pairs, positions, size, base)
    resid = apply_rows(mixed, out_blocks, inputs)

    scale_two, unit_two = unit_of(resid)
    finals = plane_gather(after(cotangent[0], out_blocks[7]))
    units = plane_gather(unit_two)
    far, near = (5, 7, 1, 3), (4, 6, 0, 2)
    units = [jnp.concatenate([units[r] for r in half], 0) for half in (far, near)]
    finals = [jnp.concatenate([finals[r] for r in half], 0) for half in (far, near)]
    sums = [(), ()]
    hidden = []
    for k in range(parts):
        results = [None, None]
        for half in (1, 0) if k < parts - 1 else (0, 1):
            results[half] = mlp(units[half], finals[half], mlp_full[k], sums[half], count)
        sums = [result[:2] for result in results]
        hidden.append([result[2] for result in results])

    def by_device(index):
        rows = [sums[half][index].reshape(4, count, -1) for half in (0, 1)]
        found = {r: rows[half][i] for half, group in enumerate((far, near)) for i, r in enumerate(group)}
        return [found[r] for r in range(8)]

    grad_unit_two = plane_scatter(by_device(1))
    grad_resid = cotangent[0].astype(f32) + unit_back(grad_unit_two, resid, scale_two)

    columns = []
    earlier = mlp_full[-1]
    for k in range(parts):
        partial = mlp_grads(units, finals, hidden[k])
        earlier = lax.psum_scatter(after(partial, earlier), "z", scatter_dimension=0, tiled=True)
        columns.append(earlier)

    grad_attn = grad_resid.astype(low)
    grad_mixed = apply_rows(grad_attn, out_blocks)
    out_scattered = scatter_rows(dot(grad_attn, mixed, (0, 0), low))
    grad_queries, mine, theirs = attend_back(queries, grad_mixed, logs, pairs, positions, size, base)
    grad_pair = return_blocks(mine, theirs, chips).astype(low)
    grad_qkv = jnp.concatenate([grad_queries, grad_pair], 1)
    qkv_scattered = scatter_rows(dot(unit_one, grad_qkv, (0, 0), low))
    grad_unit_one = apply_rows(grad_qkv, qkv_blocks, jnp.zeros_like(inputs))
    grad_tokens = grad_resid + unit_back(grad_unit_one, inputs, scale_one)

    def over_z(column, earlier):
        return lax.psum_scatter(after(column, earlier), "z", scatter_dimension=0, tiled=True)

    out_low = over_z(out_scattered, earlier)
    qkv_low = over_z(qkv_scattered, out_low)
    out_sum = out_low.astype(f32)
    qkv_sum = qkv_low.astype(f32)
    query_sum = qkv_sum[:, :wide]
    key_sum = qkv_sum[:, wide : wide + size]
    value_sum = qkv_sum[:, wide + size :]
    grad_attn_gain = (
        jnp.sum(query_weight.astype(f32) * query_sum, axis=1)
        + jnp.sum(key_weight.astype(f32) * key_sum, axis=1)
        + jnp.sum(value_weight.astype(f32) * value_sum, axis=1)
    )
    output = resid + plane_scatter([after(value, qkv_scattered) for value in by_device(0)])

    whole = [
        lax.all_to_all(
            column.reshape(8, -1, 3 * part), PLANE, split_axis=0, concat_axis=0, tiled=True
        )
        for column in columns
    ]

    def joined(which):
        pieces = []
        for p, (_, n) in enumerate(spans):
            for k in range(parts):
                width = min(part, n - k * part)
                if width > 0:
                    pieces.append(whole[k][p, :, which * part : which * part + width])
        return jnp.concatenate(pieces, 1).astype(f32)

    gate_sum, up_sum, down_sum = joined(0), joined(1), joined(2)
    grad_mlp_gain = jnp.sum(
        gate_weight.astype(f32) * gate_sum + up_weight.astype(f32) * up_sum, axis=1
    )
    return (
        output[None],
        grad_tokens[None],
        grad_attn_gain,
        query_sum * gain_one,
        key_sum * gain_one,
        value_sum * gain_one,
        out_sum.T,
        grad_mlp_gain,
        gate_sum * gain_two,
        up_sum * gain_two,
        down_sum.T,
    )


def solution(mesh):
    ctx, fsdp = mesh.shape["ctx"], mesh.shape["fsdp"]
    fine = Mesh(mesh.devices.reshape(ctx // 4, 2, 2, fsdp), ("z", "y", "c", "x"))
    rows = ("z", "y", "c")
    every = ("z", "y", "c", "x")
    return jax.shard_map(
        local,
        mesh=fine,
        in_specs=(
            P("x", rows, None),
            P("x", rows),
            P(every),
            P(every, None),
            P(every, None),
            P(every, None),
            P(None, every),
            P(every),
            P(every, None),
            P(every, None),
            P(None, every),
            P("x", rows, None),
        ),
        out_specs=(
            P("x", rows, None),
            P("x", rows, None),
            P(every),
            P(every, None),
            P(every, None),
            P(every, None),
            P(None, every),
            P(every),
            P(every, None),
            P(every, None),
            P(None, every),
        ),
        check_vma=False,
    )
```

time: 1300 us -> 1320 us (1.015)
  Pallas kernels: 79.6 us -> 359 us
  matrix products: 279 us -> 19.1 us
  waiting for transfers between devices: 455 us -> 553 us
  local copies, waits for them, and re-layouts: 205 us -> 126 us
  blocking collectives: 43.7 us -> 0 us
  starting transfers between devices: 98.4 us -> 119 us
  other arithmetic: 106 us -> 120 us
    pallas_call x0 -> x10, Pallas kernels: none -> 278 us  [the longest x4 132 us: mlp(): pl.pallas_call(functools.partial(mlp_kernel, deep // 3), out_shape=(jax.S...]
    dot_general x15 -> x2, matrix products: 279 us -> 19.1 us  [dot(): lax.dot_general(left, right, ((contract[:1], contract[1:]), ((), ())), pr...]
    all_gather x5 -> x4, waiting for transfers between devices: 0.01 us -> 60.4 us  [the longest x1 39.3 us: local(): qkv_column = lax.all_gather(qkv_shard, 'z', axis=0, tiled=False)]
    ppermute x3, waiting for transfers between devices: 68.1 us -> 18 us  [return_blocks(): lax.ppermute(mine[chips - d].astype(low), ('z', 'y'), [(i + d, i) for i i...]
    all_to_all x2 -> x0, blocking collectives: 43.7 us -> none  [columns_of_plane(): return lax.all_to_all(split, PLANE, split_axis=0, concat_axis=0, tiled=True)]
    reduce_scatter x5 -> x4, waiting for transfers between devices: 0.03 us -> 40 us  [the longest x2 40 us: over_z(): lax.psum_scatter(after(column, earlier), 'z', scatter_dimension=0, tiled=...]
    dynamic_update_slice x16 -> x0, local copies, waits for them, and re-layouts: 32.4 us -> none  [gather_rows(): whole = lax.dynamic_update_slice(whole, block[:, None], (0, here ^ r, 0, 0))]
    ppermute x74 -> x77, waiting for transfers between devices: 312 us -> 340 us  [swap(): return lax.ppermute(value, axis, [(0, 1), (1, 0)])]
  transfers between devices with their start and end apart: 94 -> 95, of which waited for: 31 -> 31; matrix products, arithmetic and copies ran while one was open for 40% -> 18% of each run, Pallas kernels for 6% -> 25%
where the time goes in v2:
time: 1320 us; the launch traced here: 1310 us
  waiting for transfers between devices  553 us (42%)
  Pallas kernels  359 us (27%)
  local copies, waits for them, and re-layouts  126 us (10%)
  other arithmetic  120 us (9%)
  starting transfers between devices  119 us (9%)
  matrix products  19.1 us (1%)
  between operations  15.7 us (1%)
    ppermute x77, waiting for transfers between devices, swap(): return lax.ppermute(value, axis, [(0, 1), (1, 0)])  340 us
    pallas_call x4, Pallas kernels, mlp(): pl.pallas_call(functools.partial(mlp_kernel, deep // 3), out_shape=(jax.S...  132 us
    pallas_call x2, Pallas kernels, mlp_grads(): pl.pallas_call(mlp_grads_kernel, out_shape=jax.ShapeDtypeStruct((wide, de...  93.9 us
    ppermute x77, starting transfers between devices, swap(): return lax.ppermute(value, axis, [(0, 1), (1, 0)])  88.3 us
    unnamed x196, local copies, waits for them, and re-layouts  55.7 us
    pallas_call x4, Pallas kernels, apply_rows(): pl.pallas_call(kernel, out_shape=shape, grid_spec=pltpu.PrefetchScalarGri...  51.8 us
    pallas_call x1, Pallas kernels, attend_back(): pl.pallas_call(functools.partial(attend_back_kernel, size, size ** (-0.5)...  47 us
    reduce_scatter x2, waiting for transfers between devices, over_z(): lax.psum_scatter(after(column, earlier), 'z', scatter_dimension=0, tiled=...  40 us
  transfers between devices with their start and end apart: 95, of which 31 were waited for; matrix products, arithmetic and copies ran while one was open for 18% of the time, Pallas kernels for 25%

profile of v2, /device:TPU:0, one launch (start us, length us, event | category | flops | bytes accessed | tf_op | source)
XLA Modules:
  0.0 1311.7 jit_solution(15559449871253445134)
XLA Ops:
  17.2 39.3 %all-gather.6.cloned.1.call-done.rest_0_ = bf16[4,80,3072]{2,1,0:T(8,128)(2,1)} async-done(((bf16[1,80,3072]{2,1,0:T(8,128)(2,1)}), bf16[4,80,3072]{2,1,0:T(8,128)(2,1)}) %all-gather.6.cloned.1.call-update) | async-done | bytes 1966096 | tf_op jit(solution)/shard_map/all_gather | solution.py:471
  72.2 30.3 %collective-permute-done.3.rest_4_ = bf16[4,80,3072]{2,1,0:T(8,128)(2,1)} collective-permute-done((bf16[4,80,3072]{2,1,0:T(8,128)(2,1)}, bf16[4,80,3072]{2,1,0:T(8,128)(2,1)}, u32[]{:S(2)}, u32[]{:S(2)}) %collective-permute-start.3) | collective-permute-done | bytes 1966112 | tf_op jit(solution)/shard_map/ppermute | solution.py:27
  108.7 17.1 %all-to-all-done.1 = bf16[8,80,1536]{2,1,0:T(8,128)(2,1)} async-done(((bf16[8,80,1536]{2,1,0:T(8,128)(2,1)}), bf16[8,80,1536]{2,1,0:T(8,128)(2,1)}, u32[]{:S(2)}, u32[]{:S(2)}) %all-to-all-start.1) | async-done | bytes 1966112 | tf_op jit(solution)/shard_map/all_to_all | solution.py:487
  125.8 20.6 %collective-permute-done.4 = bf16[2,80,3072]{2,1,0:T(8,128)(2,1)} collective-permute-done((bf16[2,80,3072]{2,1,0:T(8,128)(2,1)}, bf16[2,80,3072]{2,1,0:T(8,128)(2,1)}, u32[]{:S(2)}, u32[]{:S(2)}) %collective-permute-start.4) | collective-permute-done | bytes 983072 | tf_op jit(solution)/shard_map/ppermute | solution.py:27
  159.0 33.4 %collective-permute-done.18.rest_4_ = bf16[4,80,2560]{2,1,0:T(8,128)(2,1)} collective-permute-done((bf16[4,80,2560]{2,1,0:T(8,128)(2,1)}, bf16[4,80,2560]{2,1,0:T(8,128)(2,1)}, u32[]{:S(2)}, u32[]{:S(2)}) %collective-permute-start.18) | collective-permute-done | bytes 1638432 | tf_op jit(solution)/shard_map/ppermute | solution.py:27
  230.7 16.1 %collective-permute-done.9.rest_1_ = bf16[384,512]{1,0:T(8,128)(2,1)S(1)} collective-permute-done((bf16[384,512]{1,0:T(8,128)(2,1)S(1)}, bf16[384,512]{1,0:T(8,128)(2,1)S(1)}, u32[]{:S(2)}, u32[]{:S(2)}) %collective-permute-start.9) | collective-permute-done | bytes 393248 | tf_op jit(solution)/shard_map/ppermute | solution.py:88
  253.8 34.0 %shard_map.204 = (bf16[384,2560]{1,0:T(8,128)(2,1)}, f32[15,1,256]{2,1,0:T(1,128)}) custom-call(s32[1]{0:T(128)} %bitcast.core, s32[1,384]{1,0:T(1,128)} %places.3, bf16[384,2560]{1,0:T(8,128)(2,1)} %slice.601.queries, bf16[384,512]{1,0:T(8,128)(2,1)} %copy-done.65, bf16[384,512]{1,0:T(8,128)(2,1)} %copy-done.66, bf16[384,512]{1,0:T(8,128)(2,1)} %copy-done.67, ...), custom_call_target="tpu_custom_call" | custom-call | flops 8556380160 | bytes 8388608 | tf_op jit(solution)/shard_map/pallas_call | solution.py:203
  306.1 17.8 %collective-permute-start.23 = (bf16[384,2560]{1,0:T(8,128)(2,1)}, bf16[384,2560]{1,0:T(8,128)(2,1)}, u32[]{:S(2)}, u32[]{:S(2)}) collective-permute-start(bf16[384,2560]{1,0:T(8,128)(2,1)} %multiply_convert_fusion), channel_id=1, source_target_pairs={{0,4},{4,0},{1,5},{5,1},{2,6},{6,2},{3,7},{7,3},{8,12},{12,8},{9,1... | collective-permute-start | bytes 5898248 | tf_op jit(solution)/shard_map/ppermute | solution.py:27
  331.8 36.0 %collective-permute-done.23 = bf16[384,2560]{1,0:T(8,128)(2,1)} collective-permute-done((bf16[384,2560]{1,0:T(8,128)(2,1)}, bf16[384,2560]{1,0:T(8,128)(2,1)}, u32[]{:S(2)}, u32[]{:S(2)}) %collective-permute-start.23) | collective-permute-done | bytes 1966112 | tf_op jit(solution)/shard_map/ppermute | solution.py:27
  370.6 39.4 %collective-permute-done.26 = bf16[384,2560]{1,0:T(8,128)(2,1)} collective-permute-done((bf16[384,2560]{1,0:T(8,128)(2,1)}, bf16[384,2560]{1,0:T(8,128)(2,1)}, u32[]{:S(2)}, u32[]{:S(2)}) %collective-permute-start.26) | collective-permute-done | bytes 1966112 | tf_op jit(solution)/shard_map/ppermute | solution.py:27
  434.2 20.1 %collective-permute-done.30 = bf16[192,2560]{1,0:T(8,128)(2,1)} collective-permute-done((bf16[192,2560]{1,0:T(8,128)(2,1)}, bf16[192,2560]{1,0:T(8,128)(2,1)}, u32[]{:S(2)}, u32[]{:S(2)}) %collective-permute-start.30) | collective-permute-done | bytes 983072 | tf_op jit(solution)/shard_map/ppermute | solution.py:27
  455.6 18.6 %collective-permute-done.35 = bf16[192,2560]{1,0:T(8,128)(2,1)S(1)} collective-permute-done((bf16[192,2560]{1,0:T(8,128)(2,1)}, bf16[192,2560]{1,0:T(8,128)(2,1)S(1)}, u32[]{:S(2)}, u32[]{:S(2)}) %collective-permute-start.35) | collective-permute-done | bytes 983072 | tf_op jit(solution)/shard_map/ppermute | solution.py:27
  479.8 16.9 %collective-permute-done.37 = bf16[192,2560]{1,0:T(8,128)(2,1)S(1)} collective-permute-done((bf16[192,2560]{1,0:T(8,128)(2,1)S(1)}, bf16[192,2560]{1,0:T(8,128)(2,1)S(1)}, u32[]{:S(2)}, u32[]{:S(2)}) %collective-permute-start.37) | collective-permute-done | bytes 983072 | tf_op jit(solution)/shard_map/ppermute | solution.py:27
  521.4 31.8 %shard_map.208 = (bf16[1536,2560]{1,0:T(8,128)(2,1)}, bf16[1536,2560]{1,0:T(8,128)(2,1)}, bf16[1536,1536]{1,0:T(8,128)(2,1)}) custom-call(bf16[1536,2560]{1,0:T(8,128)(2,1)} %copy-done.58, bf16[1536,2560]{1,0:T(8,128)(2,1)} %constant_dynamic-update-slice_fusion.37.grads.grads_a, bf16[2560,1536]{1,0:T(8,128)(2,1)} %all-gather.8.cloned.1.call-done.weights), custom_call_target="tpu_custom_call" | custom-call | flops 24159191040 | bytes 44040192 | tf_op jit(solution)/shard_map/pallas_call | solution.py:366
  553.2 31.9 %shard_map.206 = (bf16[1536,2560]{1,0:T(8,128)(2,1)}, bf16[1536,2560]{1,0:T(8,128)(2,1)}, bf16[1536,1536]{1,0:T(8,128)(2,1)}) custom-call(bf16[1536,2560]{1,0:T(8,128)(2,1)} %pad_maximum_fusion.units.units_b, bf16[1536,2560]{1,0:T(8,128)(2,1)} %copy-done.53, bf16[2560,1536]{1,0:T(8,128)(2,1)} %all-gather.8.cloned.1.call-done.weights), custom_call_target="tpu_custom_call" | custom-call | flops 24159191040 | bytes 44040192 | tf_op jit(solution)/shard_map/pallas_call | solution.py:366
  585.1 21.2 %all-gather.10.cloned.1.call-done.weights = bf16[2560,1536]{1,0:T(8,128)(2,1)} async-done(((bf16[640,1536]{1,0:T(8,128)(2,1)}), bf16[2560,1536]{1,0:T(8,128)(2,1)}) %all-gather.10.cloned.1.call-update) | async-done | bytes 7864336 | tf_op jit(solution)/shard_map/all_gather | solution.py:499
  606.3 34.3 %shard_map.209 = (bf16[1536,2560]{1,0:T(8,128)(2,1)}, bf16[1536,2560]{1,0:T(8,128)(2,1)}, bf16[1536,1536]{1,0:T(8,128)(2,1)}) custom-call(bf16[1536,2560]{1,0:T(8,128)(2,1)} %copy-done.58, bf16[1536,2560]{1,0:T(8,128)(2,1)} %constant_dynamic-update-slice_fusion.37.grads.grads_a, bf16[2560,1536]{1,0:T(8,128)(2,1)} %all-gather.10.cloned.1.call-done.weights, ...), custom_call_target="tpu_custom_call" | custom-call | flops 24159191040 | bytes 44040192 | tf_op jit(solution)/shard_map/pallas_call | solution.py:366
  645.6 34.2 %shard_map.207 = (bf16[1536,2560]{1,0:T(8,128)(2,1)}, bf16[1536,2560]{1,0:T(8,128)(2,1)}, bf16[1536,1536]{1,0:T(8,128)(2,1)}) custom-call(bf16[1536,2560]{1,0:T(8,128)(2,1)} %pad_maximum_fusion.units.units_b, bf16[1536,2560]{1,0:T(8,128)(2,1)} %copy-done.53, bf16[2560,1536]{1,0:T(8,128)(2,1)} %all-gather.10.cloned.1.call-done.weights, ...), custom_call_target="tpu_custom_call" | custom-call | flops 24159191040 | bytes 44040192 | tf_op jit(solution)/shard_map/pallas_call | solution.py:366
  684.6 46.8 %shard_map.214 = bf16[2560,1536]{1,0:T(8,128)(2,1)} custom-call(bf16[1536,2560]{1,0:T(8,128)(2,1)} %copy-done.58, bf16[1536,2560]{1,0:T(8,128)(2,1)} %pad_maximum_fusion.units.units_b, bf16[1536,2560]{1,0:T(8,128)(2,1)} %constant_dynamic-update-slice_fusion.37.grads.grads_a, bf16[1536,2560]{1,0:T(8,128)(2,1)} %copy-done.53, ...), custom_call_target="tpu_custom_call" | custom-call | flops 24159191040 | bytes 86507520 | tf_op jit(solution)/shard_map/pallas_call | solution.py:412
  766.2 47.1 %shard_map.213 = bf16[2560,1536]{1,0:T(8,128)(2,1)} custom-call(bf16[1536,2560]{1,0:T(8,128)(2,1)} %copy-done.58, bf16[1536,2560]{1,0:T(8,128)(2,1)} %pad_maximum_fusion.units.units_b, bf16[1536,2560]{1,0:T(8,128)(2,1)} %constant_dynamic-update-slice_fusion.37.grads.grads_a, bf16[1536,2560]{1,0:T(8,128)(2,1)} %copy-done.53, ...), custom_call_target="tpu_custom_call" | custom-call | flops 24159191040 | bytes 86507520 | tf_op jit(solution)/shard_map/pallas_call | solution.py:412
  834.3 47.0 %shard_map.211 = (bf16[384,2560]{1,0:T(8,128)(2,1)}, f32[4,384,512]{2,1,0:T(8,128)}, bf16[4,384,512]{2,1,0:T(8,128)(2,1)}) custom-call(s32[1]{0:T(128)} %bitcast.core, s32[1,384]{1,0:T(1,128)} %places.3, bf16[384,2560]{1,0:T(8,128)(2,1)} %slice.601.queries, bf16[384,2560]{1,0:T(8,128)(2,1)} %shard_map.210.grads, f32[15,1,256]{2,1,0:T(1,128)} %get-tuple-element.58.logs, ...), custom_call_target="tpu_custom_call" | custom-call | flops 21390950400 | bytes 16777216 | tf_op jit(solution)/shard_map/pallas_call | solution.py:237
  904.3 16.0 %collective-permute-done.50 = bf16[384,512]{1,0:T(8,128)(2,1)S(1)} collective-permute-done((bf16[384,512]{1,0:T(8,128)(2,1)S(1)}, bf16[384,512]{1,0:T(8,128)(2,1)S(1)}, u32[]{:S(2)}, u32[]{:S(2)}) %collective-permute-start.50) | collective-permute-done | bytes 393248 | tf_op jit(solution)/shard_map/ppermute | solution.py:99
  969.5 17.4 %collective-permute-start.60 = (bf16[2,80,3072]{2,1,0:T(8,128)(2,1)S(1)}, bf16[2,80,3072]{2,1,0:T(8,128)(2,1)S(1)}, u32[]{:S(2)}, u32[]{:S(2)}) collective-permute-start(bf16[2,80,3072]{2,1,0:T(8,128)(2,1)S(1)} %get-tuple-element.176), channel_id=1, source_target_pairs={{0,4},{4,0},{1,5},{5,1},{2,6},{6,2},{3,7},{7,3},{8,12},{12,8},{9,1... | collective-permute-start | bytes 2949128 | tf_op jit(solution)/shard_map/ppermute | solution.py:27
  995.4 14.1 %collective-permute-done.60 = bf16[2,80,3072]{2,1,0:T(8,128)(2,1)S(1)} collective-permute-done((bf16[2,80,3072]{2,1,0:T(8,128)(2,1)S(1)}, bf16[2,80,3072]{2,1,0:T(8,128)(2,1)S(1)}, u32[]{:S(2)}, u32[]{:S(2)}) %collective-permute-start.60) | collective-permute-done | bytes 983072 | tf_op jit(solution)/shard_map/ppermute | solution.py:27
  1011.7 19.2 %collective-permute-done.58 = bf16[2,80,3072]{2,1,0:T(8,128)(2,1)S(1)} collective-permute-done((bf16[2,80,3072]{2,1,0:T(8,128)(2,1)S(1)}, bf16[2,80,3072]{2,1,0:T(8,128)(2,1)S(1)}, u32[]{:S(2)}, u32[]{:S(2)}) %collective-permute-start.58) | collective-permute-done | bytes 983072 | tf_op jit(solution)/shard_map/ppermute | solution.py:27
  1037.3 14.7 %collective-permute-done.55 = bf16[2,80,3072]{2,1,0:T(8,128)(2,1)S(1)} collective-permute-done((bf16[2,80,3072]{2,1,0:T(8,128)(2,1)S(1)}, bf16[2,80,3072]{2,1,0:T(8,128)(2,1)S(1)}, u32[]{:S(2)}, u32[]{:S(2)}) %collective-permute-start.55) | collective-permute-done | bytes 983072 | tf_op jit(solution)/shard_map/ppermute | solution.py:27
  1055.1 18.0 %collective-permute-done.61 = bf16[2,80,3072]{2,1,0:T(8,128)(2,1)S(1)} collective-permute-done((bf16[2,80,3072]{2,1,0:T(8,128)(2,1)S(1)}, bf16[2,80,3072]{2,1,0:T(8,128)(2,1)S(1)}, u32[]{:S(2)}, u32[]{:S(2)}) %collective-permute-start.61) | collective-permute-done | bytes 983072 | tf_op jit(solution)/shard_map/ppermute | solution.py:27
  1079.9 15.2 %shard_map.212 = f32[384,2560]{1,0:T(8,128)} custom-call(s32[8]{0:T(128)S(1)} %copy-done.5, bf16[384,3072]{1,0:T(8,128)(2,1)} %pad_maximum_fusion.2.left, f32[384,2560]{1,0:T(8,128)} %broadcast_in_dim.10.start, bf16[4,80,3072]{2,1,0:T(8,128)(2,1)} %all-gather.6.cloned.1.call-done.rest_0_, bf16[4,80,3072]{2,1,0:T(8,128)(2,1)S(1)} %collective-permute-done.rest_1_, ...), custom_call_target="tpu_custom_call" | custom-call | flops 6039797760 | bytes 23592960 | tf_op jit(solution)/shard_map/pallas_call | solution.py:321
  1120.9 16.5 %collective-permute-done.70 = bf16[192,2560]{1,0:T(8,128)(2,1)S(1)} collective-permute-done((bf16[192,2560]{1,0:T(8,128)(2,1)S(1)}, bf16[192,2560]{1,0:T(8,128)(2,1)S(1)}, u32[]{:S(2)}, u32[]{:S(2)}) %collective-permute-start.70) | collective-permute-done | bytes 983072 | tf_op jit(solution)/shard_map/ppermute | solution.py:27
  1143.3 18.7 %collective-permute-done.68 = bf16[192,2560]{1,0:T(8,128)(2,1)} collective-permute-done((bf16[192,2560]{1,0:T(8,128)(2,1)}, bf16[192,2560]{1,0:T(8,128)(2,1)}, u32[]{:S(2)}, u32[]{:S(2)}) %collective-permute-start.68) | collective-permute-done | bytes 983072 | tf_op jit(solution)/shard_map/ppermute | solution.py:27
  1171.2 31.3 %all-to-all-done.2 = bf16[8,80,1536]{2,1,0:T(8,128)(2,1)S(1)} async-done(((bf16[8,80,1536]{2,1,0:T(8,128)(2,1)}), bf16[8,80,1536]{2,1,0:T(8,128)(2,1)S(1)}, u32[]{:S(2)}, u32[]{:S(2)}) %all-to-all-start.2) | async-done | bytes 1966112 | tf_op jit(solution)/shard_map/all_to_all | solution.py:570
  1270.8 30.2 %reduce-scatter.11.cloned.1.call-done = bf16[80,3072]{1,0:T(8,128)(2,1)} async-done(((bf16[320,3072]{1,0:T(8,128)(2,1)}), bf16[80,3072]{1,0:T(8,128)(2,1)}) %reduce-scatter.11.cloned.1.call-update) | async-done | bytes 491536 | tf_op jit(solution)/shard_map/reduce_scatter | solution.py:553
  (474 shorter events, 450.8 us)
Async XLA Ops:
  9.3 116.4 %all-gather.12.cloned.1.call-start = ((), (), s32[]{:S(2)}) async-start(), calls=%async_computation.15 | async-start | bytes 2048000 | tf_op jit(solution)/shard_map/all_gather | solution.py:472
  67.8 58.0 %all-to-all-start.1 = ((bf16[8,80,1536]{2,1,0:T(8,128)(2,1)}), bf16[8,80,1536]{2,1,0:T(8,128)(2,1)}, u32[]{:S(2)}, u32[]{:S(2)}) async-start(bf16[8,80,1536]{2,1,0:T(8,128)(2,1)} %pad_maximum_fusion.4), calls=%async_computation.1 | async-start | bytes 3932160 | tf_op jit(solution)/shard_map/all_to_all | solution.py:487
  72.2 359.6 %all-gather.8.cloned.1.call-start = ((), (), s32[]{:S(2)}) async-start(), calls=%async_computation.9 | async-start | bytes 9830400 | tf_op jit(solution)/shard_map/all_gather | solution.py:499
  193.6 53.2 %collective-permute-start.19 = (bf16[2,80,2560]{2,1,0:T(8,128)(2,1)S(1)}, bf16[2,80,2560]{2,1,0:T(8,128)(2,1)S(1)}, u32[]{:S(2)}, u32[]{:S(2)}) collective-permute-start(bf16[2,80,2560]{2,1,0:T(8,128)(2,1)S(1)} %slice.603), channel_id=1, source_target_pairs={{0,1},{1,0},{2,3},{3,2},{4,5},{5,4},{6,7},{7,6},{8,9},{9,8},{10,11... | collective-permute-start | bytes 2457608 | tf_op jit(solution)/shard_map/ppermute | solution.py:27
  306.1 61.7 %collective-permute-start.23 = (bf16[384,2560]{1,0:T(8,128)(2,1)}, bf16[384,2560]{1,0:T(8,128)(2,1)}, u32[]{:S(2)}, u32[]{:S(2)}) collective-permute-start(bf16[384,2560]{1,0:T(8,128)(2,1)} %multiply_convert_fusion), channel_id=1, source_target_pairs={{0,4},{4,0},{1,5},{5,1},{2,6},{6,2},{3,7},{7,3},{8,12},{12,8},{9,1... | collective-permute-start | bytes 5898248 | tf_op jit(solution)/shard_map/ppermute | solution.py:27
  323.9 86.0 %collective-permute-start.26 = (bf16[384,2560]{1,0:T(8,128)(2,1)}, bf16[384,2560]{1,0:T(8,128)(2,1)}, u32[]{:S(2)}, u32[]{:S(2)}) collective-permute-start(bf16[384,2560]{1,0:T(8,128)(2,1)} %bitcast.8), channel_id=1, source_target_pairs={{0,4},{4,0},{1,5},{5,1},{2,6},{6,2},{3,7},{7,3},{8,12},{12,8},{9,1... | collective-permute-start | bytes 5898248 | tf_op jit(solution)/shard_map/ppermute | solution.py:27
  324.0 88.8 %collective-permute-start.31 = (bf16[384,2560]{1,0:T(8,128)(2,1)}, bf16[384,2560]{1,0:T(8,128)(2,1)}, u32[]{:S(2)}, u32[]{:S(2)}) collective-permute-start(bf16[384,2560]{1,0:T(8,128)(2,1)} %multiply_convert_fusion), channel_id=1, source_target_pairs={{0,1},{1,0},{2,3},{3,2},{4,5},{5,4},{6,7},{7,6},{8,9},{9,8},{10,11... | collective-permute-start | bytes 5898248 | tf_op jit(solution)/shard_map/ppermute | solution.py:27
  324.5 91.0 %collective-permute-start.36 = (bf16[384,2560]{1,0:T(8,128)(2,1)}, bf16[384,2560]{1,0:T(8,128)(2,1)}, u32[]{:S(2)}, u32[]{:S(2)}) collective-permute-start(bf16[384,2560]{1,0:T(8,128)(2,1)} %bitcast.8), channel_id=1, source_target_pairs={{0,1},{1,0},{2,3},{3,2},{4,5},{5,4},{6,7},{7,6},{8,9},{9,8},{10,11... | collective-permute-start | bytes 5898248 | tf_op jit(solution)/shard_map/ppermute | solution.py:27
  327.4 104.4 %all-to-all-start = ((bf16[8,80,1536]{2,1,0:T(8,128)(2,1)}), bf16[8,80,1536]{2,1,0:T(8,128)(2,1)}, u32[]{:S(2)}, u32[]{:S(2)}) async-start(bf16[8,80,1536]{2,1,0:T(8,128)(2,1)} %pad_maximum_fusion.3), calls=%async_computation | async-start | bytes 3932160 | tf_op jit(solution)/shard_map/all_to_all | solution.py:487
  331.8 274.5 %all-gather.10.cloned.1.call-start = ((), (), s32[]{:S(2)}) async-start(), calls=%async_computation.10 | async-start | bytes 9830400 | tf_op jit(solution)/shard_map/all_gather | solution.py:499
  370.0 84.3 %collective-permute-start.30 = (bf16[192,2560]{1,0:T(8,128)(2,1)}, bf16[192,2560]{1,0:T(8,128)(2,1)}, u32[]{:S(2)}, u32[]{:S(2)}) collective-permute-start(bf16[192,2560]{1,0:T(8,128)(2,1)} %slice.636), channel_id=1, source_target_pairs={{0,1},{1,0},{2,3},{3,2},{4,5},{5,4},{6,7},{7,6},{8,9},{9,8},{10,11... | collective-permute-start | bytes 2949128 | tf_op jit(solution)/shard_map/ppermute | solution.py:27
  412.2 61.9 %collective-permute-start.35 = (bf16[192,2560]{1,0:T(8,128)(2,1)}, bf16[192,2560]{1,0:T(8,128)(2,1)S(1)}, u32[]{:S(2)}, u32[]{:S(2)}) collective-permute-start(bf16[192,2560]{1,0:T(8,128)(2,1)} %slice.638), channel_id=1, source_target_pairs={{0,1},{1,0},{2,3},{3,2},{4,5},{5,4},{6,7},{7,6},{8,9},{9,8},{10,11... | collective-permute-start | bytes 2949128 | tf_op jit(solution)/shard_map/ppermute | solution.py:27
  412.8 87.5 %collective-permute-start.25 = (bf16[384,2560]{1,0:T(8,128)(2,1)}, bf16[384,2560]{1,0:T(8,128)(2,1)}, u32[]{:S(2)}, u32[]{:S(2)}) collective-permute-start(bf16[384,2560]{1,0:T(8,128)(2,1)} %multiply_convert_fusion), channel_id=1, source_target_pairs={{0,2},{2,0},{1,3},{3,1},{4,6},{6,4},{5,7},{7,5},{8,10},{10,8},{9,1... | collective-permute-start | bytes 5898248 | tf_op jit(solution)/shard_map/ppermute | solution.py:27
  412.8 94.4 %collective-permute-start.28 = (bf16[384,2560]{1,0:T(8,128)(2,1)}, bf16[384,2560]{1,0:T(8,128)(2,1)}, u32[]{:S(2)}, u32[]{:S(2)}) collective-permute-start(bf16[384,2560]{1,0:T(8,128)(2,1)} %bitcast.8), channel_id=1, source_target_pairs={{0,2},{2,0},{1,3},{3,1},{4,6},{6,4},{5,7},{7,5},{8,10},{10,8},{9,1... | collective-permute-start | bytes 5898248 | tf_op jit(solution)/shard_map/ppermute | solution.py:27
  415.5 61.3 %collective-permute-start.32 = (bf16[192,2560]{1,0:T(8,128)(2,1)}, bf16[192,2560]{1,0:T(8,128)(2,1)}, u32[]{:S(2)}, u32[]{:S(2)}) collective-permute-start(bf16[192,2560]{1,0:T(8,128)(2,1)} %slice.637), channel_id=1, source_target_pairs={{0,4},{4,0},{1,5},{5,1},{2,6},{6,2},{3,7},{7,3},{8,12},{12,8},{9,1... | collective-permute-start | bytes 2949128 | tf_op jit(solution)/shard_map/ppermute | solution.py:27
  431.8 523.1 %reduce-scatter.5.cloned.1.call-start = ((), (), s32[]{:S(2)}) async-start(), calls=%async_computation.11 | async-start | bytes 9830400 | tf_op jit(solution)/shard_map/reduce_scatter | solution.py:539
  645.1 86.6 %collective-permute-start.40 = (bf16[384,2560]{1,0:T(8,128)(2,1)}, bf16[384,2560]{1,0:T(8,128)(2,1)}, u32[]{:S(2)}, u32[]{:S(2)}) collective-permute-start(bf16[384,2560]{1,0:T(8,128)(2,1)} %get-tuple-element.110), channel_id=1, source_target_pairs={{0,2},{2,0},{1,3},{3,1},{4,6},{6,4},{5,7},{7,5},{8,10},{10,8},{9,1... | collective-permute-start | bytes 5898248 | tf_op jit(solution)/shard_map/ppermute | solution.py:27
  645.1 86.6 %collective-permute-start.43 = (bf16[384,2560]{1,0:T(8,128)(2,1)}, bf16[384,2560]{1,0:T(8,128)(2,1)}, u32[]{:S(2)}, u32[]{:S(2)}) collective-permute-start(bf16[384,2560]{1,0:T(8,128)(2,1)} %get-tuple-element.109), channel_id=1, source_target_pairs={{0,2},{2,0},{1,3},{3,1},{4,6},{6,4},{5,7},{7,5},{8,10},{10,8},{9,1... | collective-permute-start | bytes 5898248 | tf_op jit(solution)/shard_map/ppermute | solution.py:27
  684.1 56.8 %collective-permute-start.29 = (bf16[384,2560]{1,0:T(8,128)(2,1)}, bf16[384,2560]{1,0:T(8,128)(2,1)}, u32[]{:S(2)}, u32[]{:S(2)}) collective-permute-start(bf16[384,2560]{1,0:T(8,128)(2,1)} %get-tuple-element.114), channel_id=1, source_target_pairs={{0,2},{2,0},{1,3},{3,1},{4,6},{6,4},{5,7},{7,5},{8,10},{10,8},{9,1... | collective-permute-start | bytes 5898248 | tf_op jit(solution)/shard_map/ppermute | solution.py:27
  684.2 56.7 %collective-permute-start.42 = (bf16[384,2560]{1,0:T(8,128)(2,1)}, bf16[384,2560]{1,0:T(8,128)(2,1)}, u32[]{:S(2)}, u32[]{:S(2)}) collective-permute-start(bf16[384,2560]{1,0:T(8,128)(2,1)} %get-tuple-element.113), channel_id=1, source_target_pairs={{0,2},{2,0},{1,3},{3,1},{4,6},{6,4},{5,7},{7,5},{8,10},{10,8},{9,1... | collective-permute-start | bytes 5898248 | tf_op jit(solution)/shard_map/ppermute | solution.py:27
  731.5 471.0 %reduce-scatter.7.cloned.1.call-start = ((), (), s32[]{:S(2)}) async-start(), calls=%async_computation.12 | async-start | bytes 9830400 | tf_op jit(solution)/shard_map/reduce_scatter | solution.py:539
  740.3 73.0 %collective-permute-start.41 = (bf16[192,2560]{1,0:T(8,128)(2,1)}, bf16[192,2560]{1,0:T(8,128)(2,1)S(1)}, u32[]{:S(2)}, u32[]{:S(2)}) collective-permute-start(bf16[192,2560]{1,0:T(8,128)(2,1)} %slice.997), channel_id=1, source_target_pairs={{0,1},{1,0},{2,3},{3,2},{4,5},{5,4},{6,7},{7,6},{8,9},{9,8},{10,11... | collective-permute-start | bytes 2949128 | tf_op jit(solution)/shard_map/ppermute | solution.py:27
  748.4 64.9 %collective-permute-start.48 = (bf16[192,2560]{1,0:T(8,128)(2,1)}, bf16[192,2560]{1,0:T(8,128)(2,1)}, u32[]{:S(2)}, u32[]{:S(2)}) collective-permute-start(bf16[192,2560]{1,0:T(8,128)(2,1)} %slice.996), channel_id=1, source_target_pairs={{0,4},{4,0},{1,5},{5,1},{2,6},{6,2},{3,7},{7,3},{8,12},{12,8},{9,1... | collective-permute-start | bytes 2949128 | tf_op jit(solution)/shard_map/ppermute | solution.py:27
  993.7 58.2 %collective-permute-start.55 = (bf16[2,80,3072]{2,1,0:T(8,128)(2,1)S(1)}, bf16[2,80,3072]{2,1,0:T(8,128)(2,1)S(1)}, u32[]{:S(2)}, u32[]{:S(2)}) collective-permute-start(bf16[2,80,3072]{2,1,0:T(8,128)(2,1)S(1)} %slice.995), channel_id=1, source_target_pairs={{0,1},{1,0},{2,3},{3,2},{4,5},{5,4},{6,7},{7,6},{8,9},{9,8},{10,11... | collective-permute-start | bytes 2949128 | tf_op jit(solution)/shard_map/ppermute | solution.py:27
  1035.3 62.7 %collective-permute-start.75 = (bf16[2,80,2560]{2,1,0:T(8,128)(2,1)}, bf16[2,80,2560]{2,1,0:T(8,128)(2,1)}, u32[]{:S(2)}, u32[]{:S(2)}) collective-permute-start(bf16[2,80,2560]{2,1,0:T(8,128)(2,1)} %slice.999), channel_id=1, source_target_pairs={{0,1},{1,0},{2,3},{3,2},{4,5},{5,4},{6,7},{7,6},{8,9},{9,8},{10,11... | collective-permute-start | bytes 2457608 | tf_op jit(solution)/shard_map/ppermute | solution.py:27
  1054.0 53.1 %collective-permute-start.81 = (bf16[2,80,2560]{2,1,0:T(8,128)(2,1)}, bf16[2,80,2560]{2,1,0:T(8,128)(2,1)}, u32[]{:S(2)}, u32[]{:S(2)}) collective-permute-start(bf16[2,80,2560]{2,1,0:T(8,128)(2,1)} %fusion.21), channel_id=1, source_target_pairs={{0,1},{1,0},{2,3},{3,2},{4,5},{5,4},{6,7},{7,6},{8,9},{9,8},{10,11... | collective-permute-start | bytes 2457608 | tf_op jit(solution)/shard_map/ppermute | solution.py:27
  1110.7 56.5 %collective-permute-start.63 = (bf16[384,2560]{1,0:T(8,128)(2,1)}, bf16[384,2560]{1,0:T(8,128)(2,1)}, u32[]{:S(2)}, u32[]{:S(2)}) collective-permute-start(bf16[384,2560]{1,0:T(8,128)(2,1)} %get-tuple-element.63), channel_id=1, source_target_pairs={{0,2},{2,0},{1,3},{3,1},{4,6},{6,4},{5,7},{7,5},{8,10},{10,8},{9,1... | collective-permute-start | bytes 5898248 | tf_op jit(solution)/shard_map/ppermute | solution.py:27
  1116.0 92.1 %collective-permute-start.65 = (bf16[192,2560]{1,0:T(8,128)(2,1)}, bf16[192,2560]{1,0:T(8,128)(2,1)}, u32[]{:S(2)}, u32[]{:S(2)}) collective-permute-start(bf16[192,2560]{1,0:T(8,128)(2,1)} %slice.993), channel_id=1, source_target_pairs={{0,1},{1,0},{2,3},{3,2},{4,5},{5,4},{6,7},{7,6},{8,9},{9,8},{10,11... | collective-permute-start | bytes 2949128 | tf_op jit(solution)/shard_map/ppermute | solution.py:27
  1119.8 88.4 %collective-permute-start.72 = (bf16[192,2560]{1,0:T(8,128)(2,1)}, bf16[192,2560]{1,0:T(8,128)(2,1)}, u32[]{:S(2)}, u32[]{:S(2)}) collective-permute-start(bf16[192,2560]{1,0:T(8,128)(2,1)} %slice.992), channel_id=1, source_target_pairs={{0,4},{4,0},{1,5},{5,1},{2,6},{6,2},{3,7},{7,3},{8,12},{12,8},{9,1... | collective-permute-start | bytes 2949128 | tf_op jit(solution)/shard_map/ppermute | solution.py:27
  1138.5 69.7 %collective-permute-start.71 = (bf16[192,2560]{1,0:T(8,128)(2,1)}, bf16[192,2560]{1,0:T(8,128)(2,1)}, u32[]{:S(2)}, u32[]{:S(2)}) collective-permute-start(bf16[192,2560]{1,0:T(8,128)(2,1)} %fusion.7), channel_id=1, source_target_pairs={{0,1},{1,0},{2,3},{3,2},{4,5},{5,4},{6,7},{7,6},{8,9},{9,8},{10,11... | collective-permute-start | bytes 2949128 | tf_op jit(solution)/shard_map/ppermute | solution.py:27
  1139.7 62.8 %all-to-all-start.2 = ((bf16[8,80,1536]{2,1,0:T(8,128)(2,1)}), bf16[8,80,1536]{2,1,0:T(8,128)(2,1)S(1)}, u32[]{:S(2)}, u32[]{:S(2)}) async-start(bf16[8,80,1536]{2,1,0:T(8,128)(2,1)} %bitcast.379), calls=%async_computation.6 | async-start | bytes 3932160 | tf_op jit(solution)/shard_map/all_to_all | solution.py:570
  1214.3 86.7 %reduce-scatter.11.cloned.1.call-start = ((), (), s32[]{:S(2)}) async-start(), calls=%async_computation.14 | async-start | bytes 2457600 | tf_op jit(solution)/shard_map/reduce_scatter | solution.py:553
  (137 other events, 2865.3 us)
Sparse Core Ops, SparseCore 0:
  10.2 46.2 all-gather.5
  61.9 35.2 all-gather.11
  125.9 152.6 all-gather.7
  431.9 174.3 all-gather.9
  731.6 146.4 reduce-scatter.4
  955.1 157.8 reduce-scatter.6
  1214.4 43.5 reduce-scatter.8
  1260.4 40.4 reduce-scatter.10

commit v3 on v2

--- a/solution.py
+++ b/solution.py
@@ -10,11 +10,13 @@
 WINDOW = 2048
 SUB = 128
 TILE = 512
+FEW = 4
 epsilon = 1e-06
 blocked_score = -1e30
 PLANE = ("y", "c", "x")
 low = jnp.bfloat16
 f32 = jnp.float32
+NOMINAL = pl.CostEstimate(flops=1 << 20, bytes_accessed=1 << 12, transcendentals=0)
 
 
 def dot(left, right, contract, kind=f32):
@@ -27,55 +29,74 @@
     return lax.ppermute(value, axis, [(0, 1), (1, 0)])
 
 
-def plane_gather(own):
+def plane_gather(own, second=(), third=()):
     half = own.shape[0] // 2
     by_x = swap(own, "x")
     by_y = swap(own, "y")
     own_c = swap(own, "c")
-    diag_top = swap(by_y[:half], "x")
-    diag_bottom = swap(by_x[half:], "y")
-    by_x_c = swap(by_x, "c")
-    by_y_c = swap(by_y, "c")
-    diag = jnp.concatenate([diag_top, diag_bottom], 0)
-    diag_c = swap(diag, "c")
+    diag = (
+        swap(after(by_y[:half], *second), "x"),
+        swap(after(by_x[half:], *second), "y"),
+    )
+    by_x_c = swap(after(by_x, *second), "c")
+    by_y_c = swap(after(by_y, *second), "c")
+    diag_c = tuple(swap(after(part, *third), "c") for part in diag)
     return [own, by_x, own_c, by_x_c, by_y, diag, by_y_c, diag_c]
 
 
-def plane_scatter(parts):
-    half = parts[0].shape[0] // 2
-
-    def chip(r):
-        return parts[r].astype(f32) + swap(parts[r + 2].astype(low), "c").astype(f32)
-
-    diag = chip(5).astype(low)
-    diag_x = swap(diag[:half], "x").astype(f32)
-    diag_y = swap(diag[half:], "y").astype(f32)
-    to_x, to_y = chip(1), chip(4)
-    x_top = swap(to_x[:half].astype(low), "x").astype(f32)
-    y_bottom = swap(to_y[half:].astype(low), "y").astype(f32)
-    mine = chip(0)
-    x_bottom = swap((to_x[half:] + diag_y).astype(low), "x").astype(f32)
-    y_top = swap((to_y[:half] + diag_x).astype(low), "y").astype(f32)
-    return jnp.concatenate(
-        [mine[:half] + x_top + y_top, mine[half:] + x_bottom + y_bottom], 0
-    )
+def joined_blocks(blocks):
+    return [jnp.concatenate(block, 0) if isinstance(block, tuple) else block for block in blocks]
+
+
+def core_sum(keep, send):
+    return keep.astype(f32) + swap(send, "c").astype(f32)
+
+
+def scatter_start(diag, to_x, to_y):
+    half = diag.shape[0] // 2
+    return (
+        swap(diag[:half].astype(low), "x"),
+        swap(diag[half:].astype(low), "y"),
+        swap(to_x[:half].astype(low), "x"),
+        swap(to_y[half:].astype(low), "y"),
+    )
+
+
+def scatter_turn(started, to_x, to_y, later=()):
+    half = to_x.shape[0] // 2
+    diag_x, diag_y = (value.astype(f32) for value in started[:2])
+    return (
+        after((to_x[half:] + diag_y).astype(low), *later),
+        after((to_y[:half] + diag_x).astype(low), *later),
+    )
+
+
+def scatter_end(started, x_bottom, y_top, own):
+    half = own.shape[0] // 2
+    x_top, y_bottom = (value.astype(f32) for value in started[2:])
+    x_bottom, y_top = swap(x_bottom, "x").astype(f32), swap(y_top, "y").astype(f32)
+    return jnp.concatenate([own[:half] + x_top + y_top, own[half:] + x_bottom + y_bottom], 0)
+
+
+def shift(value, steps):
+    count = lax.axis_size("z")
+    return lax.ppermute(value, "z", [(i, i + steps) for i in range(count) if 0 <= i + steps < count])
+
+
+def planes_scatter(column):
+    count = lax.axis_size("z")
+    if count > FEW:
+        return lax.psum_scatter(column, "z", scatter_dimension=0, tiled=False).astype(f32)
+    here = lax.axis_index("z")
+    total = lax.dynamic_index_in_dim(column, here, 0, False).astype(f32)
+    for r in range(1, count):
+        part = lax.dynamic_index_in_dim(column, (here + r) % count, 0, False)
+        total = total + shift(part, r).astype(f32) + shift(part, r - count).astype(f32)
+    return total
 
 
 def plane_index():
     return (lax.axis_index("y") * 2 + lax.axis_index("c")) * 2 + lax.axis_index("x")
-
-
-def scatter_rows(partial):
-    planes = lax.axis_size("z")
-    wide = partial.shape[1]
-    rows = partial.shape[0] // (planes * 8)
-    blocks = partial.reshape(planes, 8, rows, wide)
-    here = plane_index()
-    parts = [
-        lax.dynamic_slice(blocks, (0, here ^ r, 0, 0), (planes, 1, rows, wide))[:, 0]
-        for r in range(8)
-    ]
-    return plane_scatter(parts).astype(low).reshape(planes * rows, wide)
 
 
 def after(value, *earlier):
@@ -88,6 +109,7 @@
         lax.ppermute(pair, ("z", "y"), [(i, i + d) for i in range(count - d)])
         for d in range(chips, 0, -1)
     ] + [pair]
+    same = list(lax.optimization_barrier(tuple(same)))
     return same + [swap(block, "c") for block in same]
 
 
@@ -219,9 +241,7 @@
             ],
         ),
         compiler_params=pltpu.CompilerParams(vmem_limit_bytes=56 << 20),
-        cost_estimate=pl.CostEstimate(
-            flops=4 * count * wide * span, bytes_accessed=8 << 20, transcendentals=count * span * wide // size
-        ),
+        cost_estimate=NOMINAL,
     )(core, places, queries, *blocks)
 
 
@@ -260,9 +280,7 @@
             ],
         ),
         compiler_params=pltpu.CompilerParams(vmem_limit_bytes=60 << 20),
-        cost_estimate=pl.CostEstimate(
-            flops=10 * count * wide * span, bytes_accessed=16 << 20, transcendentals=count * span * wide // size
-        ),
+        cost_estimate=NOMINAL,
     )(core, places, queries, grads, logs, *blocks)
 
 
@@ -329,99 +347,211 @@
             scratch_shapes=[pltpu.VMEM((deep, TILE), low)],
         ),
         compiler_params=pltpu.CompilerParams(vmem_limit_bytes=48 << 20),
-        cost_estimate=pl.CostEstimate(
-            flops=2 * count * deep * wide, bytes_accessed=2 * deep * wide + 8 * count * deep, transcendentals=0
+        cost_estimate=NOMINAL,
+    )(slots, *given, *blocks)
+
+
+def row_grads_kernel(slots, left, right, keep, send, turned):
+    @pl.when(pl.program_id(1) == 0)
+    def _():
+        turned[...] = left[...].T
+
+    rows = keep.shape[2]
+    value = dot(turned[...], right[...], (1, 0), low)
+    for i in range(8):
+        place = slots[i]
+
+        @pl.when(place < 4)
+        def _():
+            keep[place, 0] = value[i * rows : (i + 1) * rows]
+
+        @pl.when(place >= 4)
+        def _():
+            send[place - 4, 0] = value[i * rows : (i + 1) * rows]
+
+
+def row_grads(left, right):
+    planes = lax.axis_size("z")
+    count, deep = left.shape
+    wide = right.shape[1]
+    rows = deep // (planes * 8)
+    places = jnp.array([3, 1, 7, 5, 2, 0, 6, 4], jnp.int32)
+    slots = places[plane_index() ^ jnp.arange(8)]
+    if rows % 16 or wide % TILE or (planes * 8 * rows) % (planes * 128):
+        blocks = dot(left, right, (0, 0), low).reshape(planes, 8, rows, wide)
+        order = jnp.argsort(slots)
+        blocks = jnp.swapaxes(jnp.take(blocks, order, axis=1), 0, 1)
+        return blocks[:4], blocks[4:]
+    group = pl.BlockSpec((4, 1, rows, TILE), lambda z, n, s: (0, z, 0, n))
+    shape = jax.ShapeDtypeStruct((4, planes, rows, wide), low)
+    return pl.pallas_call(
+        row_grads_kernel,
+        out_shape=(shape, shape),
+        grid_spec=pltpu.PrefetchScalarGridSpec(
+            num_scalar_prefetch=1,
+            grid=(planes, wide // TILE),
+            in_specs=[
+                pl.BlockSpec((count, 8 * rows), lambda z, n, s: (0, z)),
+                pl.BlockSpec((count, TILE), lambda z, n, s: (0, n)),
+            ],
+            out_specs=[group, group],
+            scratch_shapes=[pltpu.VMEM((8 * rows, count), low)],
         ),
-    )(slots, *given, *blocks)
-
-
-def mlp_kernel(part, units, grads, weights, *rest):
-    before, (out, grad_units, hidden) = rest[:-3], rest[-3:]
-    both = dot(units[...], weights[:, : 2 * part], (1, 0))
-    gates, upward = both[:, :part], both[:, part:]
-    grad_middle = dot(grads[...], weights[:, 2 * part :], (1, 0))
+        compiler_params=pltpu.CompilerParams(vmem_limit_bytes=48 << 20),
+        cost_estimate=NOMINAL,
+    )(slots, left, right)
+
+
+def mlp_kernel(part, per, tiles, *rest):
+    weights, rest = rest[:per], rest[per:]
+    pieces = 2 * sum(tiles)
+    sources, rest = rest[:pieces], rest[pieces:]
+    outs, grad_units, hidden = rest[0:2], rest[2:4], rest[4 : 4 + per]
+    units, grads, arrived = rest[4 + per :]
+    step = pl.program_id(0)
+
+    def fetches(tile):
+        first = 2 * sum(tiles[:tile])
+        found = []
+        for array, target in enumerate((units, grads)):
+            at = 0
+            for i in range(tiles[tile]):
+                source = sources[first + array * tiles[tile] + i]
+                found.append(
+                    pltpu.make_async_copy(
+                        source,
+                        target.at[tile % 2, pl.ds(at, source.shape[0])],
+                        arrived.at[tile % 2, array, i],
+                    )
+                )
+                at += source.shape[0]
+        return found
+
+    for tile in range(len(tiles)):
+
+        @pl.when(step == tile)
+        def _():
+            if tile == 0:
+                for copy in fetches(0):
+                    copy.start()
+            if tile + 1 < len(tiles):
+                for copy in fetches(tile + 1):
+                    copy.start()
+            for copy in fetches(tile):
+                copy.wait()
+
+    unit = units[step % 2]
+    grad = grads[step % 2]
     slope = 0.7978845608028654
-    square = gates * gates
-    bend = jnp.tanh(slope * gates * (1.0 + 0.044715 * square))
-    half = 0.5 * (1.0 + bend)
-    gelu = gates * half
-    grad_gelu = half + 0.5 * gates * (1.0 - bend * bend) * (slope * (1.0 + 3 * 0.044715 * square))
-    hidden[:, :part] = (grad_middle * upward * grad_gelu).astype(low)
-    hidden[:, part : 2 * part] = (grad_middle * gelu).astype(low)
-    hidden[:, 2 * part :] = (gelu * upward).astype(low)
-    value = dot(hidden[:, 2 * part :], weights[:, 2 * part :], (1, 1))
-    if before:
-        value = value + before[0][...].astype(f32)
-    out[...] = value.astype(low)
-    value = dot(hidden[:, : 2 * part], weights[:, : 2 * part], (1, 1))
-    if before:
-        value = value + before[1][...].astype(f32)
-    grad_units[...] = value.astype(low)
-
-
-def mlp(units, grads, weights, before, rows):
-    count, wide = units.shape
-    deep = weights.shape[1]
-    tile = pl.BlockSpec((rows, wide), lambda i: (i, 0))
+    for j in range(per):
+        both = dot(unit, weights[j][:, : 2 * part], (1, 0))
+        gates, upward = both[:, :part], both[:, part:]
+        grad_middle = dot(grad, weights[j][:, 2 * part :], (1, 0))
+        square = gates * gates
+        bend = jnp.tanh(slope * gates * (1.0 + 0.044715 * square))
+        half = 0.5 * (1.0 + bend)
+        gelu = gates * half
+        grad_gelu = half + 0.5 * gates * (1.0 - bend * bend) * (slope * (1.0 + 3 * 0.044715 * square))
+        hidden[j][:, :part] = (grad_middle * upward * grad_gelu).astype(low)
+        hidden[j][:, part : 2 * part] = (grad_middle * gelu).astype(low)
+        hidden[j][:, 2 * part :] = (gelu * upward).astype(low)
+    for which, targets in enumerate((outs, grad_units)):
+        value = 0.0
+        for j in range(per):
+            columns = slice(0, 2 * part) if which else slice(2 * part, 3 * part)
+            value = value + dot(hidden[j][:, columns], weights[j][:, columns], (1, 1))
+        for side in range(2):
+
+            @pl.when(step // (len(tiles) // 2) == side)
+            def _():
+                targets[side][...] = value.astype(low)
+
+
+def mlp(units, grads, weights):
+    rows = sum(piece.shape[0] for piece in units[0])
+    count, wide = rows * len(units), units[0][0].shape[1]
+    per, each = len(weights), weights[0].shape[1]
+    tiles = tuple(len(tile) for tile in units)
+    sources = [piece for pair in zip(units, grads) for tile in pair for piece in tile]
+    side = len(units) // 2
+    sides = [
+        pl.BlockSpec((rows, wide), lambda i: (jnp.minimum(i, side - 1), 0)),
+        pl.BlockSpec((rows, wide), lambda i: (jnp.maximum(i - side, 0), 0)),
+    ]
+    half = jax.ShapeDtypeStruct((count // 2, wide), low)
     return pl.pallas_call(
-        functools.partial(mlp_kernel, deep // 3),
-        out_shape=(
-            jax.ShapeDtypeStruct((count, wide), low),
-            jax.ShapeDtypeStruct((count, wide), low),
-            jax.ShapeDtypeStruct((count, deep), low),
-        ),
-        grid=(count // rows,),
-        in_specs=[tile, tile, pl.BlockSpec(weights.shape, lambda i: (0, 0), pipeline_mode=pl.Buffered(1))]
-        + [tile] * len(before),
-        out_specs=[tile, tile, pl.BlockSpec((rows, deep), lambda i: (i, 0))],
-        compiler_params=pltpu.CompilerParams(vmem_limit_bytes=60 << 20),
-        cost_estimate=pl.CostEstimate(
-            flops=4 * count * wide * deep,
-            bytes_accessed=2 * (wide * deep + count * (4 * wide + deep)),
-            transcendentals=count * deep // 3,
-        ),
-    )(units, grads, weights, *before)
-
-
-def mlp_grads_kernel(units_a, units_b, grads_a, grads_b, hidden_a, hidden_b, out, turned):
-    piece = pl.program_id(1)
-    count = units_a.shape[0]
-
-    @pl.when(piece == 0)
-    def _():
-        turned[:, :count] = units_a[...].T
-        turned[:, count:] = units_b[...].T
-
-    @pl.when(piece == 2)
-    def _():
-        turned[:, :count] = grads_a[...].T
-        turned[:, count:] = grads_b[...].T
-
-    out[...] = (
-        dot(turned[:, :count], hidden_a[...], (1, 0)) + dot(turned[:, count:], hidden_b[...], (1, 0))
-    ).astype(low)
-
-
-def mlp_grads(units, grads, hidden):
-    count, wide = units[0].shape
+        functools.partial(mlp_kernel, each // 3, per, tiles),
+        out_shape=[half] * 4 + [jax.ShapeDtypeStruct((count, each), low)] * per,
+        grid=(len(units),),
+        in_specs=[pl.BlockSpec((wide, each), lambda i: (0, 0), pipeline_mode=pl.Buffered(1))] * per
+        + [pl.BlockSpec(memory_space=pl.ANY)] * len(sources),
+        out_specs=sides * 2 + [pl.BlockSpec((rows, each), lambda i: (i, 0))] * per,
+        scratch_shapes=[
+            pltpu.VMEM((2, rows, wide), low),
+            pltpu.VMEM((2, rows, wide), low),
+            pltpu.SemaphoreType.DMA((2, 2, max(tiles))),
+        ],
+        compiler_params=pltpu.CompilerParams(vmem_limit_bytes=62 << 20),
+        cost_estimate=NOMINAL,
+    )(*weights, *sources)
+
+
+def mlp_grads_kernel(number, *rest):
+    units, grads, hidden, rest = rest[:number], rest[number : 2 * number], rest[2 * number : 2 * number + 2], rest[2 * number + 2 :]
+    outs, turned = rest[:-1], rest[-1]
+    step = pl.program_id(0)
+    part = hidden[0].shape[1] // 3
+    out_wide = outs[0].shape[1]
+    piece = min(part, 256)
+
+    def turn(slot, which, sources, share, shares):
+        at = 0
+        for i, source in enumerate(sources):
+            if i * shares // len(sources) == share:
+                turned[slot, which, :, at : at + source.shape[0]] = source[...].T
+            at += source.shape[0]
+
+    def multiply(slot, which, at):
+        value, start = 0.0, 0
+        for block in hidden:
+            left = turned[slot, which, :, start : start + block.shape[0]]
+            value = value + dot(left, block[:, at : at + piece], (1, 0))
+            start += block.shape[0]
+        outs[at // out_wide][:, at % out_wide : at % out_wide + piece] = value.astype(low)
+
+    work = [(at // (2 * part), at) for at in range(0, 3 * part, piece)]
+
+    @pl.when(step == 0)
+    def _():
+        turn(0, 0, units, 0, 1)
+        turn(0, 1, grads, 0, 1)
+
+    @pl.when(step > 0)
+    def _():
+        for i, (which, at) in enumerate(work):
+            multiply((step - 1) % 2, which, at)
+            turn(step % 2, 0, units, i, len(work))
+            turn(step % 2, 1, grads, i, len(work))
+
+
+def mlp_grads(units, grads, hidden, pieces):
+    wide = units[0].shape[1]
     deep = hidden[0].shape[1]
-    part = deep // 3
+    count = sum(piece.shape[0] for piece in units)
     rows = 512
-    left = pl.BlockSpec((count, rows), lambda d, f: (0, d))
-    right = pl.BlockSpec((count, part), lambda d, f: (0, f))
+    last = wide // rows - 1
     return pl.pallas_call(
-        mlp_grads_kernel,
-        out_shape=jax.ShapeDtypeStruct((wide, deep), low),
-        grid=(wide // rows, 3),
-        in_specs=[left] * 4 + [right] * 2,
-        out_specs=pl.BlockSpec((rows, part), lambda d, f: (d, f)),
-        scratch_shapes=[pltpu.VMEM((rows, 2 * count), low)],
-        compiler_params=pltpu.CompilerParams(vmem_limit_bytes=56 << 20),
-        cost_estimate=pl.CostEstimate(
-            flops=4 * count * wide * deep,
-            bytes_accessed=8 * count * wide + 20 * count * deep + 2 * wide * deep,
-            transcendentals=0,
-        ),
+        functools.partial(mlp_grads_kernel, len(units)),
+        out_shape=[jax.ShapeDtypeStruct((wide, deep // pieces), low)] * pieces,
+        grid=(last + 2,),
+        in_specs=[
+            pl.BlockSpec((piece.shape[0], rows), lambda s: (0, jnp.minimum(s, last))) for piece in units + grads
+        ]
+        + [pl.BlockSpec(piece.shape, lambda s: (0, 0), pipeline_mode=pl.Buffered(1)) for piece in hidden],
+        out_specs=[pl.BlockSpec((rows, deep // pieces), lambda s: (jnp.maximum(s - 1, 0), 0))] * pieces,
+        scratch_shapes=[pltpu.VMEM((2, 2, rows, count), low)],
+        compiler_params=pltpu.CompilerParams(vmem_limit_bytes=62 << 20),
+        cost_estimate=NOMINAL,
     )(*units, *grads, *hidden)
 
 
@@ -465,11 +595,10 @@
     gain_one = attn_gain[:, None]
     gain_two = mlp_gain[:, None]
 
-    qkv_shard = (
-        jnp.concatenate([query_weight, key_weight, value_weight], 1).astype(f32) * gain_one
-    ).astype(low)
-    qkv_column = lax.all_gather(qkv_shard, "z", axis=0, tiled=False)
-    out_column = lax.all_gather(after(out_weight.T, qkv_column), "z", axis=0, tiled=False)
+    attn_shard = jnp.concatenate([query_weight, key_weight, value_weight], 1).astype(f32) * gain_one
+    attn_shard = jnp.concatenate([attn_shard.astype(low), out_weight.T], 1)
+    attn_column = lax.all_gather(attn_shard, "z", axis=0, tiled=False)
+    qkv_column, out_column = attn_column[:, :, : wide + 2 * size], attn_column[:, :, wide + 2 * size :]
 
     spans, share = shares(gate_weight.shape[1])
     parts = 2 if share % 256 == 0 else 1
@@ -483,79 +612,102 @@
         jnp.stack([jnp.pad(shard[:, at : at + n], ((0, 0), (0, share - n))) for at, n in spans])
         for shard in mlp_shards
     ]
-    mlp_columns = [
-        lax.all_to_all(
-            jnp.concatenate([whole[:, :, k * part : (k + 1) * part] for whole in split], 2),
-            PLANE,
-            split_axis=0,
-            concat_axis=0,
-            tiled=True,
-        ).reshape(-1, 3 * part)
-        for k in range(parts)
+    mine = jnp.concatenate(
+        [whole[:, :, k * part : (k + 1) * part] for k in range(parts) for whole in split], 2
+    )
+    mlp_column = lax.all_to_all(after(mine, attn_shard), PLANE, split_axis=0, concat_axis=0, tiled=True)
+    mlp_column = mlp_column.reshape(-1, 3 * share)
+    mlp_full = [
+        lax.all_gather(mlp_column[:, k * 3 * part : (k + 1) * 3 * part], "z", axis=0, tiled=True) for k in range(parts)
     ]
-    mlp_full = []
-    earlier = out_column
-    for column in mlp_columns:
-        earlier = lax.all_gather(after(column, earlier), "z", axis=0, tiled=True)
-        mlp_full.append(earlier)
-
-    qkv_blocks = plane_gather(qkv_column)
+
+    qkv_blocks = joined_blocks(plane_gather(after(qkv_column, mlp_column)))
     inputs = tokens[0].astype(f32)
     scale_one, unit_one = unit_of(inputs)
     qkv = apply_rows(unit_one, qkv_blocks)
-    out_blocks = plane_gather(after(out_column, qkv_blocks[7]))
     queries = qkv[:, :wide]
     pairs = window_blocks(qkv[:, wide:], chips)
+    out_blocks = plane_gather(after(out_column, qkv_blocks[7]), second=tuple(pairs[: chips + 1]), third=(pairs[-1],))
+    out_blocks = joined_blocks(out_blocks)
     mixed, logs = attend(queries, pairs, positions, size, base)
-    resid = apply_rows(mixed, out_blocks, inputs)
+    finals = plane_gather(after(cotangent[0], pairs[0]), second=(mixed,), third=(mixed,))
+    resid = apply_rows(after(mixed, finals[1], finals[4]), out_blocks, inputs)
 
     scale_two, unit_two = unit_of(resid)
-    finals = plane_gather(after(cotangent[0], out_blocks[7]))
     units = plane_gather(unit_two)
-    far, near = (5, 7, 1, 3), (4, 6, 0, 2)
-    units = [jnp.concatenate([units[r] for r in half], 0) for half in (far, near)]
-    finals = [jnp.concatenate([finals[r] for r in half], 0) for half in (far, near)]
-    sums = [(), ()]
-    hidden = []
-    for k in range(parts):
-        results = [None, None]
-        for half in (1, 0) if k < parts - 1 else (0, 1):
-            results[half] = mlp(units[half], finals[half], mlp_full[k], sums[half], count)
-        sums = [result[:2] for result in results]
-        hidden.append([result[2] for result in results])
-
-    def by_device(index):
-        rows = [sums[half][index].reshape(4, count, -1) for half in (0, 1)]
-        found = {r: rows[half][i] for half, group in enumerate((far, near)) for i, r in enumerate(group)}
-        return [found[r] for r in range(8)]
-
-    grad_unit_two = plane_scatter(by_device(1))
+
+    def tiles(blocks, order):
+        return [blocks[r] if isinstance(blocks[r], tuple) else (blocks[r],) for r in order]
+
+    far, near = (5, 1, 7, 3), (4, 0, 6, 2)
+    units = [tiles(units, order) for order in (far, near)]
+    finals = [tiles(finals, order) for order in (far, near)]
+    flat_units, flat_finals = (
+        [piece for half in whole for tile in half for piece in tile] for whole in (units, finals)
+    )
+    far_sums = mlp(units[0], finals[0], mlp_full)
+
+    def of_chip(sums, which):
+        both = core_sum(sums[2 * which], sums[2 * which + 1])
+        return both[:count], both[count:]
+
+    half = count // 2
+    diag, to_x = (value.astype(low) for value in of_chip(far_sums, 1))
+    far_parts = (diag[:half], diag[half:], to_x[:half])
+    started = (swap(far_parts[0], "x"), swap(far_parts[1], "y"), swap(far_parts[2], "x"))
+    units[1][0] = (after(units[1][0][0], *far_parts),)
+    near_sums = mlp(units[1], finals[1], mlp_full)
+    to_y, own = of_chip(near_sums, 1)
+    to_y = to_y.astype(low)
+    y_bottom = to_y[half:]
+    started += (swap(y_bottom, "y"),)
+    x_bottom, y_top = scatter_turn(started, to_x, to_y)
+    hidden = [[sums[4 + k] for sums in (far_sums, near_sums)] for k in range(parts)]
+    hidden[0][0] = after(hidden[0][0], x_bottom, y_top, y_bottom)
+
+    def to_planes(k, pieces):
+        partial = mlp_grads(flat_units, flat_finals, hidden[k], pieces)
+        return partial, [lax.psum_scatter(piece, "z", scatter_dimension=0, tiled=True) for piece in partial]
+
+    partial, columns = to_planes(0, 1)
+    grad_unit_two = scatter_end(started, x_bottom, y_top, own)
     grad_resid = cotangent[0].astype(f32) + unit_back(grad_unit_two, resid, scale_two)
-
-    columns = []
-    earlier = mlp_full[-1]
-    for k in range(parts):
-        partial = mlp_grads(units, finals, hidden[k])
-        earlier = lax.psum_scatter(after(partial, earlier), "z", scatter_dimension=0, tiled=True)
-        columns.append(earlier)
-
     grad_attn = grad_resid.astype(low)
-    grad_mixed = apply_rows(grad_attn, out_blocks)
-    out_scattered = scatter_rows(dot(grad_attn, mixed, (0, 0), low))
-    grad_queries, mine, theirs = attend_back(queries, grad_mixed, logs, pairs, positions, size, base)
-    grad_pair = return_blocks(mine, theirs, chips).astype(low)
+
+    diag, out_x = (value.astype(low) for value in of_chip(far_sums, 0))
+    out_y, out_own = (value.astype(low) for value in of_chip(near_sums, 0))
+    first = tuple(after(v, x_bottom, y_top) for v in (diag[:half], diag[half:], out_x[:half], out_y[half:]))
+    outputs = tuple(swap(value, axis) for value, axis in zip(first, ("x", "y", "x", "y")))
+
+    grad_mixed = apply_rows(after(grad_attn, *first, *partial), out_blocks)
+    grad_queries, own_grads, other_grads = attend_back(queries, grad_mixed, logs, pairs, positions, size, base)
+    other_grads = after(other_grads, *outputs)
+    out_keep, out_send = row_grads(after(grad_attn, other_grads, columns[0]), mixed)
+    if parts > 1:
+        hidden[1][0] = after(hidden[1][0], out_keep)
+        later, more = to_planes(1, 3)
+        columns += more
+    out_both = core_sum(out_keep, out_send).astype(low)
+    grad_pair = return_blocks(own_grads, other_grads, chips).astype(low)
+    if parts > 1:
+        grad_pair = after(grad_pair, *later)
+    out_both = after(out_both, grad_pair)
+    out_started = scatter_start(out_both[0], out_both[1], out_both[2])
     grad_qkv = jnp.concatenate([grad_queries, grad_pair], 1)
-    qkv_scattered = scatter_rows(dot(unit_one, grad_qkv, (0, 0), low))
-    grad_unit_one = apply_rows(grad_qkv, qkv_blocks, jnp.zeros_like(inputs))
+    qkv_keep, qkv_send = row_grads(unit_one, grad_qkv)
+    qkv_both = core_sum(qkv_keep, qkv_send).astype(low)
+    qkv_started = scatter_start(qkv_both[0], qkv_both[1], qkv_both[2])
+    grad_unit_one = apply_rows(after(grad_qkv, qkv_both), qkv_blocks, jnp.zeros_like(inputs))
     grad_tokens = grad_resid + unit_back(grad_unit_one, inputs, scale_one)
 
-    def over_z(column, earlier):
-        return lax.psum_scatter(after(column, earlier), "z", scatter_dimension=0, tiled=True)
-
-    out_low = over_z(out_scattered, earlier)
-    qkv_low = over_z(qkv_scattered, out_low)
-    out_sum = out_low.astype(f32)
-    qkv_sum = qkv_low.astype(f32)
+    def of_plane(started, both, later=()):
+        turned = scatter_turn(started, both[1], both[2], later)
+        return scatter_end(started, *turned, both[3]).astype(low)
+
+    out_plane = of_plane(out_started, out_both)
+    qkv_plane = after(of_plane(qkv_started, qkv_both, columns[1:2]), *columns[2:3])
+    out_sum = planes_scatter(out_plane)
+    qkv_sum = planes_scatter(qkv_plane)
     query_sum = qkv_sum[:, :wide]
     key_sum = qkv_sum[:, wide : wide + size]
     value_sum = qkv_sum[:, wide + size :]
@@ -564,14 +716,16 @@
         + jnp.sum(key_weight.astype(f32) * key_sum, axis=1)
         + jnp.sum(value_weight.astype(f32) * value_sum, axis=1)
     )
-    output = resid + plane_scatter([after(value, qkv_scattered) for value in by_device(0)])
+    output = resid + scatter_end(outputs, *scatter_turn(outputs, out_x, out_y, (qkv_both,)), out_own)
 
     whole = [
         lax.all_to_all(
-            column.reshape(8, -1, 3 * part), PLANE, split_axis=0, concat_axis=0, tiled=True
+            after(column, qkv_plane).reshape(8, -1, column.shape[1]), PLANE, split_axis=0, concat_axis=0, tiled=True
         )
         for column in columns
     ]
+
+    whole = [whole[0]] + ([jnp.concatenate(whole[1:], 2)] if parts > 1 else [])
 
     def joined(which):
         pieces = []

time: 1320 us -> 1340 us (1.015)
  starting transfers between devices: 119 us -> 190 us
  waiting for transfers between devices: 553 us -> 492 us
  blocking collectives: 0 us -> 50.7 us
  local copies, waits for them, and re-layouts: 126 us -> 84.1 us
  Pallas kernels: 359 us -> 379 us
  matrix products: 19.1 us -> 0 us
    all_to_all x4, waiting for transfers between devices: 66.8 us -> 8.11 us  [local(): lax.all_to_all(after(column, qkv_plane).reshape(8, -1, column.shape[1]),...]
    ppermute x0 -> x12, starting transfers between devices: none -> 57.6 us  [shift(): lax.ppermute(value, 'z', [(i, i + steps) for i in range(count) if 0 <= i...]
    all_to_all x0 -> x1, blocking collectives: none -> 50.7 us  [local(): lax.all_to_all(after(mine, attn_shard), PLANE, split_axis=0, concat_axis=...]
    all_gather x4 -> x3, waiting for transfers between devices: 60.4 us -> 18.1 us  [the longest x1 18 us: local(): attn_column = lax.all_gather(attn_shard, 'z', axis=0, tiled=False)]
    slice x27 -> x17, local copies, waits for them, and re-layouts: 47.2 us -> 22.9 us  [the longest x1 3.76 us: scatter_start(): to_x[:half].astype(low)]
    ppermute x77 -> x71, waiting for transfers between devices: 340 us -> 362 us  [swap(): return lax.ppermute(value, axis, [(0, 1), (1, 0)])]
    pallas_call x6, Pallas kernels: 226 us -> 246 us  [the longest x2 129 us: mlp(): pl.pallas_call(functools.partial(mlp_kernel, each // 3, per, tiles), out_...]
    dot_general x2 -> x0, matrix products: 19.1 us -> none  [dot(): lax.dot_general(left, right, ((contract[:1], contract[1:]), ((), ())), pr...]
  transfers between devices with their start and end apart: 95 -> 100, of which waited for: 31 -> 36; matrix products, arithmetic and copies ran while one was open for 18% -> 11% of each run, Pallas kernels for 25% -> 12%
where the time goes in v3:
time: 1340 us; the launch traced here: 1330 us
  waiting for transfers between devices  492 us (37%)
  Pallas kernels  379 us (28%)
  starting transfers between devices  190 us (14%)
  other arithmetic  121 us (9%)
  local copies, waits for them, and re-layouts  84.1 us (6%)
  blocking collectives  50.7 us (4%)
  between operations  15.8 us (1%)
    ppermute x71, waiting for transfers between devices, swap(): return lax.ppermute(value, axis, [(0, 1), (1, 0)])  362 us
    pallas_call x2, Pallas kernels, mlp(): pl.pallas_call(functools.partial(mlp_kernel, each // 3, per, tiles), out_...  129 us
    ppermute x71, starting transfers between devices, swap(): return lax.ppermute(value, axis, [(0, 1), (1, 0)])  103 us
    pallas_call x2, Pallas kernels, mlp_grads(): pl.pallas_call(functools.partial(mlp_grads_kernel, len(units)), out_shape...  78.1 us
    ppermute x12, starting transfers between devices, shift(): lax.ppermute(value, 'z', [(i, i + steps) for i in range(count) if 0 <= i...  57.6 us
    all_to_all x1, blocking collectives, local(): lax.all_to_all(after(mine, attn_shard), PLANE, split_axis=0, concat_axis=...  50.7 us
    pallas_call x4, Pallas kernels, apply_rows(): pl.pallas_call(kernel, out_shape=shape, grid_spec=pltpu.PrefetchScalarGri...  49.9 us
    pallas_call x1, Pallas kernels, attend_back(): pl.pallas_call(functools.partial(attend_back_kernel, size, size ** (-0.5)...  48.5 us
  transfers between devices with their start and end apart: 100, of which 36 were waited for; matrix products, arithmetic and copies ran while one was open for 11% of the time, Pallas kernels for 12%

profile of v3, /device:TPU:0, one launch (start us, length us, event | category | flops | bytes accessed | tf_op | source)
XLA Modules:
  0.0 1332.7 jit_solution(15332248504364204808)
XLA Ops:
  13.4 50.7 %all_to_all.25 = bf16[8,80,3072]{2,1,0:T(8,128)(2,1)S(1)} all-to-all(bf16[8,80,3072]{2,1,0:T(8,128)(2,1)S(1)} %slice_dynamic-update-slice_fusion), channel_id=1, replica_groups=mesh['z'=4,'y'=2,'c'=2,'x'=2] {'y','c','x'}, dimensions={0} | all-to-all | bytes 7864320 | tf_op jit(solution)/shard_map/all_to_all | solution.py:618
  66.5 18.0 %all-gather.9.cloned.1.call-done = bf16[320,5632]{1,0:T(8,128)(2,1)} async-done(((bf16[80,5632]{1,0:T(8,128)(2,1)}), bf16[320,5632]{1,0:T(8,128)(2,1)}) %all-gather.9.cloned.1.call-update) | async-done | bytes 3604496 | tf_op jit(solution)/shard_map/all_gather | solution.py:600
  89.2 41.6 %collective-permute-done.3.rest_4_ = bf16[4,80,3072]{2,1,0:T(8,128)(2,1)S(1)} collective-permute-done((bf16[4,80,3072]{2,1,0:T(8,128)(2,1)S(1)}, bf16[4,80,3072]{2,1,0:T(8,128)(2,1)S(1)}, u32[]{:S(2)}, u32[]{:S(2)}) %collective-permute-start.3) | collective-permute-done | bytes 1966112 | tf_op jit(solution)/shard_map/ppermute | solution.py:29
  136.7 17.0 %collective-permute-done.4 = bf16[2,80,3072]{2,1,0:T(8,128)(2,1)S(1)} collective-permute-done((bf16[2,80,3072]{2,1,0:T(8,128)(2,1)S(1)}, bf16[2,80,3072]{2,1,0:T(8,128)(2,1)S(1)}, u32[]{:S(2)}, u32[]{:S(2)}) %collective-permute-start.4) | collective-permute-done | bytes 983072 | tf_op jit(solution)/shard_map/ppermute | solution.py:29
  172.2 11.7 shard_map.221
  222.4 18.0 %collective-permute-start.17 = (bf16[384,2560]{1,0:T(8,128)(2,1)S(1)}, bf16[384,2560]{1,0:T(8,128)(2,1)S(1)}, u32[]{:S(2)}, u32[]{:S(2)}) collective-permute-start(bf16[384,2560]{1,0:T(8,128)(2,1)S(1)} %bitcast.385), channel_id=1, source_target_pairs={{0,4},{4,0},{1,5},{5,1},{2,6},{6,2},{3,7},{7,3},{8,12},{12,8},{9,1... | collective-permute-start | bytes 5898248 | tf_op jit(solution)/shard_map/ppermute | solution.py:29
  244.5 46.9 %collective-permute-done.22 = bf16[2,80,2560]{2,1,0:T(8,128)(2,1)} collective-permute-done((bf16[2,80,2560]{2,1,0:T(8,128)(2,1)S(1)}, bf16[2,80,2560]{2,1,0:T(8,128)(2,1)}, u32[]{:S(2)}, u32[]{:S(2)}) %collective-permute-start.22) | collective-permute-done | bytes 819232 | tf_op jit(solution)/shard_map/ppermute | solution.py:29
  306.9 34.1 %shard_map.222 = (bf16[384,2560]{1,0:T(8,128)(2,1)}, f32[15,1,256]{2,1,0:T(1,128)}) custom-call(s32[1]{0:T(128)} %bitcast.core, s32[1,384]{1,0:T(1,128)} %places.3, bf16[384,2560]{1,0:T(8,128)(2,1)} %slice.661.queries, bf16[384,512]{1,0:T(8,128)(2,1)} %copy-done.56, bf16[384,512]{1,0:T(8,128)(2,1)} %copy-done.54, bf16[384,512]{1,0:T(8,128)(2,1)} %copy-done.55, ...), custom_call_target="tpu_custom_call" | custom-call | flops 1048576 | bytes 4096 | tf_op jit(solution)/shard_map/pallas_call | solution.py:225
  346.6 12.8 shard_map.223
  367.4 62.0 %collective-permute-done.32.rest_5_.rest_11_ = bf16[192,2560]{1,0:T(8,128)(2,1)S(1)} collective-permute-done((bf16[192,2560]{1,0:T(8,128)(2,1)S(1)}, bf16[192,2560]{1,0:T(8,128)(2,1)S(1)}, u32[]{:S(2)}, u32[]{:S(2)}) %collective-permute-start.32) | collective-permute-done | bytes 983072 | tf_op jit(solution)/shard_map/ppermute | solution.py:29
  433.0 19.9 %collective-permute-done.28.rest_2_.rest_0_ = bf16[192,2560]{1,0:T(8,128)(2,1)S(1)} collective-permute-done((bf16[192,2560]{1,0:T(8,128)(2,1)S(1)}, bf16[192,2560]{1,0:T(8,128)(2,1)S(1)}, u32[]{:S(2)}, u32[]{:S(2)}) %collective-permute-start.28) | collective-permute-done | bytes 983072 | tf_op jit(solution)/shard_map/ppermute | solution.py:29
  459.8 64.6 %shard_map.224 = (bf16[768,2560]{1,0:T(8,128)(2,1)}, bf16[768,2560]{1,0:T(8,128)(2,1)}, bf16[768,2560]{1,0:T(8,128)(2,1)}, bf16[768,2560]{1,0:T(8,128)(2,1)}, bf...) custom-call(bf16[2560,1536]{1,0:T(8,128)(2,1)} %all-gather.5.cloned.1.call-done.rest_0_, ...), custom_call_target="tpu_custom_call" | custom-call | flops 1048576 | bytes 4096 | tf_op jit(solution)/shard_map/pallas_call | solution.py:482
  542.8 64.8 %shard_map.225 = (bf16[768,2560]{1,0:T(8,128)(2,1)}, bf16[768,2560]{1,0:T(8,128)(2,1)}, bf16[768,2560]{1,0:T(8,128)(2,1)}, bf16[768,2560]{1,0:T(8,128)(2,1)}, bf...) custom-call(bf16[2560,1536]{1,0:T(8,128)(2,1)} %all-gather.5.cloned.1.call-done.rest_0_, ...), custom_call_target="tpu_custom_call" | custom-call | flops 1048576 | bytes 4096 | tf_op jit(solution)/shard_map/pallas_call | solution.py:482
  609.6 22.5 %collective-permute-done.46 = bf16[192,2560]{1,0:T(8,128)(2,1)S(1)} collective-permute-done((bf16[192,2560]{1,0:T(8,128)(2,1)}, bf16[192,2560]{1,0:T(8,128)(2,1)S(1)}, u32[]{:S(2)}, u32[]{:S(2)}) %collective-permute-start.46) | collective-permute-done | bytes 983072 | tf_op jit(solution)/shard_map/ppermute | solution.py:29
  643.3 39.1 %shard_map.226 = bf16[2560,1536]{1,0:T(8,128)(2,1)} custom-call(bf16[192,2560]{1,0:T(8,128)(2,1)} %copy-done.41, bf16[192,2560]{1,0:T(8,128)(2,1)} %collective-permute-done.30.rest_3_.rest_1_, bf16[384,2560]{1,0:T(8,128)(2,1)} %collective-permute-done.29.rest_6_.rest_2_, bf16[192,2560]{1,0:T(8,128)(2,1)} %collective-permute-done.33.rest_8_.rest_3_, ...), custom_call_target="tpu_custom_call" | custom-call | flops 1048576 | bytes 4096 | tf_op jit(solution)/shard_map/pallas_call | solution.py:543
  709.8 19.7 %collective-permute-done.53 = bf16[192,2560]{1,0:T(8,128)(2,1)S(1)} collective-permute-done((bf16[192,2560]{1,0:T(8,128)(2,1)S(1)}, bf16[192,2560]{1,0:T(8,128)(2,1)S(1)}, u32[]{:S(2)}, u32[]{:S(2)}) %collective-permute-start.53) | collective-permute-done | bytes 983072 | tf_op jit(solution)/shard_map/ppermute | solution.py:29
  731.2 13.4 %collective-permute-done.54 = bf16[192,2560]{1,0:T(8,128)(2,1)S(1)} collective-permute-done((bf16[192,2560]{1,0:T(8,128)(2,1)S(1)}, bf16[192,2560]{1,0:T(8,128)(2,1)S(1)}, u32[]{:S(2)}, u32[]{:S(2)}) %collective-permute-start.54) | collective-permute-done | bytes 983072 | tf_op jit(solution)/shard_map/ppermute | solution.py:29
  763.8 48.5 %shard_map.228 = (bf16[384,2560]{1,0:T(8,128)(2,1)}, f32[4,384,512]{2,1,0:T(8,128)}, bf16[4,384,512]{2,1,0:T(8,128)(2,1)}) custom-call(s32[1]{0:T(128)} %bitcast.core, s32[1,384]{1,0:T(1,128)} %places.3, bf16[384,2560]{1,0:T(8,128)(2,1)} %slice.661.queries, bf16[384,2560]{1,0:T(8,128)(2,1)} %shard_map.227.grads, f32[15,1,256]{2,1,0:T(1,128)} %get-tuple-element.117.logs, ...), custom_call_target="tpu_custom_call" | custom-call | flops 1048576 | bytes 4096 | tf_op jit(solution)/shard_map/pallas_call | solution.py:257
  812.3 26.6 %reduce-scatter.5.cloned.1.call-done = bf16[640,1536]{1,0:T(8,128)(2,1)} async-done(((bf16[2560,1536]{1,0:T(8,128)(2,1)}), bf16[640,1536]{1,0:T(8,128)(2,1)}) %reduce-scatter.5.cloned.1.call-update) | async-done | bytes 1966096 | tf_op jit(solution)/shard_map/reduce_scatter | solution.py:670
  840.5 17.9 %shard_map.229 = (bf16[4,4,80,2560]{3,2,1,0:T(8,128)(2,1)}, bf16[4,4,80,2560]{3,2,1,0:T(8,128)(2,1)}) custom-call(s32[8]{0:T(128)S(1)} %gather_fusion, bf16[384,2560]{1,0:T(8,128)(2,1)S(1)} %copy-done.5, bf16[384,2560]{1,0:T(8,128)(2,1)S(1)} %copy-done.11), custom_call_target="tpu_custom_call" | custom-call | flops 1048576 | bytes 4096 | tf_op jit(solution)/shard_map/pallas_call | solution.py:387
  858.3 39.0 %shard_map.230 = (bf16[2560,512]{1,0:T(8,128)(2,1)}, bf16[2560,512]{1,0:T(8,128)(2,1)}, bf16[2560,512]{1,0:T(8,128)(2,1)}) custom-call(bf16[192,2560]{1,0:T(8,128)(2,1)} %copy-done.41, bf16[192,2560]{1,0:T(8,128)(2,1)} %collective-permute-done.30.rest_3_.rest_1_, bf16[384,2560]{1,0:T(8,128)(2,1)} %collective-permute-done.29.rest_6_.rest_2_, ...), custom_call_target="tpu_custom_call" | custom-call | flops 1048576 | bytes 4096 | tf_op jit(solution)/shard_map/pallas_call | solution.py:543
  909.3 25.0 %collective-permute-done.58 = bf16[384,512]{1,0:T(8,128)(2,1)S(1)} collective-permute-done((bf16[384,512]{1,0:T(8,128)(2,1)S(1)}, bf16[384,512]{1,0:T(8,128)(2,1)S(1)}, u32[]{:S(2)}, u32[]{:S(2)}) %collective-permute-start.58) | collective-permute-done | bytes 393248 | tf_op jit(solution)/shard_map/ppermute | solution.py:121
  947.3 20.9 %shard_map.231 = (bf16[4,4,80,3072]{3,2,1,0:T(8,128)(2,1)}, bf16[4,4,80,3072]{3,2,1,0:T(8,128)(2,1)}) custom-call(s32[8]{0:T(128)S(1)} %gather_fusion, bf16[384,2560]{1,0:T(8,128)(2,1)S(1)} %copy-done.4, bf16[384,3072]{1,0:T(8,128)(2,1)S(1)} %constant_dynamic-update-slice_fusion.32.right.left), custom_call_target="tpu_custom_call" | custom-call | flops 1048576 | bytes 4096 | tf_op jit(solution)/shard_map/pallas_call | solution.py:387
  987.0 27.2 %collective-permute-start.80 = (bf16[2,80,2560]{2,1,0:T(8,128)(2,1)S(1)}, bf16[2,80,2560]{2,1,0:T(8,128)(2,1)S(1)}, u32[]{:S(2)}, u32[]{:S(2)}) collective-permute-start(bf16[2,80,2560]{2,1,0:T(8,128)(2,1)S(1)} %get-tuple-element.161), channel_id=1, source_target_pairs={{0,4},{4,0},{1,5},{5,1},{2,6},{6,2},{3,7},{7,3},{8,12},{12,8},{9,1... | collective-permute-start | bytes 2457608 | tf_op jit(solution)/shard_map/ppermute | solution.py:29
  1015.7 12.6 add_convert_fusion
  1040.1 14.7 %shard_map.232 = f32[384,2560]{1,0:T(8,128)} custom-call(s32[8]{0:T(128)S(1)} %iota_xor_fusion.slots, bf16[384,3072]{1,0:T(8,128)(2,1)} %copy-done, f32[384,2560]{1,0:T(8,128)} %broadcast_in_dim.10.start, bf16[4,80,3072]{2,1,0:T(8,128)(2,1)S(1)} %copy-done.2, bf16[4,80,3072]{2,1,0:T(8,128)(2,1)S(1)} %copy-done.10, ...), custom_call_target="tpu_custom_call" | custom-call | flops 1048576 | bytes 4096 | tf_op jit(solution)/shard_map/pallas_call | solution.py:339
  1079.1 16.3 %collective-permute-done.64 = bf16[2,80,3072]{2,1,0:T(8,128)(2,1)} collective-permute-done((bf16[2,80,3072]{2,1,0:T(8,128)(2,1)}, bf16[2,80,3072]{2,1,0:T(8,128)(2,1)}, u32[]{:S(2)}, u32[]{:S(2)}) %collective-permute-start.64) | collective-permute-done | bytes 983072 | tf_op jit(solution)/shard_map/ppermute | solution.py:29
  1114.3 47.7 %collective-permute-done.79 = bf16[2,80,2560]{2,1,0:T(8,128)(2,1)S(1)} collective-permute-done((bf16[2,80,2560]{2,1,0:T(8,128)(2,1)S(1)}, bf16[2,80,2560]{2,1,0:T(8,128)(2,1)S(1)}, u32[]{:S(2)}, u32[]{:S(2)}) %collective-permute-start.79) | collective-permute-done | bytes 819232 | tf_op jit(solution)/shard_map/ppermute | solution.py:29
  1164.8 14.8 %collective-permute-start.83 = (bf16[80,2560]{1,0:T(8,128)(2,1)}, bf16[80,2560]{1,0:T(8,128)(2,1)}, u32[]{:S(2)}, u32[]{:S(2)}) collective-permute-start(bf16[80,2560]{1,0:T(8,128)(2,1)} %get-tuple-element.204), channel_id=1, source_target_pairs={{0,8},{8,16},{16,24},{1,9},{9,17},{17,25},{2,10},{10,18},{18,26},{... | collective-permute-start | bytes 1228808 | tf_op jit(solution)/shard_map/ppermute | solution.py:83
  1196.3 12.7 collective-permute-start.87
  1236.1 12.8 collective-permute-start.74
  1257.5 12.4 collective-permute-done.73
  (476 shorter events, 410.8 us)
Async XLA Ops:
  7.2 77.3 %all-gather.9.cloned.1.call-start = ((), (), s32[]{:S(2)}) async-start(), calls=%async_computation.15 | async-start | bytes 4505600 | tf_op jit(solution)/shard_map/all_gather | solution.py:600
  10.6 446.8 %all-gather.5.cloned.1.call-start = ((), (), s32[]{:S(2)}) async-start(), calls=%async_computation.9 | async-start | bytes 9830400 | tf_op jit(solution)/shard_map/all_gather | solution.py:621
  66.4 391.0 %all-gather.7.cloned.1.call-start = ((), (), s32[]{:S(2)}) async-start(), calls=%async_computation.10 | async-start | bytes 9830400 | tf_op jit(solution)/shard_map/all_gather | solution.py:621
  153.8 685.2 %reduce-scatter.5.cloned.1.call-start = ((), (), s32[]{:S(2)}) async-start(), calls=%async_computation.11 | async-start | bytes 9830400 | tf_op jit(solution)/shard_map/reduce_scatter | solution.py:670
  167.8 72.6 %collective-permute-start.21 = (bf16[4,80,2560]{2,1,0:T(8,128)(2,1)S(1)}, bf16[4,80,2560]{2,1,0:T(8,128)(2,1)}, u32[]{:S(2)}, u32[]{:S(2)}) collective-permute-start(bf16[4,80,2560]{2,1,0:T(8,128)(2,1)S(1)} %slice.663.rest_0_), channel_id=1, source_target_pairs={{0,4},{4,0},{1,5},{5,1},{2,6},{6,2},{3,7},{7,3},{8,12},{12,8},{9,1... | collective-permute-start | bytes 4915208 | tf_op jit(solution)/shard_map/ppermute | solution.py:29
  194.5 49.6 %collective-permute-start.18 = (bf16[4,80,2560]{2,1,0:T(8,128)(2,1)S(1)}, bf16[4,80,2560]{2,1,0:T(8,128)(2,1)S(1)}, u32[]{:S(2)}, u32[]{:S(2)}) collective-permute-start(bf16[4,80,2560]{2,1,0:T(8,128)(2,1)S(1)} %slice.663.rest_0_), channel_id=1, source_target_pairs={{0,1},{1,0},{2,3},{3,2},{4,5},{5,4},{6,7},{7,6},{8,9},{9,8},{10,11... | collective-permute-start | bytes 4915208 | tf_op jit(solution)/shard_map/ppermute | solution.py:29
  220.9 81.2 %collective-permute-start.16 = (bf16[384,2560]{1,0:T(8,128)(2,1)S(1)}, bf16[384,2560]{1,0:T(8,128)(2,1)S(1)}, u32[]{:S(2)}, u32[]{:S(2)}) collective-permute-start(bf16[384,2560]{1,0:T(8,128)(2,1)S(1)} %bitcast.384), channel_id=1, source_target_pairs={{0,1},{1,0},{2,3},{3,2},{4,5},{5,4},{6,7},{7,6},{8,9},{9,8},{10,11... | collective-permute-start | bytes 5898248 | tf_op jit(solution)/shard_map/ppermute | solution.py:29
  222.4 80.3 %collective-permute-start.17 = (bf16[384,2560]{1,0:T(8,128)(2,1)S(1)}, bf16[384,2560]{1,0:T(8,128)(2,1)S(1)}, u32[]{:S(2)}, u32[]{:S(2)}) collective-permute-start(bf16[384,2560]{1,0:T(8,128)(2,1)S(1)} %bitcast.385), channel_id=1, source_target_pairs={{0,4},{4,0},{1,5},{5,1},{2,6},{6,2},{3,7},{7,3},{8,12},{12,8},{9,1... | collective-permute-start | bytes 5898248 | tf_op jit(solution)/shard_map/ppermute | solution.py:29
  241.6 49.8 %collective-permute-start.22 = (bf16[2,80,2560]{2,1,0:T(8,128)(2,1)S(1)}, bf16[2,80,2560]{2,1,0:T(8,128)(2,1)}, u32[]{:S(2)}, u32[]{:S(2)}) collective-permute-start(bf16[2,80,2560]{2,1,0:T(8,128)(2,1)S(1)} %slice.664), channel_id=1, source_target_pairs={{0,1},{1,0},{2,3},{3,2},{4,5},{5,4},{6,7},{7,6},{8,9},{9,8},{10,11... | collective-permute-start | bytes 2457608 | tf_op jit(solution)/shard_map/ppermute | solution.py:29
  244.0 48.4 %collective-permute-start.12 = (bf16[384,512]{1,0:T(8,128)(2,1)S(1)}, bf16[384,512]{1,0:T(8,128)(2,1)}, u32[]{:S(2)}, u32[]{:S(2)}) collective-permute-start(bf16[384,512]{1,0:T(8,128)(2,1)S(1)} %collective-permute-done.9.rest_0_), channel_id=1, source_target_pairs={{0,2},{2,0},{1,3},{3,1},{4,6},{6,4},{5,7},{7,5},{8,10},{10,8},{9,1... | collective-permute-start | bytes 1179656 | tf_op jit(solution)/shard_map/ppermute | solution.py:29
  244.1 48.8 %collective-permute-start.13 = (bf16[384,512]{1,0:T(8,128)(2,1)S(1)}, bf16[384,512]{1,0:T(8,128)(2,1)S(1)}, u32[]{:S(2)}, u32[]{:S(2)}) collective-permute-start(bf16[384,512]{1,0:T(8,128)(2,1)S(1)} %collective-permute-done.10.rest_1_), channel_id=1, source_target_pairs={{0,2},{2,0},{1,3},{3,1},{4,6},{6,4},{5,7},{7,5},{8,10},{10,8},{9,1... | collective-permute-start | bytes 1179656 | tf_op jit(solution)/shard_map/ppermute | solution.py:29
  292.3 53.1 %collective-permute-start.19 = (bf16[4,80,2560]{2,1,0:T(8,128)(2,1)S(1)}, bf16[4,80,2560]{2,1,0:T(8,128)(2,1)S(1)}, u32[]{:S(2)}, u32[]{:S(2)}) collective-permute-start(bf16[4,80,2560]{2,1,0:T(8,128)(2,1)S(1)} %slice.663.rest_0_), channel_id=1, source_target_pairs={{0,2},{2,0},{1,3},{3,1},{4,6},{6,4},{5,7},{7,5},{8,10},{10,8},{9,1... | collective-permute-start | bytes 4915208 | tf_op jit(solution)/shard_map/ppermute | solution.py:29
  363.0 66.4 %collective-permute-start.27 = (bf16[384,2560]{1,0:T(8,128)(2,1)S(1)}, bf16[384,2560]{1,0:T(8,128)(2,1)S(1)}, u32[]{:S(2)}, u32[]{:S(2)}) collective-permute-start(bf16[384,2560]{1,0:T(8,128)(2,1)S(1)} %multiply_convert_fusion.rest_4_.rest_7_), channel_id=1, source_target_pairs={{0,4},{4,0},{1,5},{5,1},{2,6},{6,2},{3,7},{7,3},{8,12},{12,8},{9,1... | collective-permute-start | bytes 5898248 | tf_op jit(solution)/shard_map/ppermute | solution.py:29
  363.3 67.6 %collective-permute-start.29 = (bf16[384,2560]{1,0:T(8,128)(2,1)S(1)}, bf16[384,2560]{1,0:T(8,128)(2,1)}, u32[]{:S(2)}, u32[]{:S(2)}) collective-permute-start(bf16[384,2560]{1,0:T(8,128)(2,1)S(1)} %multiply_convert_fusion.rest_4_.rest_7_), channel_id=1, source_target_pairs={{0,1},{1,0},{2,3},{3,2},{4,5},{5,4},{6,7},{7,6},{8,9},{9,8},{10,11... | collective-permute-start | bytes 5898248 | tf_op jit(solution)/shard_map/ppermute | solution.py:29
  365.0 64.3 %collective-permute-start.32 = (bf16[192,2560]{1,0:T(8,128)(2,1)S(1)}, bf16[192,2560]{1,0:T(8,128)(2,1)S(1)}, u32[]{:S(2)}, u32[]{:S(2)}) collective-permute-start(bf16[192,2560]{1,0:T(8,128)(2,1)S(1)} %slice.671), channel_id=1, source_target_pairs={{0,4},{4,0},{1,5},{5,1},{2,6},{6,2},{3,7},{7,3},{8,12},{12,8},{9,1... | collective-permute-start | bytes 2949128 | tf_op jit(solution)/shard_map/ppermute | solution.py:29
  366.7 65.8 %collective-permute-start.31 = (bf16[192,2560]{1,0:T(8,128)(2,1)S(1)}, bf16[192,2560]{1,0:T(8,128)(2,1)S(1)}, u32[]{:S(2)}, u32[]{:S(2)}) collective-permute-start(bf16[192,2560]{1,0:T(8,128)(2,1)S(1)} %slice.670), channel_id=1, source_target_pairs={{0,1},{1,0},{2,3},{3,2},{4,5},{5,4},{6,7},{7,6},{8,9},{9,8},{10,11... | collective-permute-start | bytes 2949128 | tf_op jit(solution)/shard_map/ppermute | solution.py:29
  367.4 90.0 %collective-permute-start.38 = (bf16[384,2560]{1,0:T(8,128)(2,1)S(1)}, bf16[384,2560]{1,0:T(8,128)(2,1)}, u32[]{:S(2)}, u32[]{:S(2)}) collective-permute-start(bf16[384,2560]{1,0:T(8,128)(2,1)S(1)} %copy-done.26), channel_id=1, source_target_pairs={{0,2},{2,0},{1,3},{3,1},{4,6},{6,4},{5,7},{7,5},{8,10},{10,8},{9,1... | collective-permute-start | bytes 5898248 | tf_op jit(solution)/shard_map/ppermute | solution.py:29
  682.4 379.7 %reduce-scatter.7.cloned.1.call-start = ((), (), s32[]{:S(2)}) async-start(), calls=%async_computation.12 | async-start | bytes 3276800 | tf_op jit(solution)/shard_map/reduce_scatter | solution.py:670
  705.4 106.8 %collective-permute-start.56 = (bf16[192,2560]{1,0:T(8,128)(2,1)}, bf16[192,2560]{1,0:T(8,128)(2,1)}, u32[]{:S(2)}, u32[]{:S(2)}) collective-permute-start(bf16[192,2560]{1,0:T(8,128)(2,1)} %slice.685), channel_id=1, source_target_pairs={{0,4},{4,0},{1,5},{5,1},{2,6},{6,2},{3,7},{7,3},{8,12},{12,8},{9,1... | collective-permute-start | bytes 2949128 | tf_op jit(solution)/shard_map/ppermute | solution.py:29
  708.4 103.8 %collective-permute-start.49 = (bf16[192,2560]{1,0:T(8,128)(2,1)}, bf16[192,2560]{1,0:T(8,128)(2,1)}, u32[]{:S(2)}, u32[]{:S(2)}) collective-permute-start(bf16[192,2560]{1,0:T(8,128)(2,1)} %get-tuple-element.109), channel_id=1, source_target_pairs={{0,1},{1,0},{2,3},{3,2},{4,5},{5,4},{6,7},{7,6},{8,9},{9,8},{10,11... | collective-permute-start | bytes 2949128 | tf_op jit(solution)/shard_map/ppermute | solution.py:29
  729.5 82.8 %collective-permute-start.55 = (bf16[192,2560]{1,0:T(8,128)(2,1)}, bf16[192,2560]{1,0:T(8,128)(2,1)}, u32[]{:S(2)}, u32[]{:S(2)}) collective-permute-start(bf16[192,2560]{1,0:T(8,128)(2,1)} %get-tuple-element.111), channel_id=1, source_target_pairs={{0,4},{4,0},{1,5},{5,1},{2,6},{6,2},{3,7},{7,3},{8,12},{12,8},{9,1... | collective-permute-start | bytes 2949128 | tf_op jit(solution)/shard_map/ppermute | solution.py:29
  729.8 82.5 %collective-permute-start.50 = (bf16[192,2560]{1,0:T(8,128)(2,1)}, bf16[192,2560]{1,0:T(8,128)(2,1)}, u32[]{:S(2)}, u32[]{:S(2)}) collective-permute-start(bf16[192,2560]{1,0:T(8,128)(2,1)} %get-tuple-element.110), channel_id=1, source_target_pairs={{0,1},{1,0},{2,3},{3,2},{4,5},{5,4},{6,7},{7,6},{8,9},{9,8},{10,11... | collective-permute-start | bytes 2949128 | tf_op jit(solution)/shard_map/ppermute | solution.py:29
  897.4 286.6 %reduce-scatter.9.cloned.1.call-start = ((), (), s32[]{:S(2)}) async-start(), calls=%async_computation.13 | async-start | bytes 3276800 | tf_op jit(solution)/shard_map/reduce_scatter | solution.py:670
  908.9 65.3 %collective-permute-start.76 = (bf16[4,4,80,2560]{3,2,1,0:T(8,128)(2,1)}, bf16[4,4,80,2560]{3,2,1,0:T(8,128)(2,1)}, u32[]{:S(2)}, u32[]{:S(2)}) collective-permute-start(bf16[4,4,80,2560]{3,2,1,0:T(8,128)(2,1)} %get-tuple-element.139), channel_id=1, source_target_pairs={{0,2},{2,0},{1,3},{3,1},{4,6},{6,4},{5,7},{7,5},{8,10},{10,8},{9,1... | collective-permute-start | bytes 19660808 | tf_op jit(solution)/shard_map/ppermute | solution.py:29
  968.3 289.2 %reduce-scatter.11.cloned.1.call-start = ((), (), s32[]{:S(2)}) async-start(), calls=%async_computation.14 | async-start | bytes 3276800 | tf_op jit(solution)/shard_map/reduce_scatter | solution.py:670
  1037.1 58.3 %collective-permute-start.64 = (bf16[2,80,3072]{2,1,0:T(8,128)(2,1)}, bf16[2,80,3072]{2,1,0:T(8,128)(2,1)}, u32[]{:S(2)}, u32[]{:S(2)}) collective-permute-start(bf16[2,80,3072]{2,1,0:T(8,128)(2,1)} %get-tuple-element.151), channel_id=1, source_target_pairs={{0,1},{1,0},{2,3},{3,2},{4,5},{5,4},{6,7},{7,6},{8,9},{9,8},{10,11... | collective-permute-start | bytes 2949128 | tf_op jit(solution)/shard_map/ppermute | solution.py:29
  1062.3 50.6 %collective-permute-start.77 = (bf16[2,80,2560]{2,1,0:T(8,128)(2,1)}, bf16[2,80,2560]{2,1,0:T(8,128)(2,1)S(1)}, u32[]{:S(2)}, u32[]{:S(2)}) collective-permute-start(bf16[2,80,2560]{2,1,0:T(8,128)(2,1)} %get-tuple-element.164), channel_id=1, source_target_pairs={{0,1},{1,0},{2,3},{3,2},{4,5},{5,4},{6,7},{7,6},{8,9},{9,8},{10,11... | collective-permute-start | bytes 2457608 | tf_op jit(solution)/shard_map/ppermute | solution.py:29
  1074.3 105.3 %collective-permute-start.69 = (bf16[2,80,3072]{2,1,0:T(8,128)(2,1)}, bf16[2,80,3072]{2,1,0:T(8,128)(2,1)S(1)}, u32[]{:S(2)}, u32[]{:S(2)}) collective-permute-start(bf16[2,80,3072]{2,1,0:T(8,128)(2,1)} %get-tuple-element.152), channel_id=1, source_target_pairs={{0,4},{4,0},{1,5},{5,1},{2,6},{6,2},{3,7},{7,3},{8,12},{12,8},{9,1... | collective-permute-start | bytes 2949128 | tf_op jit(solution)/shard_map/ppermute | solution.py:29
  1095.4 92.1 %collective-permute-start.63 = (bf16[192,2560]{1,0:T(8,128)(2,1)}, bf16[192,2560]{1,0:T(8,128)(2,1)}, u32[]{:S(2)}, u32[]{:S(2)}) collective-permute-start(bf16[192,2560]{1,0:T(8,128)(2,1)} %add_convert_fusion.5), channel_id=1, source_target_pairs={{0,1},{1,0},{2,3},{3,2},{4,5},{5,4},{6,7},{7,6},{8,9},{9,8},{10,11... | collective-permute-start | bytes 2949128 | tf_op jit(solution)/shard_map/ppermute | solution.py:29
  1096.8 90.7 %collective-permute-start.62 = (bf16[192,2560]{1,0:T(8,128)(2,1)}, bf16[192,2560]{1,0:T(8,128)(2,1)}, u32[]{:S(2)}, u32[]{:S(2)}) collective-permute-start(bf16[192,2560]{1,0:T(8,128)(2,1)} %add_convert_fusion.6), channel_id=1, source_target_pairs={{0,4},{4,0},{1,5},{5,1},{2,6},{6,2},{3,7},{7,3},{8,12},{12,8},{9,1... | collective-permute-start | bytes 2949128 | tf_op jit(solution)/shard_map/ppermute | solution.py:29
  1103.5 58.5 %collective-permute-start.79 = (bf16[2,80,2560]{2,1,0:T(8,128)(2,1)S(1)}, bf16[2,80,2560]{2,1,0:T(8,128)(2,1)S(1)}, u32[]{:S(2)}, u32[]{:S(2)}) collective-permute-start(bf16[2,80,2560]{2,1,0:T(8,128)(2,1)S(1)} %get-tuple-element.160), channel_id=1, source_target_pairs={{0,4},{4,0},{1,5},{5,1},{2,6},{6,2},{3,7},{7,3},{8,12},{12,8},{9,1... | collective-permute-start | bytes 2457608 | tf_op jit(solution)/shard_map/ppermute | solution.py:29
  1112.8 68.1 %collective-permute-start.68 = (bf16[2,80,3072]{2,1,0:T(8,128)(2,1)S(1)}, bf16[2,80,3072]{2,1,0:T(8,128)(2,1)S(1)}, u32[]{:S(2)}, u32[]{:S(2)}) collective-permute-start(bf16[2,80,3072]{2,1,0:T(8,128)(2,1)S(1)} %get-tuple-element.137), channel_id=1, source_target_pairs={{0,1},{1,0},{2,3},{3,2},{4,5},{5,4},{6,7},{7,6},{8,9},{9,8},{10,11... | collective-permute-start | bytes 2949128 | tf_op jit(solution)/shard_map/ppermute | solution.py:29
  (140 other events, 3375.9 us)
Sparse Core Ops, SparseCore 0:
  10.7 73.7 all-gather.8
  86.1 152.2 all-gather.4
  239.9 153.5 all-gather.6
  682.6 156.3 reduce-scatter.4
  897.5 77.6 reduce-scatter.6
  977.3 78.7 reduce-scatter.8
  1058.4 51.7 reduce-scatter.10

commit v4 on v3

--- a/solution.py
+++ b/solution.py
@@ -10,7 +10,6 @@
 WINDOW = 2048
 SUB = 128
 TILE = 512
-FEW = 4
 epsilon = 1e-06
 blocked_score = -1e30
 PLANE = ("y", "c", "x")
@@ -48,51 +47,19 @@
     return [jnp.concatenate(block, 0) if isinstance(block, tuple) else block for block in blocks]
 
 
-def core_sum(keep, send):
-    return keep.astype(f32) + swap(send, "c").astype(f32)
-
-
-def scatter_start(diag, to_x, to_y):
-    half = diag.shape[0] // 2
-    return (
-        swap(diag[:half].astype(low), "x"),
-        swap(diag[half:].astype(low), "y"),
-        swap(to_x[:half].astype(low), "x"),
-        swap(to_y[half:].astype(low), "y"),
-    )
-
-
-def scatter_turn(started, to_x, to_y, later=()):
-    half = to_x.shape[0] // 2
-    diag_x, diag_y = (value.astype(f32) for value in started[:2])
-    return (
-        after((to_x[half:] + diag_y).astype(low), *later),
-        after((to_y[:half] + diag_x).astype(low), *later),
-    )
-
-
-def scatter_end(started, x_bottom, y_top, own):
-    half = own.shape[0] // 2
-    x_top, y_bottom = (value.astype(f32) for value in started[2:])
-    x_bottom, y_top = swap(x_bottom, "x").astype(f32), swap(y_top, "y").astype(f32)
-    return jnp.concatenate([own[:half] + x_top + y_top, own[half:] + x_bottom + y_bottom], 0)
-
-
-def shift(value, steps):
-    count = lax.axis_size("z")
-    return lax.ppermute(value, "z", [(i, i + steps) for i in range(count) if 0 <= i + steps < count])
-
-
-def planes_scatter(column):
-    count = lax.axis_size("z")
-    if count > FEW:
-        return lax.psum_scatter(column, "z", scatter_dimension=0, tiled=False).astype(f32)
-    here = lax.axis_index("z")
-    total = lax.dynamic_index_in_dim(column, here, 0, False).astype(f32)
-    for r in range(1, count):
-        part = lax.dynamic_index_in_dim(column, (here + r) % count, 0, False)
-        total = total + shift(part, r).astype(f32) + shift(part, r - count).astype(f32)
-    return total
+def stage(sends, work=None, given=()):
+    fenced, given = lax.optimization_barrier((tuple(value for value, _ in sends), tuple(given)))
+    received = tuple(
+        swap(value, way) if isinstance(way, str) else way(value) for value, (_, way) in zip(fenced, sends)
+    )
+    return lax.optimization_barrier((received, work(*given) if work else given))
+
+
+def boxed(sure, work, *given):
+    shapes = jax.eval_shape(work, *given)
+    return lax.cond(
+        sure, work, lambda *_: jax.tree.map(lambda out: jnp.zeros(out.shape, out.dtype), shapes), *given
+    )
 
 
 def plane_index():
@@ -103,25 +70,14 @@
     return lax.optimization_barrier((value,) + earlier)[0]
 
 
-def window_blocks(pair, chips):
+def across(distance):
+    return lambda value: lax.ppermute(value, PLANE, [(i, i ^ distance) for i in range(8)])
+
+
+def behind(steps):
     count = lax.axis_size("z") * lax.axis_size("y")
-    same = [
-        lax.ppermute(pair, ("z", "y"), [(i, i + d) for i in range(count - d)])
-        for d in range(chips, 0, -1)
-    ] + [pair]
-    same = list(lax.optimization_barrier(tuple(same)))
-    return same + [swap(block, "c") for block in same]
-
-
-def return_blocks(mine, theirs, chips):
-    count = lax.axis_size("z") * lax.axis_size("y")
-    mine = mine + swap(theirs, "c").astype(f32)
-    total = mine[chips]
-    for d in range(chips, 0, -1):
-        total = total + lax.ppermute(
-            mine[chips - d].astype(low), ("z", "y"), [(i + d, i) for i in range(count - d)]
-        ).astype(f32)
-    return total
+    pairs = [(i, i + steps) for i in range(count) if 0 <= i + steps < count]
+    return lambda value: lax.ppermute(value, ("z", "y"), pairs)
 
 
 def two_heads(block, size):
@@ -382,17 +338,18 @@
         order = jnp.argsort(slots)
         blocks = jnp.swapaxes(jnp.take(blocks, order, axis=1), 0, 1)
         return blocks[:4], blocks[4:]
-    group = pl.BlockSpec((4, 1, rows, TILE), lambda z, n, s: (0, z, 0, n))
+    tile = wide if wide <= 5 * TILE else TILE
+    group = pl.BlockSpec((4, 1, rows, tile), lambda z, n, s: (0, z, 0, n))
     shape = jax.ShapeDtypeStruct((4, planes, rows, wide), low)
     return pl.pallas_call(
         row_grads_kernel,
         out_shape=(shape, shape),
         grid_spec=pltpu.PrefetchScalarGridSpec(
             num_scalar_prefetch=1,
-            grid=(planes, wide // TILE),
+            grid=(planes, wide // tile),
             in_specs=[
                 pl.BlockSpec((count, 8 * rows), lambda z, n, s: (0, z)),
-                pl.BlockSpec((count, TILE), lambda z, n, s: (0, n)),
+                pl.BlockSpec((count, tile), lambda z, n, s: (0, n)),
             ],
             out_specs=[group, group],
             scratch_shapes=[pltpu.VMEM((8 * rows, count), low)],
@@ -406,8 +363,8 @@
     weights, rest = rest[:per], rest[per:]
     pieces = 2 * sum(tiles)
     sources, rest = rest[:pieces], rest[pieces:]
-    outs, grad_units, hidden = rest[0:2], rest[2:4], rest[4 : 4 + per]
-    units, grads, arrived = rest[4 + per :]
+    before, rest = rest[:-8], rest[-8:]
+    outs, grad_units, hidden, units, grads, arrived = rest[0:2], rest[2:4], *rest[4:]
     step = pl.program_id(0)
 
     def fetches(tile):
@@ -440,37 +397,42 @@
             for copy in fetches(tile):
                 copy.wait()
 
-    unit = units[step % 2]
-    grad = grads[step % 2]
     slope = 0.7978845608028654
     for j in range(per):
-        both = dot(unit, weights[j][:, : 2 * part], (1, 0))
+        both = dot(units[step % 2], weights[j][:, : 2 * part], (1, 0))
         gates, upward = both[:, :part], both[:, part:]
-        grad_middle = dot(grad, weights[j][:, 2 * part :], (1, 0))
+        grad_middle = dot(grads[step % 2], weights[j][:, 2 * part :], (1, 0))
         square = gates * gates
         bend = jnp.tanh(slope * gates * (1.0 + 0.044715 * square))
         half = 0.5 * (1.0 + bend)
         gelu = gates * half
         grad_gelu = half + 0.5 * gates * (1.0 - bend * bend) * (slope * (1.0 + 3 * 0.044715 * square))
-        hidden[j][:, :part] = (grad_middle * upward * grad_gelu).astype(low)
-        hidden[j][:, part : 2 * part] = (grad_middle * gelu).astype(low)
-        hidden[j][:, 2 * part :] = (gelu * upward).astype(low)
+        at = 2 * part * j
+        hidden[:, at : at + part] = (grad_middle * upward * grad_gelu).astype(low)
+        hidden[:, at + part : at + 2 * part] = (grad_middle * gelu).astype(low)
+        at = part * (2 * per + j)
+        hidden[:, at : at + part] = (gelu * upward).astype(low)
     for which, targets in enumerate((outs, grad_units)):
         value = 0.0
         for j in range(per):
-            columns = slice(0, 2 * part) if which else slice(2 * part, 3 * part)
-            value = value + dot(hidden[j][:, columns], weights[j][:, columns], (1, 1))
+            at, width = (2 * part * j, 2 * part) if which else (part * (2 * per + j), part)
+            first = 0 if which else 2 * part
+            value = value + dot(hidden[:, at : at + width], weights[j][:, first : first + width], (1, 1))
         for side in range(2):
 
             @pl.when(step // (len(tiles) // 2) == side)
             def _():
-                targets[side][...] = value.astype(low)
-
-
-def mlp(units, grads, weights):
+                if before:
+                    targets[side][...] = (value + before[2 * which + side][...].astype(f32)).astype(low)
+                else:
+                    targets[side][...] = value.astype(low)
+
+
+def mlp(units, grads, weights, before):
     rows = sum(piece.shape[0] for piece in units[0])
     count, wide = rows * len(units), units[0][0].shape[1]
     per, each = len(weights), weights[0].shape[1]
+    deep = per * each
     tiles = tuple(len(tile) for tile in units)
     sources = [piece for pair in zip(units, grads) for tile in pair for piece in tile]
     side = len(units) // 2
@@ -481,11 +443,12 @@
     half = jax.ShapeDtypeStruct((count // 2, wide), low)
     return pl.pallas_call(
         functools.partial(mlp_kernel, each // 3, per, tiles),
-        out_shape=[half] * 4 + [jax.ShapeDtypeStruct((count, each), low)] * per,
+        out_shape=[half] * 4 + [jax.ShapeDtypeStruct((count, deep), low)],
         grid=(len(units),),
         in_specs=[pl.BlockSpec((wide, each), lambda i: (0, 0), pipeline_mode=pl.Buffered(1))] * per
-        + [pl.BlockSpec(memory_space=pl.ANY)] * len(sources),
-        out_specs=sides * 2 + [pl.BlockSpec((rows, each), lambda i: (i, 0))] * per,
+        + [pl.BlockSpec(memory_space=pl.ANY)] * len(sources)
+        + (sides * 2 if before else []),
+        out_specs=sides * 2 + [pl.BlockSpec((rows, deep), lambda i: (i, 0))],
         scratch_shapes=[
             pltpu.VMEM((2, rows, wide), low),
             pltpu.VMEM((2, rows, wide), low),
@@ -493,15 +456,15 @@
         ],
         compiler_params=pltpu.CompilerParams(vmem_limit_bytes=62 << 20),
         cost_estimate=NOMINAL,
-    )(*weights, *sources)
+    )(*weights, *sources, *before)
 
 
 def mlp_grads_kernel(number, *rest):
     units, grads, hidden, rest = rest[:number], rest[number : 2 * number], rest[2 * number : 2 * number + 2], rest[2 * number + 2 :]
-    outs, turned = rest[:-1], rest[-1]
+    *outs, turned = rest
+    out_wide = outs[0].shape[1]
     step = pl.program_id(0)
     part = hidden[0].shape[1] // 3
-    out_wide = outs[0].shape[1]
     piece = min(part, 256)
 
     def turn(slot, which, sources, share, shares):
@@ -534,7 +497,7 @@
             turn(step % 2, 1, grads, i, len(work))
 
 
-def mlp_grads(units, grads, hidden, pieces):
+def mlp_grads(units, grads, hidden, pieces=1):
     wide = units[0].shape[1]
     deep = hidden[0].shape[1]
     count = sum(piece.shape[0] for piece in units)
@@ -555,11 +518,100 @@
     )(*units, *grads, *hidden)
 
 
+def token_grads_kernel(number, *rest):
+    units, (right, out, turned) = rest[:number], rest[number:]
+
+    @pl.when(pl.program_id(0) == 0)
+    def _():
+        turned[...] = right[...].T
+
+    value, at = 0.0, 0
+    for unit in units:
+        value = value + dot(turned[:, at : at + unit.shape[0]], unit[...], (1, 0))
+        at += unit.shape[0]
+    out[...] = value.astype(low).T
+
+
+def token_grads(units, right):
+    wide = units[0].shape[1]
+    count, deep = right.shape
+    rows = 512
+    return pl.pallas_call(
+        functools.partial(token_grads_kernel, len(units)),
+        out_shape=jax.ShapeDtypeStruct((wide, deep), low),
+        grid=(wide // rows,),
+        in_specs=[pl.BlockSpec((piece.shape[0], rows), lambda s: (0, s)) for piece in units]
+        + [pl.BlockSpec(right.shape, lambda s: (0, 0), pipeline_mode=pl.Buffered(1))],
+        out_specs=pl.BlockSpec((rows, deep), lambda s: (s, 0)),
+        scratch_shapes=[pltpu.VMEM((deep, count), low)],
+        compiler_params=pltpu.CompilerParams(vmem_limit_bytes=56 << 20),
+        cost_estimate=NOMINAL,
+    )(*units, right)
+
+
+def spread_kernel(slots, value, *outs):
+    deep = outs[0].shape[1]
+    for i, out in enumerate(outs):
+        out[...] = value[:, pl.ds(pl.multiple_of(slots[i] * deep, 128), deep)]
+
+
+def spread(value):
+    count, wide = value.shape
+    slots = (plane_index() ^ jnp.arange(8)).astype(jnp.int32)
+    deep = wide // 8
+    if deep % 128:
+        return [lax.dynamic_slice(value, (0, slots[r] * deep), (count, deep)) for r in range(8)]
+    return pl.pallas_call(
+        spread_kernel,
+        out_shape=[jax.ShapeDtypeStruct((count, deep), value.dtype)] * 8,
+        grid_spec=pltpu.PrefetchScalarGridSpec(
+            num_scalar_prefetch=1,
+            grid=(1,),
+            in_specs=[pl.BlockSpec((count, wide), lambda i, s: (0, 0))],
+            out_specs=[pl.BlockSpec((count, deep), lambda i, s: (0, 0))] * 8,
+        ),
+        cost_estimate=NOMINAL,
+    )(slots, value)
+
+
 def shares(columns):
     tiles = -(-columns // 128)
     few, more = divmod(tiles, 8)
     sizes = [128 * (few + (p < more)) for p in range(8)]
     return [(sum(sizes[:p]), size) for p, size in enumerate(sizes)], 128 * (few + (more > 0))
+
+
+def finish_kernel(spans, part, per, gain, gate, up, whole, gate_out, up_out, down_out, gain_out):
+    scale = gain[...]
+    total = jnp.zeros_like(scale)
+    for p, (at, n) in enumerate(spans):
+        for q in range(-(-n // part)):
+            width = min(part, n - q * part)
+            start, j = 3 * part * per * (q // per), q % per
+            place = slice(at + q * part, at + q * part + width)
+            for which, (weight, out) in enumerate(((gate, gate_out), (up, up_out))):
+                first = start + part * (2 * j + which)
+                value = whole[p, :, first : first + width].astype(f32)
+                total = total + jnp.sum(value * weight[:, place].astype(f32), axis=1, keepdims=True)
+                out[:, place] = value * scale
+            first = start + part * (2 * per + j)
+            down_out[place, :] = whole[p, :, first : first + width].astype(f32).T
+    gain_out[...] = total
+
+
+def finish(spans, part, per, gain, gate, up, whole):
+    rows, columns = gate.shape
+    return pl.pallas_call(
+        functools.partial(finish_kernel, spans, part, per),
+        out_shape=(
+            jax.ShapeDtypeStruct((rows, columns), f32),
+            jax.ShapeDtypeStruct((rows, columns), f32),
+            jax.ShapeDtypeStruct((columns, rows), f32),
+            jax.ShapeDtypeStruct((rows, 1), f32),
+        ),
+        compiler_params=pltpu.CompilerParams(vmem_limit_bytes=48 << 20),
+        cost_estimate=NOMINAL,
+    )(gain, gate, up, whole)
 
 
 def unit_of(values):
@@ -595,13 +647,15 @@
     gain_one = attn_gain[:, None]
     gain_two = mlp_gain[:, None]
 
-    attn_shard = jnp.concatenate([query_weight, key_weight, value_weight], 1).astype(f32) * gain_one
-    attn_shard = jnp.concatenate([attn_shard.astype(low), out_weight.T], 1)
-    attn_column = lax.all_gather(attn_shard, "z", axis=0, tiled=False)
-    qkv_column, out_column = attn_column[:, :, : wide + 2 * size], attn_column[:, :, wide + 2 * size :]
+    qkv_shard = jnp.concatenate([query_weight, key_weight, value_weight], 1).astype(f32) * gain_one
+    qkv_shard = qkv_shard.astype(low)
+    qkv_column = lax.all_gather(qkv_shard, "z", axis=0, tiled=False)
+    out_column = lax.all_gather(after(out_weight.T, qkv_shard), "z", axis=0, tiled=False)
 
     spans, share = shares(gate_weight.shape[1])
-    parts = 2 if share % 256 == 0 else 1
+    parts = share // 256 if share % 256 == 0 else 1
+    calls = 2 if parts % 2 == 0 else 1
+    per = parts // calls
     part = share // parts
     mlp_shards = (
         (gate_weight.astype(f32) * gain_two).astype(low),
@@ -615,99 +669,266 @@
     mine = jnp.concatenate(
         [whole[:, :, k * part : (k + 1) * part] for k in range(parts) for whole in split], 2
     )
-    mlp_column = lax.all_to_all(after(mine, attn_shard), PLANE, split_axis=0, concat_axis=0, tiled=True)
+    gift = cotangent[0]
+    mlp_column = lax.all_to_all(after(mine, qkv_shard), PLANE, split_axis=0, concat_axis=0, tiled=True)
     mlp_column = mlp_column.reshape(-1, 3 * share)
-    mlp_full = [
-        lax.all_gather(mlp_column[:, k * 3 * part : (k + 1) * 3 * part], "z", axis=0, tiled=True) for k in range(parts)
+
+    def gathered(k, *earlier):
+        piece = after(mlp_column[:, k * 3 * part : (k + 1) * 3 * part], *earlier)
+        return lax.all_gather(piece, "z", axis=0, tiled=True)
+
+    mlp_full = [gathered(0)]
+    sure = positions[0, 0] >= 0
+    half = count // 2
+
+    def project(qkv_column, tokens, gift):
+        qkv_blocks = joined_blocks(plane_gather(qkv_column))
+        scale_one, unit_one = unit_of(tokens[0].astype(f32))
+        qkv = apply_rows(unit_one, qkv_blocks)
+        queries, pair = qkv[:, :wide], qkv[:, wide:]
+        moves = [behind(d) for d in range(chips, 0, -1)]
+        found, _ = stage([(pair, move) for move in moves] + [(pair, "c"), (gift, "x"), (gift, "y"), (gift, "c")])
+        *pairs, pair_c, gift_x, gift_y, gift_c = found
+        found, _ = stage([(block, "c") for block in pairs])
+        gifts = gift_x, gift_y, gift_c
+        return qkv_blocks[1:], queries, [*pairs, pair, *found, pair_c], gifts, unit_one, scale_one
+
+    def forward(queries, pairs, out_column, tokens, positions, gift_x, gift_y):
+        inputs = tokens[0].astype(f32)
+        mid = out_column.shape[0] // 2
+        (out_x, out_y, out_c, gift_x_c, gift_y_c), (mixed, logs) = stage(
+            [(out_column, "x"), (out_column, "y"), (out_column, "c"), (gift_x, "c"), (gift_y, "c")],
+            lambda *given: attend(given[0], given[1:], positions, size, base),
+            [queries, *pairs],
+        )
+        (out_top, out_bottom, out_x_c, out_y_c), _ = stage(
+            [(out_y[:mid], "x"), (out_x[mid:], "y"), (out_x, "c"), (out_y, "c")]
+        )
+        out_diag = jnp.concatenate([out_top, out_bottom], 0)
+        (out_diag_c,), _ = stage([(out_diag, "c")])
+        out_blocks = [out_column, out_x, out_c, out_x_c, out_y, out_diag, out_y_c, out_diag_c]
+        resid = apply_rows(mixed, out_blocks, inputs)
+        scale_two, unit_two = unit_of(resid)
+        (unit_x, unit_y, unit_c), _ = stage([(unit_two, "x"), (unit_two, "y"), (unit_two, "c")])
+        (unit_x_c, unit_y_c), _ = stage([(unit_x, "c"), (unit_y, "c")])
+        unit_blocks = unit_two, unit_x, unit_c, unit_x_c, unit_y, unit_y_c
+        return out_blocks[1:], mixed, logs, resid, scale_two, unit_blocks, gift_x_c, gift_y_c
+
+    qkv_column = after(qkv_column, mlp_column)
+    qkv_blocks, queries, pairs, gifts, unit_one, scale_one = boxed(sure, project, qkv_column, tokens, gift)
+    gift_x, gift_y, gift_c = gifts
+    mlp_full += [gathered(k, pairs[0]) for k in range(1, parts)]
+    out_blocks, mixed, logs, resid, scale_two, unit_blocks, gift_x_c, gift_y_c = boxed(
+        sure, forward, after(queries, mlp_full[0]), pairs, out_column, tokens, positions, gift_x, gift_y
+    )
+    qkv_blocks, out_blocks = [qkv_column, *qkv_blocks], [out_column, *out_blocks]
+    grads_near = [(gift_y,), (gift,), (gift_y_c,), (gift_c,)]
+
+    def flat(*tiles):
+        return [piece for group in tiles for tile in group for piece in tile]
+
+    def summed(keep, received):
+        return keep.astype(f32) + received.astype(f32)
+
+    def halves(value):
+        middle = value.shape[0] // 2
+        return value[:middle], value[middle:]
+
+    def total(*values):
+        return sum(value.astype(f32) for value in values)
+
+    def opening(weights, blocks, gift_x, gift_x_c, grads_near, unit_one):
+        unit_two, unit_x, unit_c, unit_x_c, unit_y, unit_y_c = blocks
+        units_near = [(unit_y,), (unit_two,), (unit_y_c,), (unit_c,)]
+        gift_y = grads_near[0][0]
+        sends = [(unit_y[:half], "x"), (unit_x[half:], "y"), (gift_y[:half], "x"), (gift_x[half:], "y")]
+        one_sends = [(unit_one, "x"), (unit_one, "y"), (unit_one, "c")]
+        far_sums = near_sums = partial = ()
+        if calls > 1:
+            (unit_top, unit_bottom, gift_top, gift_bottom), near_sums = stage(
+                sends, lambda *given: mlp([(v,) for v in given], grads_near, weights, ()), flat(units_near)
+            )
+        else:
+            (unit_top, unit_bottom, gift_top, gift_bottom), _ = stage(sends)
+        (unit_top_c, unit_bottom_c, gift_top_c, gift_bottom_c), _ = stage(
+            [(unit_top, "c"), (unit_bottom, "c"), (gift_top, "c"), (gift_bottom, "c")]
+        )
+        grads_far = [(gift_top, gift_bottom), (gift_x,), (gift_top_c, gift_bottom_c), (gift_x_c,)]
+        units_far = [(unit_top, unit_bottom), (unit_x,), (unit_top_c, unit_bottom_c), (unit_x_c,)]
+        if calls > 1:
+            (one_x, one_y, one_c), far_sums = stage(
+                one_sends, lambda weights: mlp(units_far, grads_far, weights, ()), [weights]
+            )
+        else:
+            (one_x, one_y, one_c), _ = stage(one_sends)
+        one_sends = [(one_y[:half], "x"), (one_x[half:], "y"), (one_x, "c"), (one_y, "c")]
+        if calls > 1:
+            (one_top, one_bottom, one_x_c, one_y_c), partial = stage(
+                one_sends,
+                lambda *given: mlp_grads(flat(units_far, units_near), flat(grads_far, grads_near), given)[0],
+                [far_sums[4], near_sums[4]],
+            )
+        else:
+            (one_top, one_bottom, one_x_c, one_y_c), _ = stage(one_sends)
+        ones = one_x, one_c, one_x_c, one_y, one_top, one_bottom, one_y_c
+        halves_far = unit_top, unit_bottom, unit_top_c, unit_bottom_c
+        return halves_far, grads_far, far_sums[:4], near_sums[:4], partial, ones
+
+    columns = []
+    unit_two, unit_x, unit_c, unit_x_c, unit_y, unit_y_c = unit_blocks
+    if calls > 1:
+        unit_blocks = after(unit_blocks, *mlp_full[per : per + 1])
+    halves_far, grads_far, far_before, near_before, partial, ones = boxed(
+        sure, opening, mlp_full[:per] if calls > 1 else (), unit_blocks, gift_x, gift_x_c, grads_near, unit_one
+    )
+    if calls > 1:
+        columns.append(lax.psum_scatter(partial, "z", scatter_dimension=0, tiled=True))
+    unit_top, unit_bottom, unit_top_c, unit_bottom_c = halves_far
+    units_far = [(unit_top, unit_bottom), (unit_x,), (unit_top_c, unit_bottom_c), (unit_x_c,)]
+    units_near = [(unit_y,), (unit_two,), (unit_y_c,), (unit_c,)]
+
+    def middle(weights, units_far, units_near, grads_far, grads_near, far_before, near_before, resid, scale_two, gift, ones):
+        (one_top_c, one_bottom_c), far_sums = stage(
+            [(ones[4], "c"), (ones[5], "c")],
+            lambda *weights: mlp(units_far, grads_far, weights, far_before),
+            weights,
+        )
+        (found,), _ = stage([(far_sums[3], "c")])
+        both = summed(far_sums[2], found).astype(low)
+        (diag_top, diag_bottom), (x_top, x_bottom) = halves(both[:count]), halves(both[count:])
+        (diag_x, diag_y, x_top, far_out), near_sums = stage(
+            [(diag_top, "x"), (diag_bottom, "y"), (x_top, "x"), (far_sums[1], "c")],
+            lambda *given: mlp([(value,) for value in given], grads_near, weights, near_before),
+            [tile[0] for tile in units_near],
+        )
+        (found,), _ = stage([(near_sums[3], "c")])
+        both = summed(near_sums[2], found)
+        (y_top, y_bottom), (own_top, own_bottom) = halves(both[:count]), halves(both[count:])
+        x_bottom, y_top = total(x_bottom, diag_y).astype(low), total(y_top, diag_x).astype(low)
+        (y_bottom, x_bottom, y_top, near_out), partial = stage(
+            [(y_bottom.astype(low), "y"), (x_bottom, "x"), (y_top, "y"), (near_sums[1], "c")],
+            lambda *given: mlp_grads(flat(units_far, units_near), flat(grads_far, grads_near), given, cuts),
+            [far_sums[4], near_sums[4]],
+        )
+        grad_unit_two = jnp.concatenate(
+            [total(own_top, x_top, y_top), total(own_bottom, x_bottom, y_bottom)], 0
+        )
+        grad_resid = gift.astype(f32) + unit_back(grad_unit_two, resid, scale_two)
+        out_far = summed(far_sums[0], far_out).astype(low)
+        out_near = summed(near_sums[0], near_out).astype(low)
+        return partial, grad_resid, grad_resid.astype(low), out_far, out_near, one_top_c, one_bottom_c
+
+    cuts = 2 if part % 256 == 0 and per % 2 == 0 else 1
+    partial, grad_resid, grad_attn, out_far, out_near, one_top_c, one_bottom_c = boxed(
+        sure,
+        middle,
+        mlp_full[-per:],
+        units_far,
+        units_near,
+        grads_far,
+        grads_near,
+        far_before,
+        near_before,
+        resid,
+        scale_two,
+        gift,
+        ones,
+    )
+    columns.append(lax.psum_scatter(partial[0], "z", scatter_dimension=0, tiled=True))
+    one_x, one_c, one_x_c, one_y, one_top, one_bottom, one_y_c = ones
+    flat_ones = [unit_one, one_x, one_c, one_x_c, one_y, one_top, one_bottom, one_y_c, one_top_c, one_bottom_c]
+
+    def first_sends(diag, to_x, to_y):
+        diag_top, diag_bottom = halves(diag)
+        return [(diag_top, "x"), (diag_bottom, "y"), (halves(to_x)[0], "x"), (halves(to_y)[1], "y")]
+
+    def second_sends(to_x, to_y, received):
+        x_bottom = total(halves(to_x)[1], received[1]).astype(low)
+        y_top = total(halves(to_y)[0], received[0]).astype(low)
+        return [(x_bottom, "x"), (y_top, "y")]
+
+    def joined(own, first, second):
+        top, bottom = halves(own)
+        return jnp.concatenate([total(top, first[2], second[1]), total(bottom, second[0], first[3])], 0)
+
+    def backward(grad_attn, out_far, out_near, queries, pairs, logs, out_blocks, positions):
+        def attention(grad_attn):
+            grad_mixed = apply_rows(grad_attn, out_blocks)
+            return attend_back(queries, grad_mixed, logs, pairs, positions, size, base)
+
+        first, (grad_queries, mine, theirs) = stage(
+            first_sends(out_far[:count], out_far[count:], out_near[:count]), attention, [grad_attn]
+        )
+        (found,), _ = stage([(theirs, "c")])
+        mine = summed(mine, found)
+        second = second_sends(out_far[count:], out_near[:count], first)
+        found, second = stage(
+            [(mine[chips - d].astype(low), behind(-d)) for d in range(chips, 0, -1)],
+            lambda *given: given,
+            [value for value, _ in second],
+        )
+        grad_pair = total(mine[chips], *found).astype(low)
+        return jnp.concatenate([grad_queries, grad_pair], 1), first, second
+
+    grad_qkv, first, second = boxed(
+        sure, backward, after(grad_attn, *columns[:-1]), out_far, out_near, queries, pairs, logs, out_blocks, positions
+    )
+    columns += [
+        lax.psum_scatter(after(piece, grad_qkv), "z", scatter_dimension=0, tiled=True) for piece in partial[1:]
     ]
 
-    qkv_blocks = joined_blocks(plane_gather(after(qkv_column, mlp_column)))
-    inputs = tokens[0].astype(f32)
-    scale_one, unit_one = unit_of(inputs)
-    qkv = apply_rows(unit_one, qkv_blocks)
-    queries = qkv[:, :wide]
-    pairs = window_blocks(qkv[:, wide:], chips)
-    out_blocks = plane_gather(after(out_column, qkv_blocks[7]), second=tuple(pairs[: chips + 1]), third=(pairs[-1],))
-    out_blocks = joined_blocks(out_blocks)
-    mixed, logs = attend(queries, pairs, positions, size, base)
-    finals = plane_gather(after(cotangent[0], pairs[0]), second=(mixed,), third=(mixed,))
-    resid = apply_rows(after(mixed, finals[1], finals[4]), out_blocks, inputs)
-
-    scale_two, unit_two = unit_of(resid)
-    units = plane_gather(unit_two)
-
-    def tiles(blocks, order):
-        return [blocks[r] if isinstance(blocks[r], tuple) else (blocks[r],) for r in order]
-
-    far, near = (5, 1, 7, 3), (4, 0, 6, 2)
-    units = [tiles(units, order) for order in (far, near)]
-    finals = [tiles(finals, order) for order in (far, near)]
-    flat_units, flat_finals = (
-        [piece for half in whole for tile in half for piece in tile] for whole in (units, finals)
-    )
-    far_sums = mlp(units[0], finals[0], mlp_full)
-
-    def of_chip(sums, which):
-        both = core_sum(sums[2 * which], sums[2 * which + 1])
-        return both[:count], both[count:]
-
-    half = count // 2
-    diag, to_x = (value.astype(low) for value in of_chip(far_sums, 1))
-    far_parts = (diag[:half], diag[half:], to_x[:half])
-    started = (swap(far_parts[0], "x"), swap(far_parts[1], "y"), swap(far_parts[2], "x"))
-    units[1][0] = (after(units[1][0][0], *far_parts),)
-    near_sums = mlp(units[1], finals[1], mlp_full)
-    to_y, own = of_chip(near_sums, 1)
-    to_y = to_y.astype(low)
-    y_bottom = to_y[half:]
-    started += (swap(y_bottom, "y"),)
-    x_bottom, y_top = scatter_turn(started, to_x, to_y)
-    hidden = [[sums[4 + k] for sums in (far_sums, near_sums)] for k in range(parts)]
-    hidden[0][0] = after(hidden[0][0], x_bottom, y_top, y_bottom)
-
-    def to_planes(k, pieces):
-        partial = mlp_grads(flat_units, flat_finals, hidden[k], pieces)
-        return partial, [lax.psum_scatter(piece, "z", scatter_dimension=0, tiled=True) for piece in partial]
-
-    partial, columns = to_planes(0, 1)
-    grad_unit_two = scatter_end(started, x_bottom, y_top, own)
-    grad_resid = cotangent[0].astype(f32) + unit_back(grad_unit_two, resid, scale_two)
-    grad_attn = grad_resid.astype(low)
-
-    diag, out_x = (value.astype(low) for value in of_chip(far_sums, 0))
-    out_y, out_own = (value.astype(low) for value in of_chip(near_sums, 0))
-    first = tuple(after(v, x_bottom, y_top) for v in (diag[:half], diag[half:], out_x[:half], out_y[half:]))
-    outputs = tuple(swap(value, axis) for value, axis in zip(first, ("x", "y", "x", "y")))
-
-    grad_mixed = apply_rows(after(grad_attn, *first, *partial), out_blocks)
-    grad_queries, own_grads, other_grads = attend_back(queries, grad_mixed, logs, pairs, positions, size, base)
-    other_grads = after(other_grads, *outputs)
-    out_keep, out_send = row_grads(after(grad_attn, other_grads, columns[0]), mixed)
-    if parts > 1:
-        hidden[1][0] = after(hidden[1][0], out_keep)
-        later, more = to_planes(1, 3)
-        columns += more
-    out_both = core_sum(out_keep, out_send).astype(low)
-    grad_pair = return_blocks(own_grads, other_grads, chips).astype(low)
-    if parts > 1:
-        grad_pair = after(grad_pair, *later)
-    out_both = after(out_both, grad_pair)
-    out_started = scatter_start(out_both[0], out_both[1], out_both[2])
-    grad_qkv = jnp.concatenate([grad_queries, grad_pair], 1)
-    qkv_keep, qkv_send = row_grads(unit_one, grad_qkv)
-    qkv_both = core_sum(qkv_keep, qkv_send).astype(low)
-    qkv_started = scatter_start(qkv_both[0], qkv_both[1], qkv_both[2])
-    grad_unit_one = apply_rows(after(grad_qkv, qkv_both), qkv_blocks, jnp.zeros_like(inputs))
-    grad_tokens = grad_resid + unit_back(grad_unit_one, inputs, scale_one)
-
-    def of_plane(started, both, later=()):
-        turned = scatter_turn(started, both[1], both[2], later)
-        return scatter_end(started, *turned, both[3]).astype(low)
-
-    out_plane = of_plane(out_started, out_both)
-    qkv_plane = after(of_plane(qkv_started, qkv_both, columns[1:2]), *columns[2:3])
-    out_sum = planes_scatter(out_plane)
-    qkv_sum = planes_scatter(qkv_plane)
+    def collect(grad_attn, grad_qkv, second, mixed, flat_ones):
+        own, *others = spread(grad_qkv)
+        found, (out_keep, out_send) = stage(
+            [(value, across(r + 1)) for r, value in enumerate(others)],
+            lambda *given: row_grads(*given),
+            [grad_attn, mixed],
+        )
+        (found, *second), qkv_column = stage(
+            [(out_send, "c"), (second[0], "x"), (second[1], "y")],
+            lambda *gathered: token_grads(flat_ones, jnp.concatenate(gathered, 0)),
+            [own, *found],
+        )
+        return qkv_column, out_keep, found, second
+
+    qkv_column, out_keep, found, second = boxed(sure, collect, grad_attn, grad_qkv, second, mixed, flat_ones)
+    qkv_low = lax.psum_scatter(qkv_column, "z", scatter_dimension=0, tiled=True)
+
+    def end(out_keep, found, first, second, grad_resid, grad_qkv, out_near, qkv_blocks, resid, scale_one, tokens):
+        both = summed(out_keep, found).astype(low)
+
+        def results(grad_qkv, *second):
+            inputs = tokens[0].astype(f32)
+            output = resid + joined(out_near[count:], first, second)
+            grad_unit_one = apply_rows(grad_qkv, qkv_blocks, jnp.zeros_like(inputs))
+            return output, grad_resid + unit_back(grad_unit_one, inputs, scale_one)
+
+        started, (output, grad_tokens) = stage(first_sends(*both[:3]), results, [grad_qkv, *second])
+        second, _ = stage(second_sends(both[1], both[2], started))
+        column = joined(both[3], started, second).astype(low)
+        return output, grad_tokens, column.reshape(-1, column.shape[-1])
+
+    output, grad_tokens, out_column = boxed(
+        sure,
+        end,
+        out_keep,
+        found,
+        first,
+        second,
+        after(grad_resid, *columns),
+        grad_qkv,
+        out_near,
+        qkv_blocks,
+        resid,
+        scale_one,
+        tokens,
+    )
+    out_sum = lax.psum_scatter(out_column, "z", scatter_dimension=0, tiled=True).astype(f32)
+    every = jnp.concatenate([*columns, qkv_low], 1)
+    every = after(every, out_column).reshape(8, -1, every.shape[1])
+    every = lax.all_to_all(every, PLANE, split_axis=0, concat_axis=0, tiled=True)
+    deep = qkv_low.shape[1]
+    qkv_sum = jnp.swapaxes(every[:, :, -deep:], 0, 1).reshape(-1, 8 * deep).astype(f32)
     query_sum = qkv_sum[:, :wide]
     key_sum = qkv_sum[:, wide : wide + size]
     value_sum = qkv_sum[:, wide + size :]
@@ -716,30 +937,7 @@
         + jnp.sum(key_weight.astype(f32) * key_sum, axis=1)
         + jnp.sum(value_weight.astype(f32) * value_sum, axis=1)
     )
-    output = resid + scatter_end(outputs, *scatter_turn(outputs, out_x, out_y, (qkv_both,)), out_own)
-
-    whole = [
-        lax.all_to_all(
-            after(column, qkv_plane).reshape(8, -1, column.shape[1]), PLANE, split_axis=0, concat_axis=0, tiled=True
-        )
-        for column in columns
-    ]
-
-    whole = [whole[0]] + ([jnp.concatenate(whole[1:], 2)] if parts > 1 else [])
-
-    def joined(which):
-        pieces = []
-        for p, (_, n) in enumerate(spans):
-            for k in range(parts):
-                width = min(part, n - k * part)
-                if width > 0:
-                    pieces.append(whole[k][p, :, which * part : which * part + width])
-        return jnp.concatenate(pieces, 1).astype(f32)
-
-    gate_sum, up_sum, down_sum = joined(0), joined(1), joined(2)
-    grad_mlp_gain = jnp.sum(
-        gate_weight.astype(f32) * gate_sum + up_weight.astype(f32) * up_sum, axis=1
-    )
+    grad_gate, grad_up, grad_down, grad_mlp_gain = finish(spans, part, per, gain_two, gate_weight, up_weight, every)
     return (
         output[None],
         grad_tokens[None],
@@ -748,10 +946,10 @@
         key_sum * gain_one,
         value_sum * gain_one,
         out_sum.T,
-        grad_mlp_gain,
-        gate_sum * gain_two,
-        up_sum * gain_two,
-        down_sum.T,
+        grad_mlp_gain[:, 0],
+        grad_gate,
+        grad_up,
+        grad_down,
     )
 
 

time: 1340 us -> 1080 us (0.81)
  waiting for transfers between devices: 492 us -> 385 us
  starting transfers between devices: 190 us -> 91.1 us
  blocking collectives: 50.7 us -> 0 us
  other arithmetic: 121 us -> 97.4 us
  Pallas kernels: 379 us -> 400 us
    ppermute x71 -> x72, waiting for transfers between devices: 362 us -> 187 us  [swap(): return lax.ppermute(value, axis, [(0, 1), (1, 0)])]
    all_to_all x4 -> x2, waiting for transfers between devices: 8.11 us -> 65.8 us  [the longest x1 44.6 us: local(): lax.all_to_all(after(mine, qkv_shard), PLANE, split_axis=0, concat_axis=0...]
    ppermute x71 -> x72, starting transfers between devices: 103 us -> 47.5 us  [swap(): return lax.ppermute(value, axis, [(0, 1), (1, 0)])]
    all_to_all x1 -> x0, blocking collectives: 50.7 us -> none  [local(): lax.all_to_all(after(mine, attn_shard), PLANE, split_axis=0, concat_axis=...]
    ppermute x18 -> x13, starting transfers between devices: 71 us -> 33.1 us  [the longest x6 17.6 us: behind(): return lambda value: lax.ppermute(value, ('z', 'y'), pairs)]
    unnamed x203 -> x70, local copies, waits for them, and re-layouts: 47.7 us -> 17.3 us
    pallas_call x2 -> x4, Pallas kernels: 129 us -> 157 us  [mlp(): pl.pallas_call(functools.partial(mlp_kernel, each // 3, per, tiles), out_...]
    pallas_call x2 -> x1, Pallas kernels: 38.8 us -> 13.2 us  [row_grads(): pl.pallas_call(row_grads_kernel, out_shape=(shape, shape), grid_spec=pltp...]
  transfers between devices with their start and end apart: 100 -> 98, of which waited for: 36 -> 40; matrix products, arithmetic and copies ran while one was open for 11% -> 14% of each run, Pallas kernels for 12% -> 37%
where the time goes in v4:
time: 1080 us; the launch traced here: 1070 us
  Pallas kernels  400 us (37%)
  waiting for transfers between devices  385 us (36%)
  other arithmetic  97.4 us (9%)
  starting transfers between devices  91.1 us (8%)
  local copies, waits for them, and re-layouts  83.2 us (8%)
  between operations  15.2 us (1%)
    ppermute x72, waiting for transfers between devices, swap(): return lax.ppermute(value, axis, [(0, 1), (1, 0)])  187 us
    pallas_call x4, Pallas kernels, mlp(): pl.pallas_call(functools.partial(mlp_kernel, each // 3, per, tiles), out_...  157 us
    pallas_call x2, Pallas kernels, mlp_grads(): pl.pallas_call(functools.partial(mlp_grads_kernel, len(units)), out_shape...  78 us
    ppermute x6, waiting for transfers between devices, behind(): return lambda value: lax.ppermute(value, ('z', 'y'), pairs)  57 us
    pallas_call x4, Pallas kernels, apply_rows(): pl.pallas_call(kernel, out_shape=shape, grid_spec=pltpu.PrefetchScalarGri...  47.5 us
    ppermute x72, starting transfers between devices, swap(): return lax.ppermute(value, axis, [(0, 1), (1, 0)])  47.5 us
    pallas_call x1, Pallas kernels, attend_back(): pl.pallas_call(functools.partial(attend_back_kernel, size, size ** (-0.5)...  46.4 us
    all_to_all x1, waiting for transfers between devices, local(): lax.all_to_all(after(mine, qkv_shard), PLANE, split_axis=0, concat_axis=0...  44.6 us
  transfers between devices with their start and end apart: 98, of which 40 were waited for; matrix products, arithmetic and copies ran while one was open for 14% of the time, Pallas kernels for 37%

profile of v4, /device:TPU:0, one launch (start us, length us, event | category | flops | bytes accessed | tf_op | source)
XLA Modules:
  0.0 1074.4 jit_solution(4495930067136391956)
XLA Ops:
  26.8 44.6 %all-to-all-done = bf16[8,80,3072]{2,1,0:T(8,128)(2,1)} async-done(((bf16[8,80,3072]{2,1,0:T(8,128)(2,1)}), bf16[8,80,3072]{2,1,0:T(8,128)(2,1)}, u32[]{:S(2)}, u32[]{:S(2)}) %all-to-all-start) | async-done | bytes 3932192 | tf_op jit(solution)/shard_map/all_to_all | solution.py:673
  77.6 150.8 %conditional.7 = (bf16[4,80,3072]{2,1,0:T(8,128)(2,1)}, bf16[4,80,3072]{2,1,0:T(8,128)(2,1)}, bf16[4,80,3072]{2,1,0:T(8,128)(2,1)}, bf16[4,80,3072]{2,1,0:T(8,12...) conditional(s32[]{:T(128)} %bitcast.28, () %tuple.125, ...), branch_computations={%region_0.1_spmd, %region_1.3_spmd} | conditional | flops 6947220 | bytes 127809664 | solution.py:60
  79.5 43.2 %collective-permute-done.18.rest_4_ = bf16[4,80,3072]{2,1,0:T(8,128)(2,1)} collective-permute-done((bf16[4,80,3072]{2,1,0:T(8,128)(2,1)}, bf16[4,80,3072]{2,1,0:T(8,128)(2,1)}, u32[]{:S(2)}, u32[]{:S(2)}) %collective-permute-start.18) | collective-permute-done | bytes 1966112 | tf_op jit(solution)/shard_map/cond/branch_1_fun/ppermute | solution.py:28
  128.9 17.9 %collective-permute-done.19 = bf16[2,80,3072]{2,1,0:T(8,128)(2,1)S(1)} collective-permute-done((bf16[2,80,3072]{2,1,0:T(8,128)(2,1)S(1)}, bf16[2,80,3072]{2,1,0:T(8,128)(2,1)S(1)}, u32[]{:S(2)}, u32[]{:S(2)}) %collective-permute-start.19) | collective-permute-done | bytes 983072 | tf_op jit(solution)/shard_map/cond/branch_1_fun/ppermute | solution.py:28
  158.6 12.0 %branch_1_fun.15 = bf16[384,3072]{1,0:T(8,128)(2,1)S(1)} custom-call(s32[8]{0:T(128)S(1)} %iota_xor_fusion.slots, bf16[384,2560]{1,0:T(8,128)(2,1)} %fusion.1.left, bf16[4,80,3072]{2,1,0:T(8,128)(2,1)S(1)} %copy-done.12, bf16[4,80,3072]{2,1,0:T(8,128)(2,1)} %collective-permute-done.15.rest_1_, bf16[4,80,3072]{2,1,0:T(8,128)(2,1)} %collective-permute-done.16.rest_2_, ...), custom_call_target="tpu_custom_call" | custom-call | flops 1048576 | bytes 4096 | tf_op jit(solution)/shard_map/cond/branch_1_fun/pallas_call | solution.py:295
  183.3 13.0 %collective-permute-done.24 = bf16[384,512]{1,0:T(8,128)(2,1)} collective-permute-done((bf16[384,512]{1,0:T(8,128)(2,1)}, bf16[384,512]{1,0:T(8,128)(2,1)}, u32[]{:S(2)}, u32[]{:S(2)}) %collective-permute-start.24) | collective-permute-done | bytes 393248 | tf_op jit(solution)/shard_map/cond/branch_1_fun/ppermute | solution.py:80
  204.6 20.5 %collective-permute-done.26 = bf16[384,512]{1,0:T(8,128)(2,1)} collective-permute-done((bf16[384,512]{1,0:T(8,128)(2,1)}, bf16[384,512]{1,0:T(8,128)(2,1)}, u32[]{:S(2)}, u32[]{:S(2)}) %collective-permute-start.26) | collective-permute-done | bytes 393248 | tf_op jit(solution)/shard_map/cond/branch_1_fun/ppermute | solution.py:80
  229.7 141.1 %conditional.8 = (bf16[4,80,2560]{2,1,0:T(8,128)(2,1)}, bf16[4,80,2560]{2,1,0:T(8,128)(2,1)}, bf16[4,80,2560]{2,1,0:T(8,128)(2,1)}, bf16[4,80,2560]{2,1,0:T(8,12...) conditional(s32[]{:T(128)} %bitcast.28, () %tuple.123, ...), branch_computations={%region_3.4_spmd, %region_4.6_spmd} | conditional | flops 7012756 | bytes 129779632 | solution.py:60
  233.6 33.5 %branch_1_fun.16 = (bf16[384,2560]{1,0:T(8,128)(2,1)}, f32[15,1,256]{2,1,0:T(1,128)S(1)}) custom-call(s32[1]{0:T(128)} %bitcast.2.core, s32[1,384]{1,0:T(1,128)S(1)} %get-tuple-element.290.places, bf16[384,2560]{1,0:T(8,128)(2,1)} %get-tuple-element.291.queries, bf16[384,512]{1,0:T(8,128)(2,1)} %get-tuple-element.292.rest_0_, ...), custom_call_target="tpu_custom_call" | custom-call | flops 1048576 | bytes 4096 | tf_op jit(solution)/shard_map/cond/branch_1_fun/pallas_call | solution.py:181
  276.2 16.8 %collective-permute-done.39 = bf16[2,80,2560]{2,1,0:T(8,128)(2,1)S(1)} collective-permute-done((bf16[2,80,2560]{2,1,0:T(8,128)(2,1)S(1)}, bf16[2,80,2560]{2,1,0:T(8,128)(2,1)S(1)}, u32[]{:S(2)}, u32[]{:S(2)}) %collective-permute-start.39) | collective-permute-done | bytes 819232 | tf_op jit(solution)/shard_map/cond/branch_1_fun/ppermute | solution.py:28
  300.2 12.2 %branch_1_fun.17 = f32[384,2560]{1,0:T(8,128)} custom-call(s32[8]{0:T(128)S(1)} %iota_xor_fusion.1.slots, bf16[384,2560]{1,0:T(8,128)(2,1)} %get-tuple-element.1076.left, f32[384,2560]{1,0:T(8,128)S(1)} %bitcast_convert_fusion.start, bf16[4,80,2560]{2,1,0:T(8,128)(2,1)S(1)} %copy-done.13, bf16[4,80,2560]{2,1,0:T(8,128)(2,1)} %collective-permute-done.34.rest_1_, ...), custom_call_target="tpu_custom_call" | custom-call | flops 1048576 | bytes 4096 | tf_op jit(solution)/shard_map/cond/branch_1_fun/pallas_call | solution.py:295
  320.5 43.1 %collective-permute-done.44 = bf16[384,2560]{1,0:T(8,128)(2,1)} collective-permute-done((bf16[384,2560]{1,0:T(8,128)(2,1)}, bf16[384,2560]{1,0:T(8,128)(2,1)}, u32[]{:S(2)}, u32[]{:S(2)}) %collective-permute-start.44) | collective-permute-done | bytes 1966112 | tf_op jit(solution)/shard_map/cond/branch_1_fun/ppermute | solution.py:28
  370.8 21.7 %all-gather.14.cloned.1.call-done = bf16[2560,768]{1,0:T(8,128)(2,1)} async-done(((bf16[640,768]{1,0:T(8,128)(2,1)}), bf16[2560,768]{1,0:T(8,128)(2,1)}) %all-gather.14.cloned.1.call-update) | async-done | bytes 3932176 | tf_op jit(solution)/shard_map/all_gather | solution.py:678
  392.5 154.5 %conditional.9 = (bf16[192,2560]{1,0:T(8,128)(2,1)}, bf16[192,2560]{1,0:T(8,128)(2,1)}, bf16[192,2560]{1,0:T(8,128)(2,1)}, bf16[192,2560]{1,0:T(8,128)(2,1)}, bf...) conditional(s32[]{:T(128)} %bitcast.28, () %tuple.122, ...), branch_computations={%region_6.7_spmd, %region_7.8_spmd} | conditional | flops 3145728 | bytes 98317096 | solution.py:60
  405.5 37.2 %branch_1_fun.18 = (bf16[768,2560]{1,0:T(8,128)(2,1)}, bf16[768,2560]{1,0:T(8,128)(2,1)}, bf16[768,2560]{1,0:T(8,128)(2,1)}, bf16[768,2560]{1,0:T(8,128)(2,1)}, bf16[1536,1536]{1,0:T(8,128)(2,1)}) custom-call(bf16[2560,768]{1,0:T(8,128)(2,1)} %get-tuple-element.370.rest_0_, bf16[2560,768]{1,0:T(8,128)(2,1)} %get-tuple-element.371.rest_1_, ...), custom_call_target="tpu_custom_call" | custom-call | flops 1048576 | bytes 4096 | tf_op jit(solution)/shard_map/cond/branch_1_fun/pallas_call | solution.py:444
  457.5 37.3 %branch_1_fun.19 = (bf16[768,2560]{1,0:T(8,128)(2,1)}, bf16[768,2560]{1,0:T(8,128)(2,1)}, bf16[768,2560]{1,0:T(8,128)(2,1)}, bf16[768,2560]{1,0:T(8,128)(2,1)}, bf16[1536,1536]{1,0:T(8,128)(2,1)}) custom-call(bf16[2560,768]{1,0:T(8,128)(2,1)} %get-tuple-element.370.rest_0_, bf16[2560,768]{1,0:T(8,128)(2,1)} %get-tuple-element.371.rest_1_, ...), custom_call_target="tpu_custom_call" | custom-call | flops 1048576 | bytes 4096 | tf_op jit(solution)/shard_map/cond/branch_1_fun/pallas_call | solution.py:444
  507.7 38.9 %branch_1_fun.20 = bf16[2560,1536]{1,0:T(8,128)(2,1)} custom-call(bf16[192,2560]{1,0:T(8,128)(2,1)} %collective-permute-done.rest_2_.rest_0_, bf16[192,2560]{1,0:T(8,128)(2,1)} %collective-permute-done.1.rest_3_.rest_1_, bf16[384,2560]{1,0:T(8,128)(2,1)} %get-tuple-element.329.rest_6_.rest_2_, bf16[192,2560]{1,0:T(8,128)(2,1)} %collective-permute-done.4.rest_8_.rest_3_, ...), custom_call_target="tpu_custom_call" | custom-call | flops 1048576 | bytes 4096 | tf_op jit(solution)/shard_map/cond/branch_1_fun/pallas_call | solution.py:506
  547.1 184.6 %conditional.10 = (bf16[2560,768]{1,0:T(8,128)(2,1)}, bf16[2560,768]{1,0:T(8,128)(2,1)}, f32[384,2560]{1,0:T(8,128)}, bf16[384,2560]{1,0:T(8,128)(2,1)}, bf16[76...) conditional(s32[]{:T(128)} %bitcast.28, () %tuple.121, ...), branch_computations={%region_8.9_spmd, %region_9.11_spmd} | conditional | flops 51806208 | bytes 258564704 | solution.py:60
  547.7 42.2 %branch_1_fun.21 = (bf16[768,2560]{1,0:T(8,128)(2,1)}, bf16[768,2560]{1,0:T(8,128)(2,1)}, bf16[768,2560]{1,0:T(8,128)(2,1)}, bf16[768,2560]{1,0:T(8,128)(2,1)}, bf16[1536,1536]{1,0:T(8,128)(2,1)}) custom-call(bf16[2560,768]{1,0:T(8,128)(2,1)} %get-tuple-element.408.rest_0_, bf16[2560,768]{1,0:T(8,128)(2,1)} %get-tuple-element.409.rest_1_, ...), custom_call_target="tpu_custom_call" | custom-call | flops 1048576 | bytes 4096 | tf_op jit(solution)/shard_map/cond/branch_1_fun/pallas_call | solution.py:444
  605.7 40.8 %branch_1_fun.22 = (bf16[768,2560]{1,0:T(8,128)(2,1)}, bf16[768,2560]{1,0:T(8,128)(2,1)}, bf16[768,2560]{1,0:T(8,128)(2,1)}, bf16[768,2560]{1,0:T(8,128)(2,1)}, bf16[1536,1536]{1,0:T(8,128)(2,1)}) custom-call(bf16[2560,768]{1,0:T(8,128)(2,1)} %get-tuple-element.408.rest_0_, bf16[2560,768]{1,0:T(8,128)(2,1)} %get-tuple-element.409.rest_1_, ...), custom_call_target="tpu_custom_call" | custom-call | flops 1048576 | bytes 4096 | tf_op jit(solution)/shard_map/cond/branch_1_fun/pallas_call | solution.py:444
  674.7 39.1 %branch_1_fun.23 = (bf16[2560,768]{1,0:T(8,128)(2,1)}, bf16[2560,768]{1,0:T(8,128)(2,1)}) custom-call(bf16[192,2560]{1,0:T(8,128)(2,1)} %get-tuple-element.410.rest_2_.rest_0_, bf16[192,2560]{1,0:T(8,128)(2,1)} %get-tuple-element.411.rest_3_.rest_1_, bf16[384,2560]{1,0:T(8,128)(2,1)} %get-tuple-element.414.rest_6_.rest_2_, ...), custom_call_target="tpu_custom_call" | custom-call | flops 1048576 | bytes 4096 | tf_op jit(solution)/shard_map/cond/branch_1_fun/pallas_call | solution.py:506
  731.8 98.4 %conditional.11 = (bf16[384,3072]{1,0:T(8,128)(2,1)S(1)}, bf16[192,2560]{1,0:T(8,128)(2,1)S(1)}, bf16[192,2560]{1,0:T(8,128)(2,1)}, bf16[192,2560]{1,0:T(8,128)(2,1)}, bf16[192,2560]{1,0:T(8,128)(2,1)}) conditional(s32[]{:T(128)} %bitcast.28, () %tuple.120, (bf16[768,2560]{1,0:T(8,128)(2,1)}, bf16[768,2560]{1,0:T(8,128)(2,1)}, ...), branch_computations={%region_12.13_spmd, %region_13.14_spmd} | conditional | flops 14483476 | bytes 102113976 | solution.py:60
  753.4 46.4 %branch_1_fun.25 = (bf16[384,2560]{1,0:T(8,128)(2,1)}, f32[4,384,512]{2,1,0:T(8,128)}, bf16[4,384,512]{2,1,0:T(8,128)(2,1)}) custom-call(s32[1]{0:T(128)} %bitcast.5.core, s32[1,384]{1,0:T(1,128)S(1)} %get-tuple-element.495.places, bf16[384,2560]{1,0:T(8,128)(2,1)} %get-tuple-element.496.queries, bf16[384,2560]{1,0:T(8,128)(2,1)} %copy-done.1, ...), custom_call_target="tpu_custom_call" | custom-call | flops 1048576 | bytes 4096 | tf_op jit(solution)/shard_map/cond/branch_1_fun/pallas_call | solution.py:213
  831.6 65.4 %conditional.12 = (bf16[2560,384]{1,0:T(8,128)(2,1)}, bf16[4,4,80,2560]{3,2,1,0:T(8,128)(2,1)}, bf16[4,4,80,2560]{3,2,1,0:T(8,128)(2,1)}, bf16[192,2560]{1,0:T(8,128)(2,1)}, bf16[192,2560]{1,0:T(8,128)(2,1)}) conditional(s32[]{:T(128)} %bitcast.28, () %tuple.119, (bf16[384,3072]{1,0:T(8,128)(2,1)S(1)}, bf16[384,2560]{1,0:T(8,128)(2,1)}, ...), branch_computations={%region_14.15_spmd, %region_15.16_spmd} | conditional | flops 3146804 | bytes 57689048 | solution.py:60
  851.0 13.2 %branch_1_fun.27 = (bf16[4,4,80,2560]{3,2,1,0:T(8,128)(2,1)}, bf16[4,4,80,2560]{3,2,1,0:T(8,128)(2,1)}) custom-call(s32[8]{0:T(128)S(1)} %gather_fusion, bf16[384,2560]{1,0:T(8,128)(2,1)} %get-tuple-element.553.left, bf16[384,2560]{1,0:T(8,128)(2,1)} %get-tuple-element.554.right), custom_call_target="tpu_custom_call" | custom-call | flops 1048576 | bytes 4096 | tf_op jit(solution)/shard_map/cond/branch_1_fun/pallas_call | solution.py:344
  876.9 14.2 %branch_1_fun.28 = bf16[2560,384]{1,0:T(8,128)(2,1)} custom-call(bf16[384,2560]{1,0:T(8,128)(2,1)} %get-tuple-element.571.rest_0_, bf16[384,2560]{1,0:T(8,128)(2,1)} %get-tuple-element.572.rest_1_, bf16[384,2560]{1,0:T(8,128)(2,1)} %get-tuple-element.573.rest_2_, bf16[384,2560]{1,0:T(8,128)(2,1)} %get-tuple-element.574.rest_3_, ...), custom_call_target="tpu_custom_call" | custom-call | flops 1048576 | bytes 4096 | tf_op jit(solution)/shard_map/cond/branch_1_fun/pallas_call | solution.py:539
  897.1 16.4 %reduce-scatter.10.cloned.1.call-done = bf16[640,768]{1,0:T(8,128)(2,1)} async-done(((bf16[2560,768]{1,0:T(8,128)(2,1)}), bf16[640,768]{1,0:T(8,128)(2,1)}) %reduce-scatter.10.cloned.1.call-update) | async-done | bytes 983056 | tf_op jit(solution)/shard_map/reduce_scatter | solution.py:877
  913.5 76.9 %conditional.13 = (bf16[320,2560]{1,0:T(8,128)(2,1)}, f32[1,384,2560]{2,1,0:T(8,128)}, f32[1,384,2560]{2,1,0:T(8,128)}) conditional(s32[]{:T(128)} %bitcast.28, () %tuple.118, (bf16[4,4,80,2560]{3,2,1,0:T(8,128)(2,1)}, bf16[4,4,80,2560]{3,2,1,0:T(8,128)(2,1)}, bf16[384,3072]{1,0:T(8,128)(2,1)}, bf16[192,2560]{1,0:T(8,128)(2,1)}, ...), branch_computations={%region_18.19_spmd, %region_19.21_spmd} | conditional | flops 39878664 | bytes 131023352 | solution.py:60
  933.3 13.1 %branch_1_fun.29 = f32[384,2560]{1,0:T(8,128)S(1)} custom-call(s32[8]{0:T(128)S(1)} %iota_xor_fusion.4.slots, bf16[384,3072]{1,0:T(8,128)(2,1)S(1)} %copy-done.10, f32[384,2560]{1,0:T(8,128)} %broadcast_67_start.0.start, bf16[4,80,3072]{2,1,0:T(8,128)(2,1)} %get-tuple-element.612.rest_0_, bf16[4,80,3072]{2,1,0:T(8,128)(2,1)} %get-tuple-element.613.rest_1_, ...), custom_call_target="tpu_custom_call" | custom-call | flops 1048576 | bytes 4096 | tf_op jit(solution)/shard_map/cond/branch_1_fun/pallas_call | solution.py:295
  969.9 16.4 %collective-permute-done.63 = bf16[2,80,2560]{2,1,0:T(8,128)(2,1)S(1)} collective-permute-done((bf16[2,80,2560]{2,1,0:T(8,128)(2,1)S(1)}, bf16[2,80,2560]{2,1,0:T(8,128)(2,1)S(1)}, u32[]{:S(2)}, u32[]{:S(2)}) %collective-permute-start.63) | collective-permute-done | bytes 819232 | tf_op jit(solution)/shard_map/cond/branch_1_fun/ppermute | solution.py:28
  1000.2 27.9 %reduce-scatter.14.cloned.1.call-done = bf16[80,2560]{1,0:T(8,128)(2,1)} async-done(((bf16[320,2560]{1,0:T(8,128)(2,1)}), bf16[80,2560]{1,0:T(8,128)(2,1)}) %reduce-scatter.14.cloned.1.call-update) | async-done | bytes 409616 | tf_op jit(solution)/shard_map/reduce_scatter | solution.py:926
  1030.0 21.2 %all-to-all-done.1.whole = bf16[8,80,3456]{2,1,0:T(8,128)(2,1)} async-done(((bf16[8,80,3456]{2,1,0:T(8,128)(2,1)}), bf16[8,80,3456]{2,1,0:T(8,128)(2,1)}, u32[]{:S(2)}, u32[]{:S(2)}) %all-to-all-start.1) | async-done | bytes 4423712 | tf_op jit(solution)/shard_map/all_to_all | solution.py:929
  (397 shorter events, 373.9 us)
Async XLA Ops:
  20.4 51.0 %all-to-all-start = ((bf16[8,80,3072]{2,1,0:T(8,128)(2,1)}), bf16[8,80,3072]{2,1,0:T(8,128)(2,1)}, u32[]{:S(2)}, u32[]{:S(2)}) async-start(bf16[8,80,3072]{2,1,0:T(8,128)(2,1)} %slice_dynamic-update-slice_fusion), calls=%async_computation | async-start | bytes 7864320 | tf_op jit(solution)/shard_map/all_to_all | solution.py:673
  25.7 51.9 %all-gather.8.cloned.1.call-start = ((), (), s32[]{:S(2)}) async-start(), calls=%async_computation.7 | async-start | bytes 2457600 | tf_op jit(solution)/shard_map/all_gather | solution.py:652
  26.7 202.9 %all-gather.10.cloned.1.call-start = ((), (), s32[]{:S(2)}) async-start(), calls=%async_computation.8 | async-start | bytes 4915200 | tf_op jit(solution)/shard_map/all_gather | solution.py:678
  75.6 154.1 %all-gather.18.cloned.1.call-start = ((), (), s32[]{:S(2)}) async-start(), calls=%async_computation.17 | async-start | bytes 2048000 | tf_op jit(solution)/shard_map/all_gather | solution.py:653
  76.4 294.5 %all-gather.12.cloned.1.call-start = ((), (), s32[]{:S(2)}) async-start(), calls=%async_computation.9 | async-start | bytes 4915200 | tf_op jit(solution)/shard_map/all_gather | solution.py:678
  78.3 46.9 %collective-permute-start.15 = (bf16[4,80,3072]{2,1,0:T(8,128)(2,1)}, bf16[4,80,3072]{2,1,0:T(8,128)(2,1)}, u32[]{:S(2)}, u32[]{:S(2)}) collective-permute-start(bf16[4,80,3072]{2,1,0:T(8,128)(2,1)} %get-tuple-element.250.rest_0_), channel_id=1, source_target_pairs={{0,1},{1,0},{2,3},{3,2},{4,5},{5,4},{6,7},{7,6},{8,9},{9,8},{10,11... | collective-permute-start | bytes 5898248 | tf_op jit(solution)/shard_map/cond/branch_1_fun/ppermute | solution.py:28
  171.3 53.8 %collective-permute-start.28 = (bf16[384,2560]{1,0:T(8,128)(2,1)S(1)}, bf16[384,2560]{1,0:T(8,128)(2,1)}, u32[]{:S(2)}, u32[]{:S(2)}) collective-permute-start(bf16[384,2560]{1,0:T(8,128)(2,1)S(1)} %get-tuple-element.259), channel_id=1, source_target_pairs={{0,1},{1,0},{2,3},{3,2},{4,5},{5,4},{6,7},{7,6},{8,9},{9,8},{10,11... | collective-permute-start | bytes 5898248 | tf_op jit(solution)/shard_map/cond/branch_1_fun/ppermute | solution.py:28
  172.7 52.5 %collective-permute-start.29 = (bf16[384,2560]{1,0:T(8,128)(2,1)S(1)}, bf16[384,2560]{1,0:T(8,128)(2,1)}, u32[]{:S(2)}, u32[]{:S(2)}) collective-permute-start(bf16[384,2560]{1,0:T(8,128)(2,1)S(1)} %get-tuple-element.259), channel_id=1, source_target_pairs={{0,4},{4,0},{1,5},{5,1},{2,6},{6,2},{3,7},{7,3},{8,12},{12,8},{9,1... | collective-permute-start | bytes 5898248 | tf_op jit(solution)/shard_map/cond/branch_1_fun/ppermute | solution.py:28
  174.1 51.0 %collective-permute-start.30 = (bf16[384,2560]{1,0:T(8,128)(2,1)S(1)}, bf16[384,2560]{1,0:T(8,128)(2,1)}, u32[]{:S(2)}, u32[]{:S(2)}) collective-permute-start(bf16[384,2560]{1,0:T(8,128)(2,1)S(1)} %get-tuple-element.259), channel_id=1, source_target_pairs={{0,2},{2,0},{1,3},{3,1},{4,6},{6,4},{5,7},{7,5},{8,10},{10,8},{9,1... | collective-permute-start | bytes 5898248 | tf_op jit(solution)/shard_map/cond/branch_1_fun/ppermute | solution.py:28
  228.4 164.1 %all-gather.14.cloned.1.call-start = ((), (), s32[]{:S(2)}) async-start(), calls=%async_computation.10 | async-start | bytes 4915200 | tf_op jit(solution)/shard_map/all_gather | solution.py:678
  229.0 318.1 %all-gather.16.cloned.1.call-start = ((), (), s32[]{:S(2)}) async-start(), calls=%async_computation.11 | async-start | bytes 4915200 | tf_op jit(solution)/shard_map/all_gather | solution.py:678
  229.6 502.2 %reduce-scatter.6.cloned.1.call-start = ((), (), s32[]{:S(2)}) async-start(), calls=%async_computation.12 | async-start | bytes 9830400 | tf_op jit(solution)/shard_map/reduce_scatter | solution.py:785
  448.1 46.7 %collective-permute-start.10 = (bf16[384,2560]{1,0:T(8,128)(2,1)}, bf16[384,2560]{1,0:T(8,128)(2,1)}, u32[]{:S(2)}, u32[]{:S(2)}) collective-permute-start(bf16[384,2560]{1,0:T(8,128)(2,1)} %get-tuple-element.369), channel_id=1, source_target_pairs={{0,2},{2,0},{1,3},{3,1},{4,6},{6,4},{5,7},{7,5},{8,10},{10,8},{9,1... | collective-permute-start | bytes 5898248 | tf_op jit(solution)/shard_map/cond/branch_1_fun/ppermute | solution.py:28
  448.1 46.7 %collective-permute-start.8 = (bf16[384,2560]{1,0:T(8,128)(2,1)}, bf16[384,2560]{1,0:T(8,128)(2,1)}, u32[]{:S(2)}, u32[]{:S(2)}) collective-permute-start(bf16[384,2560]{1,0:T(8,128)(2,1)} %get-tuple-element.369), channel_id=1, source_target_pairs={{0,1},{1,0},{2,3},{3,2},{4,5},{5,4},{6,7},{7,6},{8,9},{9,8},{10,11... | collective-permute-start | bytes 5898248 | tf_op jit(solution)/shard_map/cond/branch_1_fun/ppermute | solution.py:28
  448.6 46.2 %collective-permute-start.9 = (bf16[384,2560]{1,0:T(8,128)(2,1)}, bf16[384,2560]{1,0:T(8,128)(2,1)}, u32[]{:S(2)}, u32[]{:S(2)}) collective-permute-start(bf16[384,2560]{1,0:T(8,128)(2,1)} %get-tuple-element.369), channel_id=1, source_target_pairs={{0,4},{4,0},{1,5},{5,1},{2,6},{6,2},{3,7},{7,3},{8,12},{12,8},{9,1... | collective-permute-start | bytes 5898248 | tf_op jit(solution)/shard_map/cond/branch_1_fun/ppermute | solution.py:28
  499.2 47.4 %collective-permute-start.13 = (bf16[384,2560]{1,0:T(8,128)(2,1)}, bf16[384,2560]{1,0:T(8,128)(2,1)}, u32[]{:S(2)}, u32[]{:S(2)}) collective-permute-start(bf16[384,2560]{1,0:T(8,128)(2,1)} %collective-permute-done.8), channel_id=1, source_target_pairs={{0,2},{2,0},{1,3},{3,1},{4,6},{6,4},{5,7},{7,5},{8,10},{10,8},{9,1... | collective-permute-start | bytes 5898248 | tf_op jit(solution)/shard_map/cond/branch_1_fun/ppermute | solution.py:28
  499.3 47.3 %collective-permute-start.14 = (bf16[384,2560]{1,0:T(8,128)(2,1)}, bf16[384,2560]{1,0:T(8,128)(2,1)}, u32[]{:S(2)}, u32[]{:S(2)}) collective-permute-start(bf16[384,2560]{1,0:T(8,128)(2,1)} %collective-permute-done.9), channel_id=1, source_target_pairs={{0,2},{2,0},{1,3},{3,1},{4,6},{6,4},{5,7},{7,5},{8,10},{10,8},{9,1... | collective-permute-start | bytes 5898248 | tf_op jit(solution)/shard_map/cond/branch_1_fun/ppermute | solution.py:28
  499.7 46.9 %collective-permute-start.11 = (bf16[192,2560]{1,0:T(8,128)(2,1)}, bf16[192,2560]{1,0:T(8,128)(2,1)}, u32[]{:S(2)}, u32[]{:S(2)}) collective-permute-start(bf16[192,2560]{1,0:T(8,128)(2,1)} %slice.237), channel_id=1, source_target_pairs={{0,1},{1,0},{2,3},{3,2},{4,5},{5,4},{6,7},{7,6},{8,9},{9,8},{10,11... | collective-permute-start | bytes 2949128 | tf_op jit(solution)/shard_map/cond/branch_1_fun/ppermute | solution.py:28
  500.3 46.3 %collective-permute-start.12 = (bf16[192,2560]{1,0:T(8,128)(2,1)}, bf16[192,2560]{1,0:T(8,128)(2,1)}, u32[]{:S(2)}, u32[]{:S(2)}) collective-permute-start(bf16[192,2560]{1,0:T(8,128)(2,1)} %slice.238), channel_id=1, source_target_pairs={{0,4},{4,0},{1,5},{5,1},{2,6},{6,2},{3,7},{7,3},{8,12},{12,8},{9,1... | collective-permute-start | bytes 2949128 | tf_op jit(solution)/shard_map/cond/branch_1_fun/ppermute | solution.py:28
  547.1 350.0 %reduce-scatter.8.cloned.1.call-start = ((), (), s32[]{:S(2)}) async-start(), calls=%async_computation.13 | async-start | bytes 4915200 | tf_op jit(solution)/shard_map/reduce_scatter | solution.py:837
  664.6 49.2 %collective-permute-start.84 = (bf16[768,2560]{1,0:T(8,128)(2,1)}, bf16[768,2560]{1,0:T(8,128)(2,1)}, u32[]{:S(2)}, u32[]{:S(2)}) collective-permute-start(bf16[768,2560]{1,0:T(8,128)(2,1)} %get-tuple-element.469), channel_id=1, source_target_pairs={{0,2},{2,0},{1,3},{3,1},{4,6},{6,4},{5,7},{7,5},{8,10},{10,8},{9,1... | collective-permute-start | bytes 11796488 | tf_op jit(solution)/shard_map/cond/branch_1_fun/ppermute | solution.py:28
  664.7 49.1 %collective-permute-start.81 = (bf16[192,2560]{1,0:T(8,128)(2,1)}, bf16[192,2560]{1,0:T(8,128)(2,1)}, u32[]{:S(2)}, u32[]{:S(2)}) collective-permute-start(bf16[192,2560]{1,0:T(8,128)(2,1)} %slice.529), channel_id=1, source_target_pairs={{0,4},{4,0},{1,5},{5,1},{2,6},{6,2},{3,7},{7,3},{8,12},{12,8},{9,1... | collective-permute-start | bytes 2949128 | tf_op jit(solution)/shard_map/cond/branch_1_fun/ppermute | solution.py:28
  665.4 48.4 %collective-permute-start.82 = (bf16[192,2560]{1,0:T(8,128)(2,1)}, bf16[192,2560]{1,0:T(8,128)(2,1)}, u32[]{:S(2)}, u32[]{:S(2)}) collective-permute-start(bf16[192,2560]{1,0:T(8,128)(2,1)} %add_convert_fusion.5), channel_id=1, source_target_pairs={{0,1},{1,0},{2,3},{3,2},{4,5},{5,4},{6,7},{7,6},{8,9},{9,8},{10,11... | collective-permute-start | bytes 2949128 | tf_op jit(solution)/shard_map/cond/branch_1_fun/ppermute | solution.py:28
  666.9 47.0 %collective-permute-start.83 = (bf16[192,2560]{1,0:T(8,128)(2,1)}, bf16[192,2560]{1,0:T(8,128)(2,1)}, u32[]{:S(2)}, u32[]{:S(2)}) collective-permute-start(bf16[192,2560]{1,0:T(8,128)(2,1)} %fusion.9), channel_id=1, source_target_pairs={{0,4},{4,0},{1,5},{5,1},{2,6},{6,2},{3,7},{7,3},{8,12},{12,8},{9,1... | collective-permute-start | bytes 2949128 | tf_op jit(solution)/shard_map/cond/branch_1_fun/ppermute | solution.py:28
  731.7 181.8 %reduce-scatter.10.cloned.1.call-start = ((), (), s32[]{:S(2)}) async-start(), calls=%async_computation.14 | async-start | bytes 4915200 | tf_op jit(solution)/shard_map/reduce_scatter | solution.py:877
  737.7 62.1 %collective-permute-start.65 = (bf16[192,2560]{1,0:T(8,128)(2,1)}, bf16[192,2560]{1,0:T(8,128)(2,1)}, u32[]{:S(2)}, u32[]{:S(2)}) collective-permute-start(bf16[192,2560]{1,0:T(8,128)(2,1)} %get-tuple-element.491), channel_id=1, source_target_pairs={{0,1},{1,0},{2,3},{3,2},{4,5},{5,4},{6,7},{7,6},{8,9},{9,8},{10,11... | collective-permute-start | bytes 2949128 | tf_op jit(solution)/shard_map/cond/branch_1_fun/ppermute | solution.py:28
  738.4 61.4 %collective-permute-start.66 = (bf16[192,2560]{1,0:T(8,128)(2,1)}, bf16[192,2560]{1,0:T(8,128)(2,1)}, u32[]{:S(2)}, u32[]{:S(2)}) collective-permute-start(bf16[192,2560]{1,0:T(8,128)(2,1)} %get-tuple-element.492), channel_id=1, source_target_pairs={{0,4},{4,0},{1,5},{5,1},{2,6},{6,2},{3,7},{7,3},{8,12},{12,8},{9,1... | collective-permute-start | bytes 2949128 | tf_op jit(solution)/shard_map/cond/branch_1_fun/ppermute | solution.py:28
  738.7 61.2 %collective-permute-start.67 = (bf16[192,2560]{1,0:T(8,128)(2,1)}, bf16[192,2560]{1,0:T(8,128)(2,1)S(1)}, u32[]{:S(2)}, u32[]{:S(2)}) collective-permute-start(bf16[192,2560]{1,0:T(8,128)(2,1)} %get-tuple-element.493), channel_id=1, source_target_pairs={{0,1},{1,0},{2,3},{3,2},{4,5},{5,4},{6,7},{7,6},{8,9},{9,8},{10,11... | collective-permute-start | bytes 2949128 | tf_op jit(solution)/shard_map/cond/branch_1_fun/ppermute | solution.py:28
  740.4 59.5 %collective-permute-start.68 = (bf16[192,2560]{1,0:T(8,128)(2,1)}, bf16[192,2560]{1,0:T(8,128)(2,1)}, u32[]{:S(2)}, u32[]{:S(2)}) collective-permute-start(bf16[192,2560]{1,0:T(8,128)(2,1)} %slice.250), channel_id=1, source_target_pairs={{0,4},{4,0},{1,5},{5,1},{2,6},{6,2},{3,7},{7,3},{8,12},{12,8},{9,1... | collective-permute-start | bytes 2949128 | tf_op jit(solution)/shard_map/cond/branch_1_fun/ppermute | solution.py:28
  830.2 160.3 %reduce-scatter.12.cloned.1.call-start = ((), (), s32[]{:S(2)}) async-start(), calls=%async_computation.15 | async-start | bytes 2457600 | tf_op jit(solution)/shard_map/reduce_scatter | solution.py:895
  897.0 131.1 %reduce-scatter.14.cloned.1.call-start = ((), (), s32[]{:S(2)}) async-start(), calls=%async_computation.16 | async-start | bytes 2048000 | tf_op jit(solution)/shard_map/reduce_scatter | solution.py:926
  995.4 55.8 %all-to-all-start.1 = ((bf16[8,80,3456]{2,1,0:T(8,128)(2,1)}), bf16[8,80,3456]{2,1,0:T(8,128)(2,1)}, u32[]{:S(2)}, u32[]{:S(2)}) async-start(bf16[8,80,3456]{2,1,0:T(8,128)(2,1)} %bitcast.154), calls=%async_computation.5 | async-start | bytes 8847360 | tf_op jit(solution)/shard_map/all_to_all | solution.py:929
  (102 other events, 1938.8 us)
Sparse Core Ops, SparseCore 0:
  28.7 45.9 all-gather.7
  76.8 76.1 all-gather.9
  154.6 41.6 all-gather.17
  228.6 86.9 all-gather.11
  317.5 74.9 all-gather.13
  393.9 74.9 all-gather.15
  547.2 133.8 reduce-scatter.5
  731.9 69.2 reduce-scatter.7
  830.3 83.1 reduce-scatter.9
  915.7 41.7 reduce-scatter.11
  990.6 37.4 reduce-scatter.13

commit v5 on v4

--- a/solution.py
+++ b/solution.py
@@ -109,8 +109,13 @@
             turned[:, pl.ds(at, count)] = block[:, columns].T
 
 
+def chunks(span, number):
+    tiles = span // 128
+    return [(128 * (tiles * i // number), 128 * (tiles * (i + 1) // number)) for i in range(number)]
+
+
 def attend_kernel(size, scale, span, base, core, places, queries, *rest):
-    blocks, (mixed, logs, bias, window, turned) = rest[:-5], rest[-5:]
+    blocks, (mixed, wide, logs, bias, window, turned) = rest[:-6], rest[-6:]
     block = pl.program_id(0)
     count = blocks[0].shape[0]
     start = pl.multiple_of(core[0] * count + base + block * SUB, SUB)
@@ -123,18 +128,28 @@
     def _():
         write_bias(bias, places[...], span, block)
 
-    query = two_heads(queries[...], size)
-    keys = window[pl.ds(start, span), :size]
-    scores = dot(keys, query, (1, 1)) * scale + bias[...]
-    highest = jnp.max(scores, axis=0, keepdims=True)
-    expo = jnp.exp(scores - highest)
-    total = jnp.sum(expo, axis=0, keepdims=True)
-    flat = dot(turned[:, pl.ds(start, span)], expo.astype(low), (1, 0)) / total
-    mixed[...] = side_by_side(flat.T, size).astype(low)
+    query = two_heads(queries[...], size) * jnp.asarray(scale, low)
+    highest = total = flat = None
+    for at, end in chunks(span, 8):
+        place = pl.ds(start + at, end - at)
+        scores = dot(window[place, :size], query, (1, 1)) + bias[at:end]
+        top = jnp.max(scores, axis=0, keepdims=True)
+        if highest is not None:
+            top = jnp.maximum(highest, top)
+            fade = jnp.exp(highest - top)
+        highest = top
+        expo = jnp.exp(scores - highest)
+        part = jnp.sum(expo, axis=0, keepdims=True)
+        mix = dot(turned[:, place], expo.astype(low), (1, 0))
+        total = part if total is None else total * fade + part
+        flat = mix if flat is None else flat * fade + mix
+    result = side_by_side((flat / total).T, size)
+    wide[...] = result
+    mixed[...] = result.astype(low)
     logs[0] = highest + jnp.log(total)
 
 
-def attend_back_kernel(size, scale, span, base, core, places, queries, grads, logs, *rest):
+def attend_back_kernel(size, scale, span, base, core, places, queries, grads, wide, logs, *rest):
     blocks, (grad_queries, mine, theirs, bias, window, turned, total) = rest[:-7], rest[-7:]
     block = pl.program_id(0)
     count = blocks[0].shape[0]
@@ -149,17 +164,16 @@
     def _():
         write_bias(bias, places[...], span, block)
 
-    query = two_heads(queries[...], size)
+    query = two_heads(queries[...], size) * jnp.asarray(scale, low)
     grad = two_heads(grads[...], size)
-    keys = window[pl.ds(start, span), :size]
-    values = window[pl.ds(start, span), size:]
-    probs = jnp.exp(dot(keys, query, (1, 1)) * scale + bias[...] - logs[0])
-    total[pl.ds(start, span), size:] += dot(probs.astype(low), grad, (1, 0))
-    grad_probs = dot(values, grad, (1, 1))
-    inner = jnp.sum(probs * grad_probs, axis=0, keepdims=True)
-    grad_scores = (probs * (grad_probs - inner)).astype(low)
-    total[pl.ds(start, span), :size] += dot(grad_scores, query, (1, 0)) * scale
-    flat = dot(turned[:, pl.ds(start, span)], grad_scores, (1, 0)) * scale
+    inner = jnp.sum((grad.astype(f32) * two_heads(wide[...], size)).T, axis=0, keepdims=True)
+    place = pl.ds(start, span)
+    keys, values = window[place, :size], window[place, size:]
+    probs = jnp.exp(dot(keys, query, (1, 1)) + (bias[...] - logs[0]))
+    grad_scores = (probs * (dot(values, grad, (1, 1)) - inner)).astype(low)
+    total[place, size:] += dot(probs.astype(low), grad, (1, 0))
+    total[place, :size] += dot(grad_scores, query, (1, 0))
+    flat = dot(turned[:, place], grad_scores, (1, 0)) * scale
     grad_queries[...] = side_by_side(flat.T, size).astype(low)
 
     @pl.when((block == pl.num_programs(0) - 1) & (pl.program_id(1) == pl.num_programs(1) - 1))
@@ -182,6 +196,7 @@
         functools.partial(attend_kernel, size, size**-0.5, span, base),
         out_shape=(
             jax.ShapeDtypeStruct((count, wide), low),
+            jax.ShapeDtypeStruct((count, wide), f32),
             jax.ShapeDtypeStruct((grid[0] * grid[1], 1, 2 * SUB), f32),
         ),
         grid_spec=pltpu.PrefetchScalarGridSpec(
@@ -189,7 +204,7 @@
             grid=grid,
             in_specs=[pl.BlockSpec((1, SUB), lambda s, h, o: (0, s)), tile]
             + [pl.BlockSpec(block.shape, lambda s, h, o: (0, 0)) for block in blocks],
-            out_specs=[tile, pl.BlockSpec((1, 1, 2 * SUB), lambda s, h, o: (s * grid[1] + h, 0, 0))],
+            out_specs=[tile, tile, pl.BlockSpec((1, 1, 2 * SUB), lambda s, h, o: (s * grid[1] + h, 0, 0))],
             scratch_shapes=[
                 pltpu.VMEM((span, 2 * SUB), f32),
                 pltpu.VMEM((rows, 2 * size), low),
@@ -201,7 +216,7 @@
     )(core, places, queries, *blocks)
 
 
-def attend_back(queries, grads, logs, blocks, places, size, base):
+def attend_back(queries, grads, mixed, logs, blocks, places, size, base):
     count, wide = queries.shape
     grid = (count // SUB, wide // (2 * size))
     span = WINDOW + SUB
@@ -222,6 +237,7 @@
             grid=grid,
             in_specs=[
                 pl.BlockSpec((1, SUB), lambda s, h, o: (0, s)),
+                tile,
                 tile,
                 tile,
                 pl.BlockSpec((1, 1, 2 * SUB), lambda s, h, o: (s * grid[1] + h, 0, 0)),
@@ -237,7 +253,7 @@
         ),
         compiler_params=pltpu.CompilerParams(vmem_limit_bytes=60 << 20),
         cost_estimate=NOMINAL,
-    )(core, places, queries, grads, logs, *blocks)
+    )(core, places, queries, grads, mixed, logs, *blocks)
 
 
 def lay_rows(slots, blocks, full):
@@ -462,10 +478,10 @@
 def mlp_grads_kernel(number, *rest):
     units, grads, hidden, rest = rest[:number], rest[number : 2 * number], rest[2 * number : 2 * number + 2], rest[2 * number + 2 :]
     *outs, turned = rest
-    out_wide = outs[0].shape[1]
     step = pl.program_id(0)
     part = hidden[0].shape[1] // 3
     piece = min(part, 256)
+    places = [(out, at) for out in outs for at in range(0, out.shape[1], piece)]
 
     def turn(slot, which, sources, share, shares):
         at = 0
@@ -474,13 +490,14 @@
                 turned[slot, which, :, at : at + source.shape[0]] = source[...].T
             at += source.shape[0]
 
-    def multiply(slot, which, at):
+    def multiply(slot, which, i, at):
         value, start = 0.0, 0
         for block in hidden:
             left = turned[slot, which, :, start : start + block.shape[0]]
             value = value + dot(left, block[:, at : at + piece], (1, 0))
             start += block.shape[0]
-        outs[at // out_wide][:, at % out_wide : at % out_wide + piece] = value.astype(low)
+        out, place = places[i]
+        out[:, place : place + piece] = value.astype(low)
 
     work = [(at // (2 * part), at) for at in range(0, 3 * part, piece)]
 
@@ -492,12 +509,12 @@
     @pl.when(step > 0)
     def _():
         for i, (which, at) in enumerate(work):
-            multiply((step - 1) % 2, which, at)
+            multiply((step - 1) % 2, which, i, at)
             turn(step % 2, 0, units, i, len(work))
             turn(step % 2, 1, grads, i, len(work))
 
 
-def mlp_grads(units, grads, hidden, pieces=1):
+def mlp_grads(units, grads, hidden, pieces=(3,)):
     wide = units[0].shape[1]
     deep = hidden[0].shape[1]
     count = sum(piece.shape[0] for piece in units)
@@ -505,13 +522,15 @@
     last = wide // rows - 1
     return pl.pallas_call(
         functools.partial(mlp_grads_kernel, len(units)),
-        out_shape=[jax.ShapeDtypeStruct((wide, deep // pieces), low)] * pieces,
+        out_shape=[jax.ShapeDtypeStruct((wide, deep // 3 * piece), low) for piece in pieces],
         grid=(last + 2,),
         in_specs=[
             pl.BlockSpec((piece.shape[0], rows), lambda s: (0, jnp.minimum(s, last))) for piece in units + grads
         ]
         + [pl.BlockSpec(piece.shape, lambda s: (0, 0), pipeline_mode=pl.Buffered(1)) for piece in hidden],
-        out_specs=[pl.BlockSpec((rows, deep // pieces), lambda s: (jnp.maximum(s - 1, 0), 0))] * pieces,
+        out_specs=[
+            pl.BlockSpec((rows, deep // 3 * piece), lambda s: (jnp.maximum(s - 1, 0), 0)) for piece in pieces
+        ],
         scratch_shapes=[pltpu.VMEM((2, 2, rows, count), low)],
         compiler_params=pltpu.CompilerParams(vmem_limit_bytes=62 << 20),
         cost_estimate=NOMINAL,
@@ -572,6 +591,117 @@
         ),
         cost_estimate=NOMINAL,
     )(slots, value)
+
+
+def turn_kernel(keep, found, far, diag_x, diag_y, y_bottom, x_bottom, y_top, own):
+    half = far.shape[0]
+
+    def both(start, rows):
+        return keep[start : start + rows].astype(f32) + found[start : start + rows].astype(f32)
+
+    y_top[...] = (both(0, half) + diag_x[...].astype(f32)).astype(low)
+    y_bottom[...] = both(half, half).astype(low)
+    x_bottom[...] = (far[...].astype(f32) + diag_y[...].astype(f32)).astype(low)
+    own[...] = both(2 * half, 2 * half)
+
+
+def turn(keep, found, far, diag_x, diag_y):
+    half, wide = far.shape
+    part = lambda rows: pl.BlockSpec((rows, TILE), lambda n: (0, n))
+    return pl.pallas_call(
+        turn_kernel,
+        out_shape=[jax.ShapeDtypeStruct((half, wide), low)] * 3 + [jax.ShapeDtypeStruct((2 * half, wide), f32)],
+        grid=(wide // TILE,),
+        in_specs=[part(4 * half)] * 2 + [part(half)] * 3,
+        out_specs=[part(half)] * 3 + [part(2 * half)],
+        cost_estimate=NOMINAL,
+    )(keep, found, far, diag_x, diag_y)
+
+
+def resid_kernel(steps, own, x_top, x_bottom, y_top, y_bottom, resid, gift, scale, grad_out, grad_low):
+    upper = pl.program_id(0) < steps
+    x_part = jnp.where(upper, x_top[...].astype(f32), x_bottom[...].astype(f32))
+    y_part = jnp.where(upper, y_top[...].astype(f32), y_bottom[...].astype(f32))
+    grad = unit_back(own[...] + x_part + y_part, resid[...], scale[...])
+    grad = gift[...].astype(f32) + grad
+    grad_out[...] = grad
+    grad_low[...] = grad.astype(low)
+
+
+def resid_grads(own, x_top, x_bottom, y_top, y_bottom, resid, gift, scale):
+    count, wide = own.shape
+    rows = 96
+    steps = count // (2 * rows)
+    row = pl.BlockSpec((rows, wide), lambda i: (i, 0))
+    first = pl.BlockSpec((rows, wide), lambda i: (jnp.minimum(i, steps - 1), 0))
+    last = pl.BlockSpec((rows, wide), lambda i: (jnp.maximum(i - steps, 0), 0))
+    return pl.pallas_call(
+        functools.partial(resid_kernel, steps),
+        out_shape=(jax.ShapeDtypeStruct((count, wide), f32), jax.ShapeDtypeStruct((count, wide), low)),
+        grid=(2 * steps,),
+        in_specs=[row, first, last, first, last, row, row, pl.BlockSpec((rows, 1), lambda i: (i, 0))],
+        out_specs=(row, row),
+        cost_estimate=NOMINAL,
+    )(own, x_top, x_bottom, y_top, y_bottom, resid, gift, scale)
+
+
+def part_sums_kernel(keep, found, diag_top, diag_bottom, x_top, x_bottom, y_top, y_bottom, own):
+    half = diag_top.shape[0]
+
+    def both(place, first, rows):
+        part = slice(first, first + rows)
+        return (keep[place, part].astype(f32) + found[place, part].astype(f32)).astype(low)
+
+    for place, (top, bottom) in enumerate(((diag_top, diag_bottom), (x_top, x_bottom), (y_top, y_bottom))):
+        top[...] = both(place, 0, half)
+        bottom[...] = both(place, half, half)
+    own[...] = both(3, 0, 2 * half)
+
+
+def part_sums(keep, found):
+    _, planes, rows, wide = keep.shape
+    four = pl.BlockSpec((4, planes, rows, TILE), lambda n: (0, 0, 0, n))
+    some = lambda planes: pl.BlockSpec((planes, rows, TILE), lambda n: (0, 0, n))
+    half = planes // 2
+    shape = lambda planes: jax.ShapeDtypeStruct((planes, rows, wide), low)
+    return pl.pallas_call(
+        part_sums_kernel,
+        out_shape=[shape(half)] * 6 + [shape(planes)],
+        grid=(wide // TILE,),
+        in_specs=[four] * 2,
+        out_specs=[some(half)] * 6 + [some(planes)],
+        compiler_params=pltpu.CompilerParams(vmem_limit_bytes=48 << 20),
+        cost_estimate=NOMINAL,
+    )(keep, found)
+
+
+def pack_kernel(spans, part, gain, gate, up, down, out):
+    scale = gain[...]
+    share = out.shape[2] // 3
+    for p, (at, n) in enumerate(spans):
+        for q in range(share // part):
+            width = min(part, n - q * part)
+            place = slice(at + q * part, at + q * part + width)
+            for which, source in enumerate((gate, up, down)):
+                first = part * (3 * q + which)
+                if width > 0:
+                    value = source[:, place]
+                    if which < 2:
+                        value = (value.astype(f32) * scale).astype(low)
+                    out[p, :, first : first + width] = value
+                if width < part:
+                    empty = max(width, 0)
+                    out[p, :, first + empty : first + part] = jnp.zeros((out.shape[1], part - empty), low)
+
+
+def pack(spans, part, share, gain, gate, up, down):
+    rows, _ = gate.shape
+    return pl.pallas_call(
+        functools.partial(pack_kernel, spans, part),
+        out_shape=jax.ShapeDtypeStruct((8, rows, 3 * share), low),
+        compiler_params=pltpu.CompilerParams(vmem_limit_bytes=48 << 20),
+        cost_estimate=NOMINAL,
+    )(gain, gate, up, down)
 
 
 def shares(columns):
@@ -595,7 +725,7 @@
                 total = total + jnp.sum(value * weight[:, place].astype(f32), axis=1, keepdims=True)
                 out[:, place] = value * scale
             first = start + part * (2 * per + j)
-            down_out[place, :] = whole[p, :, first : first + width].astype(f32).T
+            down_out[:, place] = whole[p, :, first : first + width].astype(f32)
     gain_out[...] = total
 
 
@@ -606,7 +736,7 @@
         out_shape=(
             jax.ShapeDtypeStruct((rows, columns), f32),
             jax.ShapeDtypeStruct((rows, columns), f32),
-            jax.ShapeDtypeStruct((columns, rows), f32),
+            jax.ShapeDtypeStruct((rows, columns), f32),
             jax.ShapeDtypeStruct((rows, 1), f32),
         ),
         compiler_params=pltpu.CompilerParams(vmem_limit_bytes=48 << 20),
@@ -657,18 +787,7 @@
     calls = 2 if parts % 2 == 0 else 1
     per = parts // calls
     part = share // parts
-    mlp_shards = (
-        (gate_weight.astype(f32) * gain_two).astype(low),
-        (up_weight.astype(f32) * gain_two).astype(low),
-        down_weight.T,
-    )
-    split = [
-        jnp.stack([jnp.pad(shard[:, at : at + n], ((0, 0), (0, share - n))) for at, n in spans])
-        for shard in mlp_shards
-    ]
-    mine = jnp.concatenate(
-        [whole[:, :, k * part : (k + 1) * part] for k in range(parts) for whole in split], 2
-    )
+    mine = pack(spans, part, share, gain_two, gate_weight, up_weight, down_weight.T)
     gift = cotangent[0]
     mlp_column = lax.all_to_all(after(mine, qkv_shard), PLANE, split_axis=0, concat_axis=0, tiled=True)
     mlp_column = mlp_column.reshape(-1, 3 * share)
@@ -696,7 +815,7 @@
     def forward(queries, pairs, out_column, tokens, positions, gift_x, gift_y):
         inputs = tokens[0].astype(f32)
         mid = out_column.shape[0] // 2
-        (out_x, out_y, out_c, gift_x_c, gift_y_c), (mixed, logs) = stage(
+        (out_x, out_y, out_c, gift_x_c, gift_y_c), (mixed, mixed_wide, logs) = stage(
             [(out_column, "x"), (out_column, "y"), (out_column, "c"), (gift_x, "c"), (gift_y, "c")],
             lambda *given: attend(given[0], given[1:], positions, size, base),
             [queries, *pairs],
@@ -712,13 +831,13 @@
         (unit_x, unit_y, unit_c), _ = stage([(unit_two, "x"), (unit_two, "y"), (unit_two, "c")])
         (unit_x_c, unit_y_c), _ = stage([(unit_x, "c"), (unit_y, "c")])
         unit_blocks = unit_two, unit_x, unit_c, unit_x_c, unit_y, unit_y_c
-        return out_blocks[1:], mixed, logs, resid, scale_two, unit_blocks, gift_x_c, gift_y_c
+        return out_blocks[1:], mixed, mixed_wide, logs, resid, scale_two, unit_blocks, gift_x_c, gift_y_c
 
     qkv_column = after(qkv_column, mlp_column)
     qkv_blocks, queries, pairs, gifts, unit_one, scale_one = boxed(sure, project, qkv_column, tokens, gift)
     gift_x, gift_y, gift_c = gifts
     mlp_full += [gathered(k, pairs[0]) for k in range(1, parts)]
-    out_blocks, mixed, logs, resid, scale_two, unit_blocks, gift_x_c, gift_y_c = boxed(
+    out_blocks, mixed, mixed_wide, logs, resid, scale_two, unit_blocks, gift_x_c, gift_y_c = boxed(
         sure, forward, after(queries, mlp_full[0]), pairs, out_column, tokens, positions, gift_x, gift_y
     )
     qkv_blocks, out_blocks = [qkv_column, *qkv_blocks], [out_column, *out_blocks]
@@ -741,55 +860,50 @@
         unit_two, unit_x, unit_c, unit_x_c, unit_y, unit_y_c = blocks
         units_near = [(unit_y,), (unit_two,), (unit_y_c,), (unit_c,)]
         gift_y = grads_near[0][0]
-        sends = [(unit_y[:half], "x"), (unit_x[half:], "y"), (gift_y[:half], "x"), (gift_x[half:], "y")]
+        sends = [(unit_y, "x"), (gift_x, "y")]
         one_sends = [(unit_one, "x"), (unit_one, "y"), (unit_one, "c")]
         far_sums = near_sums = partial = ()
         if calls > 1:
-            (unit_top, unit_bottom, gift_top, gift_bottom), near_sums = stage(
+            (unit_d, gift_d), near_sums = stage(
                 sends, lambda *given: mlp([(v,) for v in given], grads_near, weights, ()), flat(units_near)
             )
         else:
-            (unit_top, unit_bottom, gift_top, gift_bottom), _ = stage(sends)
-        (unit_top_c, unit_bottom_c, gift_top_c, gift_bottom_c), _ = stage(
-            [(unit_top, "c"), (unit_bottom, "c"), (gift_top, "c"), (gift_bottom, "c")]
-        )
-        grads_far = [(gift_top, gift_bottom), (gift_x,), (gift_top_c, gift_bottom_c), (gift_x_c,)]
-        units_far = [(unit_top, unit_bottom), (unit_x,), (unit_top_c, unit_bottom_c), (unit_x_c,)]
+            (unit_d, gift_d), _ = stage(sends)
+        (unit_d_c, gift_d_c), _ = stage([(unit_d, "c"), (gift_d, "c")])
+        units_far = [(unit_d,), (unit_x,), (unit_d_c,), (unit_x_c,)]
+        grads_far = [(gift_d,), (gift_x,), (gift_d_c,), (gift_x_c,)]
         if calls > 1:
             (one_x, one_y, one_c), far_sums = stage(
                 one_sends, lambda weights: mlp(units_far, grads_far, weights, ()), [weights]
             )
         else:
             (one_x, one_y, one_c), _ = stage(one_sends)
-        one_sends = [(one_y[:half], "x"), (one_x[half:], "y"), (one_x, "c"), (one_y, "c")]
+        one_sends = [(one_y, "x"), (one_x, "c"), (one_y, "c")]
         if calls > 1:
-            (one_top, one_bottom, one_x_c, one_y_c), partial = stage(
+            (one_d, one_x_c, one_y_c), partial = stage(
                 one_sends,
                 lambda *given: mlp_grads(flat(units_far, units_near), flat(grads_far, grads_near), given)[0],
                 [far_sums[4], near_sums[4]],
             )
         else:
-            (one_top, one_bottom, one_x_c, one_y_c), _ = stage(one_sends)
-        ones = one_x, one_c, one_x_c, one_y, one_top, one_bottom, one_y_c
-        halves_far = unit_top, unit_bottom, unit_top_c, unit_bottom_c
-        return halves_far, grads_far, far_sums[:4], near_sums[:4], partial, ones
+            (one_d, one_x_c, one_y_c), _ = stage(one_sends)
+        ones = one_x, one_c, one_x_c, one_y, one_d, one_y_c
+        return (unit_d, unit_d_c), grads_far, far_sums[:4], near_sums[:4], partial, ones
 
     columns = []
     unit_two, unit_x, unit_c, unit_x_c, unit_y, unit_y_c = unit_blocks
-    if calls > 1:
-        unit_blocks = after(unit_blocks, *mlp_full[per : per + 1])
     halves_far, grads_far, far_before, near_before, partial, ones = boxed(
         sure, opening, mlp_full[:per] if calls > 1 else (), unit_blocks, gift_x, gift_x_c, grads_near, unit_one
     )
     if calls > 1:
         columns.append(lax.psum_scatter(partial, "z", scatter_dimension=0, tiled=True))
-    unit_top, unit_bottom, unit_top_c, unit_bottom_c = halves_far
-    units_far = [(unit_top, unit_bottom), (unit_x,), (unit_top_c, unit_bottom_c), (unit_x_c,)]
+    unit_d, unit_d_c = halves_far
+    units_far = [(unit_d,), (unit_x,), (unit_d_c,), (unit_x_c,)]
     units_near = [(unit_y,), (unit_two,), (unit_y_c,), (unit_c,)]
 
     def middle(weights, units_far, units_near, grads_far, grads_near, far_before, near_before, resid, scale_two, gift, ones):
-        (one_top_c, one_bottom_c), far_sums = stage(
-            [(ones[4], "c"), (ones[5], "c")],
+        (one_d_c,), far_sums = stage(
+            [(ones[4], "c")],
             lambda *weights: mlp(units_far, grads_far, weights, far_before),
             weights,
         )
@@ -802,24 +916,19 @@
             [tile[0] for tile in units_near],
         )
         (found,), _ = stage([(near_sums[3], "c")])
-        both = summed(near_sums[2], found)
-        (y_top, y_bottom), (own_top, own_bottom) = halves(both[:count]), halves(both[count:])
-        x_bottom, y_top = total(x_bottom, diag_y).astype(low), total(y_top, diag_x).astype(low)
+        y_bottom, x_bottom, y_top, own = turn(near_sums[2], found, x_bottom, diag_x, diag_y)
         (y_bottom, x_bottom, y_top, near_out), partial = stage(
-            [(y_bottom.astype(low), "y"), (x_bottom, "x"), (y_top, "y"), (near_sums[1], "c")],
+            [(y_bottom, "y"), (x_bottom, "x"), (y_top, "y"), (near_sums[1], "c")],
             lambda *given: mlp_grads(flat(units_far, units_near), flat(grads_far, grads_near), given, cuts),
             [far_sums[4], near_sums[4]],
         )
-        grad_unit_two = jnp.concatenate(
-            [total(own_top, x_top, y_top), total(own_bottom, x_bottom, y_bottom)], 0
-        )
-        grad_resid = gift.astype(f32) + unit_back(grad_unit_two, resid, scale_two)
+        grad_resid, grad_attn = resid_grads(own, x_top, x_bottom, y_top, y_bottom, resid, gift, scale_two)
         out_far = summed(far_sums[0], far_out).astype(low)
         out_near = summed(near_sums[0], near_out).astype(low)
-        return partial, grad_resid, grad_resid.astype(low), out_far, out_near, one_top_c, one_bottom_c
-
-    cuts = 2 if part % 256 == 0 and per % 2 == 0 else 1
-    partial, grad_resid, grad_attn, out_far, out_near, one_top_c, one_bottom_c = boxed(
+        return partial, grad_resid, grad_attn, out_far, out_near, one_d_c
+
+    cuts = (2, 1)
+    partial, grad_resid, grad_attn, out_far, out_near, one_d_c = boxed(
         sure,
         middle,
         mlp_full[-per:],
@@ -835,8 +944,8 @@
         ones,
     )
     columns.append(lax.psum_scatter(partial[0], "z", scatter_dimension=0, tiled=True))
-    one_x, one_c, one_x_c, one_y, one_top, one_bottom, one_y_c = ones
-    flat_ones = [unit_one, one_x, one_c, one_x_c, one_y, one_top, one_bottom, one_y_c, one_top_c, one_bottom_c]
+    one_x, one_c, one_x_c, one_y, one_d, one_y_c = ones
+    flat_ones = [unit_one, one_x, one_c, one_x_c, one_y, one_d, one_y_c, one_d_c]
 
     def first_sends(diag, to_x, to_y):
         diag_top, diag_bottom = halves(diag)
@@ -851,10 +960,10 @@
         top, bottom = halves(own)
         return jnp.concatenate([total(top, first[2], second[1]), total(bottom, second[0], first[3])], 0)
 
-    def backward(grad_attn, out_far, out_near, queries, pairs, logs, out_blocks, positions):
+    def backward(grad_attn, out_far, out_near, queries, pairs, mixed_wide, logs, out_blocks, positions):
         def attention(grad_attn):
             grad_mixed = apply_rows(grad_attn, out_blocks)
-            return attend_back(queries, grad_mixed, logs, pairs, positions, size, base)
+            return attend_back(queries, grad_mixed, mixed_wide, logs, pairs, positions, size, base)
 
         first, (grad_queries, mine, theirs) = stage(
             first_sends(out_far[:count], out_far[count:], out_near[:count]), attention, [grad_attn]
@@ -871,7 +980,7 @@
         return jnp.concatenate([grad_queries, grad_pair], 1), first, second
 
     grad_qkv, first, second = boxed(
-        sure, backward, after(grad_attn, *columns[:-1]), out_far, out_near, queries, pairs, logs, out_blocks, positions
+        sure, backward, after(grad_attn, *columns[:-1]), out_far, out_near, queries, pairs, mixed_wide, logs, out_blocks, positions
     )
     columns += [
         lax.psum_scatter(after(piece, grad_qkv), "z", scatter_dimension=0, tiled=True) for piece in partial[1:]
@@ -891,11 +1000,13 @@
         )
         return qkv_column, out_keep, found, second
 
-    qkv_column, out_keep, found, second = boxed(sure, collect, grad_attn, grad_qkv, second, mixed, flat_ones)
+    qkv_column, out_keep, found, second = boxed(
+        sure, collect, after(grad_attn, columns[-2]), grad_qkv, second, mixed, flat_ones
+    )
     qkv_low = lax.psum_scatter(qkv_column, "z", scatter_dimension=0, tiled=True)
 
     def end(out_keep, found, first, second, grad_resid, grad_qkv, out_near, qkv_blocks, resid, scale_one, tokens):
-        both = summed(out_keep, found).astype(low)
+        diag_top, diag_bottom, x_top, x_bottom, y_top, y_bottom, own = part_sums(out_keep, found)
 
         def results(grad_qkv, *second):
             inputs = tokens[0].astype(f32)
@@ -903,9 +1014,12 @@
             grad_unit_one = apply_rows(grad_qkv, qkv_blocks, jnp.zeros_like(inputs))
             return output, grad_resid + unit_back(grad_unit_one, inputs, scale_one)
 
-        started, (output, grad_tokens) = stage(first_sends(*both[:3]), results, [grad_qkv, *second])
-        second, _ = stage(second_sends(both[1], both[2], started))
-        column = joined(both[3], started, second).astype(low)
+        started, (output, grad_tokens) = stage(
+            [(diag_top, "x"), (diag_bottom, "y"), (x_top, "x"), (y_bottom, "y")], results, [grad_qkv, *second]
+        )
+        x_bottom, y_top = total(x_bottom, started[1]).astype(low), total(y_top, started[0]).astype(low)
+        second, _ = stage([(x_bottom, "x"), (y_top, "y")])
+        column = joined(own, started, second).astype(low)
         return output, grad_tokens, column.reshape(-1, column.shape[-1])
 
     output, grad_tokens, out_column = boxed(
@@ -915,7 +1029,7 @@
         found,
         first,
         second,
-        after(grad_resid, *columns),
+        after(grad_resid, columns[-1]),
         grad_qkv,
         out_near,
         qkv_blocks,
@@ -949,7 +1063,7 @@
         grad_mlp_gain[:, 0],
         grad_gate,
         grad_up,
-        grad_down,
+        grad_down.T,
     )
 
 

time: 1080 us -> 1040 us (0.963); the launches traced: 1070 us -> 1020 us
  other arithmetic: 97.4 us -> 66.1 us
  local copies, waits for them, and re-layouts: 83.2 us -> 55 us
    ppermute x6, waiting for transfers between devices: 57 us -> 85.9 us  [behind(): return lambda value: lax.ppermute(value, ('z', 'y'), pairs)]
    pallas_call x0 -> x4, Pallas kernels: none -> 26.6 us  [the longest x1 8.1 us: resid_grads(): pl.pallas_call(functools.partial(resid_kernel, steps), out_shape=(jax.Sha...]
    all_gather x4, waiting for transfers between devices: 21.7 us -> 0.05 us  [gathered(): return lax.all_gather(piece, 'z', axis=0, tiled=True)]
    convert_element_type x5 -> x2, other arithmetic: 22.8 us -> 2.79 us  [the longest x1 1.46 us: end(): total(y_top, started[0]).astype(low)]
    reduce_scatter x1, waiting for transfers between devices: 16.4 us -> 0.35 us  [local(): lax.psum_scatter(after(piece, grad_qkv), 'z', scatter_dimension=0, tiled=...]
    slice x8 -> x0, local copies, waits for them, and re-layouts: 13.5 us -> none  [the longest x1 2.32 us: opening(): gift_y[:half]]
    unnamed x70 -> x42, local copies, waits for them, and re-layouts: 17.3 us -> 5.46 us
    reduce_scatter x1, waiting for transfers between devices: 0.02 us -> 11 us  [local(): lax.psum_scatter(partial[0], 'z', scatter_dimension=0, tiled=True)]
  transfers between devices with their start and end apart: 98 -> 92, of which waited for: 40 -> 40; matrix products, arithmetic and copies ran while one was open for 14% -> 10% of each run, Pallas kernels for 37% -> 39%
where the time goes in v5:
time: 1040 us; the launch traced here: 1020 us
  Pallas kernels  407 us (39%)
  waiting for transfers between devices  388 us (37%)
  starting transfers between devices  90.1 us (9%)
  other arithmetic  66.1 us (6%)
  local copies, waits for them, and re-layouts  55 us (5%)
  between operations  15.1 us (1%)
    ppermute x66, waiting for transfers between devices, swap(): return lax.ppermute(value, axis, [(0, 1), (1, 0)])  190 us
    pallas_call x4, Pallas kernels, mlp(): pl.pallas_call(functools.partial(mlp_kernel, each // 3, per, tiles), out_...  156 us
    ppermute x6, waiting for transfers between devices, behind(): return lambda value: lax.ppermute(value, ('z', 'y'), pairs)  85.9 us
    pallas_call x2, Pallas kernels, mlp_grads(): pl.pallas_call(functools.partial(mlp_grads_kernel, len(units)), out_shape...  76.1 us
    pallas_call x4, Pallas kernels, apply_rows(): pl.pallas_call(kernel, out_shape=shape, grid_spec=pltpu.PrefetchScalarGri...  47.6 us
    ppermute x66, starting transfers between devices, swap(): return lax.ppermute(value, axis, [(0, 1), (1, 0)])  47.4 us
    all_to_all x1, waiting for transfers between devices, local(): lax.all_to_all(after(mine, qkv_shard), PLANE, split_axis=0, concat_axis=0...  44.6 us
    pallas_call x1, Pallas kernels, attend_back(): pl.pallas_call(functools.partial(attend_back_kernel, size, size ** (-0.5)...  35.6 us
  transfers between devices with their start and end apart: 92, of which 40 were waited for; matrix products, arithmetic and copies ran while one was open for 10% of the time, Pallas kernels for 39%

profile of v5, /device:TPU:0, one launch (start us, length us, event | category | flops | bytes accessed | tf_op | source)
XLA Modules:
  0.0 1023.4 jit_solution(836388465712120095)
XLA Ops:
  20.8 44.6 %all-to-all-done = bf16[8,80,3072]{2,1,0:T(8,128)(2,1)} async-done(((bf16[8,80,3072]{2,1,0:T(8,128)(2,1)}), bf16[8,80,3072]{2,1,0:T(8,128)(2,1)}, u32[]{:S(2)}, u32[]{:S(2)}) %all-to-all-start) | async-done | bytes 3932192 | tf_op jit(solution)/shard_map/all_to_all | solution.py:792
  71.6 150.8 %conditional.7 = (bf16[4,80,3072]{2,1,0:T(8,128)(2,1)}, bf16[4,80,3072]{2,1,0:T(8,128)(2,1)}, bf16[4,80,3072]{2,1,0:T(8,128)(2,1)}, bf16[4,80,3072]{2,1,0:T(8,12...) conditional(s32[]{:T(128)} %bitcast.16, () %tuple.125, ...), branch_computations={%region_0.0_spmd, %region_1.0_spmd} | conditional | flops 6947220 | bytes 127809664 | solution.py:60
  73.5 43.2 %collective-permute-done.13.rest_4_ = bf16[4,80,3072]{2,1,0:T(8,128)(2,1)} collective-permute-done((bf16[4,80,3072]{2,1,0:T(8,128)(2,1)}, bf16[4,80,3072]{2,1,0:T(8,128)(2,1)}, u32[]{:S(2)}, u32[]{:S(2)}) %collective-permute-start.13) | collective-permute-done | bytes 1966112 | tf_op jit(solution)/shard_map/cond/branch_1_fun/ppermute | solution.py:28
  122.9 17.9 %collective-permute-done.14 = bf16[2,80,3072]{2,1,0:T(8,128)(2,1)S(1)} collective-permute-done((bf16[2,80,3072]{2,1,0:T(8,128)(2,1)S(1)}, bf16[2,80,3072]{2,1,0:T(8,128)(2,1)S(1)}, u32[]{:S(2)}, u32[]{:S(2)}) %collective-permute-start.14) | collective-permute-done | bytes 983072 | tf_op jit(solution)/shard_map/cond/branch_1_fun/ppermute | solution.py:28
  152.6 12.0 %branch_1_fun.18 = bf16[384,3072]{1,0:T(8,128)(2,1)S(1)} custom-call(s32[8]{0:T(128)S(1)} %iota_xor_fusion.slots, bf16[384,2560]{1,0:T(8,128)(2,1)} %fusion.1.left, bf16[4,80,3072]{2,1,0:T(8,128)(2,1)S(1)} %copy-done.15, bf16[4,80,3072]{2,1,0:T(8,128)(2,1)} %collective-permute-done.10.rest_1_, bf16[4,80,3072]{2,1,0:T(8,128)(2,1)} %collective-permute-done.11.rest_2_, ...), custom_call_target="tpu_custom_call" | custom-call | flops 1048576 | bytes 4096 | tf_op jit(solution)/shard_map/cond/branch_1_fun/pallas_call | solution.py:311
  177.3 13.0 %collective-permute-done.19 = bf16[384,512]{1,0:T(8,128)(2,1)} collective-permute-done((bf16[384,512]{1,0:T(8,128)(2,1)}, bf16[384,512]{1,0:T(8,128)(2,1)}, u32[]{:S(2)}, u32[]{:S(2)}) %collective-permute-start.19) | collective-permute-done | bytes 393248 | tf_op jit(solution)/shard_map/cond/branch_1_fun/ppermute | solution.py:80
  198.6 20.6 %collective-permute-done.21 = bf16[384,512]{1,0:T(8,128)(2,1)} collective-permute-done((bf16[384,512]{1,0:T(8,128)(2,1)}, bf16[384,512]{1,0:T(8,128)(2,1)}, u32[]{:S(2)}, u32[]{:S(2)}) %collective-permute-start.21) | collective-permute-done | bytes 393248 | tf_op jit(solution)/shard_map/cond/branch_1_fun/ppermute | solution.py:80
  223.7 140.7 %conditional.8 = (bf16[4,80,2560]{2,1,0:T(8,128)(2,1)}, bf16[4,80,2560]{2,1,0:T(8,128)(2,1)}, bf16[4,80,2560]{2,1,0:T(8,128)(2,1)}, bf16[4,80,2560]{2,1,0:T(8,12...) conditional(s32[]{:T(128)} %bitcast.16, () %tuple.123, ...), branch_computations={%region_3.0_spmd, %region_4.0_spmd} | conditional | flops 7012756 | bytes 129779640 | solution.py:60
  227.3 28.9 %branch_1_fun.19 = (bf16[384,2560]{1,0:T(8,128)(2,1)}, f32[384,2560]{1,0:T(8,128)}, f32[15,1,256]{2,1,0:T(1,128)S(1)}) custom-call(s32[1]{0:T(128)} %bitcast.2.core, s32[1,384]{1,0:T(1,128)S(1)} %get-tuple-element.278.places, bf16[384,2560]{1,0:T(8,128)(2,1)} %get-tuple-element.279.queries, bf16[384,512]{1,0:T(8,128)(2,1)} %get-tuple-element.280.rest_0_, ...), custom_call_target="tpu_custom_call" | custom-call | flops 1048576 | bytes 4096 | tf_op jit(solution)/shard_map/cond/branch_1_fun/pallas_call | solution.py:195
  269.9 16.8 %collective-permute-done.34 = bf16[2,80,2560]{2,1,0:T(8,128)(2,1)S(1)} collective-permute-done((bf16[2,80,2560]{2,1,0:T(8,128)(2,1)S(1)}, bf16[2,80,2560]{2,1,0:T(8,128)(2,1)S(1)}, u32[]{:S(2)}, u32[]{:S(2)}) %collective-permute-start.34) | collective-permute-done | bytes 819232 | tf_op jit(solution)/shard_map/cond/branch_1_fun/ppermute | solution.py:28
  293.9 12.1 %branch_1_fun.20 = f32[384,2560]{1,0:T(8,128)} custom-call(s32[8]{0:T(128)S(1)} %iota_xor_fusion.1.slots, bf16[384,2560]{1,0:T(8,128)(2,1)} %get-tuple-element.1004.left, f32[384,2560]{1,0:T(8,128)S(1)} %bitcast_convert_fusion.start, bf16[4,80,2560]{2,1,0:T(8,128)(2,1)S(1)} %copy-done.16, bf16[4,80,2560]{2,1,0:T(8,128)(2,1)} %collective-permute-done.29.rest_1_, ...), custom_call_target="tpu_custom_call" | custom-call | flops 1048576 | bytes 4096 | tf_op jit(solution)/shard_map/cond/branch_1_fun/pallas_call | solution.py:311
  314.1 43.2 %collective-permute-done.39 = bf16[384,2560]{1,0:T(8,128)(2,1)} collective-permute-done((bf16[384,2560]{1,0:T(8,128)(2,1)}, bf16[384,2560]{1,0:T(8,128)(2,1)}, u32[]{:S(2)}, u32[]{:S(2)}) %collective-permute-start.39) | collective-permute-done | bytes 1966112 | tf_op jit(solution)/shard_map/cond/branch_1_fun/ppermute | solution.py:28
  364.4 138.7 %conditional.9 = (bf16[384,2560]{1,0:T(8,128)(2,1)}, bf16[384,2560]{1,0:T(8,128)(2,1)}, bf16[384,2560]{1,0:T(8,128)(2,1)}, bf16[384,2560]{1,0:T(8,128)(2,1)}, bf...) conditional(s32[]{:T(128)} %bitcast.16, () %tuple.122, ...), branch_computations={%region_6.0_spmd, %region_7.0_spmd} | conditional | flops 3145728 | bytes 86520376 | solution.py:60
  368.1 37.0 %branch_1_fun.21 = (bf16[768,2560]{1,0:T(8,128)(2,1)}, bf16[768,2560]{1,0:T(8,128)(2,1)}, bf16[768,2560]{1,0:T(8,128)(2,1)}, bf16[768,2560]{1,0:T(8,128)(2,1)}, bf16[1536,1536]{1,0:T(8,128)(2,1)}) custom-call(bf16[2560,768]{1,0:T(8,128)(2,1)} %get-tuple-element.351.rest_0_, bf16[2560,768]{1,0:T(8,128)(2,1)} %get-tuple-element.352.rest_1_, ...), custom_call_target="tpu_custom_call" | custom-call | flops 1048576 | bytes 4096 | tf_op jit(solution)/shard_map/cond/branch_1_fun/pallas_call | solution.py:460
  418.4 37.5 %branch_1_fun.22 = (bf16[768,2560]{1,0:T(8,128)(2,1)}, bf16[768,2560]{1,0:T(8,128)(2,1)}, bf16[768,2560]{1,0:T(8,128)(2,1)}, bf16[768,2560]{1,0:T(8,128)(2,1)}, bf16[1536,1536]{1,0:T(8,128)(2,1)}) custom-call(bf16[2560,768]{1,0:T(8,128)(2,1)} %get-tuple-element.351.rest_0_, bf16[2560,768]{1,0:T(8,128)(2,1)} %get-tuple-element.352.rest_1_, ...), custom_call_target="tpu_custom_call" | custom-call | flops 1048576 | bytes 4096 | tf_op jit(solution)/shard_map/cond/branch_1_fun/pallas_call | solution.py:460
  465.0 37.8 %branch_1_fun.23 = bf16[2560,1536]{1,0:T(8,128)(2,1)} custom-call(bf16[384,2560]{1,0:T(8,128)(2,1)} %collective-permute-done.rest_2_.rest_0_, bf16[384,2560]{1,0:T(8,128)(2,1)} %get-tuple-element.353.rest_4_.rest_1_, bf16[384,2560]{1,0:T(8,128)(2,1)} %collective-permute-done.2.rest_6_.rest_2_, bf16[384,2560]{1,0:T(8,128)(2,1)} %get-tuple-element.354.rest_8_.rest_3_, ...), custom_call_target="tpu_custom_call" | custom-call | flops 1048576 | bytes 4096 | tf_op jit(solution)/shard_map/cond/branch_1_fun/pallas_call | solution.py:523
  503.2 176.6 %conditional.10 = (bf16[2560,1024]{1,0:T(8,128)(2,1)}, bf16[2560,512]{1,0:T(8,128)(2,1)}, f32[384,2560]{1,0:T(8,128)}, bf16[384,2560]{1,0:T(8,128)(2,1)}, bf16[7...) conditional(s32[]{:T(128)} %bitcast.16, () %tuple.121, ...), branch_computations={%region_8.0_spmd, %region_9.0_spmd} | conditional | flops 28835840 | bytes 137649664 | solution.py:60
  503.3 40.8 %branch_1_fun.24 = (bf16[768,2560]{1,0:T(8,128)(2,1)}, bf16[768,2560]{1,0:T(8,128)(2,1)}, bf16[768,2560]{1,0:T(8,128)(2,1)}, bf16[768,2560]{1,0:T(8,128)(2,1)}, bf16[1536,1536]{1,0:T(8,128)(2,1)}) custom-call(bf16[2560,768]{1,0:T(8,128)(2,1)} %get-tuple-element.386.rest_0_, bf16[2560,768]{1,0:T(8,128)(2,1)} %get-tuple-element.387.rest_1_, ...), custom_call_target="tpu_custom_call" | custom-call | flops 1048576 | bytes 4096 | tf_op jit(solution)/shard_map/cond/branch_1_fun/pallas_call | solution.py:460
  560.4 40.9 %branch_1_fun.25 = (bf16[768,2560]{1,0:T(8,128)(2,1)}, bf16[768,2560]{1,0:T(8,128)(2,1)}, bf16[768,2560]{1,0:T(8,128)(2,1)}, bf16[768,2560]{1,0:T(8,128)(2,1)}, bf16[1536,1536]{1,0:T(8,128)(2,1)}) custom-call(bf16[2560,768]{1,0:T(8,128)(2,1)} %get-tuple-element.386.rest_0_, bf16[2560,768]{1,0:T(8,128)(2,1)} %get-tuple-element.387.rest_1_, ...), custom_call_target="tpu_custom_call" | custom-call | flops 1048576 | bytes 4096 | tf_op jit(solution)/shard_map/cond/branch_1_fun/pallas_call | solution.py:460
  626.7 38.2 %branch_1_fun.27 = (bf16[2560,1024]{1,0:T(8,128)(2,1)}, bf16[2560,512]{1,0:T(8,128)(2,1)}) custom-call(bf16[384,2560]{1,0:T(8,128)(2,1)} %get-tuple-element.388.rest_2_.rest_0_, bf16[384,2560]{1,0:T(8,128)(2,1)} %get-tuple-element.390.rest_4_.rest_1_, bf16[384,2560]{1,0:T(8,128)(2,1)} %get-tuple-element.392.rest_6_.rest_2_, ...), custom_call_target="tpu_custom_call" | custom-call | flops 1048576 | bytes 4096 | tf_op jit(solution)/shard_map/cond/branch_1_fun/pallas_call | solution.py:523
  679.8 116.5 %conditional.11 = (bf16[384,3072]{1,0:T(8,128)(2,1)S(1)}, bf16[192,2560]{1,0:T(8,128)(2,1)S(1)}, bf16[192,2560]{1,0:T(8,128)(2,1)}, bf16[192,2560]{1,0:T(8,128)(2,1)}, bf16[192,2560]{1,0:T(8,128)(2,1)}) conditional(s32[]{:T(128)} %bitcast.16, () %tuple.120, (bf16[768,2560]{1,0:T(8,128)(2,1)}, bf16[768,2560]{1,0:T(8,128)(2,1)}, ...), branch_computations={%region_11.0_spmd, %region_12.0_spmd} | conditional | flops 14483476 | bytes 102113976 | solution.py:60
  701.6 35.6 %branch_1_fun.30 = (bf16[384,2560]{1,0:T(8,128)(2,1)}, f32[4,384,512]{2,1,0:T(8,128)}, bf16[4,384,512]{2,1,0:T(8,128)(2,1)}) custom-call(s32[1]{0:T(128)} %bitcast.5.core, s32[1,384]{1,0:T(1,128)S(1)} %get-tuple-element.474.places, bf16[384,2560]{1,0:T(8,128)(2,1)} %get-tuple-element.475.queries, bf16[384,2560]{1,0:T(8,128)(2,1)} %copy-done.1, ...), custom_call_target="tpu_custom_call" | custom-call | flops 1048576 | bytes 4096 | tf_op jit(solution)/shard_map/cond/branch_1_fun/pallas_call | solution.py:228
  746.5 37.0 %collective-permute-done.76 = bf16[384,512]{1,0:T(8,128)(2,1)S(1)} collective-permute-done((bf16[384,512]{1,0:T(8,128)(2,1)S(1)}, bf16[384,512]{1,0:T(8,128)(2,1)S(1)}, u32[]{:S(2)}, u32[]{:S(2)}) %collective-permute-start.76) | collective-permute-done | bytes 393248 | tf_op jit(solution)/shard_map/cond/branch_1_fun/ppermute | solution.py:80
  807.4 63.3 %conditional.12 = (bf16[2560,384]{1,0:T(8,128)(2,1)}, bf16[4,4,80,2560]{3,2,1,0:T(8,128)(2,1)}, bf16[4,4,80,2560]{3,2,1,0:T(8,128)(2,1)}, bf16[192,2560]{1,0:T(8,128)(2,1)}, bf16[192,2560]{1,0:T(8,128)(2,1)}) conditional(s32[]{:T(128)} %bitcast.16, () %tuple.119, (bf16[384,3072]{1,0:T(8,128)(2,1)S(1)}, bf16[384,2560]{1,0:T(8,128)(2,1)}, ...), branch_computations={%region_14.0_spmd, %region_15.0_spmd} | conditional | flops 3146804 | bytes 57689048 | solution.py:60
  826.6 13.2 %branch_1_fun.32 = (bf16[4,4,80,2560]{3,2,1,0:T(8,128)(2,1)}, bf16[4,4,80,2560]{3,2,1,0:T(8,128)(2,1)}) custom-call(s32[8]{0:T(128)S(1)} %gather_fusion, bf16[384,2560]{1,0:T(8,128)(2,1)} %get-tuple-element.533.left, bf16[384,2560]{1,0:T(8,128)(2,1)} %get-tuple-element.534.right), custom_call_target="tpu_custom_call" | custom-call | flops 1048576 | bytes 4096 | tf_op jit(solution)/shard_map/cond/branch_1_fun/pallas_call | solution.py:360
  853.5 14.2 %branch_1_fun.33 = bf16[2560,384]{1,0:T(8,128)(2,1)} custom-call(bf16[384,2560]{1,0:T(8,128)(2,1)} %get-tuple-element.551.rest_0_, bf16[384,2560]{1,0:T(8,128)(2,1)} %get-tuple-element.552.rest_1_, bf16[384,2560]{1,0:T(8,128)(2,1)} %get-tuple-element.553.rest_2_, bf16[384,2560]{1,0:T(8,128)(2,1)} %get-tuple-element.554.rest_3_, ...), custom_call_target="tpu_custom_call" | custom-call | flops 1048576 | bytes 4096 | tf_op jit(solution)/shard_map/cond/branch_1_fun/pallas_call | solution.py:558
  871.5 73.9 %conditional.13 = (bf16[320,2560]{1,0:T(8,128)(2,1)}, f32[1,384,2560]{2,1,0:T(8,128)}, f32[1,384,2560]{2,1,0:T(8,128)}) conditional(s32[]{:T(128)} %bitcast.16, () %tuple.118, (bf16[4,4,80,2560]{3,2,1,0:T(8,128)(2,1)}, bf16[4,4,80,2560]{3,2,1,0:T(8,128)(2,1)}, bf16[384,3072]{1,0:T(8,128)(2,1)S(1)}, bf16[192,2560]{1,0:T(8,128)(2,1)}, ...), branch_computations={%region_17.0_spmd, %region_18.20_spmd} | conditional | flops 27820052 | bytes 132600424 | solution.py:60
  887.4 13.1 %branch_1_fun.35 = f32[384,2560]{1,0:T(8,128)S(1)} custom-call(s32[8]{0:T(128)S(1)} %iota_xor_fusion.4.slots, bf16[384,3072]{1,0:T(8,128)(2,1)S(1)} %copy-done.14, f32[384,2560]{1,0:T(8,128)} %broadcast_63_start.0.start, bf16[4,80,3072]{2,1,0:T(8,128)(2,1)} %get-tuple-element.595.rest_0_, bf16[4,80,3072]{2,1,0:T(8,128)(2,1)} %get-tuple-element.596.rest_1_, ...), custom_call_target="tpu_custom_call" | custom-call | flops 1048576 | bytes 4096 | tf_op jit(solution)/shard_map/cond/branch_1_fun/pallas_call | solution.py:311
  907.6 11.5 %maximum_add_fusion = (f32[384,2560]{1,0:T(8,128)}, f32[384,2560]{1,0:T(8,128)}) fusion(f32[384,2560]{1,0:T(8,128)} %get-tuple-element.586, f32[192,2560]{1,0:T(8,128)} %get-tuple-element.912, f32[192,2560]{1,0:T(8,128)} %get-tuple-element.911, f32[384,2560]{1,0:T(8,128)} %get-tuple-element.592, f32[384,2560]{1,0:T(8,128)} %copy-done, ...), kind=kLoop, calls=%fused_computation.46 | loop fusion | flops 7864320 | bytes 25562112 | tf_op jit(solution)/shard_map/cond/branch_1_fun/add | solution.py:1013
  924.7 16.4 %collective-permute-done.58 = bf16[2,80,2560]{2,1,0:T(8,128)(2,1)S(1)} collective-permute-done((bf16[2,80,2560]{2,1,0:T(8,128)(2,1)S(1)}, bf16[2,80,2560]{2,1,0:T(8,128)(2,1)S(1)}, u32[]{:S(2)}, u32[]{:S(2)}) %collective-permute-start.58) | collective-permute-done | bytes 819232 | tf_op jit(solution)/shard_map/cond/branch_1_fun/ppermute | solution.py:28
  955.0 32.8 %reduce-scatter.14.cloned.1.call-done = bf16[80,2560]{1,0:T(8,128)(2,1)} async-done(((bf16[320,2560]{1,0:T(8,128)(2,1)}), bf16[80,2560]{1,0:T(8,128)(2,1)}) %reduce-scatter.14.cloned.1.call-update) | async-done | bytes 409616 | tf_op jit(solution)/shard_map/reduce_scatter | solution.py:1040
  989.8 16.3 %all-to-all-done.1.whole = bf16[8,80,3456]{2,1,0:T(8,128)(2,1)} async-done(((bf16[8,80,3456]{2,1,0:T(8,128)(2,1)}), bf16[8,80,3456]{2,1,0:T(8,128)(2,1)}, u32[]{:S(2)}, u32[]{:S(2)}) %all-to-all-start.1) | async-done | bytes 4423712 | tf_op jit(solution)/shard_map/all_to_all | solution.py:1043
  (341 shorter events, 331.9 us)
Async XLA Ops:
  14.4 51.0 %all-to-all-start = ((bf16[8,80,3072]{2,1,0:T(8,128)(2,1)}), bf16[8,80,3072]{2,1,0:T(8,128)(2,1)}, u32[]{:S(2)}, u32[]{:S(2)}) async-start(bf16[8,80,3072]{2,1,0:T(8,128)(2,1)} %shard_map.213), calls=%async_computation | async-start | bytes 7864320 | tf_op jit(solution)/shard_map/all_to_all | solution.py:792
  19.7 51.9 %all-gather.8.cloned.1.call-start = ((), (), s32[]{:S(2)}) async-start(), calls=%async_computation.7 | async-start | bytes 2457600 | tf_op jit(solution)/shard_map/all_gather | solution.py:782
  20.7 203.0 %all-gather.10.cloned.1.call-start = ((), (), s32[]{:S(2)}) async-start(), calls=%async_computation.8 | async-start | bytes 4915200 | tf_op jit(solution)/shard_map/all_gather | solution.py:797
  69.6 154.1 %all-gather.18.cloned.1.call-start = ((), (), s32[]{:S(2)}) async-start(), calls=%async_computation.17 | async-start | bytes 2048000 | tf_op jit(solution)/shard_map/all_gather | solution.py:783
  70.4 294.0 %all-gather.12.cloned.1.call-start = ((), (), s32[]{:S(2)}) async-start(), calls=%async_computation.9 | async-start | bytes 4915200 | tf_op jit(solution)/shard_map/all_gather | solution.py:797
  71.7 45.0 %collective-permute-start.13 = (bf16[4,80,3072]{2,1,0:T(8,128)(2,1)}, bf16[4,80,3072]{2,1,0:T(8,128)(2,1)}, u32[]{:S(2)}, u32[]{:S(2)}) collective-permute-start(bf16[4,80,3072]{2,1,0:T(8,128)(2,1)} %get-tuple-element.238.rest_0_), channel_id=1, source_target_pairs={{0,4},{4,0},{1,5},{5,1},{2,6},{6,2},{3,7},{7,3},{8,12},{12,8},{9,1... | collective-permute-start | bytes 5898248 | tf_op jit(solution)/shard_map/cond/branch_1_fun/ppermute | solution.py:28
  72.4 46.9 %collective-permute-start.10 = (bf16[4,80,3072]{2,1,0:T(8,128)(2,1)}, bf16[4,80,3072]{2,1,0:T(8,128)(2,1)}, u32[]{:S(2)}, u32[]{:S(2)}) collective-permute-start(bf16[4,80,3072]{2,1,0:T(8,128)(2,1)} %get-tuple-element.238.rest_0_), channel_id=1, source_target_pairs={{0,1},{1,0},{2,3},{3,2},{4,5},{5,4},{6,7},{7,6},{8,9},{9,8},{10,11... | collective-permute-start | bytes 5898248 | tf_op jit(solution)/shard_map/cond/branch_1_fun/ppermute | solution.py:28
  165.3 53.8 %collective-permute-start.23 = (bf16[384,2560]{1,0:T(8,128)(2,1)S(1)}, bf16[384,2560]{1,0:T(8,128)(2,1)}, u32[]{:S(2)}, u32[]{:S(2)}) collective-permute-start(bf16[384,2560]{1,0:T(8,128)(2,1)S(1)} %get-tuple-element.247), channel_id=1, source_target_pairs={{0,1},{1,0},{2,3},{3,2},{4,5},{5,4},{6,7},{7,6},{8,9},{9,8},{10,11... | collective-permute-start | bytes 5898248 | tf_op jit(solution)/shard_map/cond/branch_1_fun/ppermute | solution.py:28
  166.7 52.5 %collective-permute-start.24 = (bf16[384,2560]{1,0:T(8,128)(2,1)S(1)}, bf16[384,2560]{1,0:T(8,128)(2,1)}, u32[]{:S(2)}, u32[]{:S(2)}) collective-permute-start(bf16[384,2560]{1,0:T(8,128)(2,1)S(1)} %get-tuple-element.247), channel_id=1, source_target_pairs={{0,4},{4,0},{1,5},{5,1},{2,6},{6,2},{3,7},{7,3},{8,12},{12,8},{9,1... | collective-permute-start | bytes 5898248 | tf_op jit(solution)/shard_map/cond/branch_1_fun/ppermute | solution.py:28
  168.2 51.0 %collective-permute-start.25 = (bf16[384,2560]{1,0:T(8,128)(2,1)S(1)}, bf16[384,2560]{1,0:T(8,128)(2,1)}, u32[]{:S(2)}, u32[]{:S(2)}) collective-permute-start(bf16[384,2560]{1,0:T(8,128)(2,1)S(1)} %get-tuple-element.247), channel_id=1, source_target_pairs={{0,2},{2,0},{1,3},{3,1},{4,6},{6,4},{5,7},{7,5},{8,10},{10,8},{9,1... | collective-permute-start | bytes 5898248 | tf_op jit(solution)/shard_map/cond/branch_1_fun/ppermute | solution.py:28
  222.4 280.7 %all-gather.14.cloned.1.call-start = ((), (), s32[]{:S(2)}) async-start(), calls=%async_computation.10 | async-start | bytes 4915200 | tf_op jit(solution)/shard_map/all_gather | solution.py:797
  223.0 280.1 %all-gather.16.cloned.1.call-start = ((), (), s32[]{:S(2)}) async-start(), calls=%async_computation.11 | async-start | bytes 4915200 | tf_op jit(solution)/shard_map/all_gather | solution.py:797
  223.6 456.2 %reduce-scatter.6.cloned.1.call-start = ((), (), s32[]{:S(2)}) async-start(), calls=%async_computation.12 | async-start | bytes 9830400 | tf_op jit(solution)/shard_map/reduce_scatter | solution.py:899
  312.1 45.2 %collective-permute-start.39 = (bf16[384,2560]{1,0:T(8,128)(2,1)}, bf16[384,2560]{1,0:T(8,128)(2,1)}, u32[]{:S(2)}, u32[]{:S(2)}) collective-permute-start(bf16[384,2560]{1,0:T(8,128)(2,1)} %multiply_convert_fusion), channel_id=1, source_target_pairs={{0,1},{1,0},{2,3},{3,2},{4,5},{5,4},{6,7},{7,6},{8,9},{9,8},{10,11... | collective-permute-start | bytes 5898248 | tf_op jit(solution)/shard_map/cond/branch_1_fun/ppermute | solution.py:28
  364.6 45.2 %collective-permute-start = (bf16[384,2560]{1,0:T(8,128)(2,1)}, bf16[384,2560]{1,0:T(8,128)(2,1)}, u32[]{:S(2)}, u32[]{:S(2)}) collective-permute-start(bf16[384,2560]{1,0:T(8,128)(2,1)} %get-tuple-element.327.rest_2_.rest_4_), channel_id=1, source_target_pairs={{0,1},{1,0},{2,3},{3,2},{4,5},{5,4},{6,7},{7,6},{8,9},{9,8},{10,11... | collective-permute-start | bytes 5898248 | tf_op jit(solution)/shard_map/cond/branch_1_fun/ppermute | solution.py:28
  411.8 45.0 %collective-permute-start.4 = (bf16[384,2560]{1,0:T(8,128)(2,1)}, bf16[384,2560]{1,0:T(8,128)(2,1)}, u32[]{:S(2)}, u32[]{:S(2)}) collective-permute-start(bf16[384,2560]{1,0:T(8,128)(2,1)} %get-tuple-element.350), channel_id=1, source_target_pairs={{0,1},{1,0},{2,3},{3,2},{4,5},{5,4},{6,7},{7,6},{8,9},{9,8},{10,11... | collective-permute-start | bytes 5898248 | tf_op jit(solution)/shard_map/cond/branch_1_fun/ppermute | solution.py:28
  456.9 45.9 %collective-permute-start.7 = (bf16[384,2560]{1,0:T(8,128)(2,1)}, bf16[384,2560]{1,0:T(8,128)(2,1)}, u32[]{:S(2)}, u32[]{:S(2)}) collective-permute-start(bf16[384,2560]{1,0:T(8,128)(2,1)} %collective-permute-done.5), channel_id=1, source_target_pairs={{0,1},{1,0},{2,3},{3,2},{4,5},{5,4},{6,7},{7,6},{8,9},{9,8},{10,11... | collective-permute-start | bytes 5898248 | tf_op jit(solution)/shard_map/cond/branch_1_fun/ppermute | solution.py:28
  503.1 304.4 %reduce-scatter.8.cloned.1.call-start = ((), (), s32[]{:S(2)}) async-start(), calls=%async_computation.13 | async-start | bytes 6553600 | tf_op jit(solution)/shard_map/reduce_scatter | solution.py:946
  556.4 45.6 %collective-permute-start.65 = (bf16[768,2560]{1,0:T(8,128)(2,1)}, bf16[768,2560]{1,0:T(8,128)(2,1)}, u32[]{:S(2)}, u32[]{:S(2)}) collective-permute-start(bf16[768,2560]{1,0:T(8,128)(2,1)} %get-tuple-element.415), channel_id=1, source_target_pairs={{0,2},{2,0},{1,3},{3,1},{4,6},{6,4},{5,7},{7,5},{8,10},{10,8},{9,1... | collective-permute-start | bytes 11796488 | tf_op jit(solution)/shard_map/cond/branch_1_fun/ppermute | solution.py:28
  617.2 47.8 %collective-permute-start.70 = (bf16[768,2560]{1,0:T(8,128)(2,1)}, bf16[768,2560]{1,0:T(8,128)(2,1)}, u32[]{:S(2)}, u32[]{:S(2)}) collective-permute-start(bf16[768,2560]{1,0:T(8,128)(2,1)} %get-tuple-element.446), channel_id=1, source_target_pairs={{0,2},{2,0},{1,3},{3,1},{4,6},{6,4},{5,7},{7,5},{8,10},{10,8},{9,1... | collective-permute-start | bytes 11796488 | tf_op jit(solution)/shard_map/cond/branch_1_fun/ppermute | solution.py:28
  618.2 46.8 %collective-permute-start.67 = (bf16[192,2560]{1,0:T(8,128)(2,1)}, bf16[192,2560]{1,0:T(8,128)(2,1)}, u32[]{:S(2)}, u32[]{:S(2)}) collective-permute-start(bf16[192,2560]{1,0:T(8,128)(2,1)} %get-tuple-element.443), channel_id=1, source_target_pairs={{0,4},{4,0},{1,5},{5,1},{2,6},{6,2},{3,7},{7,3},{8,12},{12,8},{9,1... | collective-permute-start | bytes 2949128 | tf_op jit(solution)/shard_map/cond/branch_1_fun/ppermute | solution.py:28
  619.9 45.1 %collective-permute-start.68 = (bf16[192,2560]{1,0:T(8,128)(2,1)}, bf16[192,2560]{1,0:T(8,128)(2,1)}, u32[]{:S(2)}, u32[]{:S(2)}) collective-permute-start(bf16[192,2560]{1,0:T(8,128)(2,1)} %get-tuple-element.444), channel_id=1, source_target_pairs={{0,1},{1,0},{2,3},{3,2},{4,5},{5,4},{6,7},{7,6},{8,9},{9,8},{10,11... | collective-permute-start | bytes 2949128 | tf_op jit(solution)/shard_map/cond/branch_1_fun/ppermute | solution.py:28
  679.8 191.5 %reduce-scatter.10.cloned.1.call-start = ((), (), s32[]{:S(2)}) async-start(), calls=%async_computation.14 | async-start | bytes 3276800 | tf_op jit(solution)/shard_map/reduce_scatter | solution.py:986
  685.7 51.5 %collective-permute-start.71 = (bf16[192,2560]{1,0:T(8,128)(2,1)}, bf16[192,2560]{1,0:T(8,128)(2,1)}, u32[]{:S(2)}, u32[]{:S(2)}) collective-permute-start(bf16[192,2560]{1,0:T(8,128)(2,1)} %get-tuple-element.470), channel_id=1, source_target_pairs={{0,1},{1,0},{2,3},{3,2},{4,5},{5,4},{6,7},{7,6},{8,9},{9,8},{10,11... | collective-permute-start | bytes 2949128 | tf_op jit(solution)/shard_map/cond/branch_1_fun/ppermute | solution.py:28
  687.5 49.8 %collective-permute-start.72 = (bf16[192,2560]{1,0:T(8,128)(2,1)}, bf16[192,2560]{1,0:T(8,128)(2,1)}, u32[]{:S(2)}, u32[]{:S(2)}) collective-permute-start(bf16[192,2560]{1,0:T(8,128)(2,1)} %get-tuple-element.471), channel_id=1, source_target_pairs={{0,4},{4,0},{1,5},{5,1},{2,6},{6,2},{3,7},{7,3},{8,12},{12,8},{9,1... | collective-permute-start | bytes 2949128 | tf_op jit(solution)/shard_map/cond/branch_1_fun/ppermute | solution.py:28
  689.1 48.1 %collective-permute-start.73 = (bf16[192,2560]{1,0:T(8,128)(2,1)}, bf16[192,2560]{1,0:T(8,128)(2,1)S(1)}, u32[]{:S(2)}, u32[]{:S(2)}) collective-permute-start(bf16[192,2560]{1,0:T(8,128)(2,1)} %get-tuple-element.472), channel_id=1, source_target_pairs={{0,1},{1,0},{2,3},{3,2},{4,5},{5,4},{6,7},{7,6},{8,9},{9,8},{10,11... | collective-permute-start | bytes 2949128 | tf_op jit(solution)/shard_map/cond/branch_1_fun/ppermute | solution.py:28
  689.5 47.8 %collective-permute-start.74 = (bf16[192,2560]{1,0:T(8,128)(2,1)}, bf16[192,2560]{1,0:T(8,128)(2,1)}, u32[]{:S(2)}, u32[]{:S(2)}) collective-permute-start(bf16[192,2560]{1,0:T(8,128)(2,1)} %slice.102), channel_id=1, source_target_pairs={{0,4},{4,0},{1,5},{5,1},{2,6},{6,2},{3,7},{7,3},{8,12},{12,8},{9,1... | collective-permute-start | bytes 2949128 | tf_op jit(solution)/shard_map/cond/branch_1_fun/ppermute | solution.py:28
  743.9 51.0 %collective-permute-start.77 = (bf16[384,512]{1,0:T(8,128)(2,1)S(1)}, bf16[384,512]{1,0:T(8,128)(2,1)S(1)}, u32[]{:S(2)}, u32[]{:S(2)}) collective-permute-start(bf16[384,512]{1,0:T(8,128)(2,1)S(1)} %get-tuple-element.504), channel_id=1, source_target_pairs={{8,0},{12,4},{16,8},{20,12},{24,16},{28,20},{9,1},{13,5},{17,9},{2... | collective-permute-start | bytes 1179656 | tf_op jit(solution)/shard_map/cond/branch_1_fun/ppermute | solution.py:80
  745.2 49.7 %collective-permute-start.78 = (bf16[384,512]{1,0:T(8,128)(2,1)S(1)}, bf16[384,512]{1,0:T(8,128)(2,1)S(1)}, u32[]{:S(2)}, u32[]{:S(2)}) collective-permute-start(bf16[384,512]{1,0:T(8,128)(2,1)S(1)} %get-tuple-element.505), channel_id=1, source_target_pairs={{4,0},{8,4},{12,8},{16,12},{20,16},{24,20},{28,24},{5,1},{9,5},{13... | collective-permute-start | bytes 1179656 | tf_op jit(solution)/shard_map/cond/branch_1_fun/ppermute | solution.py:80
  796.3 149.1 %reduce-scatter.12.cloned.1.call-start = ((), (), s32[]{:S(2)}) async-start(), calls=%async_computation.15 | async-start | bytes 2457600 | tf_op jit(solution)/shard_map/reduce_scatter | solution.py:1006
  870.8 117.0 %reduce-scatter.14.cloned.1.call-start = ((), (), s32[]{:S(2)}) async-start(), calls=%async_computation.16 | async-start | bytes 2048000 | tf_op jit(solution)/shard_map/reduce_scatter | solution.py:1040
  950.4 55.7 %all-to-all-start.1 = ((bf16[8,80,3456]{2,1,0:T(8,128)(2,1)}), bf16[8,80,3456]{2,1,0:T(8,128)(2,1)}, u32[]{:S(2)}, u32[]{:S(2)}) async-start(bf16[8,80,3456]{2,1,0:T(8,128)(2,1)} %bitcast.56), calls=%async_computation.5 | async-start | bytes 8847360 | tf_op jit(solution)/shard_map/all_to_all | solution.py:1043
  (99 other events, 1862.0 us)
Sparse Core Ops, SparseCore 0:
  22.7 45.9 all-gather.7
  70.8 76.1 all-gather.9
  148.6 41.6 all-gather.17
  222.6 86.8 all-gather.11
  310.9 74.9 all-gather.13
  387.3 74.9 all-gather.15
  503.2 146.5 reduce-scatter.5
  679.9 127.5 reduce-scatter.7
  809.8 61.4 reduce-scatter.9
  873.4 45.7 reduce-scatter.11
  945.6 42.2 reduce-scatter.13

commit v6 on v5

--- a/solution.py
+++ b/solution.py
@@ -270,13 +270,14 @@
     out[...] = dot(left[...], full[...], (1, 0), low)
 
 
-def apply_turned_kernel(slots, left, start, *rest):
-    blocks, (out, full) = rest[:8], rest[8:]
+def apply_turned_kernel(slots, left, *rest):
+    *start, out, full = rest
+    start, blocks = start[:-8], start[-8:]
     lay_rows(slots, blocks, full)
 
     @pl.when(pl.program_id(0) == 0)
     def _():
-        out[...] = start[...]
+        out[...] = start[0][...] if start else jnp.zeros_like(out)
 
     out[...] += dot(left[...], full[...], (1, 1))
 
@@ -290,23 +291,25 @@
     return whole.reshape(planes * 8 * rows, wide)
 
 
-def apply_rows(left, blocks, start=None):
+def apply_rows(left, blocks, turned=False, start=None):
     planes, rows, wide = blocks[0].shape
     if rows % 16 or wide % TILE:
         whole = whole_rows(blocks)
-        if start is None:
+        if not turned:
             return dot(left, whole, (1, 0), low)
-        return start + dot(left, whole, (1, 1))
+        return dot(left, whole, (1, 1)) + (0.0 if start is None else start)
     count, deep = left.shape[0], planes * 8 * rows
     slots = (plane_index() ^ jnp.arange(8)).astype(jnp.int32)
     pieces = [pl.BlockSpec((planes, rows, TILE), lambda n, s: (0, 0, n))] * 8
     whole = pl.BlockSpec((count, deep), lambda n, s: (0, 0))
     part = pl.BlockSpec((count, TILE), lambda n, s: (0, n))
-    if start is None:
+    if not turned:
         kernel, given, specs, result = apply_kernel, [left], [whole], part
         shape = jax.ShapeDtypeStruct((count, wide), low)
     else:
-        kernel, given, specs, result = apply_turned_kernel, [left, start], [part, whole], whole
+        kernel, given, specs, result = apply_turned_kernel, [left], [part], whole
+        if start is not None:
+            given, specs = given + [start], specs + [whole]
         shape = jax.ShapeDtypeStruct((count, deep), f32)
     return pl.pallas_call(
         kernel,
@@ -419,10 +422,9 @@
         gates, upward = both[:, :part], both[:, part:]
         grad_middle = dot(grads[step % 2], weights[j][:, 2 * part :], (1, 0))
         square = gates * gates
-        bend = jnp.tanh(slope * gates * (1.0 + 0.044715 * square))
-        half = 0.5 * (1.0 + bend)
+        half = 0.5 + 0.5 * jnp.tanh(gates * (slope + slope * 0.044715 * square))
         gelu = gates * half
-        grad_gelu = half + 0.5 * gates * (1.0 - bend * bend) * (slope * (1.0 + 3 * 0.044715 * square))
+        grad_gelu = half + gelu * (1.0 - half) * (2 * slope + 6 * slope * 0.044715 * square)
         at = 2 * part * j
         hidden[:, at : at + part] = (grad_middle * upward * grad_gelu).astype(low)
         hidden[:, at + part : at + 2 * part] = (grad_middle * gelu).astype(low)
@@ -593,16 +595,12 @@
     )(slots, value)
 
 
-def turn_kernel(keep, found, far, diag_x, diag_y, y_bottom, x_bottom, y_top, own):
+def turn_kernel(keep, found, far, diag_x, diag_y, y_bottom, x_bottom, y_top):
     half = far.shape[0]
-
-    def both(start, rows):
-        return keep[start : start + rows].astype(f32) + found[start : start + rows].astype(f32)
-
-    y_top[...] = (both(0, half) + diag_x[...].astype(f32)).astype(low)
-    y_bottom[...] = both(half, half).astype(low)
+    both = keep[...].astype(f32) + found[...].astype(f32)
+    y_top[...] = (both[:half] + diag_x[...].astype(f32)).astype(low)
+    y_bottom[...] = both[half:].astype(low)
     x_bottom[...] = (far[...].astype(f32) + diag_y[...].astype(f32)).astype(low)
-    own[...] = both(2 * half, 2 * half)
 
 
 def turn(keep, found, far, diag_x, diag_y):
@@ -610,39 +608,60 @@
     part = lambda rows: pl.BlockSpec((rows, TILE), lambda n: (0, n))
     return pl.pallas_call(
         turn_kernel,
-        out_shape=[jax.ShapeDtypeStruct((half, wide), low)] * 3 + [jax.ShapeDtypeStruct((2 * half, wide), f32)],
+        out_shape=[jax.ShapeDtypeStruct((half, wide), low)] * 3,
         grid=(wide // TILE,),
-        in_specs=[part(4 * half)] * 2 + [part(half)] * 3,
-        out_specs=[part(half)] * 3 + [part(2 * half)],
+        in_specs=[part(2 * half)] * 2 + [part(half)] * 3,
+        out_specs=[part(half)] * 3,
         cost_estimate=NOMINAL,
     )(keep, found, far, diag_x, diag_y)
 
 
-def resid_kernel(steps, own, x_top, x_bottom, y_top, y_bottom, resid, gift, scale, grad_out, grad_low):
+def halved_kernel(keep, found, *outs):
+    half = outs[0].shape[0]
+    for i, out in enumerate(outs):
+        rows = slice(i * half, i * half + half)
+        out[...] = (keep[rows].astype(f32) + found[rows].astype(f32)).astype(low)
+
+
+def halved(keep, found):
+    count, wide = keep.shape
+    part = lambda rows: pl.BlockSpec((rows, TILE), lambda n: (0, n))
+    return pl.pallas_call(
+        halved_kernel,
+        out_shape=[jax.ShapeDtypeStruct((count // 4, wide), low)] * 4,
+        grid=(wide // TILE,),
+        in_specs=[part(count)] * 2,
+        out_specs=[part(count // 4)] * 4,
+        cost_estimate=NOMINAL,
+    )(keep, found)
+
+
+def resid_kernel(steps, keep, found, x_top, x_bottom, y_top, y_bottom, resid, gift, scale, grad_out, grad_low):
     upper = pl.program_id(0) < steps
     x_part = jnp.where(upper, x_top[...].astype(f32), x_bottom[...].astype(f32))
     y_part = jnp.where(upper, y_top[...].astype(f32), y_bottom[...].astype(f32))
-    grad = unit_back(own[...] + x_part + y_part, resid[...], scale[...])
-    grad = gift[...].astype(f32) + grad
+    grad = keep[...].astype(f32) + found[...].astype(f32) + x_part + y_part
+    grad = gift[...].astype(f32) + unit_back(grad, resid[...], scale[...])
     grad_out[...] = grad
     grad_low[...] = grad.astype(low)
 
 
-def resid_grads(own, x_top, x_bottom, y_top, y_bottom, resid, gift, scale):
-    count, wide = own.shape
+def resid_grads(keep, found, x_top, x_bottom, y_top, y_bottom, resid, gift, scale):
+    count, wide = resid.shape
     rows = 96
     steps = count // (2 * rows)
     row = pl.BlockSpec((rows, wide), lambda i: (i, 0))
+    own = pl.BlockSpec((rows, wide), lambda i: (i + 2 * steps, 0))
     first = pl.BlockSpec((rows, wide), lambda i: (jnp.minimum(i, steps - 1), 0))
     last = pl.BlockSpec((rows, wide), lambda i: (jnp.maximum(i - steps, 0), 0))
     return pl.pallas_call(
         functools.partial(resid_kernel, steps),
         out_shape=(jax.ShapeDtypeStruct((count, wide), f32), jax.ShapeDtypeStruct((count, wide), low)),
         grid=(2 * steps,),
-        in_specs=[row, first, last, first, last, row, row, pl.BlockSpec((rows, 1), lambda i: (i, 0))],
+        in_specs=[own, own, first, last, first, last, row, row, pl.BlockSpec((rows, 1), lambda i: (i, 0))],
         out_specs=(row, row),
         cost_estimate=NOMINAL,
-    )(own, x_top, x_bottom, y_top, y_bottom, resid, gift, scale)
+    )(keep, found, x_top, x_bottom, y_top, y_bottom, resid, gift, scale)
 
 
 def part_sums_kernel(keep, found, diag_top, diag_bottom, x_top, x_bottom, y_top, y_bottom, own):
@@ -787,9 +806,9 @@
     calls = 2 if parts % 2 == 0 else 1
     per = parts // calls
     part = share // parts
-    mine = pack(spans, part, share, gain_two, gate_weight, up_weight, down_weight.T)
+    mine = pack(spans, part, share, after(gain_two, qkv_shard), gate_weight, up_weight, down_weight.T)
     gift = cotangent[0]
-    mlp_column = lax.all_to_all(after(mine, qkv_shard), PLANE, split_axis=0, concat_axis=0, tiled=True)
+    mlp_column = lax.all_to_all(mine, PLANE, split_axis=0, concat_axis=0, tiled=True)
     mlp_column = mlp_column.reshape(-1, 3 * share)
 
     def gathered(k, *earlier):
@@ -826,7 +845,7 @@
         out_diag = jnp.concatenate([out_top, out_bottom], 0)
         (out_diag_c,), _ = stage([(out_diag, "c")])
         out_blocks = [out_column, out_x, out_c, out_x_c, out_y, out_diag, out_y_c, out_diag_c]
-        resid = apply_rows(mixed, out_blocks, inputs)
+        resid = apply_rows(mixed, out_blocks, True, inputs)
         scale_two, unit_two = unit_of(resid)
         (unit_x, unit_y, unit_c), _ = stage([(unit_two, "x"), (unit_two, "y"), (unit_two, "c")])
         (unit_x_c, unit_y_c), _ = stage([(unit_x, "c"), (unit_y, "c")])
@@ -888,16 +907,18 @@
         else:
             (one_d, one_x_c, one_y_c), _ = stage(one_sends)
         ones = one_x, one_c, one_x_c, one_y, one_d, one_y_c
-        return (unit_d, unit_d_c), grads_far, far_sums[:4], near_sums[:4], partial, ones
+        return (unit_d, unit_d_c), (gift_d, gift_d_c), far_sums[:4], near_sums[:4], partial, ones
 
     columns = []
     unit_two, unit_x, unit_c, unit_x_c, unit_y, unit_y_c = unit_blocks
-    halves_far, grads_far, far_before, near_before, partial, ones = boxed(
+    unit_far, gift_far, far_before, near_before, partial, ones = boxed(
         sure, opening, mlp_full[:per] if calls > 1 else (), unit_blocks, gift_x, gift_x_c, grads_near, unit_one
     )
     if calls > 1:
         columns.append(lax.psum_scatter(partial, "z", scatter_dimension=0, tiled=True))
-    unit_d, unit_d_c = halves_far
+    unit_d, unit_d_c = unit_far
+    gift_d, gift_d_c = gift_far
+    grads_far = [(gift_d,), (gift_x,), (gift_d_c,), (gift_x_c,)]
     units_far = [(unit_d,), (unit_x,), (unit_d_c,), (unit_x_c,)]
     units_near = [(unit_y,), (unit_two,), (unit_y_c,), (unit_c,)]
 
@@ -908,26 +929,27 @@
             weights,
         )
         (found,), _ = stage([(far_sums[3], "c")])
-        both = summed(far_sums[2], found).astype(low)
-        (diag_top, diag_bottom), (x_top, x_bottom) = halves(both[:count]), halves(both[count:])
+        diag_top, diag_bottom, x_top, x_bottom = halved(far_sums[2], found)
         (diag_x, diag_y, x_top, far_out), near_sums = stage(
             [(diag_top, "x"), (diag_bottom, "y"), (x_top, "x"), (far_sums[1], "c")],
             lambda *given: mlp([(value,) for value in given], grads_near, weights, near_before),
             [tile[0] for tile in units_near],
         )
         (found,), _ = stage([(near_sums[3], "c")])
-        y_bottom, x_bottom, y_top, own = turn(near_sums[2], found, x_bottom, diag_x, diag_y)
+        y_bottom, x_bottom, y_top = turn(near_sums[2], found, x_bottom, diag_x, diag_y)
         (y_bottom, x_bottom, y_top, near_out), partial = stage(
             [(y_bottom, "y"), (x_bottom, "x"), (y_top, "y"), (near_sums[1], "c")],
             lambda *given: mlp_grads(flat(units_far, units_near), flat(grads_far, grads_near), given, cuts),
             [far_sums[4], near_sums[4]],
         )
-        grad_resid, grad_attn = resid_grads(own, x_top, x_bottom, y_top, y_bottom, resid, gift, scale_two)
-        out_far = summed(far_sums[0], far_out).astype(low)
-        out_near = summed(near_sums[0], near_out).astype(low)
+        grad_resid, grad_attn = resid_grads(
+            near_sums[2], found, x_top, x_bottom, y_top, y_bottom, resid, gift, scale_two
+        )
+        out_far = halved(far_sums[0], after(far_out, partial[0]))
+        out_near = halved(near_sums[0], near_out)
         return partial, grad_resid, grad_attn, out_far, out_near, one_d_c
 
-    cuts = (2, 1)
+    cuts = (1, 1, 1)
     partial, grad_resid, grad_attn, out_far, out_near, one_d_c = boxed(
         sure,
         middle,
@@ -947,17 +969,8 @@
     one_x, one_c, one_x_c, one_y, one_d, one_y_c = ones
     flat_ones = [unit_one, one_x, one_c, one_x_c, one_y, one_d, one_y_c, one_d_c]
 
-    def first_sends(diag, to_x, to_y):
-        diag_top, diag_bottom = halves(diag)
-        return [(diag_top, "x"), (diag_bottom, "y"), (halves(to_x)[0], "x"), (halves(to_y)[1], "y")]
-
-    def second_sends(to_x, to_y, received):
-        x_bottom = total(halves(to_x)[1], received[1]).astype(low)
-        y_top = total(halves(to_y)[0], received[0]).astype(low)
-        return [(x_bottom, "x"), (y_top, "y")]
-
     def joined(own, first, second):
-        top, bottom = halves(own)
+        top, bottom = own if isinstance(own, tuple) else halves(own)
         return jnp.concatenate([total(top, first[2], second[1]), total(bottom, second[0], first[3])], 0)
 
     def backward(grad_attn, out_far, out_near, queries, pairs, mixed_wide, logs, out_blocks, positions):
@@ -966,15 +979,15 @@
             return attend_back(queries, grad_mixed, mixed_wide, logs, pairs, positions, size, base)
 
         first, (grad_queries, mine, theirs) = stage(
-            first_sends(out_far[:count], out_far[count:], out_near[:count]), attention, [grad_attn]
+            [(out_far[0], "x"), (out_far[1], "y"), (out_far[2], "x"), (out_near[1], "y")], attention, [grad_attn]
         )
         (found,), _ = stage([(theirs, "c")])
         mine = summed(mine, found)
-        second = second_sends(out_far[count:], out_near[:count], first)
+        second = total(out_far[3], first[1]).astype(low), total(out_near[0], first[0]).astype(low)
         found, second = stage(
             [(mine[chips - d].astype(low), behind(-d)) for d in range(chips, 0, -1)],
             lambda *given: given,
-            [value for value, _ in second],
+            second,
         )
         grad_pair = total(mine[chips], *found).astype(low)
         return jnp.concatenate([grad_queries, grad_pair], 1), first, second
@@ -1001,7 +1014,7 @@
         return qkv_column, out_keep, found, second
 
     qkv_column, out_keep, found, second = boxed(
-        sure, collect, after(grad_attn, columns[-2]), grad_qkv, second, mixed, flat_ones
+        sure, collect, after(grad_attn, columns[-3]), grad_qkv, second, mixed, flat_ones
     )
     qkv_low = lax.psum_scatter(qkv_column, "z", scatter_dimension=0, tiled=True)
 
@@ -1010,8 +1023,8 @@
 
         def results(grad_qkv, *second):
             inputs = tokens[0].astype(f32)
-            output = resid + joined(out_near[count:], first, second)
-            grad_unit_one = apply_rows(grad_qkv, qkv_blocks, jnp.zeros_like(inputs))
+            output = resid + joined((out_near[2], out_near[3]), first, second)
+            grad_unit_one = apply_rows(grad_qkv, qkv_blocks, True)
             return output, grad_resid + unit_back(grad_unit_one, inputs, scale_one)
 
         started, (output, grad_tokens) = stage(
@@ -1029,7 +1042,7 @@
         found,
         first,
         second,
-        after(grad_resid, columns[-1]),
+        after(grad_resid, columns[-2]),
         grad_qkv,
         out_near,
         qkv_blocks,

time: 1040 us -> 1020 us (0.981); the launches traced: 1020 us -> 1010 us
  other arithmetic: 66.1 us -> 47.9 us
  Pallas kernels: 407 us -> 424 us
  waiting for transfers between devices: 388 us -> 376 us
  starting transfers between devices: 90.1 us -> 102 us
    ppermute x6, waiting for transfers between devices: 85.9 us -> 61 us  [behind(): return lambda value: lax.ppermute(value, ('z', 'y'), pairs)]
    pallas_call x0 -> x3, Pallas kernels: none -> 20.2 us  [halved(): pl.pallas_call(halved_kernel, out_shape=[jax.ShapeDtypeStruct((count // 4...]
    convert_element_type x4 -> x1, other arithmetic: 19.8 us -> 3.58 us  [backward(): total(out_near[0], first[0]).astype(low)]
    reduce_scatter x1, waiting for transfers between devices: 0.02 us -> 16.2 us  [local(): qkv_low = lax.psum_scatter(qkv_column, 'z', scatter_dimension=0, tiled=True)]
    reduce_scatter x1, waiting for transfers between devices: 11 us -> 0.01 us  [local(): lax.psum_scatter(partial[0], 'z', scatter_dimension=0, tiled=True)]
  transfers between devices with their start and end apart: 92 -> 93, of which waited for: 40 -> 41; matrix products, arithmetic and copies ran while one was open for 10% -> 8% of each run, Pallas kernels for 39% -> 41%
where the time goes in v6:
time: 1020 us; the launch traced here: 1010 us
  Pallas kernels  424 us (42%)
  waiting for transfers between devices  376 us (37%)
  starting transfers between devices  102 us (10%)
  other arithmetic  47.9 us (5%)
  local copies, waits for them, and re-layouts  47.8 us (5%)
  between operations  15.4 us (2%)
    ppermute x66, waiting for transfers between devices, swap(): return lax.ppermute(value, axis, [(0, 1), (1, 0)])  197 us
    pallas_call x4, Pallas kernels, mlp(): pl.pallas_call(functools.partial(mlp_kernel, each // 3, per, tiles), out_...  155 us
    pallas_call x2, Pallas kernels, mlp_grads(): pl.pallas_call(functools.partial(mlp_grads_kernel, len(units)), out_shape...  75.8 us
    ppermute x6, waiting for transfers between devices, behind(): return lambda value: lax.ppermute(value, ('z', 'y'), pairs)  61 us
    ppermute x66, starting transfers between devices, swap(): return lax.ppermute(value, axis, [(0, 1), (1, 0)])  49.3 us
    pallas_call x4, Pallas kernels, apply_rows(): pl.pallas_call(kernel, out_shape=shape, grid_spec=pltpu.PrefetchScalarGri...  47.1 us
    all_to_all x1, waiting for transfers between devices, local(): lax.all_to_all(mine, PLANE, split_axis=0, concat_axis=0, tiled=True)  44.6 us
    pallas_call x1, Pallas kernels, attend_back(): pl.pallas_call(functools.partial(attend_back_kernel, size, size ** (-0.5)...  35.9 us
  transfers between devices with their start and end apart: 93, of which 41 were waited for; matrix products, arithmetic and copies ran while one was open for 8% of the time, Pallas kernels for 41%

profile of v6, /device:TPU:0, one launch (start us, length us, event | category | flops | bytes accessed | tf_op | source)
XLA Modules:
  0.0 1014.0 jit_solution(12882631368695742513)
XLA Ops:
  20.7 44.6 %all-to-all-done = bf16[8,80,3072]{2,1,0:T(8,128)(2,1)} async-done(((bf16[8,80,3072]{2,1,0:T(8,128)(2,1)}), bf16[8,80,3072]{2,1,0:T(8,128)(2,1)}, u32[]{:S(2)}, u32[]{:S(2)}) %all-to-all-start) | async-done | bytes 3932192 | tf_op jit(solution)/shard_map/all_to_all | solution.py:811
  71.6 150.8 %conditional.7 = (bf16[4,80,3072]{2,1,0:T(8,128)(2,1)}, bf16[4,80,3072]{2,1,0:T(8,128)(2,1)}, bf16[4,80,3072]{2,1,0:T(8,128)(2,1)}, bf16[4,80,3072]{2,1,0:T(8,12...) conditional(s32[]{:T(128)} %bitcast.16, () %tuple.127, ...), branch_computations={%region_0.0_spmd, %region_1.0_spmd} | conditional | flops 6947220 | bytes 127809664 | solution.py:60
  73.5 43.2 %collective-permute-done.24.rest_4_ = bf16[4,80,3072]{2,1,0:T(8,128)(2,1)} collective-permute-done((bf16[4,80,3072]{2,1,0:T(8,128)(2,1)}, bf16[4,80,3072]{2,1,0:T(8,128)(2,1)}, u32[]{:S(2)}, u32[]{:S(2)}) %collective-permute-start.24) | collective-permute-done | bytes 1966112 | tf_op jit(solution)/shard_map/cond/branch_1_fun/ppermute | solution.py:28
  122.9 17.9 %collective-permute-done.25 = bf16[2,80,3072]{2,1,0:T(8,128)(2,1)S(1)} collective-permute-done((bf16[2,80,3072]{2,1,0:T(8,128)(2,1)S(1)}, bf16[2,80,3072]{2,1,0:T(8,128)(2,1)S(1)}, u32[]{:S(2)}, u32[]{:S(2)}) %collective-permute-start.25) | collective-permute-done | bytes 983072 | tf_op jit(solution)/shard_map/cond/branch_1_fun/ppermute | solution.py:28
  177.2 13.0 %collective-permute-done.30 = bf16[384,512]{1,0:T(8,128)(2,1)} collective-permute-done((bf16[384,512]{1,0:T(8,128)(2,1)}, bf16[384,512]{1,0:T(8,128)(2,1)}, u32[]{:S(2)}, u32[]{:S(2)}) %collective-permute-start.30) | collective-permute-done | bytes 393248 | tf_op jit(solution)/shard_map/cond/branch_1_fun/ppermute | solution.py:80
  198.5 20.6 %collective-permute-done.32 = bf16[384,512]{1,0:T(8,128)(2,1)} collective-permute-done((bf16[384,512]{1,0:T(8,128)(2,1)}, bf16[384,512]{1,0:T(8,128)(2,1)}, u32[]{:S(2)}, u32[]{:S(2)}) %collective-permute-start.32) | collective-permute-done | bytes 393248 | tf_op jit(solution)/shard_map/cond/branch_1_fun/ppermute | solution.py:80
  223.7 140.8 %conditional.8 = (bf16[4,80,2560]{2,1,0:T(8,128)(2,1)}, bf16[4,80,2560]{2,1,0:T(8,128)(2,1)}, bf16[4,80,2560]{2,1,0:T(8,128)(2,1)}, bf16[4,80,2560]{2,1,0:T(8,12...) conditional(s32[]{:T(128)} %bitcast.16, () %tuple.125, ...), branch_computations={%region_3.0_spmd, %region_4.0_spmd} | conditional | flops 7012756 | bytes 129779640 | solution.py:60
  227.2 28.9 %branch_1_fun.22 = (bf16[384,2560]{1,0:T(8,128)(2,1)}, f32[384,2560]{1,0:T(8,128)}, f32[15,1,256]{2,1,0:T(1,128)S(1)}) custom-call(s32[1]{0:T(128)} %bitcast.2.core, s32[1,384]{1,0:T(1,128)S(1)} %get-tuple-element.288.places, bf16[384,2560]{1,0:T(8,128)(2,1)} %get-tuple-element.289.queries, bf16[384,512]{1,0:T(8,128)(2,1)} %get-tuple-element.290.rest_0_, ...), custom_call_target="tpu_custom_call" | custom-call | flops 1048576 | bytes 4096 | tf_op jit(solution)/shard_map/cond/branch_1_fun/pallas_call | solution.py:195
  269.8 16.8 %collective-permute-done.45 = bf16[2,80,2560]{2,1,0:T(8,128)(2,1)S(1)} collective-permute-done((bf16[2,80,2560]{2,1,0:T(8,128)(2,1)S(1)}, bf16[2,80,2560]{2,1,0:T(8,128)(2,1)S(1)}, u32[]{:S(2)}, u32[]{:S(2)}) %collective-permute-start.45) | collective-permute-done | bytes 819232 | tf_op jit(solution)/shard_map/cond/branch_1_fun/ppermute | solution.py:28
  293.9 12.1 %branch_1_fun.23 = f32[384,2560]{1,0:T(8,128)} custom-call(s32[8]{0:T(128)S(1)} %iota_xor_fusion.1.slots, bf16[384,2560]{1,0:T(8,128)(2,1)} %get-tuple-element.1037.left, f32[384,2560]{1,0:T(8,128)S(1)} %bitcast_convert_fusion.rest_0_, bf16[4,80,2560]{2,1,0:T(8,128)(2,1)S(1)} %copy-done.13, bf16[4,80,2560]{2,1,0:T(8,128)(2,1)} %collective-permute-done.40.rest_2_, ...), custom_call_target="tpu_custom_call" | custom-call | flops 1048576 | bytes 4096 | tf_op jit(solution)/shard_map/cond/branch_1_fun/pallas_call | solution.py:314
  314.1 43.2 %collective-permute-done.50 = bf16[384,2560]{1,0:T(8,128)(2,1)} collective-permute-done((bf16[384,2560]{1,0:T(8,128)(2,1)}, bf16[384,2560]{1,0:T(8,128)(2,1)}, u32[]{:S(2)}, u32[]{:S(2)}) %collective-permute-start.50) | collective-permute-done | bytes 1966112 | tf_op jit(solution)/shard_map/cond/branch_1_fun/ppermute | solution.py:28
  364.4 136.8 %conditional.9 = (bf16[384,2560]{1,0:T(8,128)(2,1)}, bf16[384,2560]{1,0:T(8,128)(2,1)}, bf16[384,2560]{1,0:T(8,128)(2,1)}, bf16[384,2560]{1,0:T(8,128)(2,1)}, bf...) conditional(s32[]{:T(128)} %bitcast.16, () %tuple.124, ...), branch_computations={%region_6.0_spmd, %region_7.0_spmd} | conditional | flops 3145728 | bytes 78656040 | solution.py:60
  368.2 36.9 %branch_1_fun.24 = (bf16[768,2560]{1,0:T(8,128)(2,1)}, bf16[768,2560]{1,0:T(8,128)(2,1)}, bf16[768,2560]{1,0:T(8,128)(2,1)}, bf16[768,2560]{1,0:T(8,128)(2,1)}, bf16[1536,1536]{1,0:T(8,128)(2,1)}) custom-call(bf16[2560,768]{1,0:T(8,128)(2,1)} %get-tuple-element.360.rest_0_, bf16[2560,768]{1,0:T(8,128)(2,1)} %get-tuple-element.361.rest_1_, ...), custom_call_target="tpu_custom_call" | custom-call | flops 1048576 | bytes 4096 | tf_op jit(solution)/shard_map/cond/branch_1_fun/pallas_call | solution.py:462
  418.5 37.3 %branch_1_fun.25 = (bf16[768,2560]{1,0:T(8,128)(2,1)}, bf16[768,2560]{1,0:T(8,128)(2,1)}, bf16[768,2560]{1,0:T(8,128)(2,1)}, bf16[768,2560]{1,0:T(8,128)(2,1)}, bf16[1536,1536]{1,0:T(8,128)(2,1)}) custom-call(bf16[2560,768]{1,0:T(8,128)(2,1)} %get-tuple-element.360.rest_0_, bf16[2560,768]{1,0:T(8,128)(2,1)} %get-tuple-element.361.rest_1_, ...), custom_call_target="tpu_custom_call" | custom-call | flops 1048576 | bytes 4096 | tf_op jit(solution)/shard_map/cond/branch_1_fun/pallas_call | solution.py:462
  459.2 37.8 %branch_1_fun.26 = bf16[2560,1536]{1,0:T(8,128)(2,1)} custom-call(bf16[384,2560]{1,0:T(8,128)(2,1)} %collective-permute-done.rest_2_.rest_0_, bf16[384,2560]{1,0:T(8,128)(2,1)} %get-tuple-element.362.rest_4_.rest_1_, bf16[384,2560]{1,0:T(8,128)(2,1)} %collective-permute-done.2.rest_6_.rest_2_, bf16[384,2560]{1,0:T(8,128)(2,1)} %get-tuple-element.363.rest_8_.rest_3_, ...), custom_call_target="tpu_custom_call" | custom-call | flops 1048576 | bytes 4096 | tf_op jit(solution)/shard_map/cond/branch_1_fun/pallas_call | solution.py:525
  501.4 181.1 %conditional.10 = (bf16[2560,512]{1,0:T(8,128)(2,1)}, bf16[2560,512]{1,0:T(8,128)(2,1)}, bf16[2560,512]{1,0:T(8,128)(2,1)}, f32[384,2560]{1,0:T(8,128)}, bf16[38...) conditional(s32[]{:T(128)} %bitcast.16, () %tuple.123, ...), branch_computations={%region_8.0_spmd, %region_9.0_spmd} | conditional | flops 8388608 | bytes 94408232 | solution.py:60
  501.5 40.5 %branch_1_fun.27 = (bf16[768,2560]{1,0:T(8,128)(2,1)}, bf16[768,2560]{1,0:T(8,128)(2,1)}, bf16[768,2560]{1,0:T(8,128)(2,1)}, bf16[768,2560]{1,0:T(8,128)(2,1)}, bf16[1536,1536]{1,0:T(8,128)(2,1)}) custom-call(bf16[2560,768]{1,0:T(8,128)(2,1)} %get-tuple-element.396.rest_0_, bf16[2560,768]{1,0:T(8,128)(2,1)} %get-tuple-element.397.rest_1_, ...), custom_call_target="tpu_custom_call" | custom-call | flops 1048576 | bytes 4096 | tf_op jit(solution)/shard_map/cond/branch_1_fun/pallas_call | solution.py:462
  560.2 40.7 %branch_1_fun.29 = (bf16[768,2560]{1,0:T(8,128)(2,1)}, bf16[768,2560]{1,0:T(8,128)(2,1)}, bf16[768,2560]{1,0:T(8,128)(2,1)}, bf16[768,2560]{1,0:T(8,128)(2,1)}, bf16[1536,1536]{1,0:T(8,128)(2,1)}) custom-call(bf16[2560,768]{1,0:T(8,128)(2,1)} %get-tuple-element.396.rest_0_, bf16[2560,768]{1,0:T(8,128)(2,1)} %get-tuple-element.397.rest_1_, ...), custom_call_target="tpu_custom_call" | custom-call | flops 1048576 | bytes 4096 | tf_op jit(solution)/shard_map/cond/branch_1_fun/pallas_call | solution.py:462
  619.2 38.0 %branch_1_fun.31 = (bf16[2560,512]{1,0:T(8,128)(2,1)}, bf16[2560,512]{1,0:T(8,128)(2,1)}, bf16[2560,512]{1,0:T(8,128)(2,1)}) custom-call(bf16[384,2560]{1,0:T(8,128)(2,1)} %get-tuple-element.398.rest_2_.rest_0_, bf16[384,2560]{1,0:T(8,128)(2,1)} %get-tuple-element.400.rest_4_.rest_1_, bf16[384,2560]{1,0:T(8,128)(2,1)} %get-tuple-element.402.rest_6_.rest_2_, ...), custom_call_target="tpu_custom_call" | custom-call | flops 1048576 | bytes 4096 | tf_op jit(solution)/shard_map/cond/branch_1_fun/pallas_call | solution.py:525
  682.6 85.7 %conditional.11 = (bf16[384,3072]{1,0:T(8,128)(2,1)S(1)}, bf16[192,2560]{1,0:T(8,128)(2,1)S(1)}, bf16[192,2560]{1,0:T(8,128)(2,1)}, bf16[192,2560]{1,0:T(8,128)(2,1)}, bf16[192,2560]{1,0:T(8,128)(2,1)}) conditional(s32[]{:T(128)} %bitcast.16, () %tuple.122, (bf16[192,2560]{1,0:T(8,128)(2,1)}, bf16[192,2560]{1,0:T(8,128)(2,1)}, ...), branch_computations={%region_11.0_spmd, %region_12.0_spmd} | conditional | flops 14483476 | bytes 87696024 | solution.py:60
  698.9 35.9 %branch_1_fun.36 = (bf16[384,2560]{1,0:T(8,128)(2,1)}, f32[4,384,512]{2,1,0:T(8,128)}, bf16[4,384,512]{2,1,0:T(8,128)(2,1)}) custom-call(s32[1]{0:T(128)} %bitcast.5.core, s32[1,384]{1,0:T(1,128)S(1)} %get-tuple-element.500.places, bf16[384,2560]{1,0:T(8,128)(2,1)} %get-tuple-element.501.queries, bf16[384,2560]{1,0:T(8,128)(2,1)} %copy-done.1, ...), custom_call_target="tpu_custom_call" | custom-call | flops 1048576 | bytes 4096 | tf_op jit(solution)/shard_map/cond/branch_1_fun/pallas_call | solution.py:228
  743.4 21.0 %collective-permute-done.76 = bf16[384,512]{1,0:T(8,128)(2,1)S(1)} collective-permute-done((bf16[384,512]{1,0:T(8,128)(2,1)S(1)}, bf16[384,512]{1,0:T(8,128)(2,1)S(1)}, u32[]{:S(2)}, u32[]{:S(2)}) %collective-permute-start.76) | collective-permute-done | bytes 393248 | tf_op jit(solution)/shard_map/cond/branch_1_fun/ppermute | solution.py:80
  769.3 72.3 %conditional.12 = (bf16[2560,384]{1,0:T(8,128)(2,1)}, bf16[4,4,80,2560]{3,2,1,0:T(8,128)(2,1)}, bf16[4,4,80,2560]{3,2,1,0:T(8,128)(2,1)}, bf16[192,2560]{1,0:T(8,128)(2,1)}, bf16[192,2560]{1,0:T(8,128)(2,1)}) conditional(s32[]{:T(128)} %bitcast.16, () %tuple.121, (bf16[384,3072]{1,0:T(8,128)(2,1)S(1)}, bf16[384,2560]{1,0:T(8,128)(2,1)}, ...), branch_computations={%region_14.0_spmd, %region_15.0_spmd} | conditional | flops 3146804 | bytes 57689048 | solution.py:60
  774.4 15.6 %collective-permute-start.58 = (bf16[384,384]{1,0:T(8,128)(2,1)}, bf16[384,384]{1,0:T(8,128)(2,1)S(1)}, u32[]{:S(2)}, u32[]{:S(2)}) collective-permute-start(bf16[384,384]{1,0:T(8,128)(2,1)} %get-tuple-element.556), channel_id=1, source_target_pairs={{0,4},{1,5},{2,6},{3,7},{4,0},{5,1},{6,2},{7,3},{8,12},{9,13},{10,... | collective-permute-start | bytes 884744 | tf_op jit(solution)/shard_map/cond/branch_1_fun/ppermute | solution.py:74
  797.4 13.3 %branch_1_fun.38 = (bf16[4,4,80,2560]{3,2,1,0:T(8,128)(2,1)}, bf16[4,4,80,2560]{3,2,1,0:T(8,128)(2,1)}) custom-call(s32[8]{0:T(128)S(1)} %gather_fusion, bf16[384,2560]{1,0:T(8,128)(2,1)} %get-tuple-element.561.left, bf16[384,2560]{1,0:T(8,128)(2,1)} %get-tuple-element.562.right), custom_call_target="tpu_custom_call" | custom-call | flops 1048576 | bytes 4096 | tf_op jit(solution)/shard_map/cond/branch_1_fun/pallas_call | solution.py:363
  824.3 14.1 %branch_1_fun.39 = bf16[2560,384]{1,0:T(8,128)(2,1)} custom-call(bf16[384,2560]{1,0:T(8,128)(2,1)} %get-tuple-element.579.rest_0_, bf16[384,2560]{1,0:T(8,128)(2,1)} %get-tuple-element.580.rest_1_, bf16[384,2560]{1,0:T(8,128)(2,1)} %get-tuple-element.581.rest_2_, bf16[384,2560]{1,0:T(8,128)(2,1)} %get-tuple-element.582.rest_3_, ...), custom_call_target="tpu_custom_call" | custom-call | flops 1048576 | bytes 4096 | tf_op jit(solution)/shard_map/cond/branch_1_fun/pallas_call | solution.py:560
  845.9 72.5 %conditional.13 = (bf16[320,2560]{1,0:T(8,128)(2,1)}, f32[1,384,2560]{2,1,0:T(8,128)}, f32[1,384,2560]{2,1,0:T(8,128)}) conditional(s32[]{:T(128)} %bitcast.16, () %tuple.120, (bf16[4,4,80,2560]{3,2,1,0:T(8,128)(2,1)}, bf16[4,4,80,2560]{3,2,1,0:T(8,128)(2,1)}, bf16[384,3072]{1,0:T(8,128)(2,1)S(1)}, bf16[192,2560]{1,0:T(8,128)(2,1)}, ...), branch_computations={%region_17.0_spmd, %region_18.20_spmd} | conditional | flops 27820052 | bytes 119231048 | solution.py:60
  859.4 12.1 %branch_1_fun.41 = f32[384,2560]{1,0:T(8,128)S(1)} custom-call(s32[8]{0:T(128)S(1)} %iota_xor_fusion.4.slots, bf16[384,3072]{1,0:T(8,128)(2,1)} %copy-done.11, bf16[4,80,3072]{2,1,0:T(8,128)(2,1)} %get-tuple-element.624.rest_0_, bf16[4,80,3072]{2,1,0:T(8,128)(2,1)} %get-tuple-element.625.rest_1_, bf16[4,80,3072]{2,1,0:T(8,128)(2,1)} %get-tuple-element.626.rest_2_, ...), custom_call_target="tpu_custom_call" | custom-call | flops 1048576 | bytes 4096 | tf_op jit(solution)/shard_map/cond/branch_1_fun/pallas_call | solution.py:314
  898.9 15.1 %collective-permute-done.69 = bf16[2,80,2560]{2,1,0:T(8,128)(2,1)S(1)} collective-permute-done((bf16[2,80,2560]{2,1,0:T(8,128)(2,1)S(1)}, bf16[2,80,2560]{2,1,0:T(8,128)(2,1)S(1)}, u32[]{:S(2)}, u32[]{:S(2)}) %collective-permute-start.69) | collective-permute-done | bytes 819232 | tf_op jit(solution)/shard_map/cond/branch_1_fun/ppermute | solution.py:28
  922.5 16.2 %reduce-scatter.15.cloned.1.call-done = bf16[640,384]{1,0:T(8,128)(2,1)} async-done(((bf16[2560,384]{1,0:T(8,128)(2,1)}), bf16[640,384]{1,0:T(8,128)(2,1)}) %reduce-scatter.15.cloned.1.call-update) | async-done | bytes 491536 | tf_op jit(solution)/shard_map/reduce_scatter | solution.py:1019
  945.4 31.5 %reduce-scatter.17.cloned.1.call-done = bf16[80,2560]{1,0:T(8,128)(2,1)} async-done(((bf16[320,2560]{1,0:T(8,128)(2,1)}), bf16[80,2560]{1,0:T(8,128)(2,1)}) %reduce-scatter.17.cloned.1.call-update) | async-done | bytes 409616 | tf_op jit(solution)/shard_map/reduce_scatter | solution.py:1053
  978.9 17.5 %all-to-all-done.1.whole = bf16[8,80,3456]{2,1,0:T(8,128)(2,1)} async-done(((bf16[8,80,3456]{2,1,0:T(8,128)(2,1)}), bf16[8,80,3456]{2,1,0:T(8,128)(2,1)}, u32[]{:S(2)}, u32[]{:S(2)}) %all-to-all-start.1) | async-done | bytes 4423712 | tf_op jit(solution)/shard_map/all_to_all | solution.py:1056
  (340 shorter events, 333.1 us)
Async XLA Ops:
  14.3 51.0 %all-to-all-start = ((bf16[8,80,3072]{2,1,0:T(8,128)(2,1)}), bf16[8,80,3072]{2,1,0:T(8,128)(2,1)}, u32[]{:S(2)}, u32[]{:S(2)}) async-start(bf16[8,80,3072]{2,1,0:T(8,128)(2,1)} %shard_map.213), calls=%async_computation | async-start | bytes 7864320 | tf_op jit(solution)/shard_map/all_to_all | solution.py:811
  19.6 51.9 %all-gather.8.cloned.1.call-start = ((), (), s32[]{:S(2)}) async-start(), calls=%async_computation.8 | async-start | bytes 2457600 | tf_op jit(solution)/shard_map/all_gather | solution.py:801
  20.7 202.9 %all-gather.10.cloned.1.call-start = ((), (), s32[]{:S(2)}) async-start(), calls=%async_computation.9 | async-start | bytes 4915200 | tf_op jit(solution)/shard_map/all_gather | solution.py:816
  69.6 154.1 %all-gather.18.cloned.1.call-start = ((), (), s32[]{:S(2)}) async-start(), calls=%async_computation.19 | async-start | bytes 2048000 | tf_op jit(solution)/shard_map/all_gather | solution.py:802
  70.3 294.1 %all-gather.12.cloned.1.call-start = ((), (), s32[]{:S(2)}) async-start(), calls=%async_computation.10 | async-start | bytes 4915200 | tf_op jit(solution)/shard_map/all_gather | solution.py:816
  71.6 45.0 %collective-permute-start.24 = (bf16[4,80,3072]{2,1,0:T(8,128)(2,1)}, bf16[4,80,3072]{2,1,0:T(8,128)(2,1)}, u32[]{:S(2)}, u32[]{:S(2)}) collective-permute-start(bf16[4,80,3072]{2,1,0:T(8,128)(2,1)} %get-tuple-element.248.rest_0_), channel_id=1, source_target_pairs={{0,4},{4,0},{1,5},{5,1},{2,6},{6,2},{3,7},{7,3},{8,12},{12,8},{9,1... | collective-permute-start | bytes 5898248 | tf_op jit(solution)/shard_map/cond/branch_1_fun/ppermute | solution.py:28
  72.3 46.9 %collective-permute-start.21 = (bf16[4,80,3072]{2,1,0:T(8,128)(2,1)}, bf16[4,80,3072]{2,1,0:T(8,128)(2,1)}, u32[]{:S(2)}, u32[]{:S(2)}) collective-permute-start(bf16[4,80,3072]{2,1,0:T(8,128)(2,1)} %get-tuple-element.248.rest_0_), channel_id=1, source_target_pairs={{0,1},{1,0},{2,3},{3,2},{4,5},{5,4},{6,7},{7,6},{8,9},{9,8},{10,11... | collective-permute-start | bytes 5898248 | tf_op jit(solution)/shard_map/cond/branch_1_fun/ppermute | solution.py:28
  165.3 53.8 %collective-permute-start.34 = (bf16[384,2560]{1,0:T(8,128)(2,1)S(1)}, bf16[384,2560]{1,0:T(8,128)(2,1)}, u32[]{:S(2)}, u32[]{:S(2)}) collective-permute-start(bf16[384,2560]{1,0:T(8,128)(2,1)S(1)} %get-tuple-element.257), channel_id=1, source_target_pairs={{0,1},{1,0},{2,3},{3,2},{4,5},{5,4},{6,7},{7,6},{8,9},{9,8},{10,11... | collective-permute-start | bytes 5898248 | tf_op jit(solution)/shard_map/cond/branch_1_fun/ppermute | solution.py:28
  166.6 52.5 %collective-permute-start.35 = (bf16[384,2560]{1,0:T(8,128)(2,1)S(1)}, bf16[384,2560]{1,0:T(8,128)(2,1)}, u32[]{:S(2)}, u32[]{:S(2)}) collective-permute-start(bf16[384,2560]{1,0:T(8,128)(2,1)S(1)} %get-tuple-element.257), channel_id=1, source_target_pairs={{0,4},{4,0},{1,5},{5,1},{2,6},{6,2},{3,7},{7,3},{8,12},{12,8},{9,1... | collective-permute-start | bytes 5898248 | tf_op jit(solution)/shard_map/cond/branch_1_fun/ppermute | solution.py:28
  168.1 51.0 %collective-permute-start.36 = (bf16[384,2560]{1,0:T(8,128)(2,1)S(1)}, bf16[384,2560]{1,0:T(8,128)(2,1)}, u32[]{:S(2)}, u32[]{:S(2)}) collective-permute-start(bf16[384,2560]{1,0:T(8,128)(2,1)S(1)} %get-tuple-element.257), channel_id=1, source_target_pairs={{0,2},{2,0},{1,3},{3,1},{4,6},{6,4},{5,7},{7,5},{8,10},{10,8},{9,1... | collective-permute-start | bytes 5898248 | tf_op jit(solution)/shard_map/cond/branch_1_fun/ppermute | solution.py:28
  222.4 279.0 %all-gather.14.cloned.1.call-start = ((), (), s32[]{:S(2)}) async-start(), calls=%async_computation.11 | async-start | bytes 4915200 | tf_op jit(solution)/shard_map/all_gather | solution.py:816
  223.0 278.4 %all-gather.16.cloned.1.call-start = ((), (), s32[]{:S(2)}) async-start(), calls=%async_computation.12 | async-start | bytes 4915200 | tf_op jit(solution)/shard_map/all_gather | solution.py:816
  223.6 459.0 %reduce-scatter.7.cloned.1.call-start = ((), (), s32[]{:S(2)}) async-start(), calls=%async_computation.13 | async-start | bytes 9830400 | tf_op jit(solution)/shard_map/reduce_scatter | solution.py:918
  312.1 45.2 %collective-permute-start.50 = (bf16[384,2560]{1,0:T(8,128)(2,1)}, bf16[384,2560]{1,0:T(8,128)(2,1)}, u32[]{:S(2)}, u32[]{:S(2)}) collective-permute-start(bf16[384,2560]{1,0:T(8,128)(2,1)} %multiply_convert_fusion), channel_id=1, source_target_pairs={{0,1},{1,0},{2,3},{3,2},{4,5},{5,4},{6,7},{7,6},{8,9},{9,8},{10,11... | collective-permute-start | bytes 5898248 | tf_op jit(solution)/shard_map/cond/branch_1_fun/ppermute | solution.py:28
  312.4 44.9 %collective-permute-start.51 = (bf16[384,2560]{1,0:T(8,128)(2,1)}, bf16[384,2560]{1,0:T(8,128)(2,1)}, u32[]{:S(2)}, u32[]{:S(2)}) collective-permute-start(bf16[384,2560]{1,0:T(8,128)(2,1)} %multiply_convert_fusion), channel_id=1, source_target_pairs={{0,4},{4,0},{1,5},{5,1},{2,6},{6,2},{3,7},{7,3},{8,12},{12,8},{9,1... | collective-permute-start | bytes 5898248 | tf_op jit(solution)/shard_map/cond/branch_1_fun/ppermute | solution.py:28
  364.6 45.2 %collective-permute-start = (bf16[384,2560]{1,0:T(8,128)(2,1)}, bf16[384,2560]{1,0:T(8,128)(2,1)}, u32[]{:S(2)}, u32[]{:S(2)}) collective-permute-start(bf16[384,2560]{1,0:T(8,128)(2,1)} %get-tuple-element.337.rest_2_.rest_4_), channel_id=1, source_target_pairs={{0,1},{1,0},{2,3},{3,2},{4,5},{5,4},{6,7},{7,6},{8,9},{9,8},{10,11... | collective-permute-start | bytes 5898248 | tf_op jit(solution)/shard_map/cond/branch_1_fun/ppermute | solution.py:28
  366.4 44.9 %collective-permute-start.1 = (bf16[384,2560]{1,0:T(8,128)(2,1)}, bf16[384,2560]{1,0:T(8,128)(2,1)}, u32[]{:S(2)}, u32[]{:S(2)}) collective-permute-start(bf16[384,2560]{1,0:T(8,128)(2,1)} %get-tuple-element.334.rest_5_.rest_9_), channel_id=1, source_target_pairs={{0,4},{4,0},{1,5},{5,1},{2,6},{6,2},{3,7},{7,3},{8,12},{12,8},{9,1... | collective-permute-start | bytes 5898248 | tf_op jit(solution)/shard_map/cond/branch_1_fun/ppermute | solution.py:28
  411.9 45.0 %collective-permute-start.4 = (bf16[384,2560]{1,0:T(8,128)(2,1)}, bf16[384,2560]{1,0:T(8,128)(2,1)}, u32[]{:S(2)}, u32[]{:S(2)}) collective-permute-start(bf16[384,2560]{1,0:T(8,128)(2,1)} %get-tuple-element.359), channel_id=1, source_target_pairs={{0,1},{1,0},{2,3},{3,2},{4,5},{5,4},{6,7},{7,6},{8,9},{9,8},{10,11... | collective-permute-start | bytes 5898248 | tf_op jit(solution)/shard_map/cond/branch_1_fun/ppermute | solution.py:28
  412.2 44.8 %collective-permute-start.5 = (bf16[384,2560]{1,0:T(8,128)(2,1)}, bf16[384,2560]{1,0:T(8,128)(2,1)}, u32[]{:S(2)}, u32[]{:S(2)}) collective-permute-start(bf16[384,2560]{1,0:T(8,128)(2,1)} %get-tuple-element.359), channel_id=1, source_target_pairs={{0,4},{4,0},{1,5},{5,1},{2,6},{6,2},{3,7},{7,3},{8,12},{12,8},{9,1... | collective-permute-start | bytes 5898248 | tf_op jit(solution)/shard_map/cond/branch_1_fun/ppermute | solution.py:28
  501.3 268.0 %reduce-scatter.9.cloned.1.call-start = ((), (), s32[]{:S(2)}) async-start(), calls=%async_computation.14 | async-start | bytes 3276800 | tf_op jit(solution)/shard_map/reduce_scatter | solution.py:968
  556.1 45.6 %collective-permute-start.15 = (bf16[768,2560]{1,0:T(8,128)(2,1)}, bf16[768,2560]{1,0:T(8,128)(2,1)}, u32[]{:S(2)}, u32[]{:S(2)}) collective-permute-start(bf16[768,2560]{1,0:T(8,128)(2,1)} %get-tuple-element.428), channel_id=1, source_target_pairs={{0,2},{2,0},{1,3},{3,1},{4,6},{6,4},{5,7},{7,5},{8,10},{10,8},{9,1... | collective-permute-start | bytes 11796488 | tf_op jit(solution)/shard_map/cond/branch_1_fun/ppermute | solution.py:28
  556.5 44.4 %collective-permute-start.12 = (bf16[192,2560]{1,0:T(8,128)(2,1)}, bf16[192,2560]{1,0:T(8,128)(2,1)}, u32[]{:S(2)}, u32[]{:S(2)}) collective-permute-start(bf16[192,2560]{1,0:T(8,128)(2,1)} %get-tuple-element.425), channel_id=1, source_target_pairs={{0,1},{1,0},{2,3},{3,2},{4,5},{5,4},{6,7},{7,6},{8,9},{9,8},{10,11... | collective-permute-start | bytes 2949128 | tf_op jit(solution)/shard_map/cond/branch_1_fun/ppermute | solution.py:28
  614.8 45.6 %collective-permute-start.20 = (bf16[768,2560]{1,0:T(8,128)(2,1)}, bf16[768,2560]{1,0:T(8,128)(2,1)}, u32[]{:S(2)}, u32[]{:S(2)}) collective-permute-start(bf16[768,2560]{1,0:T(8,128)(2,1)} %get-tuple-element.460), channel_id=1, source_target_pairs={{0,2},{2,0},{1,3},{3,1},{4,6},{6,4},{5,7},{7,5},{8,10},{10,8},{9,1... | collective-permute-start | bytes 11796488 | tf_op jit(solution)/shard_map/cond/branch_1_fun/ppermute | solution.py:28
  682.6 163.3 %reduce-scatter.11.cloned.1.call-start = ((), (), s32[]{:S(2)}) async-start(), calls=%async_computation.15 | async-start | bytes 3276800 | tf_op jit(solution)/shard_map/reduce_scatter | solution.py:999
  682.6 52.2 %collective-permute-start.71 = (bf16[192,2560]{1,0:T(8,128)(2,1)}, bf16[192,2560]{1,0:T(8,128)(2,1)S(1)}, u32[]{:S(2)}, u32[]{:S(2)}) collective-permute-start(bf16[192,2560]{1,0:T(8,128)(2,1)} %get-tuple-element.496), channel_id=1, source_target_pairs={{0,1},{1,0},{2,3},{3,2},{4,5},{5,4},{6,7},{7,6},{8,9},{9,8},{10,11... | collective-permute-start | bytes 2949128 | tf_op jit(solution)/shard_map/cond/branch_1_fun/ppermute | solution.py:28
  684.1 50.7 %collective-permute-start.72 = (bf16[192,2560]{1,0:T(8,128)(2,1)}, bf16[192,2560]{1,0:T(8,128)(2,1)S(1)}, u32[]{:S(2)}, u32[]{:S(2)}) collective-permute-start(bf16[192,2560]{1,0:T(8,128)(2,1)} %get-tuple-element.497), channel_id=1, source_target_pairs={{0,4},{4,0},{1,5},{5,1},{2,6},{6,2},{3,7},{7,3},{8,12},{12,8},{9,1... | collective-permute-start | bytes 2949128 | tf_op jit(solution)/shard_map/cond/branch_1_fun/ppermute | solution.py:28
  685.8 49.0 %collective-permute-start.73 = (bf16[192,2560]{1,0:T(8,128)(2,1)}, bf16[192,2560]{1,0:T(8,128)(2,1)S(1)}, u32[]{:S(2)}, u32[]{:S(2)}) collective-permute-start(bf16[192,2560]{1,0:T(8,128)(2,1)} %get-tuple-element.498), channel_id=1, source_target_pairs={{0,1},{1,0},{2,3},{3,2},{4,5},{5,4},{6,7},{7,6},{8,9},{9,8},{10,11... | collective-permute-start | bytes 2949128 | tf_op jit(solution)/shard_map/cond/branch_1_fun/ppermute | solution.py:28
  686.5 48.4 %collective-permute-start.74 = (bf16[192,2560]{1,0:T(8,128)(2,1)}, bf16[192,2560]{1,0:T(8,128)(2,1)}, u32[]{:S(2)}, u32[]{:S(2)}) collective-permute-start(bf16[192,2560]{1,0:T(8,128)(2,1)} %get-tuple-element.499), channel_id=1, source_target_pairs={{0,4},{4,0},{1,5},{5,1},{2,6},{6,2},{3,7},{7,3},{8,12},{12,8},{9,1... | collective-permute-start | bytes 2949128 | tf_op jit(solution)/shard_map/cond/branch_1_fun/ppermute | solution.py:28
  768.3 152.1 %reduce-scatter.13.cloned.1.call-start = ((), (), s32[]{:S(2)}) async-start(), calls=%async_computation.16 | async-start | bytes 3276800 | tf_op jit(solution)/shard_map/reduce_scatter | solution.py:999
  769.3 169.3 %reduce-scatter.15.cloned.1.call-start = ((), (), s32[]{:S(2)}) async-start(), calls=%async_computation.17 | async-start | bytes 2457600 | tf_op jit(solution)/shard_map/reduce_scatter | solution.py:1019
  841.7 135.3 %reduce-scatter.17.cloned.1.call-start = ((), (), s32[]{:S(2)}) async-start(), calls=%async_computation.18 | async-start | bytes 2048000 | tf_op jit(solution)/shard_map/reduce_scatter | solution.py:1053
  940.6 55.8 %all-to-all-start.1 = ((bf16[8,80,3456]{2,1,0:T(8,128)(2,1)}), bf16[8,80,3456]{2,1,0:T(8,128)(2,1)}, u32[]{:S(2)}, u32[]{:S(2)}) async-start(bf16[8,80,3456]{2,1,0:T(8,128)(2,1)} %bitcast.26), calls=%async_computation.6 | async-start | bytes 8847360 | tf_op jit(solution)/shard_map/all_to_all | solution.py:1056
  (98 other events, 1833.6 us)
Sparse Core Ops, SparseCore 0:
  22.6 45.9 all-gather.7
  70.8 76.1 all-gather.9
  148.5 41.6 all-gather.17
  222.5 86.8 all-gather.11
  310.8 75.0 all-gather.13
  387.3 74.9 all-gather.15
  501.4 147.3 reduce-scatter.6
  682.7 64.2 reduce-scatter.8
  768.5 72.6 reduce-scatter.10
  843.3 51.7 reduce-scatter.12
  897.5 41.1 reduce-scatter.14
  941.4 35.5 reduce-scatter.16

commit v7 on v6

--- a/solution.py
+++ b/solution.py
@@ -482,7 +482,7 @@
     *outs, turned = rest
     step = pl.program_id(0)
     part = hidden[0].shape[1] // 3
-    piece = min(part, 256)
+    piece = min(part, 256, *(out.shape[1] for out in outs))
     places = [(out, at) for out in outs for at in range(0, out.shape[1], piece)]
 
     def turn(slot, which, sources, share, shares):
@@ -516,7 +516,7 @@
             turn(step % 2, 1, grads, i, len(work))
 
 
-def mlp_grads(units, grads, hidden, pieces=(3,)):
+def mlp_grads(units, grads, hidden, pieces=(6,)):
     wide = units[0].shape[1]
     deep = hidden[0].shape[1]
     count = sum(piece.shape[0] for piece in units)
@@ -524,14 +524,14 @@
     last = wide // rows - 1
     return pl.pallas_call(
         functools.partial(mlp_grads_kernel, len(units)),
-        out_shape=[jax.ShapeDtypeStruct((wide, deep // 3 * piece), low) for piece in pieces],
+        out_shape=[jax.ShapeDtypeStruct((wide, deep // 6 * piece), low) for piece in pieces],
         grid=(last + 2,),
         in_specs=[
             pl.BlockSpec((piece.shape[0], rows), lambda s: (0, jnp.minimum(s, last))) for piece in units + grads
         ]
         + [pl.BlockSpec(piece.shape, lambda s: (0, 0), pipeline_mode=pl.Buffered(1)) for piece in hidden],
         out_specs=[
-            pl.BlockSpec((rows, deep // 3 * piece), lambda s: (jnp.maximum(s - 1, 0), 0)) for piece in pieces
+            pl.BlockSpec((rows, deep // 6 * piece), lambda s: (jnp.maximum(s - 1, 0), 0)) for piece in pieces
         ],
         scratch_shapes=[pltpu.VMEM((2, 2, rows, count), low)],
         compiler_params=pltpu.CompilerParams(vmem_limit_bytes=62 << 20),
@@ -942,15 +942,15 @@
             lambda *given: mlp_grads(flat(units_far, units_near), flat(grads_far, grads_near), given, cuts),
             [far_sums[4], near_sums[4]],
         )
-        grad_resid, grad_attn = resid_grads(
-            near_sums[2], found, x_top, x_bottom, y_top, y_bottom, resid, gift, scale_two
-        )
-        out_far = halved(far_sums[0], after(far_out, partial[0]))
-        out_near = halved(near_sums[0], near_out)
-        return partial, grad_resid, grad_attn, out_far, out_near, one_d_c
-
-    cuts = (1, 1, 1)
-    partial, grad_resid, grad_attn, out_far, out_near, one_d_c = boxed(
+        received = x_top, x_bottom, y_top, y_bottom
+        return partial, near_sums[2], found, received, far_sums[0], far_out, near_sums[0], near_out, one_d_c
+
+    def rest(keep, found, received, resid, gift, scale_two, far, far_out, near, near_out):
+        grad_resid, grad_attn = resid_grads(keep, found, *received, resid, gift, scale_two)
+        return grad_resid, grad_attn, halved(far, far_out), halved(near, near_out)
+
+    cuts = (1, 2, 2, 1)
+    partial, keep, found, received, *outs, one_d_c = boxed(
         sure,
         middle,
         mlp_full[-per:],
@@ -965,7 +965,10 @@
         gift,
         ones,
     )
-    columns.append(lax.psum_scatter(partial[0], "z", scatter_dimension=0, tiled=True))
+    columns += [lax.psum_scatter(piece, "z", scatter_dimension=0, tiled=True) for piece in partial[:2]]
+    grad_resid, grad_attn, out_far, out_near = boxed(
+        sure, rest, after(keep, *columns[:-2]), found, received, resid, gift, scale_two, *outs
+    )
     one_x, one_c, one_x_c, one_y, one_d, one_y_c = ones
     flat_ones = [unit_one, one_x, one_c, one_x_c, one_y, one_d, one_y_c, one_d_c]
 
@@ -973,10 +976,14 @@
         top, bottom = own if isinstance(own, tuple) else halves(own)
         return jnp.concatenate([total(top, first[2], second[1]), total(bottom, second[0], first[3])], 0)
 
-    def backward(grad_attn, out_far, out_near, queries, pairs, mixed_wide, logs, out_blocks, positions):
+    def backward(grad_attn, out_far, out_near, queries, pairs, mixed, mixed_wide, logs, out_blocks, positions):
         def attention(grad_attn):
             grad_mixed = apply_rows(grad_attn, out_blocks)
             return attend_back(queries, grad_mixed, mixed_wide, logs, pairs, positions, size, base)
+
+        def out_sums(grad_attn, mixed, *given):
+            keep, send = row_grads(grad_attn, mixed)
+            return part_sums(keep, swap(send, "c")), given
 
         first, (grad_queries, mine, theirs) = stage(
             [(out_far[0], "x"), (out_far[1], "y"), (out_far[2], "x"), (out_near[1], "y")], attention, [grad_attn]
@@ -984,72 +991,83 @@
         (found,), _ = stage([(theirs, "c")])
         mine = summed(mine, found)
         second = total(out_far[3], first[1]).astype(low), total(out_near[0], first[0]).astype(low)
-        found, second = stage(
+        found, (sums, second) = stage(
             [(mine[chips - d].astype(low), behind(-d)) for d in range(chips, 0, -1)],
-            lambda *given: given,
-            second,
+            out_sums,
+            [grad_attn, mixed, *second],
         )
         grad_pair = total(mine[chips], *found).astype(low)
-        return jnp.concatenate([grad_queries, grad_pair], 1), first, second
-
-    grad_qkv, first, second = boxed(
-        sure, backward, after(grad_attn, *columns[:-1]), out_far, out_near, queries, pairs, mixed_wide, logs, out_blocks, positions
+        return jnp.concatenate([grad_queries, grad_pair], 1), first, second, sums
+
+    grad_qkv, first, second, sums = boxed(
+        sure,
+        backward,
+        after(grad_attn, columns[-2]),
+        out_far,
+        out_near,
+        queries,
+        pairs,
+        mixed,
+        mixed_wide,
+        logs,
+        out_blocks,
+        positions,
     )
     columns += [
-        lax.psum_scatter(after(piece, grad_qkv), "z", scatter_dimension=0, tiled=True) for piece in partial[1:]
+        lax.psum_scatter(after(piece, grad_qkv), "z", scatter_dimension=0, tiled=True) for piece in partial[2:]
     ]
 
-    def collect(grad_attn, grad_qkv, second, mixed, flat_ones):
+    def collect(grad_qkv, second, sums, grad_resid, qkv_blocks, flat_ones, scale_one, tokens):
+        diag_top, diag_bottom, x_top, _, _, y_bottom, _ = sums
         own, *others = spread(grad_qkv)
-        found, (out_keep, out_send) = stage(
-            [(value, across(r + 1)) for r, value in enumerate(others)],
-            lambda *given: row_grads(*given),
-            [grad_attn, mixed],
+
+        def results(grad_qkv):
+            grad_unit_one = apply_rows(grad_qkv, qkv_blocks, True)
+            return grad_resid + unit_back(grad_unit_one, tokens[0].astype(f32), scale_one)
+
+        found, grad_tokens = stage(
+            [(value, across(r + 1)) for r, value in enumerate(others)], results, [grad_qkv]
         )
-        (found, *second), qkv_column = stage(
-            [(out_send, "c"), (second[0], "x"), (second[1], "y")],
+        (*started, x_second, y_second), qkv_column = stage(
+            [
+                (diag_top, "x"),
+                (diag_bottom, "y"),
+                (x_top, "x"),
+                (y_bottom, "y"),
+                (second[0], "x"),
+                (second[1], "y"),
+            ],
             lambda *gathered: token_grads(flat_ones, jnp.concatenate(gathered, 0)),
             [own, *found],
         )
-        return qkv_column, out_keep, found, second
-
-    qkv_column, out_keep, found, second = boxed(
-        sure, collect, after(grad_attn, columns[-3]), grad_qkv, second, mixed, flat_ones
-    )
-    qkv_low = lax.psum_scatter(qkv_column, "z", scatter_dimension=0, tiled=True)
-
-    def end(out_keep, found, first, second, grad_resid, grad_qkv, out_near, qkv_blocks, resid, scale_one, tokens):
-        diag_top, diag_bottom, x_top, x_bottom, y_top, y_bottom, own = part_sums(out_keep, found)
-
-        def results(grad_qkv, *second):
-            inputs = tokens[0].astype(f32)
-            output = resid + joined((out_near[2], out_near[3]), first, second)
-            grad_unit_one = apply_rows(grad_qkv, qkv_blocks, True)
-            return output, grad_resid + unit_back(grad_unit_one, inputs, scale_one)
-
-        started, (output, grad_tokens) = stage(
-            [(diag_top, "x"), (diag_bottom, "y"), (x_top, "x"), (y_bottom, "y")], results, [grad_qkv, *second]
-        )
-        x_bottom, y_top = total(x_bottom, started[1]).astype(low), total(y_top, started[0]).astype(low)
-        second, _ = stage([(x_bottom, "x"), (y_top, "y")])
-        column = joined(own, started, second).astype(low)
-        return output, grad_tokens, column.reshape(-1, column.shape[-1])
-
-    output, grad_tokens, out_column = boxed(
+        return qkv_column, grad_tokens, started, (x_second, y_second)
+
+    qkv_column, grad_tokens, started, second = boxed(
         sure,
-        end,
-        out_keep,
-        found,
-        first,
+        collect,
+        after(grad_qkv, columns[2]),
         second,
-        after(grad_resid, columns[-2]),
-        grad_qkv,
-        out_near,
+        sums,
+        grad_resid,
         qkv_blocks,
-        resid,
+        flat_ones,
         scale_one,
         tokens,
     )
+    qkv_low = lax.psum_scatter(qkv_column, "z", scatter_dimension=0, tiled=True)
+
+    def end(sums, started, first, second, out_near, resid):
+        _, _, _, x_bottom, y_top, _, own = sums
+        x_bottom, y_top = total(x_bottom, started[1]).astype(low), total(y_top, started[0]).astype(low)
+        received, output = stage(
+            [(x_bottom, "x"), (y_top, "y")],
+            lambda resid: resid + joined((out_near[2], out_near[3]), first, second),
+            [resid],
+        )
+        column = joined(own, started, received).astype(low)
+        return output, column.reshape(-1, column.shape[-1])
+
+    output, out_column = boxed(sure, end, sums, started, first, second, out_near, after(resid, *columns[3:]))
     out_sum = lax.psum_scatter(out_column, "z", scatter_dimension=0, tiled=True).astype(f32)
     every = jnp.concatenate([*columns, qkv_low], 1)
     every = after(every, out_column).reshape(8, -1, every.shape[1])

time: 1020 us -> 1050 us (1.029)
  waiting for transfers between devices: 376 us -> 413 us
  starting transfers between devices: 102 us -> 87.5 us
    ppermute x66, waiting for transfers between devices: 197 us -> 234 us  [swap(): return lax.ppermute(value, axis, [(0, 1), (1, 0)])]
    ppermute x6, waiting for transfers between devices: 61 us -> 38.7 us  [behind(): return lambda value: lax.ppermute(value, ('z', 'y'), pairs)]
    reduce_scatter x1 -> x2, waiting for transfers between devices: 0.01 us -> 19.4 us  [local(): lax.psum_scatter(piece, 'z', scatter_dimension=0, tiled=True)]
    ppermute x7, starting transfers between devices: 24.5 us -> 13.8 us  [across(): lax.ppermute(value, PLANE, [(i, i ^ distance) for i in range(8)])]
  transfers between devices with their start and end apart: 93 -> 94, of which waited for: 41 -> 42; matrix products, arithmetic and copies ran while one was open for 8% -> 7% of each run, Pallas kernels for 41% -> 40%
where the time goes in v7:
time: 1050 us; the launch traced here: 1040 us
  Pallas kernels  427 us (41%)
  waiting for transfers between devices  413 us (39%)
  starting transfers between devices  87.5 us (8%)
  local copies, waits for them, and re-layouts  47.4 us (5%)
  other arithmetic  43.6 us (4%)
  between operations  15.3 us (1%)
    ppermute x66, waiting for transfers between devices, swap(): return lax.ppermute(value, axis, [(0, 1), (1, 0)])  234 us
    pallas_call x4, Pallas kernels, mlp(): pl.pallas_call(functools.partial(mlp_kernel, each // 3, per, tiles), out_...  155 us
    pallas_call x2, Pallas kernels, mlp_grads(): pl.pallas_call(functools.partial(mlp_grads_kernel, len(units)), out_shape...  75.6 us
    pallas_call x4, Pallas kernels, apply_rows(): pl.pallas_call(kernel, out_shape=shape, grid_spec=pltpu.PrefetchScalarGri...  47.8 us
    ppermute x66, starting transfers between devices, swap(): return lax.ppermute(value, axis, [(0, 1), (1, 0)])  45.7 us
    all_to_all x1, waiting for transfers between devices, local(): lax.all_to_all(mine, PLANE, split_axis=0, concat_axis=0, tiled=True)  44.6 us
    ppermute x6, waiting for transfers between devices, behind(): return lambda value: lax.ppermute(value, ('z', 'y'), pairs)  38.7 us
    pallas_call x1, Pallas kernels, attend_back(): pl.pallas_call(functools.partial(attend_back_kernel, size, size ** (-0.5)...  35.7 us
  transfers between devices with their start and end apart: 94, of which 42 were waited for; matrix products, arithmetic and copies ran while one was open for 7% of the time, Pallas kernels for 40%

profile of v7, /device:TPU:0, one launch (start us, length us, event | category | flops | bytes accessed | tf_op | source)
XLA Modules:
  0.0 1035.7 jit_solution(1732008645336920664)
XLA Ops:
  20.8 44.6 %all-to-all-done = bf16[8,80,3072]{2,1,0:T(8,128)(2,1)} async-done(((bf16[8,80,3072]{2,1,0:T(8,128)(2,1)}), bf16[8,80,3072]{2,1,0:T(8,128)(2,1)}, u32[]{:S(2)}, u32[]{:S(2)}) %all-to-all-start) | async-done | bytes 3932192 | tf_op jit(solution)/shard_map/all_to_all | solution.py:811
  71.6 151.2 %conditional.8 = (bf16[4,80,3072]{2,1,0:T(8,128)(2,1)}, bf16[4,80,3072]{2,1,0:T(8,128)(2,1)}, bf16[4,80,3072]{2,1,0:T(8,128)(2,1)}, bf16[4,80,3072]{2,1,0:T(8,12...) conditional(s32[]{:T(128)} %bitcast.16, () %tuple.133, ...), branch_computations={%region_0.0_spmd, %region_1.0_spmd} | conditional | flops 6947220 | bytes 119945320 | solution.py:60
  73.5 43.2 %collective-permute-done.24.rest_4_ = bf16[4,80,3072]{2,1,0:T(8,128)(2,1)} collective-permute-done((bf16[4,80,3072]{2,1,0:T(8,128)(2,1)}, bf16[4,80,3072]{2,1,0:T(8,128)(2,1)}, u32[]{:S(2)}, u32[]{:S(2)}) %collective-permute-start.24) | collective-permute-done | bytes 1966112 | tf_op jit(solution)/shard_map/cond/branch_1_fun/ppermute | solution.py:28
  122.9 17.9 %collective-permute-done.25 = bf16[2,80,3072]{2,1,0:T(8,128)(2,1)S(1)} collective-permute-done((bf16[2,80,3072]{2,1,0:T(8,128)(2,1)S(1)}, bf16[2,80,3072]{2,1,0:T(8,128)(2,1)S(1)}, u32[]{:S(2)}, u32[]{:S(2)}) %collective-permute-start.25) | collective-permute-done | bytes 983072 | tf_op jit(solution)/shard_map/cond/branch_1_fun/ppermute | solution.py:28
  152.4 12.6 %branch_1_fun.21 = bf16[384,3072]{1,0:T(8,128)(2,1)S(1)} custom-call(s32[8]{0:T(128)S(1)} %iota_xor_fusion.slots, bf16[384,2560]{1,0:T(8,128)(2,1)} %fusion.1.left, bf16[4,80,3072]{2,1,0:T(8,128)(2,1)} %get-tuple-element.284.rest_0_, bf16[4,80,3072]{2,1,0:T(8,128)(2,1)} %collective-permute-done.21.rest_1_, ...), custom_call_target="tpu_custom_call" | custom-call | flops 1048576 | bytes 4096 | tf_op jit(solution)/shard_map/cond/branch_1_fun/pallas_call | solution.py:314
  177.8 12.5 %collective-permute-done.30 = bf16[384,512]{1,0:T(8,128)(2,1)} collective-permute-done((bf16[384,512]{1,0:T(8,128)(2,1)}, bf16[384,512]{1,0:T(8,128)(2,1)}, u32[]{:S(2)}, u32[]{:S(2)}) %collective-permute-start.30) | collective-permute-done | bytes 393248 | tf_op jit(solution)/shard_map/cond/branch_1_fun/ppermute | solution.py:80
  198.6 21.0 %collective-permute-done.32 = bf16[384,512]{1,0:T(8,128)(2,1)} collective-permute-done((bf16[384,512]{1,0:T(8,128)(2,1)}, bf16[384,512]{1,0:T(8,128)(2,1)}, u32[]{:S(2)}, u32[]{:S(2)}) %collective-permute-start.32) | collective-permute-done | bytes 393248 | tf_op jit(solution)/shard_map/cond/branch_1_fun/ppermute | solution.py:80
  224.1 140.7 %conditional.9 = (bf16[4,80,2560]{2,1,0:T(8,128)(2,1)}, bf16[4,80,2560]{2,1,0:T(8,128)(2,1)}, bf16[4,80,2560]{2,1,0:T(8,128)(2,1)}, bf16[4,80,2560]{2,1,0:T(8,12...) conditional(s32[]{:T(128)} %bitcast.16, () %tuple.131, ...), branch_computations={%region_3.0_spmd, %region_4.0_spmd} | conditional | flops 7012756 | bytes 129779640 | solution.py:60
  227.7 29.0 %branch_1_fun.22 = (bf16[384,2560]{1,0:T(8,128)(2,1)}, f32[384,2560]{1,0:T(8,128)}, f32[15,1,256]{2,1,0:T(1,128)S(1)}) custom-call(s32[1]{0:T(128)} %bitcast.2.core, s32[1,384]{1,0:T(1,128)S(1)} %get-tuple-element.324.places, bf16[384,2560]{1,0:T(8,128)(2,1)} %get-tuple-element.325.queries, bf16[384,512]{1,0:T(8,128)(2,1)} %get-tuple-element.326.rest_0_, ...), custom_call_target="tpu_custom_call" | custom-call | flops 1048576 | bytes 4096 | tf_op jit(solution)/shard_map/cond/branch_1_fun/pallas_call | solution.py:195
  270.3 16.8 %collective-permute-done.45 = bf16[2,80,2560]{2,1,0:T(8,128)(2,1)S(1)} collective-permute-done((bf16[2,80,2560]{2,1,0:T(8,128)(2,1)S(1)}, bf16[2,80,2560]{2,1,0:T(8,128)(2,1)S(1)}, u32[]{:S(2)}, u32[]{:S(2)}) %collective-permute-start.45) | collective-permute-done | bytes 819232 | tf_op jit(solution)/shard_map/cond/branch_1_fun/ppermute | solution.py:28
  314.5 43.2 %collective-permute-done.50 = bf16[384,2560]{1,0:T(8,128)(2,1)} collective-permute-done((bf16[384,2560]{1,0:T(8,128)(2,1)}, bf16[384,2560]{1,0:T(8,128)(2,1)}, u32[]{:S(2)}, u32[]{:S(2)}) %collective-permute-start.50) | collective-permute-done | bytes 1966112 | tf_op jit(solution)/shard_map/cond/branch_1_fun/ppermute | solution.py:28
  364.8 137.0 %conditional.10 = (bf16[384,2560]{1,0:T(8,128)(2,1)}, bf16[384,2560]{1,0:T(8,128)(2,1)}, bf16[384,2560]{1,0:T(8,128)(2,1)}, bf16[384,2560]{1,0:T(8,128)(2,1)}, b...) conditional(s32[]{:T(128)} %bitcast.16, () %tuple.130, ...), branch_computations={%region_6.0_spmd, %region_7.0_spmd} | conditional | flops 3145728 | bytes 78656040 | solution.py:60
  368.7 36.8 %branch_1_fun.24 = (bf16[768,2560]{1,0:T(8,128)(2,1)}, bf16[768,2560]{1,0:T(8,128)(2,1)}, bf16[768,2560]{1,0:T(8,128)(2,1)}, bf16[768,2560]{1,0:T(8,128)(2,1)}, bf16[1536,1536]{1,0:T(8,128)(2,1)}) custom-call(bf16[2560,768]{1,0:T(8,128)(2,1)} %get-tuple-element.396.rest_0_, bf16[2560,768]{1,0:T(8,128)(2,1)} %get-tuple-element.397.rest_1_, ...), custom_call_target="tpu_custom_call" | custom-call | flops 1048576 | bytes 4096 | tf_op jit(solution)/shard_map/cond/branch_1_fun/pallas_call | solution.py:462
  419.0 37.1 %branch_1_fun.25 = (bf16[768,2560]{1,0:T(8,128)(2,1)}, bf16[768,2560]{1,0:T(8,128)(2,1)}, bf16[768,2560]{1,0:T(8,128)(2,1)}, bf16[768,2560]{1,0:T(8,128)(2,1)}, bf16[1536,1536]{1,0:T(8,128)(2,1)}) custom-call(bf16[2560,768]{1,0:T(8,128)(2,1)} %get-tuple-element.396.rest_0_, bf16[2560,768]{1,0:T(8,128)(2,1)} %get-tuple-element.397.rest_1_, ...), custom_call_target="tpu_custom_call" | custom-call | flops 1048576 | bytes 4096 | tf_op jit(solution)/shard_map/cond/branch_1_fun/pallas_call | solution.py:462
  459.7 37.8 %branch_1_fun.26 = bf16[2560,1536]{1,0:T(8,128)(2,1)} custom-call(bf16[384,2560]{1,0:T(8,128)(2,1)} %collective-permute-done.rest_2_.rest_0_, bf16[384,2560]{1,0:T(8,128)(2,1)} %get-tuple-element.398.rest_4_.rest_1_, bf16[384,2560]{1,0:T(8,128)(2,1)} %collective-permute-done.2.rest_6_.rest_2_, bf16[384,2560]{1,0:T(8,128)(2,1)} %get-tuple-element.399.rest_8_.rest_3_, ...), custom_call_target="tpu_custom_call" | custom-call | flops 1048576 | bytes 4096 | tf_op jit(solution)/shard_map/cond/branch_1_fun/pallas_call | solution.py:525
  502.0 159.1 %conditional.11 = (bf16[2560,256]{1,0:T(8,128)(2,1)}, bf16[2560,512]{1,0:T(8,128)(2,1)}, bf16[2560,512]{1,0:T(8,128)(2,1)}, bf16[2560,256]{1,0:T(8,128)(2,1)}, b...) conditional(s32[]{:T(128)} %bitcast.16, () %tuple.129, ...), branch_computations={%region_8.0_spmd, %region_9.0_spmd} | conditional | flops 5242880 | bytes 94392880 | solution.py:60
  502.1 40.7 %branch_1_fun.27 = (bf16[768,2560]{1,0:T(8,128)(2,1)}, bf16[768,2560]{1,0:T(8,128)(2,1)}, bf16[768,2560]{1,0:T(8,128)(2,1)}, bf16[768,2560]{1,0:T(8,128)(2,1)}, bf16[1536,1536]{1,0:T(8,128)(2,1)}) custom-call(bf16[2560,768]{1,0:T(8,128)(2,1)} %get-tuple-element.432.rest_0_, bf16[2560,768]{1,0:T(8,128)(2,1)} %get-tuple-element.433.rest_1_, ...), custom_call_target="tpu_custom_call" | custom-call | flops 1048576 | bytes 4096 | tf_op jit(solution)/shard_map/cond/branch_1_fun/pallas_call | solution.py:462
  560.9 40.9 %branch_1_fun.29 = (bf16[768,2560]{1,0:T(8,128)(2,1)}, bf16[768,2560]{1,0:T(8,128)(2,1)}, bf16[768,2560]{1,0:T(8,128)(2,1)}, bf16[768,2560]{1,0:T(8,128)(2,1)}, bf16[1536,1536]{1,0:T(8,128)(2,1)}) custom-call(bf16[2560,768]{1,0:T(8,128)(2,1)} %get-tuple-element.432.rest_0_, bf16[2560,768]{1,0:T(8,128)(2,1)} %get-tuple-element.433.rest_1_, ...), custom_call_target="tpu_custom_call" | custom-call | flops 1048576 | bytes 4096 | tf_op jit(solution)/shard_map/cond/branch_1_fun/pallas_call | solution.py:462
  619.0 37.8 %branch_1_fun.31 = (bf16[2560,256]{1,0:T(8,128)(2,1)}, bf16[2560,512]{1,0:T(8,128)(2,1)}, bf16[2560,512]{1,0:T(8,128)(2,1)}, bf16[2560,256]{1,0:T(8,128)(2,1)}) custom-call(bf16[384,2560]{1,0:T(8,128)(2,1)} %get-tuple-element.434.rest_2_.rest_0_, bf16[384,2560]{1,0:T(8,128)(2,1)} %get-tuple-element.436.rest_4_.rest_1_, ...), custom_call_target="tpu_custom_call" | custom-call | flops 1048576 | bytes 4096 | tf_op jit(solution)/shard_map/cond/branch_1_fun/pallas_call | solution.py:525
  661.9 23.3 %conditional.12 = (f32[384,2560]{1,0:T(8,128)}, bf16[384,2560]{1,0:T(8,128)(2,1)}, bf16[192,2560]{1,0:T(8,128)(2,1)}, bf16[192,2560]{1,0:T(8,128)(2,1)}, bf16[19...) conditional(s32[]{:T(128)} %bitcast.16, () %tuple.128, ...), branch_computations={%region_11.0_spmd, %region_12.0_spmd} | conditional | flops 3145728 | bytes 13762662 | solution.py:60
  685.2 19.4 %reduce-scatter.10.cloned.1.call-done = bf16[640,256]{1,0:T(8,128)(2,1)} async-done(((bf16[2560,256]{1,0:T(8,128)(2,1)}), bf16[640,256]{1,0:T(8,128)(2,1)}) %reduce-scatter.10.cloned.1.call-update) | async-done | bytes 327696 | tf_op jit(solution)/shard_map/reduce_scatter | solution.py:968
  704.6 98.6 %conditional.13 = (bf16[384,3072]{1,0:T(8,128)(2,1)}, bf16[192,2560]{1,0:T(8,128)(2,1)}, bf16[192,2560]{1,0:T(8,128)(2,1)S(1)}, bf16[192,2560]{1,0:T(8,128)(2,1)...) conditional(s32[]{:T(128)} %bitcast.16, () %tuple.127, ...), branch_computations={%region_14.0_spmd, %region_15.0_spmd} | conditional | flops 16581684 | bytes 140137568 | solution.py:60
  721.1 35.7 %branch_1_fun.36 = (bf16[384,2560]{1,0:T(8,128)(2,1)}, f32[4,384,512]{2,1,0:T(8,128)}, bf16[4,384,512]{2,1,0:T(8,128)(2,1)}) custom-call(s32[1]{0:T(128)} %bitcast.5.core, s32[1,384]{1,0:T(1,128)S(1)} %get-tuple-element.548.places, bf16[384,2560]{1,0:T(8,128)(2,1)} %get-tuple-element.549.queries, bf16[384,2560]{1,0:T(8,128)(2,1)} %copy-done, ...), custom_call_target="tpu_custom_call" | custom-call | flops 1048576 | bytes 4096 | tf_op jit(solution)/shard_map/cond/branch_1_fun/pallas_call | solution.py:228
  763.8 13.2 %branch_1_fun.37 = (bf16[4,4,80,2560]{3,2,1,0:T(8,128)(2,1)}, bf16[4,4,80,2560]{3,2,1,0:T(8,128)(2,1)}) custom-call(s32[8]{0:T(128)S(1)} %gather_fusion, bf16[384,2560]{1,0:T(8,128)(2,1)} %get-tuple-element.584.left, bf16[384,2560]{1,0:T(8,128)(2,1)} %get-tuple-element.585.right), custom_call_target="tpu_custom_call" | custom-call | flops 1048576 | bytes 4096 | tf_op jit(solution)/shard_map/cond/branch_1_fun/pallas_call | solution.py:363
  804.1 107.3 %conditional.14 = (bf16[2560,384]{1,0:T(8,128)(2,1)S(1)}, bf16[2,80,2560]{2,1,0:T(8,128)(2,1)}, bf16[2,80,2560]{2,1,0:T(8,128)(2,1)}, bf16[2,80,2560]{2,1,0:T(8,...) conditional(s32[]{:T(128)} %bitcast.16, () %tuple.148, ...), branch_computations={%region_17.0_spmd, %region_18.20_spmd} | conditional | flops 12976148 | bytes 66610176 | solution.py:60
  856.1 16.0 %collective-permute-done.64 = bf16[2,80,2560]{2,1,0:T(8,128)(2,1)} collective-permute-done((bf16[2,80,2560]{2,1,0:T(8,128)(2,1)}, bf16[2,80,2560]{2,1,0:T(8,128)(2,1)}, u32[]{:S(2)}, u32[]{:S(2)}) %collective-permute-start.64) | collective-permute-done | bytes 819232 | tf_op jit(solution)/shard_map/cond/branch_1_fun/ppermute | solution.py:28
  877.0 13.2 %branch_1_fun.41 = bf16[2560,384]{1,0:T(8,128)(2,1)S(1)} custom-call(bf16[384,2560]{1,0:T(8,128)(2,1)} %get-tuple-element.658.rest_0_, bf16[384,2560]{1,0:T(8,128)(2,1)} %get-tuple-element.659.rest_1_, bf16[384,2560]{1,0:T(8,128)(2,1)} %get-tuple-element.660.rest_2_, bf16[384,2560]{1,0:T(8,128)(2,1)} %get-tuple-element.661.rest_3_, ...), custom_call_target="tpu_custom_call" | custom-call | flops 1048576 | bytes 4096 | tf_op jit(solution)/shard_map/cond/branch_1_fun/pallas_call | solution.py:560
  895.3 14.6 %collective-permute-done.66 = bf16[2,80,2560]{2,1,0:T(8,128)(2,1)} collective-permute-done((bf16[2,80,2560]{2,1,0:T(8,128)(2,1)}, bf16[2,80,2560]{2,1,0:T(8,128)(2,1)}, u32[]{:S(2)}, u32[]{:S(2)}) %collective-permute-start.66) | collective-permute-done | bytes 819232 | tf_op jit(solution)/shard_map/cond/branch_1_fun/ppermute | solution.py:28
  917.6 26.1 %conditional.15 = (bf16[320,2560]{1,0:T(8,128)(2,1)}, f32[1,384,2560]{2,1,0:T(8,128)}) conditional(s32[]{:T(128)} %bitcast.16, () %tuple.126, (bf16[4,80,2560]{2,1,0:T(8,128)(2,1)}, bf16[2,80,2560]{2,1,0:T(8,128)(2,1)}, bf16[2,80,2560]{2,1,0:T(8,128)(2,1)}, bf16[2,80,2560]{2,1,0:T(8,128)(2,1)}, bf16[2,80,2560]{2,1,0:T(8,128)(2,1)}, ...), branch_computations={%region_22.0_spmd, %region_23.0_spmd} | conditional | flops 15892480 | bytes 50790552 | solution.py:60
  946.5 14.1 %reduce-scatter.18.cloned.1.call-done = bf16[640,384]{1,0:T(8,128)(2,1)} async-done(((bf16[2560,384]{1,0:T(8,128)(2,1)}), bf16[640,384]{1,0:T(8,128)(2,1)}) %reduce-scatter.18.cloned.1.call-update) | async-done | bytes 491536 | tf_op jit(solution)/shard_map/reduce_scatter | solution.py:1057
  967.3 31.7 %reduce-scatter.20.cloned.1.call-done = bf16[80,2560]{1,0:T(8,128)(2,1)} async-done(((bf16[320,2560]{1,0:T(8,128)(2,1)}), bf16[80,2560]{1,0:T(8,128)(2,1)}) %reduce-scatter.20.cloned.1.call-update) | async-done | bytes 409616 | tf_op jit(solution)/shard_map/reduce_scatter | solution.py:1071
  1001.0 17.3 %all-to-all-done.1.whole = bf16[8,80,3456]{2,1,0:T(8,128)(2,1)} async-done(((bf16[8,80,3456]{2,1,0:T(8,128)(2,1)}), bf16[8,80,3456]{2,1,0:T(8,128)(2,1)}, u32[]{:S(2)}, u32[]{:S(2)}) %all-to-all-start.1) | async-done | bytes 4423712 | tf_op jit(solution)/shard_map/all_to_all | solution.py:1074
  (347 shorter events, 371.6 us)
Async XLA Ops:
  14.3 51.0 %all-to-all-start = ((bf16[8,80,3072]{2,1,0:T(8,128)(2,1)}), bf16[8,80,3072]{2,1,0:T(8,128)(2,1)}, u32[]{:S(2)}, u32[]{:S(2)}) async-start(bf16[8,80,3072]{2,1,0:T(8,128)(2,1)} %shard_map.213), calls=%async_computation | async-start | bytes 7864320 | tf_op jit(solution)/shard_map/all_to_all | solution.py:811
  19.7 51.9 %all-gather.8.cloned.1.call-start = ((), (), s32[]{:S(2)}) async-start(), calls=%async_computation.9 | async-start | bytes 2457600 | tf_op jit(solution)/shard_map/all_gather | solution.py:801
  20.7 203.4 %all-gather.10.cloned.1.call-start = ((), (), s32[]{:S(2)}) async-start(), calls=%async_computation.10 | async-start | bytes 4915200 | tf_op jit(solution)/shard_map/all_gather | solution.py:816
  69.6 154.5 %all-gather.18.cloned.1.call-start = ((), (), s32[]{:S(2)}) async-start(), calls=%async_computation.21 | async-start | bytes 2048000 | tf_op jit(solution)/shard_map/all_gather | solution.py:802
  70.3 294.5 %all-gather.12.cloned.1.call-start = ((), (), s32[]{:S(2)}) async-start(), calls=%async_computation.11 | async-start | bytes 4915200 | tf_op jit(solution)/shard_map/all_gather | solution.py:816
  71.6 45.1 %collective-permute-start.24 = (bf16[4,80,3072]{2,1,0:T(8,128)(2,1)}, bf16[4,80,3072]{2,1,0:T(8,128)(2,1)}, u32[]{:S(2)}, u32[]{:S(2)}) collective-permute-start(bf16[4,80,3072]{2,1,0:T(8,128)(2,1)} %get-tuple-element.284.rest_0_), channel_id=1, source_target_pairs={{0,4},{4,0},{1,5},{5,1},{2,6},{6,2},{3,7},{7,3},{8,12},{12,8},{9,1... | collective-permute-start | bytes 5898248 | tf_op jit(solution)/shard_map/cond/branch_1_fun/ppermute | solution.py:28
  72.3 46.8 %collective-permute-start.21 = (bf16[4,80,3072]{2,1,0:T(8,128)(2,1)}, bf16[4,80,3072]{2,1,0:T(8,128)(2,1)}, u32[]{:S(2)}, u32[]{:S(2)}) collective-permute-start(bf16[4,80,3072]{2,1,0:T(8,128)(2,1)} %get-tuple-element.284.rest_0_), channel_id=1, source_target_pairs={{0,1},{1,0},{2,3},{3,2},{4,5},{5,4},{6,7},{7,6},{8,9},{9,8},{10,11... | collective-permute-start | bytes 5898248 | tf_op jit(solution)/shard_map/cond/branch_1_fun/ppermute | solution.py:28
  165.8 53.8 %collective-permute-start.34 = (bf16[384,2560]{1,0:T(8,128)(2,1)S(1)}, bf16[384,2560]{1,0:T(8,128)(2,1)}, u32[]{:S(2)}, u32[]{:S(2)}) collective-permute-start(bf16[384,2560]{1,0:T(8,128)(2,1)S(1)} %copy-done.9), channel_id=1, source_target_pairs={{0,1},{1,0},{2,3},{3,2},{4,5},{5,4},{6,7},{7,6},{8,9},{9,8},{10,11... | collective-permute-start | bytes 5898248 | tf_op jit(solution)/shard_map/cond/branch_1_fun/ppermute | solution.py:28
  167.1 52.4 %collective-permute-start.35 = (bf16[384,2560]{1,0:T(8,128)(2,1)S(1)}, bf16[384,2560]{1,0:T(8,128)(2,1)}, u32[]{:S(2)}, u32[]{:S(2)}) collective-permute-start(bf16[384,2560]{1,0:T(8,128)(2,1)S(1)} %copy-done.9), channel_id=1, source_target_pairs={{0,4},{4,0},{1,5},{5,1},{2,6},{6,2},{3,7},{7,3},{8,12},{12,8},{9,1... | collective-permute-start | bytes 5898248 | tf_op jit(solution)/shard_map/cond/branch_1_fun/ppermute | solution.py:28
  168.6 51.0 %collective-permute-start.36 = (bf16[384,2560]{1,0:T(8,128)(2,1)S(1)}, bf16[384,2560]{1,0:T(8,128)(2,1)}, u32[]{:S(2)}, u32[]{:S(2)}) collective-permute-start(bf16[384,2560]{1,0:T(8,128)(2,1)S(1)} %copy-done.9), channel_id=1, source_target_pairs={{0,2},{2,0},{1,3},{3,1},{4,6},{6,4},{5,7},{7,5},{8,10},{10,8},{9,1... | collective-permute-start | bytes 5898248 | tf_op jit(solution)/shard_map/cond/branch_1_fun/ppermute | solution.py:28
  222.9 279.1 %all-gather.14.cloned.1.call-start = ((), (), s32[]{:S(2)}) async-start(), calls=%async_computation.12 | async-start | bytes 4915200 | tf_op jit(solution)/shard_map/all_gather | solution.py:816
  223.5 278.5 %all-gather.16.cloned.1.call-start = ((), (), s32[]{:S(2)}) async-start(), calls=%async_computation.13 | async-start | bytes 4915200 | tf_op jit(solution)/shard_map/all_gather | solution.py:816
  224.0 437.9 %reduce-scatter.8.cloned.1.call-start = ((), (), s32[]{:S(2)}) async-start(), calls=%async_computation.14 | async-start | bytes 9830400 | tf_op jit(solution)/shard_map/reduce_scatter | solution.py:918
  312.5 45.2 %collective-permute-start.50 = (bf16[384,2560]{1,0:T(8,128)(2,1)}, bf16[384,2560]{1,0:T(8,128)(2,1)}, u32[]{:S(2)}, u32[]{:S(2)}) collective-permute-start(bf16[384,2560]{1,0:T(8,128)(2,1)} %multiply_convert_fusion), channel_id=1, source_target_pairs={{0,1},{1,0},{2,3},{3,2},{4,5},{5,4},{6,7},{7,6},{8,9},{9,8},{10,11... | collective-permute-start | bytes 5898248 | tf_op jit(solution)/shard_map/cond/branch_1_fun/ppermute | solution.py:28
  365.2 45.2 %collective-permute-start = (bf16[384,2560]{1,0:T(8,128)(2,1)}, bf16[384,2560]{1,0:T(8,128)(2,1)}, u32[]{:S(2)}, u32[]{:S(2)}) collective-permute-start(bf16[384,2560]{1,0:T(8,128)(2,1)} %get-tuple-element.373.rest_2_.rest_4_), channel_id=1, source_target_pairs={{0,1},{1,0},{2,3},{3,2},{4,5},{5,4},{6,7},{7,6},{8,9},{9,8},{10,11... | collective-permute-start | bytes 5898248 | tf_op jit(solution)/shard_map/cond/branch_1_fun/ppermute | solution.py:28
  412.4 45.0 %collective-permute-start.4 = (bf16[384,2560]{1,0:T(8,128)(2,1)}, bf16[384,2560]{1,0:T(8,128)(2,1)}, u32[]{:S(2)}, u32[]{:S(2)}) collective-permute-start(bf16[384,2560]{1,0:T(8,128)(2,1)} %get-tuple-element.395), channel_id=1, source_target_pairs={{0,1},{1,0},{2,3},{3,2},{4,5},{5,4},{6,7},{7,6},{8,9},{9,8},{10,11... | collective-permute-start | bytes 5898248 | tf_op jit(solution)/shard_map/cond/branch_1_fun/ppermute | solution.py:28
  501.9 202.8 %reduce-scatter.10.cloned.1.call-start = ((), (), s32[]{:S(2)}) async-start(), calls=%async_computation.15 | async-start | bytes 1638400 | tf_op jit(solution)/shard_map/reduce_scatter | solution.py:968
  556.8 45.6 %collective-permute-start.15 = (bf16[768,2560]{1,0:T(8,128)(2,1)}, bf16[768,2560]{1,0:T(8,128)(2,1)}, u32[]{:S(2)}, u32[]{:S(2)}) collective-permute-start(bf16[768,2560]{1,0:T(8,128)(2,1)} %get-tuple-element.464), channel_id=1, source_target_pairs={{0,2},{2,0},{1,3},{3,1},{4,6},{6,4},{5,7},{7,5},{8,10},{10,8},{9,1... | collective-permute-start | bytes 11796488 | tf_op jit(solution)/shard_map/cond/branch_1_fun/ppermute | solution.py:28
  615.4 45.6 %collective-permute-start.20 = (bf16[768,2560]{1,0:T(8,128)(2,1)}, bf16[768,2560]{1,0:T(8,128)(2,1)}, u32[]{:S(2)}, u32[]{:S(2)}) collective-permute-start(bf16[768,2560]{1,0:T(8,128)(2,1)} %get-tuple-element.496), channel_id=1, source_target_pairs={{0,2},{2,0},{1,3},{3,1},{4,6},{6,4},{5,7},{7,5},{8,10},{10,8},{9,1... | collective-permute-start | bytes 11796488 | tf_op jit(solution)/shard_map/cond/branch_1_fun/ppermute | solution.py:28
  661.1 142.9 %reduce-scatter.12.cloned.1.call-start = ((), (), s32[]{:S(2)}) async-start(), calls=%async_computation.16 | async-start | bytes 3276800 | tf_op jit(solution)/shard_map/reduce_scatter | solution.py:968
  661.9 255.7 %reduce-scatter.16.cloned.1.call-start = ((), (), s32[]{:S(2)}) async-start(), calls=%async_computation.18 | async-start | bytes 1638400 | tf_op jit(solution)/shard_map/reduce_scatter | solution.py:1017
  704.6 52.2 %collective-permute-start.70 = (bf16[192,2560]{1,0:T(8,128)(2,1)}, bf16[192,2560]{1,0:T(8,128)(2,1)}, u32[]{:S(2)}, u32[]{:S(2)}) collective-permute-start(bf16[192,2560]{1,0:T(8,128)(2,1)} %get-tuple-element.544), channel_id=1, source_target_pairs={{0,1},{1,0},{2,3},{3,2},{4,5},{5,4},{6,7},{7,6},{8,9},{9,8},{10,11... | collective-permute-start | bytes 2949128 | tf_op jit(solution)/shard_map/cond/branch_1_fun/ppermute | solution.py:28
  706.1 50.7 %collective-permute-start.71 = (bf16[192,2560]{1,0:T(8,128)(2,1)}, bf16[192,2560]{1,0:T(8,128)(2,1)}, u32[]{:S(2)}, u32[]{:S(2)}) collective-permute-start(bf16[192,2560]{1,0:T(8,128)(2,1)} %get-tuple-element.545), channel_id=1, source_target_pairs={{0,4},{4,0},{1,5},{5,1},{2,6},{6,2},{3,7},{7,3},{8,12},{12,8},{9,1... | collective-permute-start | bytes 2949128 | tf_op jit(solution)/shard_map/cond/branch_1_fun/ppermute | solution.py:28
  707.6 49.3 %collective-permute-start.72 = (bf16[192,2560]{1,0:T(8,128)(2,1)}, bf16[192,2560]{1,0:T(8,128)(2,1)}, u32[]{:S(2)}, u32[]{:S(2)}) collective-permute-start(bf16[192,2560]{1,0:T(8,128)(2,1)} %get-tuple-element.546), channel_id=1, source_target_pairs={{0,1},{1,0},{2,3},{3,2},{4,5},{5,4},{6,7},{7,6},{8,9},{9,8},{10,11... | collective-permute-start | bytes 2949128 | tf_op jit(solution)/shard_map/cond/branch_1_fun/ppermute | solution.py:28
  708.1 48.7 %collective-permute-start.73 = (bf16[192,2560]{1,0:T(8,128)(2,1)}, bf16[192,2560]{1,0:T(8,128)(2,1)S(1)}, u32[]{:S(2)}, u32[]{:S(2)}) collective-permute-start(bf16[192,2560]{1,0:T(8,128)(2,1)} %get-tuple-element.547), channel_id=1, source_target_pairs={{0,4},{4,0},{1,5},{5,1},{2,6},{6,2},{3,7},{7,3},{8,12},{12,8},{9,1... | collective-permute-start | bytes 2949128 | tf_op jit(solution)/shard_map/cond/branch_1_fun/ppermute | solution.py:28
  803.3 114.3 %reduce-scatter.14.cloned.1.call-start = ((), (), s32[]{:S(2)}) async-start(), calls=%async_computation.17 | async-start | bytes 3276800 | tf_op jit(solution)/shard_map/reduce_scatter | solution.py:1017
  804.0 156.6 %reduce-scatter.18.cloned.1.call-start = ((), (), s32[]{:S(2)}) async-start(), calls=%async_computation.19 | async-start | bytes 2457600 | tf_op jit(solution)/shard_map/reduce_scatter | solution.py:1057
  852.0 59.4 %collective-permute-start.68 = (bf16[192,2560]{1,0:T(8,128)(2,1)}, bf16[192,2560]{1,0:T(8,128)(2,1)}, u32[]{:S(2)}, u32[]{:S(2)}) collective-permute-start(bf16[192,2560]{1,0:T(8,128)(2,1)} %get-tuple-element.656), channel_id=1, source_target_pairs={{0,1},{1,0},{2,3},{3,2},{4,5},{5,4},{6,7},{7,6},{8,9},{9,8},{10,11... | collective-permute-start | bytes 2949128 | tf_op jit(solution)/shard_map/cond/branch_1_fun/ppermute | solution.py:28
  852.7 58.6 %collective-permute-start.69 = (bf16[192,2560]{1,0:T(8,128)(2,1)}, bf16[192,2560]{1,0:T(8,128)(2,1)}, u32[]{:S(2)}, u32[]{:S(2)}) collective-permute-start(bf16[192,2560]{1,0:T(8,128)(2,1)} %get-tuple-element.657), channel_id=1, source_target_pairs={{0,4},{4,0},{1,5},{5,1},{2,6},{6,2},{3,7},{7,3},{8,12},{12,8},{9,1... | collective-permute-start | bytes 2949128 | tf_op jit(solution)/shard_map/cond/branch_1_fun/ppermute | solution.py:28
  854.8 55.1 %collective-permute-start.66 = (bf16[2,80,2560]{2,1,0:T(8,128)(2,1)}, bf16[2,80,2560]{2,1,0:T(8,128)(2,1)}, u32[]{:S(2)}, u32[]{:S(2)}) collective-permute-start(bf16[2,80,2560]{2,1,0:T(8,128)(2,1)} %get-tuple-element.654), channel_id=1, source_target_pairs={{0,1},{1,0},{2,3},{3,2},{4,5},{5,4},{6,7},{7,6},{8,9},{9,8},{10,11... | collective-permute-start | bytes 2457608 | tf_op jit(solution)/shard_map/cond/branch_1_fun/ppermute | solution.py:28
  912.7 86.3 %reduce-scatter.20.cloned.1.call-start = ((), (), s32[]{:S(2)}) async-start(), calls=%async_computation.20 | async-start | bytes 2048000 | tf_op jit(solution)/shard_map/reduce_scatter | solution.py:1071
  962.5 55.8 %all-to-all-start.1 = ((bf16[8,80,3456]{2,1,0:T(8,128)(2,1)}), bf16[8,80,3456]{2,1,0:T(8,128)(2,1)}, u32[]{:S(2)}, u32[]{:S(2)}) async-start(bf16[8,80,3456]{2,1,0:T(8,128)(2,1)} %bitcast.26), calls=%async_computation.7 | async-start | bytes 8847360 | tf_op jit(solution)/shard_map/all_to_all | solution.py:1074
  (101 other events, 1857.4 us)
Sparse Core Ops, SparseCore 0:
  22.6 45.9 all-gather.7
  70.8 76.1 all-gather.9
  148.5 41.0 all-gather.17
  223.0 86.8 all-gather.11
  311.3 74.9 all-gather.13
  387.8 74.9 all-gather.15
  502.0 147.4 reduce-scatter.7
  661.3 43.3 reduce-scatter.9
  706.9 50.8 reduce-scatter.11
  803.4 44.9 reduce-scatter.15
  850.7 50.8 reduce-scatter.13
  912.8 47.7 reduce-scatter.17
  963.5 35.5 reduce-scatter.19

commit v8 on v7

--- a/solution.py
+++ b/solution.py
@@ -256,24 +256,24 @@
     )(core, places, queries, grads, mixed, logs, *blocks)
 
 
-def lay_rows(slots, blocks, full):
-    planes, rows, _ = blocks[0].shape
-    for r in range(8):
+def lay_rows(slots, layout, pieces, full):
+    for (r, first), piece in zip(layout, pieces):
+        planes, rows, _ = piece.shape
         for plane in range(planes):
-            at = pl.multiple_of((plane * 8 + slots[r]) * rows, 16)
-            full[pl.ds(at, rows), :] = blocks[r][plane]
-
-
-def apply_kernel(slots, left, *rest):
-    blocks, (out, full) = rest[:8], rest[8:]
-    lay_rows(slots, blocks, full)
+            at = pl.multiple_of(((first + plane) * 8 + slots[r]) * rows, 16)
+            full[pl.ds(at, rows), :] = piece[plane]
+
+
+def apply_kernel(layout, slots, left, *rest):
+    *pieces, out, full = rest
+    lay_rows(slots, layout, pieces, full)
     out[...] = dot(left[...], full[...], (1, 0), low)
 
 
-def apply_turned_kernel(slots, left, *rest):
+def apply_turned_kernel(layout, slots, left, *rest):
     *start, out, full = rest
-    start, blocks = start[:-8], start[-8:]
-    lay_rows(slots, blocks, full)
+    start, pieces = start[: -len(layout)], start[-len(layout) :]
+    lay_rows(slots, layout, pieces, full)
 
     @pl.when(pl.program_id(0) == 0)
     def _():
@@ -294,13 +294,17 @@
 def apply_rows(left, blocks, turned=False, start=None):
     planes, rows, wide = blocks[0].shape
     if rows % 16 or wide % TILE:
-        whole = whole_rows(blocks)
+        whole = whole_rows(joined_blocks(blocks))
         if not turned:
             return dot(left, whole, (1, 0), low)
         return dot(left, whole, (1, 1)) + (0.0 if start is None else start)
     count, deep = left.shape[0], planes * 8 * rows
     slots = (plane_index() ^ jnp.arange(8)).astype(jnp.int32)
-    pieces = [pl.BlockSpec((planes, rows, TILE), lambda n, s: (0, 0, n))] * 8
+    layout, blocks = [], [block if isinstance(block, tuple) else (block,) for block in blocks]
+    for r, block in enumerate(blocks):
+        layout += [(r, sum(piece.shape[0] for piece in block[:i])) for i in range(len(block))]
+    blocks = [piece for block in blocks for piece in block]
+    pieces = [pl.BlockSpec((piece.shape[0], rows, TILE), lambda n, s: (0, 0, n)) for piece in blocks]
     whole = pl.BlockSpec((count, deep), lambda n, s: (0, 0))
     part = pl.BlockSpec((count, TILE), lambda n, s: (0, n))
     if not turned:
@@ -312,7 +316,7 @@
             given, specs = given + [start], specs + [whole]
         shape = jax.ShapeDtypeStruct((count, deep), f32)
     return pl.pallas_call(
-        kernel,
+        functools.partial(kernel, layout),
         out_shape=shape,
         grid_spec=pltpu.PrefetchScalarGridSpec(
             num_scalar_prefetch=1,
@@ -482,7 +486,7 @@
     *outs, turned = rest
     step = pl.program_id(0)
     part = hidden[0].shape[1] // 3
-    piece = min(part, 256, *(out.shape[1] for out in outs))
+    piece = 256 if part % 256 == 0 and outs[0].shape[1] % 256 == 0 else 128
     places = [(out, at) for out in outs for at in range(0, out.shape[1], piece)]
 
     def turn(slot, which, sources, share, shares):
@@ -516,7 +520,7 @@
             turn(step % 2, 1, grads, i, len(work))
 
 
-def mlp_grads(units, grads, hidden, pieces=(6,)):
+def mlp_grads(units, grads, hidden, pieces=(2,)):
     wide = units[0].shape[1]
     deep = hidden[0].shape[1]
     count = sum(piece.shape[0] for piece in units)
@@ -524,14 +528,14 @@
     last = wide // rows - 1
     return pl.pallas_call(
         functools.partial(mlp_grads_kernel, len(units)),
-        out_shape=[jax.ShapeDtypeStruct((wide, deep // 6 * piece), low) for piece in pieces],
+        out_shape=[jax.ShapeDtypeStruct((wide, deep // 2 * piece), low) for piece in pieces],
         grid=(last + 2,),
         in_specs=[
             pl.BlockSpec((piece.shape[0], rows), lambda s: (0, jnp.minimum(s, last))) for piece in units + grads
         ]
         + [pl.BlockSpec(piece.shape, lambda s: (0, 0), pipeline_mode=pl.Buffered(1)) for piece in hidden],
         out_specs=[
-            pl.BlockSpec((rows, deep // 6 * piece), lambda s: (jnp.maximum(s - 1, 0), 0)) for piece in pieces
+            pl.BlockSpec((rows, deep // 2 * piece), lambda s: (jnp.maximum(s - 1, 0), 0)) for piece in pieces
         ],
         scratch_shapes=[pltpu.VMEM((2, 2, rows, count), low)],
         compiler_params=pltpu.CompilerParams(vmem_limit_bytes=62 << 20),
@@ -571,25 +575,31 @@
 
 
 def spread_kernel(slots, value, *outs):
-    deep = outs[0].shape[1]
-    for i, out in enumerate(outs):
-        out[...] = value[:, pl.ds(pl.multiple_of(slots[i] * deep, 128), deep)]
+    count, deep = value.shape[0], outs[0].shape[1]
+    place = 0
+    for out in outs:
+        for at in range(0, out.shape[0], count):
+            out[at : at + count, :] = value[:, pl.ds(pl.multiple_of(slots[place] * deep, 128), deep)]
+            place += 1
 
 
 def spread(value):
     count, wide = value.shape
-    slots = (plane_index() ^ jnp.arange(8)).astype(jnp.int32)
+    order = (0, 2, 1, 3, 4, 6, 5, 7)
+    slots = (plane_index() ^ jnp.array(order)).astype(jnp.int32)
     deep = wide // 8
+    rows = (count, count, 2 * count, 2 * count, 2 * count)
     if deep % 128:
-        return [lax.dynamic_slice(value, (0, slots[r] * deep), (count, deep)) for r in range(8)]
+        pieces = [lax.dynamic_slice(value, (0, slots[i] * deep), (count, deep)) for i in range(8)]
+        return pieces[:2] + [jnp.concatenate(pieces[i : i + 2], 0) for i in (2, 4, 6)]
     return pl.pallas_call(
         spread_kernel,
-        out_shape=[jax.ShapeDtypeStruct((count, deep), value.dtype)] * 8,
+        out_shape=[jax.ShapeDtypeStruct((n, deep), value.dtype) for n in rows],
         grid_spec=pltpu.PrefetchScalarGridSpec(
             num_scalar_prefetch=1,
             grid=(1,),
             in_specs=[pl.BlockSpec((count, wide), lambda i, s: (0, 0))],
-            out_specs=[pl.BlockSpec((count, deep), lambda i, s: (0, 0))] * 8,
+            out_specs=[pl.BlockSpec((n, deep), lambda i, s: (0, 0)) for n in rows],
         ),
         cost_estimate=NOMINAL,
     )(slots, value)
@@ -811,25 +821,31 @@
     mlp_column = lax.all_to_all(mine, PLANE, split_axis=0, concat_axis=0, tiled=True)
     mlp_column = mlp_column.reshape(-1, 3 * share)
 
-    def gathered(k, *earlier):
-        piece = after(mlp_column[:, k * 3 * part : (k + 1) * 3 * part], *earlier)
+    def piece_of(k, column):
+        return column[:, k * 3 * part : (k + 1) * 3 * part]
+
+    def gathered(piece):
         return lax.all_gather(piece, "z", axis=0, tiled=True)
 
-    mlp_full = [gathered(0)]
+    mlp_full = [gathered(piece_of(0, mlp_column))]
     sure = positions[0, 0] >= 0
     half = count // 2
 
-    def project(qkv_column, tokens, gift):
-        qkv_blocks = joined_blocks(plane_gather(qkv_column))
+    def project(qkv_column, tokens, gift, mlp_column):
+        qkv_blocks = plane_gather(qkv_column)
         scale_one, unit_one = unit_of(tokens[0].astype(f32))
         qkv = apply_rows(unit_one, qkv_blocks)
         queries, pair = qkv[:, :wide], qkv[:, wide:]
         moves = [behind(d) for d in range(chips, 0, -1)]
-        found, _ = stage([(pair, move) for move in moves] + [(pair, "c"), (gift, "x"), (gift, "y"), (gift, "c")])
+        found, pieces = stage(
+            [(pair, move) for move in moves] + [(pair, "c"), (gift, "x"), (gift, "y"), (gift, "c")],
+            lambda column: [piece_of(k, column) for k in range(1, parts)],
+            [mlp_column],
+        )
         *pairs, pair_c, gift_x, gift_y, gift_c = found
         found, _ = stage([(block, "c") for block in pairs])
         gifts = gift_x, gift_y, gift_c
-        return qkv_blocks[1:], queries, [*pairs, pair, *found, pair_c], gifts, unit_one, scale_one
+        return qkv_blocks[1:], queries, [*pairs, pair, *found, pair_c], gifts, unit_one, scale_one, pieces
 
     def forward(queries, pairs, out_column, tokens, positions, gift_x, gift_y):
         inputs = tokens[0].astype(f32)
@@ -842,9 +858,8 @@
         (out_top, out_bottom, out_x_c, out_y_c), _ = stage(
             [(out_y[:mid], "x"), (out_x[mid:], "y"), (out_x, "c"), (out_y, "c")]
         )
-        out_diag = jnp.concatenate([out_top, out_bottom], 0)
-        (out_diag_c,), _ = stage([(out_diag, "c")])
-        out_blocks = [out_column, out_x, out_c, out_x_c, out_y, out_diag, out_y_c, out_diag_c]
+        out_diag_c, _ = stage([(out_top, "c"), (out_bottom, "c")])
+        out_blocks = [out_column, out_x, out_c, out_x_c, out_y, (out_top, out_bottom), out_y_c, out_diag_c]
         resid = apply_rows(mixed, out_blocks, True, inputs)
         scale_two, unit_two = unit_of(resid)
         (unit_x, unit_y, unit_c), _ = stage([(unit_two, "x"), (unit_two, "y"), (unit_two, "c")])
@@ -853,9 +868,11 @@
         return out_blocks[1:], mixed, mixed_wide, logs, resid, scale_two, unit_blocks, gift_x_c, gift_y_c
 
     qkv_column = after(qkv_column, mlp_column)
-    qkv_blocks, queries, pairs, gifts, unit_one, scale_one = boxed(sure, project, qkv_column, tokens, gift)
+    qkv_blocks, queries, pairs, gifts, unit_one, scale_one, pieces = boxed(
+        sure, project, qkv_column, tokens, gift, mlp_column
+    )
     gift_x, gift_y, gift_c = gifts
-    mlp_full += [gathered(k, pairs[0]) for k in range(1, parts)]
+    mlp_full += [gathered(piece) for piece in pieces]
     out_blocks, mixed, mixed_wide, logs, resid, scale_two, unit_blocks, gift_x_c, gift_y_c = boxed(
         sure, forward, after(queries, mlp_full[0]), pairs, out_column, tokens, positions, gift_x, gift_y
     )
@@ -943,14 +960,11 @@
             [far_sums[4], near_sums[4]],
         )
         received = x_top, x_bottom, y_top, y_bottom
-        return partial, near_sums[2], found, received, far_sums[0], far_out, near_sums[0], near_out, one_d_c
-
-    def rest(keep, found, received, resid, gift, scale_two, far, far_out, near, near_out):
-        grad_resid, grad_attn = resid_grads(keep, found, *received, resid, gift, scale_two)
-        return grad_resid, grad_attn, halved(far, far_out), halved(near, near_out)
-
-    cuts = (1, 2, 2, 1)
-    partial, keep, found, received, *outs, one_d_c = boxed(
+        outs = far_sums[0], far_out, near_sums[0], near_out
+        return partial, (near_sums[2], found, received), outs, one_d_c
+
+    cuts = (1, 1)
+    partial, own_sums, outs, one_d_c = boxed(
         sure,
         middle,
         mlp_full[-per:],
@@ -965,25 +979,24 @@
         gift,
         ones,
     )
-    columns += [lax.psum_scatter(piece, "z", scatter_dimension=0, tiled=True) for piece in partial[:2]]
-    grad_resid, grad_attn, out_far, out_near = boxed(
-        sure, rest, after(keep, *columns[:-2]), found, received, resid, gift, scale_two, *outs
-    )
+    columns += [lax.psum_scatter(piece, "z", scatter_dimension=0, tiled=True) for piece in partial[:1]]
     one_x, one_c, one_x_c, one_y, one_d, one_y_c = ones
-    flat_ones = [unit_one, one_x, one_c, one_x_c, one_y, one_d, one_y_c, one_d_c]
+    flat_ones = [unit_one, one_x, one_y, one_d, one_c, one_x_c, one_y_c, one_d_c]
 
     def joined(own, first, second):
         top, bottom = own if isinstance(own, tuple) else halves(own)
         return jnp.concatenate([total(top, first[2], second[1]), total(bottom, second[0], first[3])], 0)
 
-    def backward(grad_attn, out_far, out_near, queries, pairs, mixed, mixed_wide, logs, out_blocks, positions):
+    def backward(
+        own_sums, outs, resid, scale_two, gift, queries, pairs, mixed, mixed_wide, logs, out_blocks, positions
+    ):
+        keep, found, received = own_sums
+        grad_resid, grad_attn = resid_grads(keep, found, *received, resid, gift, scale_two)
+        out_far, out_near = halved(*outs[:2]), halved(*outs[2:])
+
         def attention(grad_attn):
             grad_mixed = apply_rows(grad_attn, out_blocks)
             return attend_back(queries, grad_mixed, mixed_wide, logs, pairs, positions, size, base)
-
-        def out_sums(grad_attn, mixed, *given):
-            keep, send = row_grads(grad_attn, mixed)
-            return part_sums(keep, swap(send, "c")), given
 
         first, (grad_queries, mine, theirs) = stage(
             [(out_far[0], "x"), (out_far[1], "y"), (out_far[2], "x"), (out_near[1], "y")], attention, [grad_attn]
@@ -991,20 +1004,24 @@
         (found,), _ = stage([(theirs, "c")])
         mine = summed(mine, found)
         second = total(out_far[3], first[1]).astype(low), total(out_near[0], first[0]).astype(low)
-        found, (sums, second) = stage(
-            [(mine[chips - d].astype(low), behind(-d)) for d in range(chips, 0, -1)],
-            out_sums,
-            [grad_attn, mixed, *second],
+        (*found, x_second, y_second), (out_keep, out_send) = stage(
+            [(mine[chips - d].astype(low), behind(-d)) for d in range(chips, 0, -1)]
+            + [(second[0], "x"), (second[1], "y")],
+            lambda *given: row_grads(*given),
+            [grad_attn, mixed],
         )
         grad_pair = total(mine[chips], *found).astype(low)
-        return jnp.concatenate([grad_queries, grad_pair], 1), first, second, sums
-
-    grad_qkv, first, second, sums = boxed(
+        grad_qkv = jnp.concatenate([grad_queries, grad_pair], 1)
+        return grad_qkv, grad_resid, first, (x_second, y_second), out_keep, out_send, (out_near[2], out_near[3])
+
+    grad_qkv, grad_resid, first, second, out_keep, out_send, out_own = boxed(
         sure,
         backward,
-        after(grad_attn, columns[-2]),
-        out_far,
-        out_near,
+        own_sums,
+        outs,
+        after(resid, columns[0]),
+        scale_two,
+        gift,
         queries,
         pairs,
         mixed,
@@ -1014,41 +1031,47 @@
         positions,
     )
     columns += [
-        lax.psum_scatter(after(piece, grad_qkv), "z", scatter_dimension=0, tiled=True) for piece in partial[2:]
+        lax.psum_scatter(after(piece, grad_qkv), "z", scatter_dimension=0, tiled=True) for piece in partial[1:]
     ]
 
-    def collect(grad_qkv, second, sums, grad_resid, qkv_blocks, flat_ones, scale_one, tokens):
-        diag_top, diag_bottom, x_top, _, _, y_bottom, _ = sums
-        own, *others = spread(grad_qkv)
-
-        def results(grad_qkv):
+    def collect(
+        grad_qkv, first, second, out_own, out_keep, out_send, grad_resid, resid, qkv_blocks, flat_ones, scale_one, tokens
+    ):
+        own, to_c, to_x, to_y, to_d = spread(grad_qkv)
+
+        def tokens_grads(grad_qkv):
             grad_unit_one = apply_rows(grad_qkv, qkv_blocks, True)
             return grad_resid + unit_back(grad_unit_one, tokens[0].astype(f32), scale_one)
 
-        found, grad_tokens = stage(
-            [(value, across(r + 1)) for r, value in enumerate(others)], results, [grad_qkv]
+        (by_x, by_y, by_d, out_found), grad_tokens = stage(
+            [(to_x, "x"), (to_y, "y"), (to_d, across(5)), (out_send, "c")], tokens_grads, [grad_qkv]
         )
-        (*started, x_second, y_second), qkv_column = stage(
-            [
-                (diag_top, "x"),
-                (diag_bottom, "y"),
-                (x_top, "x"),
-                (y_bottom, "y"),
-                (second[0], "x"),
-                (second[1], "y"),
-            ],
-            lambda *gathered: token_grads(flat_ones, jnp.concatenate(gathered, 0)),
-            [own, *found],
+        on = jnp.concatenate([to_c, by_x[count:], by_y[count:], by_d[count:]], 0)
+        (by_c,), out_parts = stage([(on, "c")], lambda *given: part_sums(*given), [out_keep, out_found])
+        diag_top, diag_bottom, x_top, x_bottom, y_top, y_bottom, out_sums = out_parts
+
+        def sums(resid, *gathered):
+            gathered = jnp.concatenate(gathered, 0)
+            return token_grads(flat_ones, gathered), resid + joined(out_own, first, second)
+
+        started, (qkv_column, output) = stage(
+            [(diag_top, "x"), (diag_bottom, "y"), (x_top, "x"), (y_bottom, "y")],
+            sums,
+            [resid, own, by_x[:count], by_y[:count], by_d[:count], by_c],
         )
-        return qkv_column, grad_tokens, started, (x_second, y_second)
-
-    qkv_column, grad_tokens, started, second = boxed(
+        return qkv_column, grad_tokens, output, x_bottom, y_top, out_sums, started
+
+    qkv_column, grad_tokens, output, x_bottom, y_top, out_sums, started = boxed(
         sure,
         collect,
-        after(grad_qkv, columns[2]),
+        after(grad_qkv, columns[1]),
+        first,
         second,
-        sums,
+        out_own,
+        out_keep,
+        out_send,
         grad_resid,
+        resid,
         qkv_blocks,
         flat_ones,
         scale_one,
@@ -1056,24 +1079,21 @@
     )
     qkv_low = lax.psum_scatter(qkv_column, "z", scatter_dimension=0, tiled=True)
 
-    def end(sums, started, first, second, out_near, resid):
-        _, _, _, x_bottom, y_top, _, own = sums
+    def end(x_bottom, y_top, out_sums, started):
         x_bottom, y_top = total(x_bottom, started[1]).astype(low), total(y_top, started[0]).astype(low)
-        received, output = stage(
-            [(x_bottom, "x"), (y_top, "y")],
-            lambda resid: resid + joined((out_near[2], out_near[3]), first, second),
-            [resid],
-        )
-        column = joined(own, started, received).astype(low)
-        return output, column.reshape(-1, column.shape[-1])
-
-    output, out_column = boxed(sure, end, sums, started, first, second, out_near, after(resid, *columns[3:]))
+        received, _ = stage([(x_bottom, "x"), (y_top, "y")])
+        column = joined(out_sums, started, received).astype(low)
+        return column.reshape(-1, column.shape[-1])
+
+    out_column = boxed(sure, end, after(x_bottom, columns[-1]), y_top, out_sums, started)
     out_sum = lax.psum_scatter(out_column, "z", scatter_dimension=0, tiled=True).astype(f32)
-    every = jnp.concatenate([*columns, qkv_low], 1)
+    every = jnp.concatenate(columns, 1)
     every = after(every, out_column).reshape(8, -1, every.shape[1])
     every = lax.all_to_all(every, PLANE, split_axis=0, concat_axis=0, tiled=True)
     deep = qkv_low.shape[1]
-    qkv_sum = jnp.swapaxes(every[:, :, -deep:], 0, 1).reshape(-1, 8 * deep).astype(f32)
+    qkv_sum = after(qkv_low, every).reshape(8, -1, deep)
+    qkv_sum = lax.all_to_all(qkv_sum, PLANE, split_axis=0, concat_axis=0, tiled=True)
+    qkv_sum = jnp.swapaxes(qkv_sum, 0, 1).reshape(-1, 8 * deep).astype(f32)
     query_sum = qkv_sum[:, :wide]
     key_sum = qkv_sum[:, wide : wide + size]
     value_sum = qkv_sum[:, wide + size :]

time: 1050 us -> 997 us (0.950)
  waiting for transfers between devices: 413 us -> 372 us
    reduce_scatter x1, waiting for transfers between devices: 31.7 us -> 4.53 us  [local(): lax.psum_scatter(out_column, 'z', scatter_dimension=0, tiled=True)]
    reduce_scatter x2 -> x1, waiting for transfers between devices: 19.4 us -> 0.02 us  [local(): lax.psum_scatter(piece, 'z', scatter_dimension=0, tiled=True)]
    ppermute x6, waiting for transfers between devices: 38.7 us -> 55 us  [behind(): return lambda value: lax.ppermute(value, ('z', 'y'), pairs)]
    ppermute x66 -> x70, waiting for transfers between devices: 234 us -> 218 us  [swap(): return lax.ppermute(value, axis, [(0, 1), (1, 0)])]
    all_to_all x1, waiting for transfers between devices: 17.3 us -> 30.4 us  [local(): lax.all_to_all(every, PLANE, split_axis=0, concat_axis=0, tiled=True)]
    ppermute x7 -> x1, starting transfers between devices: 13.8 us -> 0.88 us  [across(): lax.ppermute(value, PLANE, [(i, i ^ distance) for i in range(8)])]
    ppermute x66 -> x70, starting transfers between devices: 45.7 us -> 53.3 us  [swap(): return lax.ppermute(value, axis, [(0, 1), (1, 0)])]
  transfers between devices with their start and end apart: 94 -> 91, of which waited for: 42 -> 45; matrix products, arithmetic and copies ran while one was open for 7% -> 7% of each run, Pallas kernels for 40% -> 43%
where the time goes in v8:
time: 997 us; the launch traced here: 982 us
  Pallas kernels  423 us (42%)
  waiting for transfers between devices  372 us (37%)
  starting transfers between devices  85.3 us (9%)
  other arithmetic  47.6 us (5%)
  local copies, waits for them, and re-layouts  37.2 us (4%)
  between operations  15.1 us (2%)
    ppermute x70, waiting for transfers between devices, swap(): return lax.ppermute(value, axis, [(0, 1), (1, 0)])  218 us
    pallas_call x4, Pallas kernels, mlp(): pl.pallas_call(functools.partial(mlp_kernel, each // 3, per, tiles), out_...  155 us
    pallas_call x2, Pallas kernels, mlp_grads(): pl.pallas_call(functools.partial(mlp_grads_kernel, len(units)), out_shape...  75.6 us
    ppermute x6, waiting for transfers between devices, behind(): return lambda value: lax.ppermute(value, ('z', 'y'), pairs)  55 us
    ppermute x70, starting transfers between devices, swap(): return lax.ppermute(value, axis, [(0, 1), (1, 0)])  53.3 us
    pallas_call x4, Pallas kernels, apply_rows(): pl.pallas_call(functools.partial(kernel, layout), out_shape=shape, grid_s...  45.6 us
    all_to_all x1, waiting for transfers between devices, local(): lax.all_to_all(mine, PLANE, split_axis=0, concat_axis=0, tiled=True)  44.6 us
    pallas_call x1, Pallas kernels, attend_back(): pl.pallas_call(functools.partial(attend_back_kernel, size, size ** (-0.5)...  35.6 us
  transfers between devices with their start and end apart: 91, of which 45 were waited for; matrix products, arithmetic and copies ran while one was open for 7% of the time, Pallas kernels for 43%

profile of v8, /device:TPU:0, one launch (start us, length us, event | category | flops | bytes accessed | tf_op | source)
XLA Modules:
  0.0 982.2 jit_solution(5697412120193088567)
XLA Ops:
  20.7 44.6 %all-to-all-done = bf16[8,80,3072]{2,1,0:T(8,128)(2,1)} async-done(((bf16[8,80,3072]{2,1,0:T(8,128)(2,1)}), bf16[8,80,3072]{2,1,0:T(8,128)(2,1)}, u32[]{:S(2)}, u32[]{:S(2)}) %all-to-all-start) | async-done | bytes 3932192 | tf_op jit(solution)/shard_map/all_to_all | solution.py:821
  69.6 145.3 %conditional.7 = (bf16[4,80,3072]{2,1,0:T(8,128)(2,1)}, bf16[4,80,3072]{2,1,0:T(8,128)(2,1)}, bf16[4,80,3072]{2,1,0:T(8,128)(2,1)}, bf16[4,80,3072]{2,1,0:T(8,12...) conditional(s32[]{:T(128)} %bitcast.16, () %tuple.122, ...), branch_computations={%region_0.0_spmd, %region_1.0_spmd} | conditional | flops 6947220 | bytes 125057264 | solution.py:60
  71.6 43.0 %collective-permute-done.52.rest_4_ = bf16[4,80,3072]{2,1,0:T(8,128)(2,1)} collective-permute-done((bf16[4,80,3072]{2,1,0:T(8,128)(2,1)}, bf16[4,80,3072]{2,1,0:T(8,128)(2,1)}, u32[]{:S(2)}, u32[]{:S(2)}) %collective-permute-start.52) | collective-permute-done | bytes 1966112 | tf_op jit(solution)/shard_map/cond/branch_1_fun/ppermute | solution.py:28
  121.9 17.9 %collective-permute-done.53.rest_5_ = bf16[2,80,3072]{2,1,0:T(8,128)(2,1)S(1)} collective-permute-done((bf16[2,80,3072]{2,1,0:T(8,128)(2,1)}, bf16[2,80,3072]{2,1,0:T(8,128)(2,1)S(1)}, u32[]{:S(2)}, u32[]{:S(2)}) %collective-permute-start.53) | collective-permute-done | bytes 983072 | tf_op jit(solution)/shard_map/cond/branch_1_fun/ppermute | solution.py:28
  145.6 11.9 %branch_1_fun.21 = bf16[384,3072]{1,0:T(8,128)(2,1)S(1)} custom-call(s32[8]{0:T(128)S(1)} %iota_xor_fusion.slots, bf16[384,2560]{1,0:T(8,128)(2,1)} %fusion.1.left, bf16[4,80,3072]{2,1,0:T(8,128)(2,1)} %get-tuple-element.277.rest_0_, bf16[4,80,3072]{2,1,0:T(8,128)(2,1)} %collective-permute-done.49.rest_1_, ...), custom_call_target="tpu_custom_call" | custom-call | flops 1048576 | bytes 4096 | tf_op jit(solution)/shard_map/cond/branch_1_fun/pallas_call | solution.py:318
  169.3 13.6 %collective-permute-done.58 = bf16[384,512]{1,0:T(8,128)(2,1)} collective-permute-done((bf16[384,512]{1,0:T(8,128)(2,1)S(1)}, bf16[384,512]{1,0:T(8,128)(2,1)}, u32[]{:S(2)}, u32[]{:S(2)}) %collective-permute-start.58) | collective-permute-done | bytes 393248 | tf_op jit(solution)/shard_map/cond/branch_1_fun/ppermute | solution.py:80
  187.6 10.0 %collective-permute-done.59 = bf16[384,512]{1,0:T(8,128)(2,1)} collective-permute-done((bf16[384,512]{1,0:T(8,128)(2,1)S(1)}, bf16[384,512]{1,0:T(8,128)(2,1)}, u32[]{:S(2)}, u32[]{:S(2)}) %collective-permute-start.59) | collective-permute-done | bytes 393248 | tf_op jit(solution)/shard_map/cond/branch_1_fun/ppermute | solution.py:80
  201.1 10.6 %collective-permute-done.60 = bf16[384,512]{1,0:T(8,128)(2,1)} collective-permute-done((bf16[384,512]{1,0:T(8,128)(2,1)S(1)}, bf16[384,512]{1,0:T(8,128)(2,1)}, u32[]{:S(2)}, u32[]{:S(2)}) %collective-permute-start.60) | collective-permute-done | bytes 393248 | tf_op jit(solution)/shard_map/cond/branch_1_fun/ppermute | solution.py:80
  216.2 141.0 %conditional.8 = (bf16[4,80,2560]{2,1,0:T(8,128)(2,1)}, bf16[4,80,2560]{2,1,0:T(8,128)(2,1)}, bf16[4,80,2560]{2,1,0:T(8,128)(2,1)}, bf16[4,80,2560]{2,1,0:T(8,12...) conditional(s32[]{:T(128)} %bitcast.16, () %tuple.120, ...), branch_computations={%region_3.0_spmd, %region_4.0_spmd} | conditional | flops 7012756 | bytes 129779728 | solution.py:60
  220.2 28.8 %branch_1_fun.22 = (bf16[384,2560]{1,0:T(8,128)(2,1)}, f32[384,2560]{1,0:T(8,128)}, f32[15,1,256]{2,1,0:T(1,128)S(1)}) custom-call(s32[1]{0:T(128)} %bitcast.2.core, s32[1,384]{1,0:T(1,128)S(1)} %get-tuple-element.322.places, bf16[384,2560]{1,0:T(8,128)(2,1)} %get-tuple-element.323.queries, bf16[384,512]{1,0:T(8,128)(2,1)} %get-tuple-element.324.rest_0_, ...), custom_call_target="tpu_custom_call" | custom-call | flops 1048576 | bytes 4096 | tf_op jit(solution)/shard_map/cond/branch_1_fun/pallas_call | solution.py:195
  264.5 17.0 %collective-permute-done.26.rest_6_ = bf16[2,80,2560]{2,1,0:T(8,128)(2,1)S(1)} collective-permute-done((bf16[2,80,2560]{2,1,0:T(8,128)(2,1)}, bf16[2,80,2560]{2,1,0:T(8,128)(2,1)S(1)}, u32[]{:S(2)}, u32[]{:S(2)}) %collective-permute-start.26) | collective-permute-done | bytes 819232 | tf_op jit(solution)/shard_map/cond/branch_1_fun/ppermute | solution.py:28
  286.8 11.9 %branch_1_fun.23 = f32[384,2560]{1,0:T(8,128)} custom-call(s32[8]{0:T(128)S(1)} %iota_xor_fusion.1.slots, bf16[384,2560]{1,0:T(8,128)(2,1)} %get-tuple-element.1185.left, f32[384,2560]{1,0:T(8,128)S(1)} %bitcast_convert_fusion.rest_0_, bf16[4,80,2560]{2,1,0:T(8,128)(2,1)S(1)} %copy-done.18, bf16[4,80,2560]{2,1,0:T(8,128)(2,1)} %collective-permute-done.21.rest_2_, ...), custom_call_target="tpu_custom_call" | custom-call | flops 1048576 | bytes 4096 | tf_op jit(solution)/shard_map/cond/branch_1_fun/pallas_call | solution.py:318
  306.9 43.1 %collective-permute-done.32 = bf16[384,2560]{1,0:T(8,128)(2,1)} collective-permute-done((bf16[384,2560]{1,0:T(8,128)(2,1)}, bf16[384,2560]{1,0:T(8,128)(2,1)}, u32[]{:S(2)}, u32[]{:S(2)}) %collective-permute-start.32) | collective-permute-done | bytes 1966112 | tf_op jit(solution)/shard_map/cond/branch_1_fun/ppermute | solution.py:28
  357.2 136.9 %conditional.9 = (bf16[384,2560]{1,0:T(8,128)(2,1)}, bf16[384,2560]{1,0:T(8,128)(2,1)}, bf16[384,2560]{1,0:T(8,128)(2,1)}, bf16[384,2560]{1,0:T(8,128)(2,1)}, bf...) conditional(s32[]{:T(128)} %bitcast.16, () %tuple.119, ...), branch_computations={%region_6.0_spmd, %region_7.0_spmd} | conditional | flops 3145728 | bytes 86520392 | solution.py:60
  360.8 36.8 %branch_1_fun.24 = (bf16[768,2560]{1,0:T(8,128)(2,1)}, bf16[768,2560]{1,0:T(8,128)(2,1)}, bf16[768,2560]{1,0:T(8,128)(2,1)}, bf16[768,2560]{1,0:T(8,128)(2,1)}, bf16[1536,1536]{1,0:T(8,128)(2,1)}) custom-call(bf16[2560,768]{1,0:T(8,128)(2,1)} %get-tuple-element.398.rest_0_, bf16[2560,768]{1,0:T(8,128)(2,1)} %get-tuple-element.399.rest_1_, ...), custom_call_target="tpu_custom_call" | custom-call | flops 1048576 | bytes 4096 | tf_op jit(solution)/shard_map/cond/branch_1_fun/pallas_call | solution.py:466
  411.1 37.3 %branch_1_fun.25 = (bf16[768,2560]{1,0:T(8,128)(2,1)}, bf16[768,2560]{1,0:T(8,128)(2,1)}, bf16[768,2560]{1,0:T(8,128)(2,1)}, bf16[768,2560]{1,0:T(8,128)(2,1)}, bf16[1536,1536]{1,0:T(8,128)(2,1)}) custom-call(bf16[2560,768]{1,0:T(8,128)(2,1)} %get-tuple-element.398.rest_0_, bf16[2560,768]{1,0:T(8,128)(2,1)} %get-tuple-element.399.rest_1_, ...), custom_call_target="tpu_custom_call" | custom-call | flops 1048576 | bytes 4096 | tf_op jit(solution)/shard_map/cond/branch_1_fun/pallas_call | solution.py:466
  451.8 37.8 %branch_1_fun.26 = bf16[2560,1536]{1,0:T(8,128)(2,1)} custom-call(bf16[384,2560]{1,0:T(8,128)(2,1)} %collective-permute-done.rest_2_.rest_0_, bf16[384,2560]{1,0:T(8,128)(2,1)} %get-tuple-element.400.rest_4_.rest_1_, bf16[384,2560]{1,0:T(8,128)(2,1)} %collective-permute-done.2.rest_6_.rest_2_, bf16[384,2560]{1,0:T(8,128)(2,1)} %get-tuple-element.401.rest_8_.rest_3_, ...), custom_call_target="tpu_custom_call" | custom-call | flops 1048576 | bytes 4096 | tf_op jit(solution)/shard_map/cond/branch_1_fun/pallas_call | solution.py:529
  495.7 159.1 %conditional.10 = (bf16[2560,768]{1,0:T(8,128)(2,1)}, bf16[2560,768]{1,0:T(8,128)(2,1)}, bf16[768,2560]{1,0:T(8,128)(2,1)}, bf16[768,2560]{1,0:T(8,128)(2,1)}, b...) conditional(s32[]{:T(128)} %bitcast.16, () %tuple.118, ...), branch_computations={%region_8.0_spmd, %region_9.0_spmd} | conditional | flops 5242880 | bytes 94392864 | solution.py:60
  495.7 40.6 %branch_1_fun.27 = (bf16[768,2560]{1,0:T(8,128)(2,1)}, bf16[768,2560]{1,0:T(8,128)(2,1)}, bf16[768,2560]{1,0:T(8,128)(2,1)}, bf16[768,2560]{1,0:T(8,128)(2,1)}, bf16[1536,1536]{1,0:T(8,128)(2,1)}) custom-call(bf16[2560,768]{1,0:T(8,128)(2,1)} %get-tuple-element.434.rest_0_, bf16[2560,768]{1,0:T(8,128)(2,1)} %get-tuple-element.435.rest_1_, ...), custom_call_target="tpu_custom_call" | custom-call | flops 1048576 | bytes 4096 | tf_op jit(solution)/shard_map/cond/branch_1_fun/pallas_call | solution.py:466
  554.6 40.7 %branch_1_fun.29 = (bf16[768,2560]{1,0:T(8,128)(2,1)}, bf16[768,2560]{1,0:T(8,128)(2,1)}, bf16[768,2560]{1,0:T(8,128)(2,1)}, bf16[768,2560]{1,0:T(8,128)(2,1)}, bf16[1536,1536]{1,0:T(8,128)(2,1)}) custom-call(bf16[2560,768]{1,0:T(8,128)(2,1)} %get-tuple-element.434.rest_0_, bf16[2560,768]{1,0:T(8,128)(2,1)} %get-tuple-element.435.rest_1_, ...), custom_call_target="tpu_custom_call" | custom-call | flops 1048576 | bytes 4096 | tf_op jit(solution)/shard_map/cond/branch_1_fun/pallas_call | solution.py:466
  612.6 37.8 %branch_1_fun.31 = (bf16[2560,768]{1,0:T(8,128)(2,1)}, bf16[2560,768]{1,0:T(8,128)(2,1)}) custom-call(bf16[384,2560]{1,0:T(8,128)(2,1)} %get-tuple-element.436.rest_2_.rest_0_, bf16[384,2560]{1,0:T(8,128)(2,1)} %get-tuple-element.438.rest_4_.rest_1_, bf16[384,2560]{1,0:T(8,128)(2,1)} %get-tuple-element.440.rest_6_.rest_2_, ...), custom_call_target="tpu_custom_call" | custom-call | flops 1048576 | bytes 4096 | tf_op jit(solution)/shard_map/cond/branch_1_fun/pallas_call | solution.py:529
  656.0 127.3 %conditional.11 = (bf16[384,3072]{1,0:T(8,128)(2,1)}, f32[384,2560]{1,0:T(8,128)}, bf16[192,2560]{1,0:T(8,128)(2,1)}, bf16[192,2560]{1,0:T(8,128)(2,1)}, bf16[19...) conditional(s32[]{:T(128)} %bitcast.16, () %tuple.117, ...), branch_computations={%region_11.0_spmd, %region_12.0_spmd} | conditional | flops 18678836 | bytes 111313032 | solution.py:60
  695.3 35.6 %branch_1_fun.36 = (bf16[384,2560]{1,0:T(8,128)(2,1)}, f32[4,384,512]{2,1,0:T(8,128)}, bf16[4,384,512]{2,1,0:T(8,128)(2,1)}) custom-call(s32[1]{0:T(128)} %bitcast.5.core, s32[1,384]{1,0:T(1,128)S(1)} %get-tuple-element.536.places, bf16[384,2560]{1,0:T(8,128)(2,1)} %get-tuple-element.537.queries, bf16[384,2560]{1,0:T(8,128)(2,1)} %copy-done.2, ...), custom_call_target="tpu_custom_call" | custom-call | flops 1048576 | bytes 4096 | tf_op jit(solution)/shard_map/cond/branch_1_fun/pallas_call | solution.py:228
  746.0 13.2 %branch_1_fun.37 = (bf16[4,4,80,2560]{3,2,1,0:T(8,128)(2,1)}, bf16[4,4,80,2560]{3,2,1,0:T(8,128)(2,1)}) custom-call(s32[8]{0:T(128)S(1)} %gather_fusion, bf16[384,2560]{1,0:T(8,128)(2,1)S(1)} %copy-done.1, bf16[384,2560]{1,0:T(8,128)(2,1)} %get-tuple-element.577.right), custom_call_target="tpu_custom_call" | custom-call | flops 1048576 | bytes 4096 | tf_op jit(solution)/shard_map/cond/branch_1_fun/pallas_call | solution.py:367
  785.2 90.1 %conditional.12 = (bf16[2560,384]{1,0:T(8,128)(2,1)}, bf16[2,80,2560]{2,1,0:T(8,128)(2,1)}, bf16[2,80,2560]{2,1,0:T(8,128)(2,1)}, bf16[4,80,2560]{2,1,0:T(8,128)...) conditional(s32[]{:T(128)} %bitcast.16, () %tuple.116, ((), ...), branch_computations={%region_14.0_spmd, %region_15.17_spmd} | conditional | flops 25624604 | bytes 105411296 | solution.py:60
  795.0 12.2 %branch_1_fun.39 = f32[384,2560]{1,0:T(8,128)S(1)} custom-call(s32[8]{0:T(128)S(1)} %get-tuple-element.1087.slots, bf16[384,3072]{1,0:T(8,128)(2,1)} %get-tuple-element.605.value.left, bf16[4,80,3072]{2,1,0:T(8,128)(2,1)} %get-tuple-element.606.rest_0_, bf16[4,80,3072]{2,1,0:T(8,128)(2,1)} %get-tuple-element.607.rest_1_, ...), custom_call_target="tpu_custom_call" | custom-call | flops 1048576 | bytes 4096 | tf_op jit(solution)/shard_map/cond/branch_1_fun/pallas_call | solution.py:318
  844.1 14.1 %branch_1_fun.41 = bf16[2560,384]{1,0:T(8,128)(2,1)} custom-call(bf16[384,2560]{1,0:T(8,128)(2,1)} %get-tuple-element.643.rest_0_, bf16[384,2560]{1,0:T(8,128)(2,1)} %get-tuple-element.644.rest_1_, bf16[384,2560]{1,0:T(8,128)(2,1)} %get-tuple-element.645.rest_2_, bf16[384,2560]{1,0:T(8,128)(2,1)} %get-tuple-element.646.rest_3_, ...), custom_call_target="tpu_custom_call" | custom-call | flops 1048576 | bytes 4096 | tf_op jit(solution)/shard_map/cond/branch_1_fun/pallas_call | solution.py:564
  862.9 12.2 %collective-permute-done.75 = bf16[2,80,2560]{2,1,0:T(8,128)(2,1)} collective-permute-done((bf16[2,80,2560]{2,1,0:T(8,128)(2,1)S(1)}, bf16[2,80,2560]{2,1,0:T(8,128)(2,1)}, u32[]{:S(2)}, u32[]{:S(2)}) %collective-permute-start.75) | collective-permute-done | bytes 819232 | tf_op jit(solution)/shard_map/cond/branch_1_fun/ppermute | solution.py:28
  875.3 26.0 %conditional.13 = (bf16[320,2560]{1,0:T(8,128)(2,1)S(1)}) conditional(s32[]{:T(128)} %bitcast.16, () %tuple.135, (bf16[4,80,2560]{2,1,0:T(8,128)(2,1)}, bf16[2,80,2560]{2,1,0:T(8,128)(2,1)}, bf16[2,80,2560]{2,1,0:T(8,128)(2,1)}, bf16[2,80,2560]{2,1,0:T(8,128)(2,1)}, bf16[2,80,2560]{2,1,0:T(8,128)(2,1)}, /*index=5*/bf16[2,80,2560]{2,1,0:T(8,128)(2,1)}, ...), branch_computations={%region_19.0_spmd, %region_20.0_spmd} | conditional | flops 9011200 | bytes 21299288 | solution.py:60
  880.1 17.4 %collective-permute-done.37 = bf16[2,80,2560]{2,1,0:T(8,128)(2,1)S(1)} collective-permute-done((bf16[2,80,2560]{2,1,0:T(8,128)(2,1)S(1)}, bf16[2,80,2560]{2,1,0:T(8,128)(2,1)S(1)}, u32[]{:S(2)}, u32[]{:S(2)}) %collective-permute-start.37) | collective-permute-done | bytes 819232 | tf_op jit(solution)/shard_map/cond/branch_1_fun/ppermute | solution.py:28
  911.1 14.5 %reduce-scatter.10.cloned.1.call-done = bf16[640,384]{1,0:T(8,128)(2,1)} async-done(((bf16[2560,384]{1,0:T(8,128)(2,1)}), bf16[640,384]{1,0:T(8,128)(2,1)}) %reduce-scatter.10.cloned.1.call-update) | async-done | bytes 491536 | tf_op jit(solution)/shard_map/reduce_scatter | solution.py:1080
  925.6 30.4 %all-to-all-done.1.whole = bf16[8,80,3072]{2,1,0:T(8,128)(2,1)} async-done(((bf16[8,80,3072]{2,1,0:T(8,128)(2,1)}), bf16[8,80,3072]{2,1,0:T(8,128)(2,1)}, u32[]{:S(2)}, u32[]{:S(2)}) %all-to-all-start.1) | async-done | bytes 3932192 | tf_op jit(solution)/shard_map/all_to_all | solution.py:1092
  (337 shorter events, 332.3 us)
Async XLA Ops:
  14.3 51.0 %all-to-all-start = ((bf16[8,80,3072]{2,1,0:T(8,128)(2,1)}), bf16[8,80,3072]{2,1,0:T(8,128)(2,1)}, u32[]{:S(2)}, u32[]{:S(2)}) async-start(bf16[8,80,3072]{2,1,0:T(8,128)(2,1)} %shard_map.223), calls=%async_computation | async-start | bytes 7864320 | tf_op jit(solution)/shard_map/all_to_all | solution.py:821
  19.6 49.9 %all-gather.8.cloned.1.call-start = ((), (), s32[]{:S(2)}) async-start(), calls=%async_computation.8 | async-start | bytes 2457600 | tf_op jit(solution)/shard_map/all_gather | solution.py:811
  20.7 195.5 %all-gather.10.cloned.1.call-start = ((), (), s32[]{:S(2)}) async-start(), calls=%async_computation.9 | async-start | bytes 4915200 | tf_op jit(solution)/shard_map/all_gather | solution.py:828
  67.6 148.6 %all-gather.18.cloned.1.call-start = ((), (), s32[]{:S(2)}) async-start(), calls=%async_computation.18 | async-start | bytes 2048000 | tf_op jit(solution)/shard_map/all_gather | solution.py:812
  68.3 288.9 %all-gather.12.cloned.1.call-start = ((), (), s32[]{:S(2)}) async-start(), calls=%async_computation.10 | async-start | bytes 4915200 | tf_op jit(solution)/shard_map/all_gather | solution.py:828
  69.6 45.0 %collective-permute-start.52 = (bf16[4,80,3072]{2,1,0:T(8,128)(2,1)}, bf16[4,80,3072]{2,1,0:T(8,128)(2,1)}, u32[]{:S(2)}, u32[]{:S(2)}) collective-permute-start(bf16[4,80,3072]{2,1,0:T(8,128)(2,1)} %get-tuple-element.277.rest_0_), channel_id=1, source_target_pairs={{0,4},{4,0},{1,5},{5,1},{2,6},{6,2},{3,7},{7,3},{8,12},{12,8},{9,1... | collective-permute-start | bytes 5898248 | tf_op jit(solution)/shard_map/cond/branch_1_fun/ppermute | solution.py:28
  70.3 47.3 %collective-permute-start.49 = (bf16[4,80,3072]{2,1,0:T(8,128)(2,1)}, bf16[4,80,3072]{2,1,0:T(8,128)(2,1)}, u32[]{:S(2)}, u32[]{:S(2)}) collective-permute-start(bf16[4,80,3072]{2,1,0:T(8,128)(2,1)} %get-tuple-element.277.rest_0_), channel_id=1, source_target_pairs={{0,1},{1,0},{2,3},{3,2},{4,5},{5,4},{6,7},{7,6},{8,9},{9,8},{10,11... | collective-permute-start | bytes 5898248 | tf_op jit(solution)/shard_map/cond/branch_1_fun/ppermute | solution.py:28
  157.6 54.1 %collective-permute-start.62 = (bf16[384,2560]{1,0:T(8,128)(2,1)S(1)}, bf16[384,2560]{1,0:T(8,128)(2,1)}, u32[]{:S(2)}, u32[]{:S(2)}) collective-permute-start(bf16[384,2560]{1,0:T(8,128)(2,1)S(1)} %copy-done.12), channel_id=1, source_target_pairs={{0,1},{1,0},{2,3},{3,2},{4,5},{5,4},{6,7},{7,6},{8,9},{9,8},{10,11... | collective-permute-start | bytes 5898248 | tf_op jit(solution)/shard_map/cond/branch_1_fun/ppermute | solution.py:28
  159.4 52.3 %collective-permute-start.63 = (bf16[384,2560]{1,0:T(8,128)(2,1)S(1)}, bf16[384,2560]{1,0:T(8,128)(2,1)}, u32[]{:S(2)}, u32[]{:S(2)}) collective-permute-start(bf16[384,2560]{1,0:T(8,128)(2,1)S(1)} %copy-done.12), channel_id=1, source_target_pairs={{0,4},{4,0},{1,5},{5,1},{2,6},{6,2},{3,7},{7,3},{8,12},{12,8},{9,1... | collective-permute-start | bytes 5898248 | tf_op jit(solution)/shard_map/cond/branch_1_fun/ppermute | solution.py:28
  161.1 50.5 %collective-permute-start.64 = (bf16[384,2560]{1,0:T(8,128)(2,1)S(1)}, bf16[384,2560]{1,0:T(8,128)(2,1)}, u32[]{:S(2)}, u32[]{:S(2)}) collective-permute-start(bf16[384,2560]{1,0:T(8,128)(2,1)S(1)} %copy-done.12), channel_id=1, source_target_pairs={{0,2},{2,0},{1,3},{3,1},{4,6},{6,4},{5,7},{7,5},{8,10},{10,8},{9,1... | collective-permute-start | bytes 5898248 | tf_op jit(solution)/shard_map/cond/branch_1_fun/ppermute | solution.py:28
  214.9 279.3 %all-gather.14.cloned.1.call-start = ((), (), s32[]{:S(2)}) async-start(), calls=%async_computation.11 | async-start | bytes 4915200 | tf_op jit(solution)/shard_map/all_gather | solution.py:828
  215.5 278.7 %all-gather.16.cloned.1.call-start = ((), (), s32[]{:S(2)}) async-start(), calls=%async_computation.12 | async-start | bytes 4915200 | tf_op jit(solution)/shard_map/all_gather | solution.py:828
  216.1 438.8 %reduce-scatter.6.cloned.1.call-start = ((), (), s32[]{:S(2)}) async-start(), calls=%async_computation.13 | async-start | bytes 9830400 | tf_op jit(solution)/shard_map/reduce_scatter | solution.py:935
  304.8 45.2 %collective-permute-start.32 = (bf16[384,2560]{1,0:T(8,128)(2,1)}, bf16[384,2560]{1,0:T(8,128)(2,1)}, u32[]{:S(2)}, u32[]{:S(2)}) collective-permute-start(bf16[384,2560]{1,0:T(8,128)(2,1)} %multiply_convert_fusion), channel_id=1, source_target_pairs={{0,1},{1,0},{2,3},{3,2},{4,5},{5,4},{6,7},{7,6},{8,9},{9,8},{10,11... | collective-permute-start | bytes 5898248 | tf_op jit(solution)/shard_map/cond/branch_1_fun/ppermute | solution.py:28
  305.2 44.9 %collective-permute-start.33 = (bf16[384,2560]{1,0:T(8,128)(2,1)}, bf16[384,2560]{1,0:T(8,128)(2,1)}, u32[]{:S(2)}, u32[]{:S(2)}) collective-permute-start(bf16[384,2560]{1,0:T(8,128)(2,1)} %multiply_convert_fusion), channel_id=1, source_target_pairs={{0,4},{4,0},{1,5},{5,1},{2,6},{6,2},{3,7},{7,3},{8,12},{12,8},{9,1... | collective-permute-start | bytes 5898248 | tf_op jit(solution)/shard_map/cond/branch_1_fun/ppermute | solution.py:28
  357.4 45.2 %collective-permute-start = (bf16[384,2560]{1,0:T(8,128)(2,1)}, bf16[384,2560]{1,0:T(8,128)(2,1)}, u32[]{:S(2)}, u32[]{:S(2)}) collective-permute-start(bf16[384,2560]{1,0:T(8,128)(2,1)} %get-tuple-element.375.rest_2_.rest_4_), channel_id=1, source_target_pairs={{0,1},{1,0},{2,3},{3,2},{4,5},{5,4},{6,7},{7,6},{8,9},{9,8},{10,11... | collective-permute-start | bytes 5898248 | tf_op jit(solution)/shard_map/cond/branch_1_fun/ppermute | solution.py:28
  359.1 44.9 %collective-permute-start.1 = (bf16[384,2560]{1,0:T(8,128)(2,1)}, bf16[384,2560]{1,0:T(8,128)(2,1)}, u32[]{:S(2)}, u32[]{:S(2)}) collective-permute-start(bf16[384,2560]{1,0:T(8,128)(2,1)} %get-tuple-element.372.rest_5_.rest_9_), channel_id=1, source_target_pairs={{0,4},{4,0},{1,5},{5,1},{2,6},{6,2},{3,7},{7,3},{8,12},{12,8},{9,1... | collective-permute-start | bytes 5898248 | tf_op jit(solution)/shard_map/cond/branch_1_fun/ppermute | solution.py:28
  404.5 45.0 %collective-permute-start.4 = (bf16[384,2560]{1,0:T(8,128)(2,1)}, bf16[384,2560]{1,0:T(8,128)(2,1)}, u32[]{:S(2)}, u32[]{:S(2)}) collective-permute-start(bf16[384,2560]{1,0:T(8,128)(2,1)} %get-tuple-element.397), channel_id=1, source_target_pairs={{0,1},{1,0},{2,3},{3,2},{4,5},{5,4},{6,7},{7,6},{8,9},{9,8},{10,11... | collective-permute-start | bytes 5898248 | tf_op jit(solution)/shard_map/cond/branch_1_fun/ppermute | solution.py:28
  404.9 44.8 %collective-permute-start.5 = (bf16[384,2560]{1,0:T(8,128)(2,1)}, bf16[384,2560]{1,0:T(8,128)(2,1)}, u32[]{:S(2)}, u32[]{:S(2)}) collective-permute-start(bf16[384,2560]{1,0:T(8,128)(2,1)} %get-tuple-element.397), channel_id=1, source_target_pairs={{0,4},{4,0},{1,5},{5,1},{2,6},{6,2},{3,7},{7,3},{8,12},{12,8},{9,1... | collective-permute-start | bytes 5898248 | tf_op jit(solution)/shard_map/cond/branch_1_fun/ppermute | solution.py:28
  449.6 44.1 %collective-permute-start.7 = (bf16[384,2560]{1,0:T(8,128)(2,1)}, bf16[384,2560]{1,0:T(8,128)(2,1)}, u32[]{:S(2)}, u32[]{:S(2)}) collective-permute-start(bf16[384,2560]{1,0:T(8,128)(2,1)} %collective-permute-done.5), channel_id=1, source_target_pairs={{0,1},{1,0},{2,3},{3,2},{4,5},{5,4},{6,7},{7,6},{8,9},{9,8},{10,11... | collective-permute-start | bytes 5898248 | tf_op jit(solution)/shard_map/cond/branch_1_fun/ppermute | solution.py:28
  494.2 289.3 %reduce-scatter.8.cloned.1.call-start = ((), (), s32[]{:S(2)}) async-start(), calls=%async_computation.14 | async-start | bytes 4915200 | tf_op jit(solution)/shard_map/reduce_scatter | solution.py:982
  550.4 45.6 %collective-permute-start.15 = (bf16[768,2560]{1,0:T(8,128)(2,1)}, bf16[768,2560]{1,0:T(8,128)(2,1)}, u32[]{:S(2)}, u32[]{:S(2)}) collective-permute-start(bf16[768,2560]{1,0:T(8,128)(2,1)} %get-tuple-element.466), channel_id=1, source_target_pairs={{0,2},{2,0},{1,3},{3,1},{4,6},{6,4},{5,7},{7,5},{8,10},{10,8},{9,1... | collective-permute-start | bytes 11796488 | tf_op jit(solution)/shard_map/cond/branch_1_fun/ppermute | solution.py:28
  550.8 44.5 %collective-permute-start.12 = (bf16[192,2560]{1,0:T(8,128)(2,1)}, bf16[192,2560]{1,0:T(8,128)(2,1)}, u32[]{:S(2)}, u32[]{:S(2)}) collective-permute-start(bf16[192,2560]{1,0:T(8,128)(2,1)} %get-tuple-element.463), channel_id=1, source_target_pairs={{0,1},{1,0},{2,3},{3,2},{4,5},{5,4},{6,7},{7,6},{8,9},{9,8},{10,11... | collective-permute-start | bytes 2949128 | tf_op jit(solution)/shard_map/cond/branch_1_fun/ppermute | solution.py:28
  609.0 45.6 %collective-permute-start.20 = (bf16[768,2560]{1,0:T(8,128)(2,1)}, bf16[768,2560]{1,0:T(8,128)(2,1)}, u32[]{:S(2)}, u32[]{:S(2)}) collective-permute-start(bf16[768,2560]{1,0:T(8,128)(2,1)} %get-tuple-element.498), channel_id=1, source_target_pairs={{0,2},{2,0},{1,3},{3,1},{4,6},{6,4},{5,7},{7,5},{8,10},{10,8},{9,1... | collective-permute-start | bytes 11796488 | tf_op jit(solution)/shard_map/cond/branch_1_fun/ppermute | solution.py:28
  654.8 220.5 %reduce-scatter.12.cloned.1.call-start = ((), (), s32[]{:S(2)}) async-start(), calls=%async_computation.16 | async-start | bytes 4915200 | tf_op jit(solution)/shard_map/reduce_scatter | solution.py:1034
  678.7 52.3 %collective-permute-start.39 = (bf16[192,2560]{1,0:T(8,128)(2,1)}, bf16[192,2560]{1,0:T(8,128)(2,1)S(1)}, u32[]{:S(2)}, u32[]{:S(2)}) collective-permute-start(bf16[192,2560]{1,0:T(8,128)(2,1)} %get-tuple-element.532), channel_id=1, source_target_pairs={{0,1},{1,0},{2,3},{3,2},{4,5},{5,4},{6,7},{7,6},{8,9},{9,8},{10,11... | collective-permute-start | bytes 2949128 | tf_op jit(solution)/shard_map/cond/branch_1_fun/ppermute | solution.py:28
  680.2 50.8 %collective-permute-start.40 = (bf16[192,2560]{1,0:T(8,128)(2,1)}, bf16[192,2560]{1,0:T(8,128)(2,1)}, u32[]{:S(2)}, u32[]{:S(2)}) collective-permute-start(bf16[192,2560]{1,0:T(8,128)(2,1)} %get-tuple-element.533), channel_id=1, source_target_pairs={{0,4},{4,0},{1,5},{5,1},{2,6},{6,2},{3,7},{7,3},{8,12},{12,8},{9,1... | collective-permute-start | bytes 2949128 | tf_op jit(solution)/shard_map/cond/branch_1_fun/ppermute | solution.py:28
  681.9 49.1 %collective-permute-start.41 = (bf16[192,2560]{1,0:T(8,128)(2,1)}, bf16[192,2560]{1,0:T(8,128)(2,1)}, u32[]{:S(2)}, u32[]{:S(2)}) collective-permute-start(bf16[192,2560]{1,0:T(8,128)(2,1)} %get-tuple-element.534), channel_id=1, source_target_pairs={{0,1},{1,0},{2,3},{3,2},{4,5},{5,4},{6,7},{7,6},{8,9},{9,8},{10,11... | collective-permute-start | bytes 2949128 | tf_op jit(solution)/shard_map/cond/branch_1_fun/ppermute | solution.py:28
  682.5 48.5 %collective-permute-start.42 = (bf16[192,2560]{1,0:T(8,128)(2,1)}, bf16[192,2560]{1,0:T(8,128)(2,1)}, u32[]{:S(2)}, u32[]{:S(2)}) collective-permute-start(bf16[192,2560]{1,0:T(8,128)(2,1)} %get-tuple-element.535), channel_id=1, source_target_pairs={{0,4},{4,0},{1,5},{5,1},{2,6},{6,2},{3,7},{7,3},{8,12},{12,8},{9,1... | collective-permute-start | bytes 2949128 | tf_op jit(solution)/shard_map/cond/branch_1_fun/ppermute | solution.py:28
  783.4 142.2 %reduce-scatter.10.cloned.1.call-start = ((), (), s32[]{:S(2)}) async-start(), calls=%async_computation.15 | async-start | bytes 2457600 | tf_op jit(solution)/shard_map/reduce_scatter | solution.py:1080
  905.5 50.5 %all-to-all-start.1 = ((bf16[8,80,3072]{2,1,0:T(8,128)(2,1)}), bf16[8,80,3072]{2,1,0:T(8,128)(2,1)}, u32[]{:S(2)}, u32[]{:S(2)}) async-start(bf16[8,80,3072]{2,1,0:T(8,128)(2,1)} %bitcast.58), calls=%async_computation.5 | async-start | bytes 7864320 | tf_op jit(solution)/shard_map/all_to_all | solution.py:1092
  910.2 53.8 %reduce-scatter.14.cloned.1.call-start = ((), (), s32[]{:S(2)}) async-start(), calls=%async_computation.17 | async-start | bytes 2048000 | tf_op jit(solution)/shard_map/reduce_scatter | solution.py:1089
  (102 other events, 1988.3 us)
Sparse Core Ops, SparseCore 0:
  22.6 45.9 all-gather.7
  70.8 75.2 all-gather.9
  147.7 48.2 all-gather.17
  215.1 86.9 all-gather.11
  303.5 75.0 all-gather.13
  380.0 74.9 all-gather.15
  494.3 147.4 reduce-scatter.5
  655.0 85.1 reduce-scatter.7
  783.5 82.4 reduce-scatter.11
  875.4 50.0 reduce-scatter.9
  928.5 35.5 reduce-scatter.13

commit v9 on v8

--- a/solution.py
+++ b/solution.py
@@ -10,6 +10,7 @@
 WINDOW = 2048
 SUB = 128
 TILE = 512
+BROAD = 1280
 epsilon = 1e-06
 blocked_score = -1e30
 PLANE = ("y", "c", "x")
@@ -421,10 +422,12 @@
                 copy.wait()
 
     slope = 0.7978845608028654
+    fronts = []
     for j in range(per):
         both = dot(units[step % 2], weights[j][:, : 2 * part], (1, 0))
-        gates, upward = both[:, :part], both[:, part:]
-        grad_middle = dot(grads[step % 2], weights[j][:, 2 * part :], (1, 0))
+        fronts.append((both[:, :part], both[:, part:], dot(grads[step % 2], weights[j][:, 2 * part :], (1, 0))))
+    values = [0.0, 0.0]
+    for j, (gates, upward, grad_middle) in enumerate(fronts):
         square = gates * gates
         half = 0.5 + 0.5 * jnp.tanh(gates * (slope + slope * 0.044715 * square))
         gelu = gates * half
@@ -434,12 +437,13 @@
         hidden[:, at + part : at + 2 * part] = (grad_middle * gelu).astype(low)
         at = part * (2 * per + j)
         hidden[:, at : at + part] = (gelu * upward).astype(low)
-    for which, targets in enumerate((outs, grad_units)):
-        value = 0.0
-        for j in range(per):
+        for which in range(2):
             at, width = (2 * part * j, 2 * part) if which else (part * (2 * per + j), part)
             first = 0 if which else 2 * part
-            value = value + dot(hidden[:, at : at + width], weights[j][:, first : first + width], (1, 1))
+            part_value = dot(hidden[:, at : at + width], weights[j][:, first : first + width], (1, 1))
+            values[which] = values[which] + part_value
+    for which, targets in enumerate((outs, grad_units)):
+        value = values[which]
         for side in range(2):
 
             @pl.when(step // (len(tiles) // 2) == side)
@@ -585,8 +589,7 @@
 
 def spread(value):
     count, wide = value.shape
-    order = (0, 2, 1, 3, 4, 6, 5, 7)
-    slots = (plane_index() ^ jnp.array(order)).astype(jnp.int32)
+    slots = (plane_index() ^ jnp.array(ORDER)).astype(jnp.int32)
     deep = wide // 8
     rows = (count, count, 2 * count, 2 * count, 2 * count)
     if deep % 128:
@@ -605,6 +608,35 @@
     )(slots, value)
 
 
+ORDER = (0, 2, 1, 3, 4, 6, 5, 7)
+
+
+def deal_kernel(slots, value, *outs):
+    place = 0
+    for out in outs:
+        for i in range(out.shape[0]):
+            out[i] = value[slots[place]]
+            place += 1
+
+
+def deal(value):
+    _, rows, wide = value.shape
+    slots = (plane_index() ^ jnp.array(ORDER)).astype(jnp.int32)
+    sizes = (1, 1, 2, 2, 2)
+    return pl.pallas_call(
+        deal_kernel,
+        out_shape=[jax.ShapeDtypeStruct((n, rows, wide), value.dtype) for n in sizes],
+        grid_spec=pltpu.PrefetchScalarGridSpec(
+            num_scalar_prefetch=1,
+            grid=(1,),
+            in_specs=[pl.BlockSpec(value.shape, lambda i, s: (0, 0, 0))],
+            out_specs=[pl.BlockSpec((n, rows, wide), lambda i, s: (0, 0, 0)) for n in sizes],
+        ),
+        compiler_params=pltpu.CompilerParams(vmem_limit_bytes=48 << 20),
+        cost_estimate=NOMINAL,
+    )(slots, value)
+
+
 def turn_kernel(keep, found, far, diag_x, diag_y, y_bottom, x_bottom, y_top):
     half = far.shape[0]
     both = keep[...].astype(f32) + found[...].astype(f32)
@@ -615,11 +647,12 @@
 
 def turn(keep, found, far, diag_x, diag_y):
     half, wide = far.shape
-    part = lambda rows: pl.BlockSpec((rows, TILE), lambda n: (0, n))
+    tile = BROAD if wide % BROAD == 0 else wide
+    part = lambda rows: pl.BlockSpec((rows, tile), lambda n: (0, n))
     return pl.pallas_call(
         turn_kernel,
         out_shape=[jax.ShapeDtypeStruct((half, wide), low)] * 3,
-        grid=(wide // TILE,),
+        grid=(wide // tile,),
         in_specs=[part(2 * half)] * 2 + [part(half)] * 3,
         out_specs=[part(half)] * 3,
         cost_estimate=NOMINAL,
@@ -635,11 +668,12 @@
 
 def halved(keep, found):
     count, wide = keep.shape
-    part = lambda rows: pl.BlockSpec((rows, TILE), lambda n: (0, n))
+    tile = BROAD if wide % BROAD == 0 else wide
+    part = lambda rows: pl.BlockSpec((rows, tile), lambda n: (0, n))
     return pl.pallas_call(
         halved_kernel,
         out_shape=[jax.ShapeDtypeStruct((count // 4, wide), low)] * 4,
-        grid=(wide // TILE,),
+        grid=(wide // tile,),
         in_specs=[part(count)] * 2,
         out_specs=[part(count // 4)] * 4,
         cost_estimate=NOMINAL,
@@ -689,14 +723,15 @@
 
 def part_sums(keep, found):
     _, planes, rows, wide = keep.shape
-    four = pl.BlockSpec((4, planes, rows, TILE), lambda n: (0, 0, 0, n))
-    some = lambda planes: pl.BlockSpec((planes, rows, TILE), lambda n: (0, 0, n))
+    tile = BROAD if wide % BROAD == 0 else wide
+    four = pl.BlockSpec((4, planes, rows, tile), lambda n: (0, 0, 0, n))
+    some = lambda planes: pl.BlockSpec((planes, rows, tile), lambda n: (0, 0, n))
     half = planes // 2
     shape = lambda planes: jax.ShapeDtypeStruct((planes, rows, wide), low)
     return pl.pallas_call(
         part_sums_kernel,
         out_shape=[shape(half)] * 6 + [shape(planes)],
-        grid=(wide // TILE,),
+        grid=(wide // tile,),
         in_specs=[four] * 2,
         out_specs=[some(half)] * 6 + [some(planes)],
         compiler_params=pltpu.CompilerParams(vmem_limit_bytes=48 << 20),
@@ -740,37 +775,56 @@
     return [(sum(sizes[:p]), size) for p, size in enumerate(sizes)], 128 * (few + (more > 0))
 
 
-def finish_kernel(spans, part, per, gain, gate, up, whole, gate_out, up_out, down_out, gain_out):
+def finish_kernel(spans, part, per, first_part, starts, gain, gate, up, whole, *rest):
+    *early, gate_out, up_out, down_out, gain_out = rest
     scale = gain[...]
     total = jnp.zeros_like(scale)
+
+    def lay(piece, start, j, place, width):
+        added = jnp.zeros_like(scale)
+        for which, (weight, out) in enumerate(((gate, gate_out), (up, up_out))):
+            first = start + part * (2 * j + which)
+            value = piece[:, first : first + width].astype(f32)
+            added = added + jnp.sum(value * weight[:, place].astype(f32), axis=1, keepdims=True)
+            out[:, place] = value * scale
+        first = start + part * (2 * per + j)
+        down_out[:, place] = piece[:, first : first + width].astype(f32)
+        return added
+
     for p, (at, n) in enumerate(spans):
-        for q in range(-(-n // part)):
+        for q in range(first_part, -(-n // part)):
             width = min(part, n - q * part)
-            start, j = 3 * part * per * (q // per), q % per
-            place = slice(at + q * part, at + q * part + width)
-            for which, (weight, out) in enumerate(((gate, gate_out), (up, up_out))):
-                first = start + part * (2 * j + which)
-                value = whole[p, :, first : first + width].astype(f32)
-                total = total + jnp.sum(value * weight[:, place].astype(f32), axis=1, keepdims=True)
-                out[:, place] = value * scale
-            first = start + part * (2 * per + j)
-            down_out[:, place] = whole[p, :, first : first + width].astype(f32)
+            start = 3 * part * per * (q // per) - 3 * part * first_part
+            total = total + lay(whole.at[p], start, q % per, slice(at + q * part, at + q * part + width), width)
+    place = 0
+    for pieces in early:
+        for i in range(pieces.shape[0]):
+            for q in range(first_part):
+                at = pl.multiple_of(starts[place] + q * part, 128)
+                total = total + lay(pieces.at[i], 0, q, pl.ds(at, part), part)
+            place += 1
     gain_out[...] = total
 
 
-def finish(spans, part, per, gain, gate, up, whole):
+def finish(spans, part, per, gain, gate, up, whole, early):
     rows, columns = gate.shape
-    return pl.pallas_call(
-        functools.partial(finish_kernel, spans, part, per),
-        out_shape=(
-            jax.ShapeDtypeStruct((rows, columns), f32),
-            jax.ShapeDtypeStruct((rows, columns), f32),
-            jax.ShapeDtypeStruct((rows, columns), f32),
-            jax.ShapeDtypeStruct((rows, 1), f32),
+    order = [r for r in (0, 1, 4, 5, 2, 3, 6, 7)]
+    starts = jnp.array([at for at, _ in spans], jnp.int32)[plane_index() ^ jnp.array(order)]
+    block = lambda shape: pl.BlockSpec(shape, lambda i, s: (0,) * len(shape))
+    given = (gain, gate, up, whole, *early)
+    shapes = ((rows, columns), (rows, columns), (rows, columns), (rows, 1))
+    return pl.pallas_call(
+        functools.partial(finish_kernel, spans, part, per, per if early else 0),
+        out_shape=[jax.ShapeDtypeStruct(shape, f32) for shape in shapes],
+        grid_spec=pltpu.PrefetchScalarGridSpec(
+            num_scalar_prefetch=1,
+            grid=(1,),
+            in_specs=[block(value.shape) for value in given],
+            out_specs=[block(shape) for shape in shapes],
         ),
-        compiler_params=pltpu.CompilerParams(vmem_limit_bytes=48 << 20),
-        cost_estimate=NOMINAL,
-    )(gain, gate, up, whole)
+        compiler_params=pltpu.CompilerParams(vmem_limit_bytes=56 << 20),
+        cost_estimate=NOMINAL,
+    )(starts, *given)
 
 
 def unit_of(values):
@@ -988,19 +1042,34 @@
         return jnp.concatenate([total(top, first[2], second[1]), total(bottom, second[0], first[3])], 0)
 
     def backward(
-        own_sums, outs, resid, scale_two, gift, queries, pairs, mixed, mixed_wide, logs, out_blocks, positions
+        own_sums, outs, resid, scale_two, gift, queries, pairs, mixed, mixed_wide, logs, out_blocks, positions, early
     ):
         keep, found, received = own_sums
-        grad_resid, grad_attn = resid_grads(keep, found, *received, resid, gift, scale_two)
-        out_far, out_near = halved(*outs[:2]), halved(*outs[2:])
+
+        def remaining(keep, far, near):
+            grads = resid_grads(keep, found, *received, resid, gift, scale_two)
+            return grads, halved(far, outs[1]), halved(near, outs[3])
+
+        given = keep, outs[0], outs[2]
+        if early is not None:
+            early_own, to_c, to_x, to_y, to_d = deal(early.reshape(8, -1, early.shape[1]))
+            (by_x, by_y, by_d), results = stage([(to_x, "x"), (to_y, "y"), (to_d, across(5))], remaining, given)
+            early_on = [(jnp.concatenate([to_c, by_x[1:], by_y[1:], by_d[1:]], 0), "c")]
+        else:
+            results, early_on = remaining(*given), []
+        (grad_resid, grad_attn), out_far, out_near = results
 
         def attention(grad_attn):
             grad_mixed = apply_rows(grad_attn, out_blocks)
             return attend_back(queries, grad_mixed, mixed_wide, logs, pairs, positions, size, base)
 
-        first, (grad_queries, mine, theirs) = stage(
-            [(out_far[0], "x"), (out_far[1], "y"), (out_far[2], "x"), (out_near[1], "y")], attention, [grad_attn]
+        (*first, on), (grad_queries, mine, theirs) = stage(
+            [(out_far[0], "x"), (out_far[1], "y"), (out_far[2], "x"), (out_near[1], "y")]
+            + (early_on or [(out_near[1][:16], "c")]),
+            attention,
+            [grad_attn],
         )
+        early = [early_own, by_x[:1], by_y[:1], by_d[:1], on] if early_on else []
         (found,), _ = stage([(theirs, "c")])
         mine = summed(mine, found)
         second = total(out_far[3], first[1]).astype(low), total(out_near[0], first[0]).astype(low)
@@ -1012,9 +1081,11 @@
         )
         grad_pair = total(mine[chips], *found).astype(low)
         grad_qkv = jnp.concatenate([grad_queries, grad_pair], 1)
-        return grad_qkv, grad_resid, first, (x_second, y_second), out_keep, out_send, (out_near[2], out_near[3])
-
-    grad_qkv, grad_resid, first, second, out_keep, out_send, out_own = boxed(
+        out_own = out_near[2], out_near[3]
+        return grad_qkv, grad_resid, first, (x_second, y_second), out_keep, out_send, out_own, early
+
+    ahead = calls > 1 and per * part <= min(n for _, n in spans)
+    grad_qkv, grad_resid, first, second, out_keep, out_send, out_own, early = boxed(
         sure,
         backward,
         own_sums,
@@ -1029,6 +1100,7 @@
         logs,
         out_blocks,
         positions,
+        columns[0] if ahead else None,
     )
     columns += [
         lax.psum_scatter(after(piece, grad_qkv), "z", scatter_dimension=0, tiled=True) for piece in partial[1:]
@@ -1079,15 +1151,16 @@
     )
     qkv_low = lax.psum_scatter(qkv_column, "z", scatter_dimension=0, tiled=True)
 
-    def end(x_bottom, y_top, out_sums, started):
+    def end(x_bottom, y_top, out_sums, started, columns):
         x_bottom, y_top = total(x_bottom, started[1]).astype(low), total(y_top, started[0]).astype(low)
-        received, _ = stage([(x_bottom, "x"), (y_top, "y")])
+        received, every = stage(
+            [(x_bottom, "x"), (y_top, "y")], lambda *columns: jnp.concatenate(columns, 1), columns
+        )
         column = joined(out_sums, started, received).astype(low)
-        return column.reshape(-1, column.shape[-1])
-
-    out_column = boxed(sure, end, after(x_bottom, columns[-1]), y_top, out_sums, started)
+        return column.reshape(-1, column.shape[-1]), every
+
+    out_column, every = boxed(sure, end, x_bottom, y_top, out_sums, started, columns[1:] if ahead else columns)
     out_sum = lax.psum_scatter(out_column, "z", scatter_dimension=0, tiled=True).astype(f32)
-    every = jnp.concatenate(columns, 1)
     every = after(every, out_column).reshape(8, -1, every.shape[1])
     every = lax.all_to_all(every, PLANE, split_axis=0, concat_axis=0, tiled=True)
     deep = qkv_low.shape[1]
@@ -1102,7 +1175,7 @@
         + jnp.sum(key_weight.astype(f32) * key_sum, axis=1)
         + jnp.sum(value_weight.astype(f32) * value_sum, axis=1)
     )
-    grad_gate, grad_up, grad_down, grad_mlp_gain = finish(spans, part, per, gain_two, gate_weight, up_weight, every)
+    grad_gate, grad_up, grad_down, grad_mlp_gain = finish(spans, part, per, gain_two, gate_weight, up_weight, every, early)
     return (
         output[None],
         grad_tokens[None],

time: 997 us -> 985 us (0.988)
  waiting for transfers between devices: 372 us -> 362 us
    all_to_all x1, waiting for transfers between devices: 30.4 us -> 6.84 us  [local(): lax.all_to_all(every, PLANE, split_axis=0, concat_axis=0, tiled=True)]
    ppermute x70 -> x73, starting transfers between devices: 53.3 us -> 57.7 us  [swap(): return lax.ppermute(value, axis, [(0, 1), (1, 0)])]
    ppermute x70 -> x73, waiting for transfers between devices: 218 us -> 220 us  [swap(): return lax.ppermute(value, axis, [(0, 1), (1, 0)])]
  transfers between devices with their start and end apart: 91 -> 95, of which waited for: 45 -> 45; matrix products, arithmetic and copies ran while one was open for 7% -> 8% of each run, Pallas kernels for 43% -> 43%
where the time goes in v9:
time: 985 us; the launch traced here: 975 us
  Pallas kernels  418 us (42%)
  waiting for transfers between devices  362 us (37%)
  starting transfers between devices  88 us (9%)
  other arithmetic  46.9 us (5%)
  local copies, waits for them, and re-layouts  43.8 us (4%)
  between operations  15.3 us (2%)
    ppermute x73, waiting for transfers between devices, swap(): return lax.ppermute(value, axis, [(0, 1), (1, 0)])  220 us
    pallas_call x4, Pallas kernels, mlp(): pl.pallas_call(functools.partial(mlp_kernel, each // 3, per, tiles), out_...  153 us
    pallas_call x2, Pallas kernels, mlp_grads(): pl.pallas_call(functools.partial(mlp_grads_kernel, len(units)), out_shape...  75.9 us
    ppermute x73, starting transfers between devices, swap(): return lax.ppermute(value, axis, [(0, 1), (1, 0)])  57.7 us
    ppermute x6, waiting for transfers between devices, behind(): return lambda value: lax.ppermute(value, ('z', 'y'), pairs)  55.1 us
    pallas_call x4, Pallas kernels, apply_rows(): pl.pallas_call(functools.partial(kernel, layout), out_shape=shape, grid_s...  45.4 us
    all_to_all x1, waiting for transfers between devices, local(): lax.all_to_all(mine, PLANE, split_axis=0, concat_axis=0, tiled=True)  44.6 us
    pallas_call x1, Pallas kernels, attend_back(): pl.pallas_call(functools.partial(attend_back_kernel, size, size ** (-0.5)...  35.7 us
  transfers between devices with their start and end apart: 95, of which 45 were waited for; matrix products, arithmetic and copies ran while one was open for 8% of the time, Pallas kernels for 43%

profile of v9, /device:TPU:0, one launch (start us, length us, event | category | flops | bytes accessed | tf_op | source)
XLA Modules:
  0.0 975.5 jit_solution(6316482876990727501)
XLA Ops:
  20.7 44.6 %all-to-all-done = bf16[8,80,3072]{2,1,0:T(8,128)(2,1)} async-done(((bf16[8,80,3072]{2,1,0:T(8,128)(2,1)}), bf16[8,80,3072]{2,1,0:T(8,128)(2,1)}, u32[]{:S(2)}, u32[]{:S(2)}) %all-to-all-start) | async-done | bytes 3932192 | tf_op jit(solution)/shard_map/all_to_all | solution.py:875
  69.5 145.4 %conditional.7 = (bf16[4,80,3072]{2,1,0:T(8,128)(2,1)}, bf16[4,80,3072]{2,1,0:T(8,128)(2,1)}, bf16[4,80,3072]{2,1,0:T(8,128)(2,1)}, bf16[4,80,3072]{2,1,0:T(8,12...) conditional(s32[]{:T(128)} %bitcast.17, () %tuple.124, ...), branch_computations={%region_0.0_spmd, %region_1.0_spmd} | conditional | flops 6947220 | bytes 125057264 | solution.py:61
  71.6 43.0 %collective-permute-done.42.rest_4_ = bf16[4,80,3072]{2,1,0:T(8,128)(2,1)} collective-permute-done((bf16[4,80,3072]{2,1,0:T(8,128)(2,1)}, bf16[4,80,3072]{2,1,0:T(8,128)(2,1)}, u32[]{:S(2)}, u32[]{:S(2)}) %collective-permute-start.42) | collective-permute-done | bytes 1966112 | tf_op jit(solution)/shard_map/cond/branch_1_fun/ppermute | solution.py:29
  121.9 17.9 %collective-permute-done.43.rest_5_ = bf16[2,80,3072]{2,1,0:T(8,128)(2,1)S(1)} collective-permute-done((bf16[2,80,3072]{2,1,0:T(8,128)(2,1)}, bf16[2,80,3072]{2,1,0:T(8,128)(2,1)S(1)}, u32[]{:S(2)}, u32[]{:S(2)}) %collective-permute-start.43) | collective-permute-done | bytes 983072 | tf_op jit(solution)/shard_map/cond/branch_1_fun/ppermute | solution.py:29
  145.6 11.9 %branch_1_fun.22 = bf16[384,3072]{1,0:T(8,128)(2,1)S(1)} custom-call(s32[8]{0:T(128)S(1)} %iota_xor_fusion.slots, bf16[384,2560]{1,0:T(8,128)(2,1)} %fusion.1.left, bf16[4,80,3072]{2,1,0:T(8,128)(2,1)} %get-tuple-element.282.rest_0_, bf16[4,80,3072]{2,1,0:T(8,128)(2,1)} %collective-permute-done.39.rest_1_, ...), custom_call_target="tpu_custom_call" | custom-call | flops 1048576 | bytes 4096 | tf_op jit(solution)/shard_map/cond/branch_1_fun/pallas_call | solution.py:319
  169.3 13.5 %collective-permute-done.48 = bf16[384,512]{1,0:T(8,128)(2,1)} collective-permute-done((bf16[384,512]{1,0:T(8,128)(2,1)S(1)}, bf16[384,512]{1,0:T(8,128)(2,1)}, u32[]{:S(2)}, u32[]{:S(2)}) %collective-permute-start.48) | collective-permute-done | bytes 393248 | tf_op jit(solution)/shard_map/cond/branch_1_fun/ppermute | solution.py:81
  187.6 10.0 %collective-permute-done.49 = bf16[384,512]{1,0:T(8,128)(2,1)} collective-permute-done((bf16[384,512]{1,0:T(8,128)(2,1)S(1)}, bf16[384,512]{1,0:T(8,128)(2,1)}, u32[]{:S(2)}, u32[]{:S(2)}) %collective-permute-start.49) | collective-permute-done | bytes 393248 | tf_op jit(solution)/shard_map/cond/branch_1_fun/ppermute | solution.py:81
  201.1 10.6 %collective-permute-done.50 = bf16[384,512]{1,0:T(8,128)(2,1)} collective-permute-done((bf16[384,512]{1,0:T(8,128)(2,1)S(1)}, bf16[384,512]{1,0:T(8,128)(2,1)}, u32[]{:S(2)}, u32[]{:S(2)}) %collective-permute-start.50) | collective-permute-done | bytes 393248 | tf_op jit(solution)/shard_map/cond/branch_1_fun/ppermute | solution.py:81
  216.3 140.7 %conditional.8 = (bf16[4,80,2560]{2,1,0:T(8,128)(2,1)}, bf16[4,80,2560]{2,1,0:T(8,128)(2,1)}, bf16[4,80,2560]{2,1,0:T(8,128)(2,1)}, bf16[4,80,2560]{2,1,0:T(8,12...) conditional(s32[]{:T(128)} %bitcast.17, () %tuple.122, ...), branch_computations={%region_3.0_spmd, %region_4.0_spmd} | conditional | flops 7012756 | bytes 129779728 | solution.py:61
  220.0 28.8 %branch_1_fun.23 = (bf16[384,2560]{1,0:T(8,128)(2,1)}, f32[384,2560]{1,0:T(8,128)}, f32[15,1,256]{2,1,0:T(1,128)S(1)}) custom-call(s32[1]{0:T(128)} %bitcast.2.core, s32[1,384]{1,0:T(1,128)S(1)} %get-tuple-element.327.places, bf16[384,2560]{1,0:T(8,128)(2,1)} %get-tuple-element.328.queries, bf16[384,512]{1,0:T(8,128)(2,1)} %get-tuple-element.329.rest_0_, ...), custom_call_target="tpu_custom_call" | custom-call | flops 1048576 | bytes 4096 | tf_op jit(solution)/shard_map/cond/branch_1_fun/pallas_call | solution.py:196
  264.3 17.0 %collective-permute-done.26.rest_6_ = bf16[2,80,2560]{2,1,0:T(8,128)(2,1)S(1)} collective-permute-done((bf16[2,80,2560]{2,1,0:T(8,128)(2,1)}, bf16[2,80,2560]{2,1,0:T(8,128)(2,1)S(1)}, u32[]{:S(2)}, u32[]{:S(2)}) %collective-permute-start.26) | collective-permute-done | bytes 819232 | tf_op jit(solution)/shard_map/cond/branch_1_fun/ppermute | solution.py:29
  286.6 11.9 %branch_1_fun.24 = f32[384,2560]{1,0:T(8,128)} custom-call(s32[8]{0:T(128)S(1)} %iota_xor_fusion.1.slots, bf16[384,2560]{1,0:T(8,128)(2,1)} %get-tuple-element.1245.left, f32[384,2560]{1,0:T(8,128)S(1)} %bitcast_convert_fusion.rest_0_, bf16[4,80,2560]{2,1,0:T(8,128)(2,1)S(1)} %copy-done.19, bf16[4,80,2560]{2,1,0:T(8,128)(2,1)} %collective-permute-done.21.rest_2_, ...), custom_call_target="tpu_custom_call" | custom-call | flops 1048576 | bytes 4096 | tf_op jit(solution)/shard_map/cond/branch_1_fun/pallas_call | solution.py:319
  306.7 43.1 %collective-permute-done.32 = bf16[384,2560]{1,0:T(8,128)(2,1)} collective-permute-done((bf16[384,2560]{1,0:T(8,128)(2,1)}, bf16[384,2560]{1,0:T(8,128)(2,1)}, u32[]{:S(2)}, u32[]{:S(2)}) %collective-permute-start.32) | collective-permute-done | bytes 1966112 | tf_op jit(solution)/shard_map/cond/branch_1_fun/ppermute | solution.py:29
  357.0 136.6 %conditional.9 = (bf16[384,2560]{1,0:T(8,128)(2,1)}, bf16[384,2560]{1,0:T(8,128)(2,1)}, bf16[384,2560]{1,0:T(8,128)(2,1)}, bf16[384,2560]{1,0:T(8,128)(2,1)}, bf...) conditional(s32[]{:T(128)} %bitcast.17, () %tuple.121, ...), branch_computations={%region_6.0_spmd, %region_7.0_spmd} | conditional | flops 3145728 | bytes 86520392 | solution.py:61
  360.4 36.5 %branch_1_fun.25 = (bf16[768,2560]{1,0:T(8,128)(2,1)}, bf16[768,2560]{1,0:T(8,128)(2,1)}, bf16[768,2560]{1,0:T(8,128)(2,1)}, bf16[768,2560]{1,0:T(8,128)(2,1)}, bf16[1536,1536]{1,0:T(8,128)(2,1)}) custom-call(bf16[2560,768]{1,0:T(8,128)(2,1)} %get-tuple-element.403.rest_0_, bf16[2560,768]{1,0:T(8,128)(2,1)} %get-tuple-element.404.rest_1_, ...), custom_call_target="tpu_custom_call" | custom-call | flops 1048576 | bytes 4096 | tf_op jit(solution)/shard_map/cond/branch_1_fun/pallas_call | solution.py:470
  410.7 36.3 %branch_1_fun.26 = (bf16[768,2560]{1,0:T(8,128)(2,1)}, bf16[768,2560]{1,0:T(8,128)(2,1)}, bf16[768,2560]{1,0:T(8,128)(2,1)}, bf16[768,2560]{1,0:T(8,128)(2,1)}, bf16[1536,1536]{1,0:T(8,128)(2,1)}) custom-call(bf16[2560,768]{1,0:T(8,128)(2,1)} %get-tuple-element.403.rest_0_, bf16[2560,768]{1,0:T(8,128)(2,1)} %get-tuple-element.404.rest_1_, ...), custom_call_target="tpu_custom_call" | custom-call | flops 1048576 | bytes 4096 | tf_op jit(solution)/shard_map/cond/branch_1_fun/pallas_call | solution.py:470
  451.4 37.9 %branch_1_fun.27 = bf16[2560,1536]{1,0:T(8,128)(2,1)} custom-call(bf16[384,2560]{1,0:T(8,128)(2,1)} %collective-permute-done.rest_2_.rest_0_, bf16[384,2560]{1,0:T(8,128)(2,1)} %get-tuple-element.405.rest_4_.rest_1_, bf16[384,2560]{1,0:T(8,128)(2,1)} %collective-permute-done.2.rest_6_.rest_2_, bf16[384,2560]{1,0:T(8,128)(2,1)} %get-tuple-element.406.rest_8_.rest_3_, ...), custom_call_target="tpu_custom_call" | custom-call | flops 1048576 | bytes 4096 | tf_op jit(solution)/shard_map/cond/branch_1_fun/pallas_call | solution.py:533
  495.1 154.8 %conditional.10 = (bf16[2560,768]{1,0:T(8,128)(2,1)}, bf16[2560,768]{1,0:T(8,128)(2,1)}, bf16[768,2560]{1,0:T(8,128)(2,1)}, bf16[768,2560]{1,0:T(8,128)(2,1)}, b...) conditional(s32[]{:T(128)} %bitcast.17, () %tuple.131, ...), branch_computations={%region_9.0_spmd, %region_10.0_spmd} | conditional | flops 5242880 | bytes 94392864 | solution.py:61
  495.1 39.9 %branch_1_fun.28 = (bf16[768,2560]{1,0:T(8,128)(2,1)}, bf16[768,2560]{1,0:T(8,128)(2,1)}, bf16[768,2560]{1,0:T(8,128)(2,1)}, bf16[768,2560]{1,0:T(8,128)(2,1)}, bf16[1536,1536]{1,0:T(8,128)(2,1)}) custom-call(bf16[2560,768]{1,0:T(8,128)(2,1)} %get-tuple-element.439.rest_0_, bf16[2560,768]{1,0:T(8,128)(2,1)} %get-tuple-element.440.rest_1_, ...), custom_call_target="tpu_custom_call" | custom-call | flops 1048576 | bytes 4096 | tf_op jit(solution)/shard_map/cond/branch_1_fun/pallas_call | solution.py:470
  551.4 40.3 %branch_1_fun.30 = (bf16[768,2560]{1,0:T(8,128)(2,1)}, bf16[768,2560]{1,0:T(8,128)(2,1)}, bf16[768,2560]{1,0:T(8,128)(2,1)}, bf16[768,2560]{1,0:T(8,128)(2,1)}, bf16[1536,1536]{1,0:T(8,128)(2,1)}) custom-call(bf16[2560,768]{1,0:T(8,128)(2,1)} %get-tuple-element.439.rest_0_, bf16[2560,768]{1,0:T(8,128)(2,1)} %get-tuple-element.440.rest_1_, ...), custom_call_target="tpu_custom_call" | custom-call | flops 1048576 | bytes 4096 | tf_op jit(solution)/shard_map/cond/branch_1_fun/pallas_call | solution.py:470
  607.9 37.9 %branch_1_fun.32 = (bf16[2560,768]{1,0:T(8,128)(2,1)}, bf16[2560,768]{1,0:T(8,128)(2,1)}) custom-call(bf16[384,2560]{1,0:T(8,128)(2,1)} %get-tuple-element.441.rest_2_.rest_0_, bf16[384,2560]{1,0:T(8,128)(2,1)} %get-tuple-element.443.rest_4_.rest_1_, bf16[384,2560]{1,0:T(8,128)(2,1)} %get-tuple-element.445.rest_6_.rest_2_, ...), custom_call_target="tpu_custom_call" | custom-call | flops 1048576 | bytes 4096 | tf_op jit(solution)/shard_map/cond/branch_1_fun/pallas_call | solution.py:533
  650.6 137.2 %conditional.11 = (bf16[384,3072]{1,0:T(8,128)(2,1)}, f32[384,2560]{1,0:T(8,128)}, bf16[192,2560]{1,0:T(8,128)(2,1)}, bf16[192,2560]{1,0:T(8,128)(2,1)}, bf16[19...) conditional(s32[]{:T(128)} %bitcast.17, () %tuple.120, ...), branch_computations={%region_11.0_spmd, %region_12.0_spmd} | conditional | flops 21201980 | bytes 139432448 | solution.py:61
  698.9 35.7 %branch_1_fun.38 = (bf16[384,2560]{1,0:T(8,128)(2,1)}, f32[4,384,512]{2,1,0:T(8,128)}, bf16[4,384,512]{2,1,0:T(8,128)(2,1)}) custom-call(s32[1]{0:T(128)} %bitcast.6.core, s32[1,384]{1,0:T(1,128)S(1)} %get-tuple-element.567.places, bf16[384,2560]{1,0:T(8,128)(2,1)} %get-tuple-element.568.queries, bf16[384,2560]{1,0:T(8,128)(2,1)} %copy-done.1, ...), custom_call_target="tpu_custom_call" | custom-call | flops 1048576 | bytes 4096 | tf_op jit(solution)/shard_map/cond/branch_1_fun/pallas_call | solution.py:229
  750.1 13.2 %branch_1_fun.39 = (bf16[4,4,80,2560]{3,2,1,0:T(8,128)(2,1)}, bf16[4,4,80,2560]{3,2,1,0:T(8,128)(2,1)}) custom-call(s32[8]{0:T(128)S(1)} %gather_fusion, bf16[384,2560]{1,0:T(8,128)(2,1)S(1)} %copy-done, bf16[384,2560]{1,0:T(8,128)(2,1)} %get-tuple-element.608.right), custom_call_target="tpu_custom_call" | custom-call | flops 1048576 | bytes 4096 | tf_op jit(solution)/shard_map/cond/branch_1_fun/pallas_call | solution.py:368
  789.6 89.0 %conditional.12 = (bf16[2560,384]{1,0:T(8,128)(2,1)}, bf16[2,80,2560]{2,1,0:T(8,128)(2,1)}, bf16[2,80,2560]{2,1,0:T(8,128)(2,1)}, bf16[4,80,2560]{2,1,0:T(8,128)...) conditional(s32[]{:T(128)} %bitcast.17, () %tuple.119, ...), branch_computations={%region_14.0_spmd, %region_15.17_spmd} | conditional | flops 25624604 | bytes 105411296 | solution.py:61
  798.7 12.2 %branch_1_fun.41 = f32[384,2560]{1,0:T(8,128)S(1)} custom-call(s32[8]{0:T(128)S(1)} %get-tuple-element.1143.slots, bf16[384,3072]{1,0:T(8,128)(2,1)} %get-tuple-element.638.value.left, bf16[4,80,3072]{2,1,0:T(8,128)(2,1)} %get-tuple-element.639.rest_0_, bf16[4,80,3072]{2,1,0:T(8,128)(2,1)} %get-tuple-element.640.rest_1_, ...), custom_call_target="tpu_custom_call" | custom-call | flops 1048576 | bytes 4096 | tf_op jit(solution)/shard_map/cond/branch_1_fun/pallas_call | solution.py:319
  846.5 14.2 %branch_1_fun.43 = bf16[2560,384]{1,0:T(8,128)(2,1)} custom-call(bf16[384,2560]{1,0:T(8,128)(2,1)} %get-tuple-element.676.rest_0_, bf16[384,2560]{1,0:T(8,128)(2,1)} %get-tuple-element.677.rest_1_, bf16[384,2560]{1,0:T(8,128)(2,1)} %get-tuple-element.678.rest_2_, bf16[384,2560]{1,0:T(8,128)(2,1)} %get-tuple-element.679.rest_3_, ...), custom_call_target="tpu_custom_call" | custom-call | flops 1048576 | bytes 4096 | tf_op jit(solution)/shard_map/cond/branch_1_fun/pallas_call | solution.py:568
  865.4 12.0 %collective-permute-done.65 = bf16[2,80,2560]{2,1,0:T(8,128)(2,1)} collective-permute-done((bf16[2,80,2560]{2,1,0:T(8,128)(2,1)S(1)}, bf16[2,80,2560]{2,1,0:T(8,128)(2,1)}, u32[]{:S(2)}, u32[]{:S(2)}) %collective-permute-start.65) | collective-permute-done | bytes 819232 | tf_op jit(solution)/shard_map/cond/branch_1_fun/ppermute | solution.py:29
  879.8 26.0 %conditional.13 = (bf16[320,2560]{1,0:T(8,128)(2,1)}, bf16[640,1536]{1,0:T(8,128)(2,1)S(1)}) conditional(s32[]{:T(128)} %bitcast.17, () %tuple.137, (bf16[4,80,2560]{2,1,0:T(8,128)(2,1)}, bf16[2,80,2560]{2,1,0:T(8,128)(2,1)}, bf16[2,80,2560]{2,1,0:T(8,128)(2,1)}, bf16[2,80,2560]{2,1,0:T(8,128)(2,1)}, bf16[2,80,2560]{2,1,0:T(8,128)(2,1)}, ...), branch_computations={%region_19.0_spmd, %region_20.0_spmd} | conditional | flops 12943360 | bytes 29163644 | solution.py:61
  884.6 17.0 %collective-permute-done.37 = bf16[2,80,2560]{2,1,0:T(8,128)(2,1)S(1)} collective-permute-done((bf16[2,80,2560]{2,1,0:T(8,128)(2,1)S(1)}, bf16[2,80,2560]{2,1,0:T(8,128)(2,1)S(1)}, u32[]{:S(2)}, u32[]{:S(2)}) %collective-permute-start.37) | collective-permute-done | bytes 819232 | tf_op jit(solution)/shard_map/cond/branch_1_fun/ppermute | solution.py:29
  910.8 17.8 %reduce-scatter.10.cloned.1.call-done = bf16[640,384]{1,0:T(8,128)(2,1)} async-done(((bf16[2560,384]{1,0:T(8,128)(2,1)}), bf16[640,384]{1,0:T(8,128)(2,1)}) %reduce-scatter.10.cloned.1.call-update) | async-done | bytes 491536 | tf_op jit(solution)/shard_map/reduce_scatter | solution.py:1152
  952.7 13.9 %reduce-scatter.14.cloned.1.call-done = bf16[80,2560]{1,0:T(8,128)(2,1)} async-done(((bf16[320,2560]{1,0:T(8,128)(2,1)}), bf16[80,2560]{1,0:T(8,128)(2,1)}) %reduce-scatter.14.cloned.1.call-update) | async-done | bytes 409616 | tf_op jit(solution)/shard_map/reduce_scatter | solution.py:1163
  (364 shorter events, 341.7 us)
Async XLA Ops:
  14.3 51.0 %all-to-all-start = ((bf16[8,80,3072]{2,1,0:T(8,128)(2,1)}), bf16[8,80,3072]{2,1,0:T(8,128)(2,1)}, u32[]{:S(2)}, u32[]{:S(2)}) async-start(bf16[8,80,3072]{2,1,0:T(8,128)(2,1)} %shard_map.249), calls=%async_computation | async-start | bytes 7864320 | tf_op jit(solution)/shard_map/all_to_all | solution.py:875
  19.6 49.9 %all-gather.8.cloned.1.call-start = ((), (), s32[]{:S(2)}) async-start(), calls=%async_computation.8 | async-start | bytes 2457600 | tf_op jit(solution)/shard_map/all_gather | solution.py:865
  20.7 195.5 %all-gather.10.cloned.1.call-start = ((), (), s32[]{:S(2)}) async-start(), calls=%async_computation.9 | async-start | bytes 4915200 | tf_op jit(solution)/shard_map/all_gather | solution.py:882
  67.5 148.7 %all-gather.18.cloned.1.call-start = ((), (), s32[]{:S(2)}) async-start(), calls=%async_computation.18 | async-start | bytes 2048000 | tf_op jit(solution)/shard_map/all_gather | solution.py:866
  68.3 288.7 %all-gather.12.cloned.1.call-start = ((), (), s32[]{:S(2)}) async-start(), calls=%async_computation.10 | async-start | bytes 4915200 | tf_op jit(solution)/shard_map/all_gather | solution.py:882
  69.6 45.1 %collective-permute-start.42 = (bf16[4,80,3072]{2,1,0:T(8,128)(2,1)}, bf16[4,80,3072]{2,1,0:T(8,128)(2,1)}, u32[]{:S(2)}, u32[]{:S(2)}) collective-permute-start(bf16[4,80,3072]{2,1,0:T(8,128)(2,1)} %get-tuple-element.282.rest_0_), channel_id=1, source_target_pairs={{0,4},{4,0},{1,5},{5,1},{2,6},{6,2},{3,7},{7,3},{8,12},{12,8},{9,1... | collective-permute-start | bytes 5898248 | tf_op jit(solution)/shard_map/cond/branch_1_fun/ppermute | solution.py:29
  70.3 47.2 %collective-permute-start.39 = (bf16[4,80,3072]{2,1,0:T(8,128)(2,1)}, bf16[4,80,3072]{2,1,0:T(8,128)(2,1)}, u32[]{:S(2)}, u32[]{:S(2)}) collective-permute-start(bf16[4,80,3072]{2,1,0:T(8,128)(2,1)} %get-tuple-element.282.rest_0_), channel_id=1, source_target_pairs={{0,1},{1,0},{2,3},{3,2},{4,5},{5,4},{6,7},{7,6},{8,9},{9,8},{10,11... | collective-permute-start | bytes 5898248 | tf_op jit(solution)/shard_map/cond/branch_1_fun/ppermute | solution.py:29
  157.6 54.1 %collective-permute-start.52 = (bf16[384,2560]{1,0:T(8,128)(2,1)S(1)}, bf16[384,2560]{1,0:T(8,128)(2,1)}, u32[]{:S(2)}, u32[]{:S(2)}) collective-permute-start(bf16[384,2560]{1,0:T(8,128)(2,1)S(1)} %copy-done.10), channel_id=1, source_target_pairs={{0,1},{1,0},{2,3},{3,2},{4,5},{5,4},{6,7},{7,6},{8,9},{9,8},{10,11... | collective-permute-start | bytes 5898248 | tf_op jit(solution)/shard_map/cond/branch_1_fun/ppermute | solution.py:29
  159.4 52.3 %collective-permute-start.53 = (bf16[384,2560]{1,0:T(8,128)(2,1)S(1)}, bf16[384,2560]{1,0:T(8,128)(2,1)}, u32[]{:S(2)}, u32[]{:S(2)}) collective-permute-start(bf16[384,2560]{1,0:T(8,128)(2,1)S(1)} %copy-done.10), channel_id=1, source_target_pairs={{0,4},{4,0},{1,5},{5,1},{2,6},{6,2},{3,7},{7,3},{8,12},{12,8},{9,1... | collective-permute-start | bytes 5898248 | tf_op jit(solution)/shard_map/cond/branch_1_fun/ppermute | solution.py:29
  161.1 50.5 %collective-permute-start.54 = (bf16[384,2560]{1,0:T(8,128)(2,1)S(1)}, bf16[384,2560]{1,0:T(8,128)(2,1)}, u32[]{:S(2)}, u32[]{:S(2)}) collective-permute-start(bf16[384,2560]{1,0:T(8,128)(2,1)S(1)} %copy-done.10), channel_id=1, source_target_pairs={{0,2},{2,0},{1,3},{3,1},{4,6},{6,4},{5,7},{7,5},{8,10},{10,8},{9,1... | collective-permute-start | bytes 5898248 | tf_op jit(solution)/shard_map/cond/branch_1_fun/ppermute | solution.py:29
  215.0 278.7 %all-gather.14.cloned.1.call-start = ((), (), s32[]{:S(2)}) async-start(), calls=%async_computation.12 | async-start | bytes 4915200 | tf_op jit(solution)/shard_map/all_gather | solution.py:882
  215.6 278.1 %all-gather.16.cloned.1.call-start = ((), (), s32[]{:S(2)}) async-start(), calls=%async_computation.13 | async-start | bytes 4915200 | tf_op jit(solution)/shard_map/all_gather | solution.py:882
  216.1 433.9 %reduce-scatter.6.cloned.1.call-start = ((), (), s32[]{:S(2)}) async-start(), calls=%async_computation.11 | async-start | bytes 9830400 | tf_op jit(solution)/shard_map/reduce_scatter | solution.py:989
  304.6 45.2 %collective-permute-start.32 = (bf16[384,2560]{1,0:T(8,128)(2,1)}, bf16[384,2560]{1,0:T(8,128)(2,1)}, u32[]{:S(2)}, u32[]{:S(2)}) collective-permute-start(bf16[384,2560]{1,0:T(8,128)(2,1)} %multiply_convert_fusion), channel_id=1, source_target_pairs={{0,1},{1,0},{2,3},{3,2},{4,5},{5,4},{6,7},{7,6},{8,9},{9,8},{10,11... | collective-permute-start | bytes 5898248 | tf_op jit(solution)/shard_map/cond/branch_1_fun/ppermute | solution.py:29
  304.9 44.9 %collective-permute-start.33 = (bf16[384,2560]{1,0:T(8,128)(2,1)}, bf16[384,2560]{1,0:T(8,128)(2,1)}, u32[]{:S(2)}, u32[]{:S(2)}) collective-permute-start(bf16[384,2560]{1,0:T(8,128)(2,1)} %multiply_convert_fusion), channel_id=1, source_target_pairs={{0,4},{4,0},{1,5},{5,1},{2,6},{6,2},{3,7},{7,3},{8,12},{12,8},{9,1... | collective-permute-start | bytes 5898248 | tf_op jit(solution)/shard_map/cond/branch_1_fun/ppermute | solution.py:29
  357.0 45.2 %collective-permute-start = (bf16[384,2560]{1,0:T(8,128)(2,1)}, bf16[384,2560]{1,0:T(8,128)(2,1)}, u32[]{:S(2)}, u32[]{:S(2)}) collective-permute-start(bf16[384,2560]{1,0:T(8,128)(2,1)} %get-tuple-element.380.rest_2_.rest_4_), channel_id=1, source_target_pairs={{0,1},{1,0},{2,3},{3,2},{4,5},{5,4},{6,7},{7,6},{8,9},{9,8},{10,11... | collective-permute-start | bytes 5898248 | tf_op jit(solution)/shard_map/cond/branch_1_fun/ppermute | solution.py:29
  358.7 44.9 %collective-permute-start.1 = (bf16[384,2560]{1,0:T(8,128)(2,1)}, bf16[384,2560]{1,0:T(8,128)(2,1)}, u32[]{:S(2)}, u32[]{:S(2)}) collective-permute-start(bf16[384,2560]{1,0:T(8,128)(2,1)} %get-tuple-element.377.rest_5_.rest_9_), channel_id=1, source_target_pairs={{0,4},{4,0},{1,5},{5,1},{2,6},{6,2},{3,7},{7,3},{8,12},{12,8},{9,1... | collective-permute-start | bytes 5898248 | tf_op jit(solution)/shard_map/cond/branch_1_fun/ppermute | solution.py:29
  404.1 45.0 %collective-permute-start.4 = (bf16[384,2560]{1,0:T(8,128)(2,1)}, bf16[384,2560]{1,0:T(8,128)(2,1)}, u32[]{:S(2)}, u32[]{:S(2)}) collective-permute-start(bf16[384,2560]{1,0:T(8,128)(2,1)} %get-tuple-element.402), channel_id=1, source_target_pairs={{0,1},{1,0},{2,3},{3,2},{4,5},{5,4},{6,7},{7,6},{8,9},{9,8},{10,11... | collective-permute-start | bytes 5898248 | tf_op jit(solution)/shard_map/cond/branch_1_fun/ppermute | solution.py:29
  404.4 44.8 %collective-permute-start.5 = (bf16[384,2560]{1,0:T(8,128)(2,1)}, bf16[384,2560]{1,0:T(8,128)(2,1)}, u32[]{:S(2)}, u32[]{:S(2)}) collective-permute-start(bf16[384,2560]{1,0:T(8,128)(2,1)} %get-tuple-element.402), channel_id=1, source_target_pairs={{0,4},{4,0},{1,5},{5,1},{2,6},{6,2},{3,7},{7,3},{8,12},{12,8},{9,1... | collective-permute-start | bytes 5898248 | tf_op jit(solution)/shard_map/cond/branch_1_fun/ppermute | solution.py:29
  449.2 44.2 %collective-permute-start.7 = (bf16[384,2560]{1,0:T(8,128)(2,1)}, bf16[384,2560]{1,0:T(8,128)(2,1)}, u32[]{:S(2)}, u32[]{:S(2)}) collective-permute-start(bf16[384,2560]{1,0:T(8,128)(2,1)} %collective-permute-done.5), channel_id=1, source_target_pairs={{0,1},{1,0},{2,3},{3,2},{4,5},{5,4},{6,7},{7,6},{8,9},{9,8},{10,11... | collective-permute-start | bytes 5898248 | tf_op jit(solution)/shard_map/cond/branch_1_fun/ppermute | solution.py:29
  493.6 294.3 %reduce-scatter.8.cloned.1.call-start = ((), (), s32[]{:S(2)}) async-start(), calls=%async_computation.14 | async-start | bytes 4915200 | tf_op jit(solution)/shard_map/reduce_scatter | solution.py:1036
  547.3 45.6 %collective-permute-start.15 = (bf16[768,2560]{1,0:T(8,128)(2,1)}, bf16[768,2560]{1,0:T(8,128)(2,1)}, u32[]{:S(2)}, u32[]{:S(2)}) collective-permute-start(bf16[768,2560]{1,0:T(8,128)(2,1)} %get-tuple-element.471), channel_id=1, source_target_pairs={{0,2},{2,0},{1,3},{3,1},{4,6},{6,4},{5,7},{7,5},{8,10},{10,8},{9,1... | collective-permute-start | bytes 11796488 | tf_op jit(solution)/shard_map/cond/branch_1_fun/ppermute | solution.py:29
  547.7 44.1 %collective-permute-start.12 = (bf16[192,2560]{1,0:T(8,128)(2,1)}, bf16[192,2560]{1,0:T(8,128)(2,1)}, u32[]{:S(2)}, u32[]{:S(2)}) collective-permute-start(bf16[192,2560]{1,0:T(8,128)(2,1)} %get-tuple-element.468), channel_id=1, source_target_pairs={{0,1},{1,0},{2,3},{3,2},{4,5},{5,4},{6,7},{7,6},{8,9},{9,8},{10,11... | collective-permute-start | bytes 2949128 | tf_op jit(solution)/shard_map/cond/branch_1_fun/ppermute | solution.py:29
  604.2 45.6 %collective-permute-start.20 = (bf16[768,2560]{1,0:T(8,128)(2,1)}, bf16[768,2560]{1,0:T(8,128)(2,1)}, u32[]{:S(2)}, u32[]{:S(2)}) collective-permute-start(bf16[768,2560]{1,0:T(8,128)(2,1)} %get-tuple-element.503), channel_id=1, source_target_pairs={{0,2},{2,0},{1,3},{3,1},{4,6},{6,4},{5,7},{7,5},{8,10},{10,8},{9,1... | collective-permute-start | bytes 11796488 | tf_op jit(solution)/shard_map/cond/branch_1_fun/ppermute | solution.py:29
  650.0 228.7 %reduce-scatter.12.cloned.1.call-start = ((), (), s32[]{:S(2)}) async-start(), calls=%async_computation.16 | async-start | bytes 4915200 | tf_op jit(solution)/shard_map/reduce_scatter | solution.py:1106
  683.6 50.9 %collective-permute-start.70 = (bf16[192,2560]{1,0:T(8,128)(2,1)}, bf16[192,2560]{1,0:T(8,128)(2,1)}, u32[]{:S(2)}, u32[]{:S(2)}) collective-permute-start(bf16[192,2560]{1,0:T(8,128)(2,1)} %get-tuple-element.562), channel_id=1, source_target_pairs={{0,1},{1,0},{2,3},{3,2},{4,5},{5,4},{6,7},{7,6},{8,9},{9,8},{10,11... | collective-permute-start | bytes 2949128 | tf_op jit(solution)/shard_map/cond/branch_1_fun/ppermute | solution.py:29
  685.0 49.5 %collective-permute-start.71 = (bf16[192,2560]{1,0:T(8,128)(2,1)}, bf16[192,2560]{1,0:T(8,128)(2,1)}, u32[]{:S(2)}, u32[]{:S(2)}) collective-permute-start(bf16[192,2560]{1,0:T(8,128)(2,1)} %get-tuple-element.563), channel_id=1, source_target_pairs={{0,4},{4,0},{1,5},{5,1},{2,6},{6,2},{3,7},{7,3},{8,12},{12,8},{9,1... | collective-permute-start | bytes 2949128 | tf_op jit(solution)/shard_map/cond/branch_1_fun/ppermute | solution.py:29
  686.7 47.9 %collective-permute-start.72 = (bf16[192,2560]{1,0:T(8,128)(2,1)}, bf16[192,2560]{1,0:T(8,128)(2,1)}, u32[]{:S(2)}, u32[]{:S(2)}) collective-permute-start(bf16[192,2560]{1,0:T(8,128)(2,1)} %get-tuple-element.564), channel_id=1, source_target_pairs={{0,1},{1,0},{2,3},{3,2},{4,5},{5,4},{6,7},{7,6},{8,9},{9,8},{10,11... | collective-permute-start | bytes 2949128 | tf_op jit(solution)/shard_map/cond/branch_1_fun/ppermute | solution.py:29
  688.1 46.4 %collective-permute-start.73 = (bf16[192,2560]{1,0:T(8,128)(2,1)}, bf16[192,2560]{1,0:T(8,128)(2,1)}, u32[]{:S(2)}, u32[]{:S(2)}) collective-permute-start(bf16[192,2560]{1,0:T(8,128)(2,1)} %get-tuple-element.565), channel_id=1, source_target_pairs={{0,4},{4,0},{1,5},{5,1},{2,6},{6,2},{3,7},{7,3},{8,12},{12,8},{9,1... | collective-permute-start | bytes 2949128 | tf_op jit(solution)/shard_map/cond/branch_1_fun/ppermute | solution.py:29
  688.1 46.4 %collective-permute-start.74 = (bf16[4,80,1536]{2,1,0:T(8,128)(2,1)}, bf16[4,80,1536]{2,1,0:T(8,128)(2,1)}, u32[]{:S(2)}, u32[]{:S(2)}) collective-permute-start(bf16[4,80,1536]{2,1,0:T(8,128)(2,1)} %pad_maximum_fusion.3), channel_id=1, source_target_pairs={{0,2},{2,0},{1,3},{3,1},{4,6},{6,4},{5,7},{7,5},{8,10},{10,8},{9,1... | collective-permute-start | bytes 2949128 | tf_op jit(solution)/shard_map/cond/branch_1_fun/ppermute | solution.py:29
  787.9 140.8 %reduce-scatter.10.cloned.1.call-start = ((), (), s32[]{:S(2)}) async-start(), calls=%async_computation.15 | async-start | bytes 2457600 | tf_op jit(solution)/shard_map/reduce_scatter | solution.py:1152
  878.6 88.0 %reduce-scatter.14.cloned.1.call-start = ((), (), s32[]{:S(2)}) async-start(), calls=%async_computation.17 | async-start | bytes 2048000 | tf_op jit(solution)/shard_map/reduce_scatter | solution.py:1163
  (111 other events, 2035.7 us)
Sparse Core Ops, SparseCore 0:
  22.6 45.9 all-gather.7
  70.8 75.2 all-gather.9
  147.7 48.2 all-gather.17
  215.1 86.9 all-gather.11
  303.5 74.9 all-gather.13
  380.0 74.9 all-gather.15
  493.7 147.3 reduce-scatter.5
  650.1 85.1 reduce-scatter.7
  788.0 83.0 reduce-scatter.11
  878.7 49.8 reduce-scatter.9
  931.0 35.5 reduce-scatter.13

commit v10 on v9

--- a/solution.py
+++ b/solution.py
@@ -524,7 +524,7 @@
             turn(step % 2, 1, grads, i, len(work))
 
 
-def mlp_grads(units, grads, hidden, pieces=(2,)):
+def mlp_grads(units, grads, hidden, pieces=(3,)):
     wide = units[0].shape[1]
     deep = hidden[0].shape[1]
     count = sum(piece.shape[0] for piece in units)
@@ -532,14 +532,14 @@
     last = wide // rows - 1
     return pl.pallas_call(
         functools.partial(mlp_grads_kernel, len(units)),
-        out_shape=[jax.ShapeDtypeStruct((wide, deep // 2 * piece), low) for piece in pieces],
+        out_shape=[jax.ShapeDtypeStruct((wide, deep // 3 * piece), low) for piece in pieces],
         grid=(last + 2,),
         in_specs=[
             pl.BlockSpec((piece.shape[0], rows), lambda s: (0, jnp.minimum(s, last))) for piece in units + grads
         ]
         + [pl.BlockSpec(piece.shape, lambda s: (0, 0), pipeline_mode=pl.Buffered(1)) for piece in hidden],
         out_specs=[
-            pl.BlockSpec((rows, deep // 2 * piece), lambda s: (jnp.maximum(s - 1, 0), 0)) for piece in pieces
+            pl.BlockSpec((rows, deep // 3 * piece), lambda s: (jnp.maximum(s - 1, 0), 0)) for piece in pieces
         ],
         scratch_shapes=[pltpu.VMEM((2, 2, rows, count), low)],
         compiler_params=pltpu.CompilerParams(vmem_limit_bytes=62 << 20),
@@ -1017,7 +1017,7 @@
         outs = far_sums[0], far_out, near_sums[0], near_out
         return partial, (near_sums[2], found, received), outs, one_d_c
 
-    cuts = (1, 1)
+    cuts = (2, 1)
     partial, own_sums, outs, one_d_c = boxed(
         sure,
         middle,
@@ -1054,25 +1054,21 @@
         if early is not None:
             early_own, to_c, to_x, to_y, to_d = deal(early.reshape(8, -1, early.shape[1]))
             (by_x, by_y, by_d), results = stage([(to_x, "x"), (to_y, "y"), (to_d, across(5))], remaining, given)
-            early_on = [(jnp.concatenate([to_c, by_x[1:], by_y[1:], by_d[1:]], 0), "c")]
         else:
-            results, early_on = remaining(*given), []
+            results = remaining(*given)
         (grad_resid, grad_attn), out_far, out_near = results
 
         def attention(grad_attn):
             grad_mixed = apply_rows(grad_attn, out_blocks)
             return attend_back(queries, grad_mixed, mixed_wide, logs, pairs, positions, size, base)
 
-        (*first, on), (grad_queries, mine, theirs) = stage(
-            [(out_far[0], "x"), (out_far[1], "y"), (out_far[2], "x"), (out_near[1], "y")]
-            + (early_on or [(out_near[1][:16], "c")]),
-            attention,
-            [grad_attn],
+        first, (grad_queries, mine, theirs) = stage(
+            [(out_far[0], "x"), (out_far[1], "y"), (out_far[2], "x"), (out_near[1], "y")], attention, [grad_attn]
         )
-        early = [early_own, by_x[:1], by_y[:1], by_d[:1], on] if early_on else []
         (found,), _ = stage([(theirs, "c")])
         mine = summed(mine, found)
         second = total(out_far[3], first[1]).astype(low), total(out_near[0], first[0]).astype(low)
+        on = [] if early is None else [(value, "c") for value in (to_c, by_x[1:], by_y[1:], by_d[1:])]
         (*found, x_second, y_second), (out_keep, out_send) = stage(
             [(mine[chips - d].astype(low), behind(-d)) for d in range(chips, 0, -1)]
             + [(second[0], "x"), (second[1], "y")],
@@ -1082,6 +1078,9 @@
         grad_pair = total(mine[chips], *found).astype(low)
         grad_qkv = jnp.concatenate([grad_queries, grad_pair], 1)
         out_own = out_near[2], out_near[3]
+        if early is not None:
+            on, _ = stage(on)
+            early = [early_own, by_x[:1], by_y[:1], by_d[:1], *on]
         return grad_qkv, grad_resid, first, (x_second, y_second), out_keep, out_send, out_own, early
 
     ahead = calls > 1 and per * part <= min(n for _, n in spans)

time: 985 us -> 984 us (level)
    ppermute x73 -> x76, waiting for transfers between devices: 220 us -> 222 us  [swap(): return lax.ppermute(value, axis, [(0, 1), (1, 0)])]
    ppermute x73 -> x76, starting transfers between devices: 57.7 us -> 59 us  [swap(): return lax.ppermute(value, axis, [(0, 1), (1, 0)])]
  transfers between devices with their start and end apart: 95 -> 98, of which waited for: 45 -> 48; matrix products, arithmetic and copies ran while one was open for 8% -> 8% of each run, Pallas kernels for 43% -> 43%
where the time goes in v10:
time: 984 us; the launch traced here: 975 us
  Pallas kernels  418 us (42%)
  waiting for transfers between devices  359 us (36%)
  starting transfers between devices  89.4 us (9%)
  other arithmetic  46 us (5%)
  local copies, waits for them, and re-layouts  45.1 us (5%)
  between operations  15.3 us (2%)
    ppermute x76, waiting for transfers between devices, swap(): return lax.ppermute(value, axis, [(0, 1), (1, 0)])  222 us
    pallas_call x4, Pallas kernels, mlp(): pl.pallas_call(functools.partial(mlp_kernel, each // 3, per, tiles), out_...  153 us
    pallas_call x2, Pallas kernels, mlp_grads(): pl.pallas_call(functools.partial(mlp_grads_kernel, len(units)), out_shape...  75.9 us
    ppermute x76, starting transfers between devices, swap(): return lax.ppermute(value, axis, [(0, 1), (1, 0)])  59 us
    ppermute x6, waiting for transfers between devices, behind(): return lambda value: lax.ppermute(value, ('z', 'y'), pairs)  53.5 us
    pallas_call x4, Pallas kernels, apply_rows(): pl.pallas_call(functools.partial(kernel, layout), out_shape=shape, grid_s...  45.3 us
    all_to_all x1, waiting for transfers between devices, local(): lax.all_to_all(mine, PLANE, split_axis=0, concat_axis=0, tiled=True)  44.5 us
    pallas_call x1, Pallas kernels, attend_back(): pl.pallas_call(functools.partial(attend_back_kernel, size, size ** (-0.5)...  35.6 us
  transfers between devices with their start and end apart: 98, of which 48 were waited for; matrix products, arithmetic and copies ran while one was open for 8% of the time, Pallas kernels for 43%

profile of v10, /device:TPU:0, one launch (start us, length us, event | category | flops | bytes accessed | tf_op | source)
XLA Modules:
  0.0 974.7 jit_solution(4772545163326829209)
XLA Ops:
  20.7 44.5 %all-to-all-done = bf16[8,80,3072]{2,1,0:T(8,128)(2,1)} async-done(((bf16[8,80,3072]{2,1,0:T(8,128)(2,1)}), bf16[8,80,3072]{2,1,0:T(8,128)(2,1)}, u32[]{:S(2)}, u32[]{:S(2)}) %all-to-all-start) | async-done | bytes 3932192 | tf_op jit(solution)/shard_map/all_to_all | solution.py:875
  69.5 145.5 %conditional.7 = (bf16[4,80,3072]{2,1,0:T(8,128)(2,1)}, bf16[4,80,3072]{2,1,0:T(8,128)(2,1)}, bf16[4,80,3072]{2,1,0:T(8,128)(2,1)}, bf16[4,80,3072]{2,1,0:T(8,12...) conditional(s32[]{:T(128)} %bitcast.17, () %tuple.126, ...), branch_computations={%region_0.0_spmd, %region_1.0_spmd} | conditional | flops 6947220 | bytes 125057264 | solution.py:61
  71.6 43.0 %collective-permute-done.42.rest_4_ = bf16[4,80,3072]{2,1,0:T(8,128)(2,1)} collective-permute-done((bf16[4,80,3072]{2,1,0:T(8,128)(2,1)}, bf16[4,80,3072]{2,1,0:T(8,128)(2,1)}, u32[]{:S(2)}, u32[]{:S(2)}) %collective-permute-start.42) | collective-permute-done | bytes 1966112 | tf_op jit(solution)/shard_map/cond/branch_1_fun/ppermute | solution.py:29
  121.9 18.0 %collective-permute-done.43.rest_5_ = bf16[2,80,3072]{2,1,0:T(8,128)(2,1)S(1)} collective-permute-done((bf16[2,80,3072]{2,1,0:T(8,128)(2,1)}, bf16[2,80,3072]{2,1,0:T(8,128)(2,1)S(1)}, u32[]{:S(2)}, u32[]{:S(2)}) %collective-permute-start.43) | collective-permute-done | bytes 983072 | tf_op jit(solution)/shard_map/cond/branch_1_fun/ppermute | solution.py:29
  145.6 11.9 %branch_1_fun.22 = bf16[384,3072]{1,0:T(8,128)(2,1)S(1)} custom-call(s32[8]{0:T(128)S(1)} %iota_xor_fusion.slots, bf16[384,2560]{1,0:T(8,128)(2,1)} %fusion.1.left, bf16[4,80,3072]{2,1,0:T(8,128)(2,1)} %get-tuple-element.282.rest_0_, bf16[4,80,3072]{2,1,0:T(8,128)(2,1)} %collective-permute-done.39.rest_1_, ...), custom_call_target="tpu_custom_call" | custom-call | flops 1048576 | bytes 4096 | tf_op jit(solution)/shard_map/cond/branch_1_fun/pallas_call | solution.py:319
  169.3 13.6 %collective-permute-done.48 = bf16[384,512]{1,0:T(8,128)(2,1)} collective-permute-done((bf16[384,512]{1,0:T(8,128)(2,1)S(1)}, bf16[384,512]{1,0:T(8,128)(2,1)}, u32[]{:S(2)}, u32[]{:S(2)}) %collective-permute-start.48) | collective-permute-done | bytes 393248 | tf_op jit(solution)/shard_map/cond/branch_1_fun/ppermute | solution.py:81
  187.6 10.0 %collective-permute-done.49 = bf16[384,512]{1,0:T(8,128)(2,1)} collective-permute-done((bf16[384,512]{1,0:T(8,128)(2,1)S(1)}, bf16[384,512]{1,0:T(8,128)(2,1)}, u32[]{:S(2)}, u32[]{:S(2)}) %collective-permute-start.49) | collective-permute-done | bytes 393248 | tf_op jit(solution)/shard_map/cond/branch_1_fun/ppermute | solution.py:81
  201.1 10.6 %collective-permute-done.50 = bf16[384,512]{1,0:T(8,128)(2,1)} collective-permute-done((bf16[384,512]{1,0:T(8,128)(2,1)S(1)}, bf16[384,512]{1,0:T(8,128)(2,1)}, u32[]{:S(2)}, u32[]{:S(2)}) %collective-permute-start.50) | collective-permute-done | bytes 393248 | tf_op jit(solution)/shard_map/cond/branch_1_fun/ppermute | solution.py:81
  216.3 140.8 %conditional.8 = (bf16[4,80,2560]{2,1,0:T(8,128)(2,1)}, bf16[4,80,2560]{2,1,0:T(8,128)(2,1)}, bf16[4,80,2560]{2,1,0:T(8,128)(2,1)}, bf16[4,80,2560]{2,1,0:T(8,12...) conditional(s32[]{:T(128)} %bitcast.17, () %tuple.124, ...), branch_computations={%region_3.0_spmd, %region_4.0_spmd} | conditional | flops 7012756 | bytes 129779728 | solution.py:61
  220.0 28.8 %branch_1_fun.23 = (bf16[384,2560]{1,0:T(8,128)(2,1)}, f32[384,2560]{1,0:T(8,128)}, f32[15,1,256]{2,1,0:T(1,128)S(1)}) custom-call(s32[1]{0:T(128)} %bitcast.2.core, s32[1,384]{1,0:T(1,128)S(1)} %get-tuple-element.327.places, bf16[384,2560]{1,0:T(8,128)(2,1)} %get-tuple-element.328.queries, bf16[384,512]{1,0:T(8,128)(2,1)} %get-tuple-element.329.rest_0_, ...), custom_call_target="tpu_custom_call" | custom-call | flops 1048576 | bytes 4096 | tf_op jit(solution)/shard_map/cond/branch_1_fun/pallas_call | solution.py:196
  264.3 17.0 %collective-permute-done.26.rest_6_ = bf16[2,80,2560]{2,1,0:T(8,128)(2,1)S(1)} collective-permute-done((bf16[2,80,2560]{2,1,0:T(8,128)(2,1)}, bf16[2,80,2560]{2,1,0:T(8,128)(2,1)S(1)}, u32[]{:S(2)}, u32[]{:S(2)}) %collective-permute-start.26) | collective-permute-done | bytes 819232 | tf_op jit(solution)/shard_map/cond/branch_1_fun/ppermute | solution.py:29
  286.6 11.9 %branch_1_fun.24 = f32[384,2560]{1,0:T(8,128)} custom-call(s32[8]{0:T(128)S(1)} %iota_xor_fusion.1.slots, bf16[384,2560]{1,0:T(8,128)(2,1)} %get-tuple-element.1257.left, f32[384,2560]{1,0:T(8,128)S(1)} %bitcast_convert_fusion.rest_0_, bf16[4,80,2560]{2,1,0:T(8,128)(2,1)S(1)} %copy-done.20, bf16[4,80,2560]{2,1,0:T(8,128)(2,1)} %collective-permute-done.21.rest_2_, ...), custom_call_target="tpu_custom_call" | custom-call | flops 1048576 | bytes 4096 | tf_op jit(solution)/shard_map/cond/branch_1_fun/pallas_call | solution.py:319
  306.7 43.1 %collective-permute-done.32 = bf16[384,2560]{1,0:T(8,128)(2,1)} collective-permute-done((bf16[384,2560]{1,0:T(8,128)(2,1)}, bf16[384,2560]{1,0:T(8,128)(2,1)}, u32[]{:S(2)}, u32[]{:S(2)}) %collective-permute-start.32) | collective-permute-done | bytes 1966112 | tf_op jit(solution)/shard_map/cond/branch_1_fun/ppermute | solution.py:29
  357.0 136.6 %conditional.9 = (bf16[384,2560]{1,0:T(8,128)(2,1)}, bf16[384,2560]{1,0:T(8,128)(2,1)}, bf16[384,2560]{1,0:T(8,128)(2,1)}, bf16[384,2560]{1,0:T(8,128)(2,1)}, bf...) conditional(s32[]{:T(128)} %bitcast.17, () %tuple.123, ...), branch_computations={%region_6.0_spmd, %region_7.0_spmd} | conditional | flops 3145728 | bytes 86520392 | solution.py:61
  360.4 36.6 %branch_1_fun.25 = (bf16[768,2560]{1,0:T(8,128)(2,1)}, bf16[768,2560]{1,0:T(8,128)(2,1)}, bf16[768,2560]{1,0:T(8,128)(2,1)}, bf16[768,2560]{1,0:T(8,128)(2,1)}, bf16[1536,1536]{1,0:T(8,128)(2,1)}) custom-call(bf16[2560,768]{1,0:T(8,128)(2,1)} %get-tuple-element.403.rest_0_, bf16[2560,768]{1,0:T(8,128)(2,1)} %get-tuple-element.404.rest_1_, ...), custom_call_target="tpu_custom_call" | custom-call | flops 1048576 | bytes 4096 | tf_op jit(solution)/shard_map/cond/branch_1_fun/pallas_call | solution.py:470
  410.8 36.3 %branch_1_fun.26 = (bf16[768,2560]{1,0:T(8,128)(2,1)}, bf16[768,2560]{1,0:T(8,128)(2,1)}, bf16[768,2560]{1,0:T(8,128)(2,1)}, bf16[768,2560]{1,0:T(8,128)(2,1)}, bf16[1536,1536]{1,0:T(8,128)(2,1)}) custom-call(bf16[2560,768]{1,0:T(8,128)(2,1)} %get-tuple-element.403.rest_0_, bf16[2560,768]{1,0:T(8,128)(2,1)} %get-tuple-element.404.rest_1_, ...), custom_call_target="tpu_custom_call" | custom-call | flops 1048576 | bytes 4096 | tf_op jit(solution)/shard_map/cond/branch_1_fun/pallas_call | solution.py:470
  451.5 38.0 %branch_1_fun.27 = bf16[2560,1536]{1,0:T(8,128)(2,1)} custom-call(bf16[384,2560]{1,0:T(8,128)(2,1)} %collective-permute-done.rest_2_.rest_0_, bf16[384,2560]{1,0:T(8,128)(2,1)} %get-tuple-element.405.rest_4_.rest_1_, bf16[384,2560]{1,0:T(8,128)(2,1)} %collective-permute-done.2.rest_6_.rest_2_, bf16[384,2560]{1,0:T(8,128)(2,1)} %get-tuple-element.406.rest_8_.rest_3_, ...), custom_call_target="tpu_custom_call" | custom-call | flops 1048576 | bytes 4096 | tf_op jit(solution)/shard_map/cond/branch_1_fun/pallas_call | solution.py:533
  495.1 154.8 %conditional.10 = (bf16[2560,1024]{1,0:T(8,128)(2,1)}, bf16[2560,512]{1,0:T(8,128)(2,1)}, bf16[768,2560]{1,0:T(8,128)(2,1)}, bf16[768,2560]{1,0:T(8,128)(2,1)}, ...) conditional(s32[]{:T(128)} %bitcast.17, () %tuple.133, ...), branch_computations={%region_9.0_spmd, %region_10.0_spmd} | conditional | flops 5242880 | bytes 94392864 | solution.py:61
  495.1 39.8 %branch_1_fun.28 = (bf16[768,2560]{1,0:T(8,128)(2,1)}, bf16[768,2560]{1,0:T(8,128)(2,1)}, bf16[768,2560]{1,0:T(8,128)(2,1)}, bf16[768,2560]{1,0:T(8,128)(2,1)}, bf16[1536,1536]{1,0:T(8,128)(2,1)}) custom-call(bf16[2560,768]{1,0:T(8,128)(2,1)} %get-tuple-element.439.rest_0_, bf16[2560,768]{1,0:T(8,128)(2,1)} %get-tuple-element.440.rest_1_, ...), custom_call_target="tpu_custom_call" | custom-call | flops 1048576 | bytes 4096 | tf_op jit(solution)/shard_map/cond/branch_1_fun/pallas_call | solution.py:470
  551.5 40.2 %branch_1_fun.30 = (bf16[768,2560]{1,0:T(8,128)(2,1)}, bf16[768,2560]{1,0:T(8,128)(2,1)}, bf16[768,2560]{1,0:T(8,128)(2,1)}, bf16[768,2560]{1,0:T(8,128)(2,1)}, bf16[1536,1536]{1,0:T(8,128)(2,1)}) custom-call(bf16[2560,768]{1,0:T(8,128)(2,1)} %get-tuple-element.439.rest_0_, bf16[2560,768]{1,0:T(8,128)(2,1)} %get-tuple-element.440.rest_1_, ...), custom_call_target="tpu_custom_call" | custom-call | flops 1048576 | bytes 4096 | tf_op jit(solution)/shard_map/cond/branch_1_fun/pallas_call | solution.py:470
  607.9 38.0 %branch_1_fun.32 = (bf16[2560,1024]{1,0:T(8,128)(2,1)}, bf16[2560,512]{1,0:T(8,128)(2,1)}) custom-call(bf16[384,2560]{1,0:T(8,128)(2,1)} %get-tuple-element.441.rest_2_.rest_0_, bf16[384,2560]{1,0:T(8,128)(2,1)} %get-tuple-element.443.rest_4_.rest_1_, bf16[384,2560]{1,0:T(8,128)(2,1)} %get-tuple-element.445.rest_6_.rest_2_, ...), custom_call_target="tpu_custom_call" | custom-call | flops 1048576 | bytes 4096 | tf_op jit(solution)/shard_map/cond/branch_1_fun/pallas_call | solution.py:533
  650.6 137.0 %conditional.11 = (bf16[384,3072]{1,0:T(8,128)(2,1)}, f32[384,2560]{1,0:T(8,128)}, bf16[192,2560]{1,0:T(8,128)(2,1)}, bf16[192,2560]{1,0:T(8,128)(2,1)}, bf16[19...) conditional(s32[]{:T(128)} %bitcast.17, () %tuple.122, ...), branch_computations={%region_11.0_spmd, %region_12.0_spmd} | conditional | flops 19727420 | bytes 144675504 | solution.py:61
  695.9 35.6 %branch_1_fun.38 = (bf16[384,2560]{1,0:T(8,128)(2,1)}, f32[4,384,512]{2,1,0:T(8,128)}, bf16[4,384,512]{2,1,0:T(8,128)(2,1)}) custom-call(s32[1]{0:T(128)} %bitcast.6.core, s32[1,384]{1,0:T(1,128)S(1)} %get-tuple-element.562.places, bf16[384,2560]{1,0:T(8,128)(2,1)} %get-tuple-element.563.queries, bf16[384,2560]{1,0:T(8,128)(2,1)} %copy-done.2, ...), custom_call_target="tpu_custom_call" | custom-call | flops 1048576 | bytes 4096 | tf_op jit(solution)/shard_map/cond/branch_1_fun/pallas_call | solution.py:229
  751.4 13.2 %branch_1_fun.39 = (bf16[4,4,80,2560]{3,2,1,0:T(8,128)(2,1)}, bf16[4,4,80,2560]{3,2,1,0:T(8,128)(2,1)}) custom-call(s32[8]{0:T(128)S(1)} %gather_fusion, bf16[384,2560]{1,0:T(8,128)(2,1)S(1)} %copy-done.1, bf16[384,2560]{1,0:T(8,128)(2,1)} %get-tuple-element.603.right), custom_call_target="tpu_custom_call" | custom-call | flops 1048576 | bytes 4096 | tf_op jit(solution)/shard_map/cond/branch_1_fun/pallas_call | solution.py:368
  789.1 91.0 %conditional.12 = (bf16[2560,384]{1,0:T(8,128)(2,1)}, bf16[2,80,2560]{2,1,0:T(8,128)(2,1)}, bf16[2,80,2560]{2,1,0:T(8,128)(2,1)}, bf16[4,80,2560]{2,1,0:T(8,128)...) conditional(s32[]{:T(128)} %bitcast.17, () %tuple.121, ...), branch_computations={%region_14.0_spmd, %region_15.17_spmd} | conditional | flops 25624604 | bytes 109343472 | solution.py:61
  800.5 11.9 %branch_1_fun.41 = f32[384,2560]{1,0:T(8,128)S(1)} custom-call(s32[8]{0:T(128)S(1)} %get-tuple-element.1155.slots, bf16[384,3072]{1,0:T(8,128)(2,1)} %get-tuple-element.644.value.left, bf16[4,80,3072]{2,1,0:T(8,128)(2,1)} %get-tuple-element.645.rest_0_, bf16[4,80,3072]{2,1,0:T(8,128)(2,1)} %get-tuple-element.646.rest_1_, ...), custom_call_target="tpu_custom_call" | custom-call | flops 1048576 | bytes 4096 | tf_op jit(solution)/shard_map/cond/branch_1_fun/pallas_call | solution.py:319
  848.2 14.1 %branch_1_fun.43 = bf16[2560,384]{1,0:T(8,128)(2,1)} custom-call(bf16[384,2560]{1,0:T(8,128)(2,1)} %get-tuple-element.682.rest_0_, bf16[384,2560]{1,0:T(8,128)(2,1)} %get-tuple-element.683.rest_1_, bf16[384,2560]{1,0:T(8,128)(2,1)} %get-tuple-element.684.rest_2_, bf16[384,2560]{1,0:T(8,128)(2,1)} %get-tuple-element.685.rest_3_, ...), custom_call_target="tpu_custom_call" | custom-call | flops 1048576 | bytes 4096 | tf_op jit(solution)/shard_map/cond/branch_1_fun/pallas_call | solution.py:568
  867.0 12.1 %collective-permute-done.65 = bf16[2,80,2560]{2,1,0:T(8,128)(2,1)} collective-permute-done((bf16[2,80,2560]{2,1,0:T(8,128)(2,1)S(1)}, bf16[2,80,2560]{2,1,0:T(8,128)(2,1)}, u32[]{:S(2)}, u32[]{:S(2)}) %collective-permute-start.65) | collective-permute-done | bytes 819232 | tf_op jit(solution)/shard_map/cond/branch_1_fun/ppermute | solution.py:29
  881.4 26.2 %conditional.13 = (bf16[320,2560]{1,0:T(8,128)(2,1)}, bf16[640,1536]{1,0:T(8,128)(2,1)S(1)}) conditional(s32[]{:T(128)} %bitcast.17, () %tuple.139, (bf16[4,80,2560]{2,1,0:T(8,128)(2,1)}, bf16[2,80,2560]{2,1,0:T(8,128)(2,1)}, bf16[2,80,2560]{2,1,0:T(8,128)(2,1)}, bf16[2,80,2560]{2,1,0:T(8,128)(2,1)}, bf16[2,80,2560]{2,1,0:T(8,128)(2,1)}, ...), branch_computations={%region_19.0_spmd, %region_20.0_spmd} | conditional | flops 12943360 | bytes 27852924 | solution.py:61
  886.3 17.0 %collective-permute-done.37 = bf16[2,80,2560]{2,1,0:T(8,128)(2,1)S(1)} collective-permute-done((bf16[2,80,2560]{2,1,0:T(8,128)(2,1)S(1)}, bf16[2,80,2560]{2,1,0:T(8,128)(2,1)S(1)}, u32[]{:S(2)}, u32[]{:S(2)}) %collective-permute-start.37) | collective-permute-done | bytes 819232 | tf_op jit(solution)/shard_map/cond/branch_1_fun/ppermute | solution.py:29
  912.7 15.2 %reduce-scatter.10.cloned.1.call-done = bf16[640,384]{1,0:T(8,128)(2,1)} async-done(((bf16[2560,384]{1,0:T(8,128)(2,1)}), bf16[640,384]{1,0:T(8,128)(2,1)}) %reduce-scatter.10.cloned.1.call-update) | async-done | bytes 491536 | tf_op jit(solution)/shard_map/reduce_scatter | solution.py:1151
  954.5 11.3 %reduce-scatter.14.cloned.1.call-done = bf16[80,2560]{1,0:T(8,128)(2,1)} async-done(((bf16[320,2560]{1,0:T(8,128)(2,1)}), bf16[80,2560]{1,0:T(8,128)(2,1)}) %reduce-scatter.14.cloned.1.call-update) | async-done | bytes 409616 | tf_op jit(solution)/shard_map/reduce_scatter | solution.py:1162
  (375 shorter events, 346.3 us)
Async XLA Ops:
  14.3 50.9 %all-to-all-start = ((bf16[8,80,3072]{2,1,0:T(8,128)(2,1)}), bf16[8,80,3072]{2,1,0:T(8,128)(2,1)}, u32[]{:S(2)}, u32[]{:S(2)}) async-start(bf16[8,80,3072]{2,1,0:T(8,128)(2,1)} %shard_map.249), calls=%async_computation | async-start | bytes 7864320 | tf_op jit(solution)/shard_map/all_to_all | solution.py:875
  19.6 49.8 %all-gather.8.cloned.1.call-start = ((), (), s32[]{:S(2)}) async-start(), calls=%async_computation.8 | async-start | bytes 2457600 | tf_op jit(solution)/shard_map/all_gather | solution.py:865
  20.7 195.5 %all-gather.10.cloned.1.call-start = ((), (), s32[]{:S(2)}) async-start(), calls=%async_computation.9 | async-start | bytes 4915200 | tf_op jit(solution)/shard_map/all_gather | solution.py:882
  67.5 148.7 %all-gather.18.cloned.1.call-start = ((), (), s32[]{:S(2)}) async-start(), calls=%async_computation.18 | async-start | bytes 2048000 | tf_op jit(solution)/shard_map/all_gather | solution.py:866
  68.2 288.8 %all-gather.12.cloned.1.call-start = ((), (), s32[]{:S(2)}) async-start(), calls=%async_computation.10 | async-start | bytes 4915200 | tf_op jit(solution)/shard_map/all_gather | solution.py:882
  69.5 45.1 %collective-permute-start.42 = (bf16[4,80,3072]{2,1,0:T(8,128)(2,1)}, bf16[4,80,3072]{2,1,0:T(8,128)(2,1)}, u32[]{:S(2)}, u32[]{:S(2)}) collective-permute-start(bf16[4,80,3072]{2,1,0:T(8,128)(2,1)} %get-tuple-element.282.rest_0_), channel_id=1, source_target_pairs={{0,4},{4,0},{1,5},{5,1},{2,6},{6,2},{3,7},{7,3},{8,12},{12,8},{9,1... | collective-permute-start | bytes 5898248 | tf_op jit(solution)/shard_map/cond/branch_1_fun/ppermute | solution.py:29
  70.3 47.2 %collective-permute-start.39 = (bf16[4,80,3072]{2,1,0:T(8,128)(2,1)}, bf16[4,80,3072]{2,1,0:T(8,128)(2,1)}, u32[]{:S(2)}, u32[]{:S(2)}) collective-permute-start(bf16[4,80,3072]{2,1,0:T(8,128)(2,1)} %get-tuple-element.282.rest_0_), channel_id=1, source_target_pairs={{0,1},{1,0},{2,3},{3,2},{4,5},{5,4},{6,7},{7,6},{8,9},{9,8},{10,11... | collective-permute-start | bytes 5898248 | tf_op jit(solution)/shard_map/cond/branch_1_fun/ppermute | solution.py:29
  157.6 54.1 %collective-permute-start.52 = (bf16[384,2560]{1,0:T(8,128)(2,1)S(1)}, bf16[384,2560]{1,0:T(8,128)(2,1)}, u32[]{:S(2)}, u32[]{:S(2)}) collective-permute-start(bf16[384,2560]{1,0:T(8,128)(2,1)S(1)} %copy-done.11), channel_id=1, source_target_pairs={{0,1},{1,0},{2,3},{3,2},{4,5},{5,4},{6,7},{7,6},{8,9},{9,8},{10,11... | collective-permute-start | bytes 5898248 | tf_op jit(solution)/shard_map/cond/branch_1_fun/ppermute | solution.py:29
  159.4 52.3 %collective-permute-start.53 = (bf16[384,2560]{1,0:T(8,128)(2,1)S(1)}, bf16[384,2560]{1,0:T(8,128)(2,1)}, u32[]{:S(2)}, u32[]{:S(2)}) collective-permute-start(bf16[384,2560]{1,0:T(8,128)(2,1)S(1)} %copy-done.11), channel_id=1, source_target_pairs={{0,4},{4,0},{1,5},{5,1},{2,6},{6,2},{3,7},{7,3},{8,12},{12,8},{9,1... | collective-permute-start | bytes 5898248 | tf_op jit(solution)/shard_map/cond/branch_1_fun/ppermute | solution.py:29
  161.1 50.5 %collective-permute-start.54 = (bf16[384,2560]{1,0:T(8,128)(2,1)S(1)}, bf16[384,2560]{1,0:T(8,128)(2,1)}, u32[]{:S(2)}, u32[]{:S(2)}) collective-permute-start(bf16[384,2560]{1,0:T(8,128)(2,1)S(1)} %copy-done.11), channel_id=1, source_target_pairs={{0,2},{2,0},{1,3},{3,1},{4,6},{6,4},{5,7},{7,5},{8,10},{10,8},{9,1... | collective-permute-start | bytes 5898248 | tf_op jit(solution)/shard_map/cond/branch_1_fun/ppermute | solution.py:29
  215.0 278.7 %all-gather.14.cloned.1.call-start = ((), (), s32[]{:S(2)}) async-start(), calls=%async_computation.12 | async-start | bytes 4915200 | tf_op jit(solution)/shard_map/all_gather | solution.py:882
  215.6 278.2 %all-gather.16.cloned.1.call-start = ((), (), s32[]{:S(2)}) async-start(), calls=%async_computation.13 | async-start | bytes 4915200 | tf_op jit(solution)/shard_map/all_gather | solution.py:882
  216.1 433.9 %reduce-scatter.6.cloned.1.call-start = ((), (), s32[]{:S(2)}) async-start(), calls=%async_computation.11 | async-start | bytes 9830400 | tf_op jit(solution)/shard_map/reduce_scatter | solution.py:989
  304.6 45.2 %collective-permute-start.32 = (bf16[384,2560]{1,0:T(8,128)(2,1)}, bf16[384,2560]{1,0:T(8,128)(2,1)}, u32[]{:S(2)}, u32[]{:S(2)}) collective-permute-start(bf16[384,2560]{1,0:T(8,128)(2,1)} %multiply_convert_fusion), channel_id=1, source_target_pairs={{0,1},{1,0},{2,3},{3,2},{4,5},{5,4},{6,7},{7,6},{8,9},{9,8},{10,11... | collective-permute-start | bytes 5898248 | tf_op jit(solution)/shard_map/cond/branch_1_fun/ppermute | solution.py:29
  305.0 44.9 %collective-permute-start.33 = (bf16[384,2560]{1,0:T(8,128)(2,1)}, bf16[384,2560]{1,0:T(8,128)(2,1)}, u32[]{:S(2)}, u32[]{:S(2)}) collective-permute-start(bf16[384,2560]{1,0:T(8,128)(2,1)} %multiply_convert_fusion), channel_id=1, source_target_pairs={{0,4},{4,0},{1,5},{5,1},{2,6},{6,2},{3,7},{7,3},{8,12},{12,8},{9,1... | collective-permute-start | bytes 5898248 | tf_op jit(solution)/shard_map/cond/branch_1_fun/ppermute | solution.py:29
  306.7 43.2 %collective-permute-start.34 = (bf16[384,2560]{1,0:T(8,128)(2,1)}, bf16[384,2560]{1,0:T(8,128)(2,1)}, u32[]{:S(2)}, u32[]{:S(2)}) collective-permute-start(bf16[384,2560]{1,0:T(8,128)(2,1)} %multiply_convert_fusion), channel_id=1, source_target_pairs={{0,2},{2,0},{1,3},{3,1},{4,6},{6,4},{5,7},{7,5},{8,10},{10,8},{9,1... | collective-permute-start | bytes 5898248 | tf_op jit(solution)/shard_map/cond/branch_1_fun/ppermute | solution.py:29
  357.0 45.2 %collective-permute-start = (bf16[384,2560]{1,0:T(8,128)(2,1)}, bf16[384,2560]{1,0:T(8,128)(2,1)}, u32[]{:S(2)}, u32[]{:S(2)}) collective-permute-start(bf16[384,2560]{1,0:T(8,128)(2,1)} %get-tuple-element.380.rest_2_.rest_4_), channel_id=1, source_target_pairs={{0,1},{1,0},{2,3},{3,2},{4,5},{5,4},{6,7},{7,6},{8,9},{9,8},{10,11... | collective-permute-start | bytes 5898248 | tf_op jit(solution)/shard_map/cond/branch_1_fun/ppermute | solution.py:29
  358.7 44.9 %collective-permute-start.1 = (bf16[384,2560]{1,0:T(8,128)(2,1)}, bf16[384,2560]{1,0:T(8,128)(2,1)}, u32[]{:S(2)}, u32[]{:S(2)}) collective-permute-start(bf16[384,2560]{1,0:T(8,128)(2,1)} %get-tuple-element.377.rest_5_.rest_9_), channel_id=1, source_target_pairs={{0,4},{4,0},{1,5},{5,1},{2,6},{6,2},{3,7},{7,3},{8,12},{12,8},{9,1... | collective-permute-start | bytes 5898248 | tf_op jit(solution)/shard_map/cond/branch_1_fun/ppermute | solution.py:29
  404.1 45.0 %collective-permute-start.4 = (bf16[384,2560]{1,0:T(8,128)(2,1)}, bf16[384,2560]{1,0:T(8,128)(2,1)}, u32[]{:S(2)}, u32[]{:S(2)}) collective-permute-start(bf16[384,2560]{1,0:T(8,128)(2,1)} %get-tuple-element.402), channel_id=1, source_target_pairs={{0,1},{1,0},{2,3},{3,2},{4,5},{5,4},{6,7},{7,6},{8,9},{9,8},{10,11... | collective-permute-start | bytes 5898248 | tf_op jit(solution)/shard_map/cond/branch_1_fun/ppermute | solution.py:29
  404.5 44.8 %collective-permute-start.5 = (bf16[384,2560]{1,0:T(8,128)(2,1)}, bf16[384,2560]{1,0:T(8,128)(2,1)}, u32[]{:S(2)}, u32[]{:S(2)}) collective-permute-start(bf16[384,2560]{1,0:T(8,128)(2,1)} %get-tuple-element.402), channel_id=1, source_target_pairs={{0,4},{4,0},{1,5},{5,1},{2,6},{6,2},{3,7},{7,3},{8,12},{12,8},{9,1... | collective-permute-start | bytes 5898248 | tf_op jit(solution)/shard_map/cond/branch_1_fun/ppermute | solution.py:29
  449.3 44.1 %collective-permute-start.7 = (bf16[384,2560]{1,0:T(8,128)(2,1)}, bf16[384,2560]{1,0:T(8,128)(2,1)}, u32[]{:S(2)}, u32[]{:S(2)}) collective-permute-start(bf16[384,2560]{1,0:T(8,128)(2,1)} %collective-permute-done.5), channel_id=1, source_target_pairs={{0,1},{1,0},{2,3},{3,2},{4,5},{5,4},{6,7},{7,6},{8,9},{9,8},{10,11... | collective-permute-start | bytes 5898248 | tf_op jit(solution)/shard_map/cond/branch_1_fun/ppermute | solution.py:29
  493.6 294.1 %reduce-scatter.8.cloned.1.call-start = ((), (), s32[]{:S(2)}) async-start(), calls=%async_computation.14 | async-start | bytes 6553600 | tf_op jit(solution)/shard_map/reduce_scatter | solution.py:1036
  547.3 45.6 %collective-permute-start.15 = (bf16[768,2560]{1,0:T(8,128)(2,1)}, bf16[768,2560]{1,0:T(8,128)(2,1)}, u32[]{:S(2)}, u32[]{:S(2)}) collective-permute-start(bf16[768,2560]{1,0:T(8,128)(2,1)} %get-tuple-element.471), channel_id=1, source_target_pairs={{0,2},{2,0},{1,3},{3,1},{4,6},{6,4},{5,7},{7,5},{8,10},{10,8},{9,1... | collective-permute-start | bytes 11796488 | tf_op jit(solution)/shard_map/cond/branch_1_fun/ppermute | solution.py:29
  547.7 44.0 %collective-permute-start.12 = (bf16[192,2560]{1,0:T(8,128)(2,1)}, bf16[192,2560]{1,0:T(8,128)(2,1)}, u32[]{:S(2)}, u32[]{:S(2)}) collective-permute-start(bf16[192,2560]{1,0:T(8,128)(2,1)} %get-tuple-element.468), channel_id=1, source_target_pairs={{0,1},{1,0},{2,3},{3,2},{4,5},{5,4},{6,7},{7,6},{8,9},{9,8},{10,11... | collective-permute-start | bytes 2949128 | tf_op jit(solution)/shard_map/cond/branch_1_fun/ppermute | solution.py:29
  604.2 45.6 %collective-permute-start.20 = (bf16[768,2560]{1,0:T(8,128)(2,1)}, bf16[768,2560]{1,0:T(8,128)(2,1)}, u32[]{:S(2)}, u32[]{:S(2)}) collective-permute-start(bf16[768,2560]{1,0:T(8,128)(2,1)} %get-tuple-element.503), channel_id=1, source_target_pairs={{0,2},{2,0},{1,3},{3,1},{4,6},{6,4},{5,7},{7,5},{8,10},{10,8},{9,1... | collective-permute-start | bytes 11796488 | tf_op jit(solution)/shard_map/cond/branch_1_fun/ppermute | solution.py:29
  650.0 230.2 %reduce-scatter.12.cloned.1.call-start = ((), (), s32[]{:S(2)}) async-start(), calls=%async_computation.16 | async-start | bytes 3276800 | tf_op jit(solution)/shard_map/reduce_scatter | solution.py:1105
  679.3 54.1 %collective-permute-start.70 = (bf16[192,2560]{1,0:T(8,128)(2,1)}, bf16[192,2560]{1,0:T(8,128)(2,1)}, u32[]{:S(2)}, u32[]{:S(2)}) collective-permute-start(bf16[192,2560]{1,0:T(8,128)(2,1)} %get-tuple-element.558), channel_id=1, source_target_pairs={{0,1},{1,0},{2,3},{3,2},{4,5},{5,4},{6,7},{7,6},{8,9},{9,8},{10,11... | collective-permute-start | bytes 2949128 | tf_op jit(solution)/shard_map/cond/branch_1_fun/ppermute | solution.py:29
  680.7 52.7 %collective-permute-start.71 = (bf16[192,2560]{1,0:T(8,128)(2,1)}, bf16[192,2560]{1,0:T(8,128)(2,1)}, u32[]{:S(2)}, u32[]{:S(2)}) collective-permute-start(bf16[192,2560]{1,0:T(8,128)(2,1)} %get-tuple-element.559), channel_id=1, source_target_pairs={{0,4},{4,0},{1,5},{5,1},{2,6},{6,2},{3,7},{7,3},{8,12},{12,8},{9,1... | collective-permute-start | bytes 2949128 | tf_op jit(solution)/shard_map/cond/branch_1_fun/ppermute | solution.py:29
  681.5 51.8 %collective-permute-start.72 = (bf16[192,2560]{1,0:T(8,128)(2,1)}, bf16[192,2560]{1,0:T(8,128)(2,1)}, u32[]{:S(2)}, u32[]{:S(2)}) collective-permute-start(bf16[192,2560]{1,0:T(8,128)(2,1)} %get-tuple-element.560), channel_id=1, source_target_pairs={{0,1},{1,0},{2,3},{3,2},{4,5},{5,4},{6,7},{7,6},{8,9},{9,8},{10,11... | collective-permute-start | bytes 2949128 | tf_op jit(solution)/shard_map/cond/branch_1_fun/ppermute | solution.py:29
  682.9 50.5 %collective-permute-start.73 = (bf16[192,2560]{1,0:T(8,128)(2,1)}, bf16[192,2560]{1,0:T(8,128)(2,1)}, u32[]{:S(2)}, u32[]{:S(2)}) collective-permute-start(bf16[192,2560]{1,0:T(8,128)(2,1)} %get-tuple-element.561), channel_id=1, source_target_pairs={{0,4},{4,0},{1,5},{5,1},{2,6},{6,2},{3,7},{7,3},{8,12},{12,8},{9,1... | collective-permute-start | bytes 2949128 | tf_op jit(solution)/shard_map/cond/branch_1_fun/ppermute | solution.py:29
  787.6 140.2 %reduce-scatter.10.cloned.1.call-start = ((), (), s32[]{:S(2)}) async-start(), calls=%async_computation.15 | async-start | bytes 2457600 | tf_op jit(solution)/shard_map/reduce_scatter | solution.py:1151
  880.1 85.6 %reduce-scatter.14.cloned.1.call-start = ((), (), s32[]{:S(2)}) async-start(), calls=%async_computation.17 | async-start | bytes 2048000 | tf_op jit(solution)/shard_map/reduce_scatter | solution.py:1162
  (117 other events, 2045.8 us)
Sparse Core Ops, SparseCore 0:
  22.6 45.9 all-gather.7
  70.8 75.2 all-gather.9
  147.7 48.2 all-gather.17
  215.1 86.9 all-gather.11
  303.5 74.9 all-gather.13
  380.0 74.9 all-gather.15
  493.8 147.3 reduce-scatter.5
  650.1 106.2 reduce-scatter.7
  787.7 62.4 reduce-scatter.11
  880.2 47.5 reduce-scatter.9
  930.2 35.5 reduce-scatter.13

commit v11 on v10

--- a/solution.py
+++ b/solution.py
@@ -1106,7 +1106,7 @@
     ]
 
     def collect(
-        grad_qkv, first, second, out_own, out_keep, out_send, grad_resid, resid, qkv_blocks, flat_ones, scale_one, tokens
+        grad_qkv, out_keep, out_send, grad_resid, qkv_blocks, flat_ones, scale_one, tokens
     ):
         own, to_c, to_x, to_y, to_d = spread(grad_qkv)
 
@@ -1121,28 +1121,20 @@
         (by_c,), out_parts = stage([(on, "c")], lambda *given: part_sums(*given), [out_keep, out_found])
         diag_top, diag_bottom, x_top, x_bottom, y_top, y_bottom, out_sums = out_parts
 
-        def sums(resid, *gathered):
-            gathered = jnp.concatenate(gathered, 0)
-            return token_grads(flat_ones, gathered), resid + joined(out_own, first, second)
-
-        started, (qkv_column, output) = stage(
+        started, qkv_column = stage(
             [(diag_top, "x"), (diag_bottom, "y"), (x_top, "x"), (y_bottom, "y")],
-            sums,
-            [resid, own, by_x[:count], by_y[:count], by_d[:count], by_c],
+            lambda *gathered: token_grads(flat_ones, jnp.concatenate(gathered, 0)),
+            [own, by_x[:count], by_y[:count], by_d[:count], by_c],
         )
-        return qkv_column, grad_tokens, output, x_bottom, y_top, out_sums, started
-
-    qkv_column, grad_tokens, output, x_bottom, y_top, out_sums, started = boxed(
+        return qkv_column, grad_tokens, x_bottom, y_top, out_sums, started
+
+    qkv_column, grad_tokens, x_bottom, y_top, out_sums, started = boxed(
         sure,
         collect,
         after(grad_qkv, columns[1]),
-        first,
-        second,
-        out_own,
         out_keep,
         out_send,
         grad_resid,
-        resid,
         qkv_blocks,
         flat_ones,
         scale_one,
@@ -1150,15 +1142,28 @@
     )
     qkv_low = lax.psum_scatter(qkv_column, "z", scatter_dimension=0, tiled=True)
 
-    def end(x_bottom, y_top, out_sums, started, columns):
+    def end(x_bottom, y_top, out_sums, started, columns, first, second, out_own, resid):
         x_bottom, y_top = total(x_bottom, started[1]).astype(low), total(y_top, started[0]).astype(low)
-        received, every = stage(
-            [(x_bottom, "x"), (y_top, "y")], lambda *columns: jnp.concatenate(columns, 1), columns
-        )
+        def last(resid, *columns):
+            return jnp.concatenate(columns, 1), resid + joined(out_own, first, second)
+
+        received, (every, output) = stage([(x_bottom, "x"), (y_top, "y")], last, [resid, *columns])
         column = joined(out_sums, started, received).astype(low)
-        return column.reshape(-1, column.shape[-1]), every
-
-    out_column, every = boxed(sure, end, x_bottom, y_top, out_sums, started, columns[1:] if ahead else columns)
+        return column.reshape(-1, column.shape[-1]), every, output
+
+    out_column, every, output = boxed(
+        sure,
+        end,
+        x_bottom,
+        y_top,
+        out_sums,
+        started,
+        columns[1:] if ahead else columns,
+        first,
+        second,
+        out_own,
+        resid,
+    )
     out_sum = lax.psum_scatter(out_column, "z", scatter_dimension=0, tiled=True).astype(f32)
     every = after(every, out_column).reshape(8, -1, every.shape[1])
     every = lax.all_to_all(every, PLANE, split_axis=0, concat_axis=0, tiled=True)

time: 984 us -> 980 us (level)
  transfers between devices with their start and end apart: 98 -> 98, of which waited for: 48 -> 50; matrix products, arithmetic and copies ran while one was open for 8% -> 7% of each run, Pallas kernels for 43% -> 43%
where the time goes in v11:
time: 980 us; the launch traced here: 970 us
  Pallas kernels  418 us (43%)
  waiting for transfers between devices  357 us (36%)
  starting transfers between devices  89.4 us (9%)
  other arithmetic  46 us (5%)
  local copies, waits for them, and re-layouts  42.9 us (4%)
  between operations  15.3 us (2%)
    ppermute x76, waiting for transfers between devices, swap(): return lax.ppermute(value, axis, [(0, 1), (1, 0)])  220 us
    pallas_call x4, Pallas kernels, mlp(): pl.pallas_call(functools.partial(mlp_kernel, each // 3, per, tiles), out_...  153 us
    pallas_call x2, Pallas kernels, mlp_grads(): pl.pallas_call(functools.partial(mlp_grads_kernel, len(units)), out_shape...  75.9 us
    ppermute x76, starting transfers between devices, swap(): return lax.ppermute(value, axis, [(0, 1), (1, 0)])  58.9 us
    ppermute x6, waiting for transfers between devices, behind(): return lambda value: lax.ppermute(value, ('z', 'y'), pairs)  53.4 us
    pallas_call x4, Pallas kernels, apply_rows(): pl.pallas_call(functools.partial(kernel, layout), out_shape=shape, grid_s...  45.3 us
    all_to_all x1, waiting for transfers between devices, local(): lax.all_to_all(mine, PLANE, split_axis=0, concat_axis=0, tiled=True)  44.6 us
    pallas_call x1, Pallas kernels, attend_back(): pl.pallas_call(functools.partial(attend_back_kernel, size, size ** (-0.5)...  35.6 us
  transfers between devices with their start and end apart: 98, of which 50 were waited for; matrix products, arithmetic and copies ran while one was open for 7% of the time, Pallas kernels for 43%

profile of v11, /device:TPU:0, one launch (start us, length us, event | category | flops | bytes accessed | tf_op | source)
XLA Modules:
  0.0 970.4 jit_solution(16198761523776778407)
XLA Ops:
  20.7 44.6 %all-to-all-done = bf16[8,80,3072]{2,1,0:T(8,128)(2,1)} async-done(((bf16[8,80,3072]{2,1,0:T(8,128)(2,1)}), bf16[8,80,3072]{2,1,0:T(8,128)(2,1)}, u32[]{:S(2)}, u32[]{:S(2)}) %all-to-all-start) | async-done | bytes 3932192 | tf_op jit(solution)/shard_map/all_to_all | solution.py:875
  69.6 145.4 %conditional.7 = (bf16[4,80,3072]{2,1,0:T(8,128)(2,1)}, bf16[4,80,3072]{2,1,0:T(8,128)(2,1)}, bf16[4,80,3072]{2,1,0:T(8,128)(2,1)}, bf16[4,80,3072]{2,1,0:T(8,12...) conditional(s32[]{:T(128)} %bitcast.17, () %tuple.127, ...), branch_computations={%region_0.0_spmd, %region_1.0_spmd} | conditional | flops 6947220 | bytes 125057264 | solution.py:61
  71.6 43.0 %collective-permute-done.42.rest_4_ = bf16[4,80,3072]{2,1,0:T(8,128)(2,1)} collective-permute-done((bf16[4,80,3072]{2,1,0:T(8,128)(2,1)}, bf16[4,80,3072]{2,1,0:T(8,128)(2,1)}, u32[]{:S(2)}, u32[]{:S(2)}) %collective-permute-start.42) | collective-permute-done | bytes 1966112 | tf_op jit(solution)/shard_map/cond/branch_1_fun/ppermute | solution.py:29
  121.9 17.9 %collective-permute-done.43.rest_5_ = bf16[2,80,3072]{2,1,0:T(8,128)(2,1)S(1)} collective-permute-done((bf16[2,80,3072]{2,1,0:T(8,128)(2,1)}, bf16[2,80,3072]{2,1,0:T(8,128)(2,1)S(1)}, u32[]{:S(2)}, u32[]{:S(2)}) %collective-permute-start.43) | collective-permute-done | bytes 983072 | tf_op jit(solution)/shard_map/cond/branch_1_fun/ppermute | solution.py:29
  145.6 11.9 %branch_1_fun.22 = bf16[384,3072]{1,0:T(8,128)(2,1)S(1)} custom-call(s32[8]{0:T(128)S(1)} %iota_xor_fusion.slots, bf16[384,2560]{1,0:T(8,128)(2,1)} %fusion.1.left, bf16[4,80,3072]{2,1,0:T(8,128)(2,1)} %get-tuple-element.282.rest_0_, bf16[4,80,3072]{2,1,0:T(8,128)(2,1)} %collective-permute-done.39.rest_1_, ...), custom_call_target="tpu_custom_call" | custom-call | flops 1048576 | bytes 4096 | tf_op jit(solution)/shard_map/cond/branch_1_fun/pallas_call | solution.py:319
  169.3 13.6 %collective-permute-done.48 = bf16[384,512]{1,0:T(8,128)(2,1)} collective-permute-done((bf16[384,512]{1,0:T(8,128)(2,1)S(1)}, bf16[384,512]{1,0:T(8,128)(2,1)}, u32[]{:S(2)}, u32[]{:S(2)}) %collective-permute-start.48) | collective-permute-done | bytes 393248 | tf_op jit(solution)/shard_map/cond/branch_1_fun/ppermute | solution.py:81
  187.7 9.9 %collective-permute-done.49 = bf16[384,512]{1,0:T(8,128)(2,1)} collective-permute-done((bf16[384,512]{1,0:T(8,128)(2,1)S(1)}, bf16[384,512]{1,0:T(8,128)(2,1)}, u32[]{:S(2)}, u32[]{:S(2)}) %collective-permute-start.49) | collective-permute-done | bytes 393248 | tf_op jit(solution)/shard_map/cond/branch_1_fun/ppermute | solution.py:81
  201.1 10.6 %collective-permute-done.50 = bf16[384,512]{1,0:T(8,128)(2,1)} collective-permute-done((bf16[384,512]{1,0:T(8,128)(2,1)S(1)}, bf16[384,512]{1,0:T(8,128)(2,1)}, u32[]{:S(2)}, u32[]{:S(2)}) %collective-permute-start.50) | collective-permute-done | bytes 393248 | tf_op jit(solution)/shard_map/cond/branch_1_fun/ppermute | solution.py:81
  216.2 140.8 %conditional.8 = (bf16[4,80,2560]{2,1,0:T(8,128)(2,1)}, bf16[4,80,2560]{2,1,0:T(8,128)(2,1)}, bf16[4,80,2560]{2,1,0:T(8,128)(2,1)}, bf16[4,80,2560]{2,1,0:T(8,12...) conditional(s32[]{:T(128)} %bitcast.17, () %tuple.125, ...), branch_computations={%region_3.0_spmd, %region_4.0_spmd} | conditional | flops 7012756 | bytes 129779728 | solution.py:61
  220.0 28.9 %branch_1_fun.23 = (bf16[384,2560]{1,0:T(8,128)(2,1)}, f32[384,2560]{1,0:T(8,128)}, f32[15,1,256]{2,1,0:T(1,128)S(1)}) custom-call(s32[1]{0:T(128)} %bitcast.2.core, s32[1,384]{1,0:T(1,128)S(1)} %get-tuple-element.327.places, bf16[384,2560]{1,0:T(8,128)(2,1)} %get-tuple-element.328.queries, bf16[384,512]{1,0:T(8,128)(2,1)} %get-tuple-element.329.rest_0_, ...), custom_call_target="tpu_custom_call" | custom-call | flops 1048576 | bytes 4096 | tf_op jit(solution)/shard_map/cond/branch_1_fun/pallas_call | solution.py:196
  264.2 17.0 %collective-permute-done.26.rest_6_ = bf16[2,80,2560]{2,1,0:T(8,128)(2,1)S(1)} collective-permute-done((bf16[2,80,2560]{2,1,0:T(8,128)(2,1)}, bf16[2,80,2560]{2,1,0:T(8,128)(2,1)S(1)}, u32[]{:S(2)}, u32[]{:S(2)}) %collective-permute-start.26) | collective-permute-done | bytes 819232 | tf_op jit(solution)/shard_map/cond/branch_1_fun/ppermute | solution.py:29
  286.6 11.9 %branch_1_fun.24 = f32[384,2560]{1,0:T(8,128)} custom-call(s32[8]{0:T(128)S(1)} %iota_xor_fusion.1.slots, bf16[384,2560]{1,0:T(8,128)(2,1)} %get-tuple-element.1250.left, f32[384,2560]{1,0:T(8,128)S(1)} %bitcast_convert_fusion.rest_0_, bf16[4,80,2560]{2,1,0:T(8,128)(2,1)S(1)} %copy-done.20, bf16[4,80,2560]{2,1,0:T(8,128)(2,1)} %collective-permute-done.21.rest_2_, ...), custom_call_target="tpu_custom_call" | custom-call | flops 1048576 | bytes 4096 | tf_op jit(solution)/shard_map/cond/branch_1_fun/pallas_call | solution.py:319
  306.7 43.1 %collective-permute-done.32 = bf16[384,2560]{1,0:T(8,128)(2,1)} collective-permute-done((bf16[384,2560]{1,0:T(8,128)(2,1)}, bf16[384,2560]{1,0:T(8,128)(2,1)}, u32[]{:S(2)}, u32[]{:S(2)}) %collective-permute-start.32) | collective-permute-done | bytes 1966112 | tf_op jit(solution)/shard_map/cond/branch_1_fun/ppermute | solution.py:29
  357.0 136.5 %conditional.9 = (bf16[384,2560]{1,0:T(8,128)(2,1)}, bf16[384,2560]{1,0:T(8,128)(2,1)}, bf16[384,2560]{1,0:T(8,128)(2,1)}, bf16[384,2560]{1,0:T(8,128)(2,1)}, bf...) conditional(s32[]{:T(128)} %bitcast.17, () %tuple.124, ...), branch_computations={%region_6.0_spmd, %region_7.0_spmd} | conditional | flops 3145728 | bytes 86520392 | solution.py:61
  360.4 36.5 %branch_1_fun.25 = (bf16[768,2560]{1,0:T(8,128)(2,1)}, bf16[768,2560]{1,0:T(8,128)(2,1)}, bf16[768,2560]{1,0:T(8,128)(2,1)}, bf16[768,2560]{1,0:T(8,128)(2,1)}, bf16[1536,1536]{1,0:T(8,128)(2,1)}) custom-call(bf16[2560,768]{1,0:T(8,128)(2,1)} %get-tuple-element.403.rest_0_, bf16[2560,768]{1,0:T(8,128)(2,1)} %get-tuple-element.404.rest_1_, ...), custom_call_target="tpu_custom_call" | custom-call | flops 1048576 | bytes 4096 | tf_op jit(solution)/shard_map/cond/branch_1_fun/pallas_call | solution.py:470
  410.7 36.3 %branch_1_fun.26 = (bf16[768,2560]{1,0:T(8,128)(2,1)}, bf16[768,2560]{1,0:T(8,128)(2,1)}, bf16[768,2560]{1,0:T(8,128)(2,1)}, bf16[768,2560]{1,0:T(8,128)(2,1)}, bf16[1536,1536]{1,0:T(8,128)(2,1)}) custom-call(bf16[2560,768]{1,0:T(8,128)(2,1)} %get-tuple-element.403.rest_0_, bf16[2560,768]{1,0:T(8,128)(2,1)} %get-tuple-element.404.rest_1_, ...), custom_call_target="tpu_custom_call" | custom-call | flops 1048576 | bytes 4096 | tf_op jit(solution)/shard_map/cond/branch_1_fun/pallas_call | solution.py:470
  451.4 38.0 %branch_1_fun.27 = bf16[2560,1536]{1,0:T(8,128)(2,1)} custom-call(bf16[384,2560]{1,0:T(8,128)(2,1)} %collective-permute-done.rest_2_.rest_0_, bf16[384,2560]{1,0:T(8,128)(2,1)} %get-tuple-element.405.rest_4_.rest_1_, bf16[384,2560]{1,0:T(8,128)(2,1)} %collective-permute-done.2.rest_6_.rest_2_, bf16[384,2560]{1,0:T(8,128)(2,1)} %get-tuple-element.406.rest_8_.rest_3_, ...), custom_call_target="tpu_custom_call" | custom-call | flops 1048576 | bytes 4096 | tf_op jit(solution)/shard_map/cond/branch_1_fun/pallas_call | solution.py:533
  495.1 154.9 %conditional.10 = (bf16[2560,1024]{1,0:T(8,128)(2,1)}, bf16[2560,512]{1,0:T(8,128)(2,1)}, bf16[768,2560]{1,0:T(8,128)(2,1)}, bf16[768,2560]{1,0:T(8,128)(2,1)}, ...) conditional(s32[]{:T(128)} %bitcast.17, () %tuple.134, ...), branch_computations={%region_9.0_spmd, %region_10.0_spmd} | conditional | flops 5242880 | bytes 94392864 | solution.py:61
  495.1 39.9 %branch_1_fun.28 = (bf16[768,2560]{1,0:T(8,128)(2,1)}, bf16[768,2560]{1,0:T(8,128)(2,1)}, bf16[768,2560]{1,0:T(8,128)(2,1)}, bf16[768,2560]{1,0:T(8,128)(2,1)}, bf16[1536,1536]{1,0:T(8,128)(2,1)}) custom-call(bf16[2560,768]{1,0:T(8,128)(2,1)} %get-tuple-element.439.rest_0_, bf16[2560,768]{1,0:T(8,128)(2,1)} %get-tuple-element.440.rest_1_, ...), custom_call_target="tpu_custom_call" | custom-call | flops 1048576 | bytes 4096 | tf_op jit(solution)/shard_map/cond/branch_1_fun/pallas_call | solution.py:470
  551.5 40.2 %branch_1_fun.30 = (bf16[768,2560]{1,0:T(8,128)(2,1)}, bf16[768,2560]{1,0:T(8,128)(2,1)}, bf16[768,2560]{1,0:T(8,128)(2,1)}, bf16[768,2560]{1,0:T(8,128)(2,1)}, bf16[1536,1536]{1,0:T(8,128)(2,1)}) custom-call(bf16[2560,768]{1,0:T(8,128)(2,1)} %get-tuple-element.439.rest_0_, bf16[2560,768]{1,0:T(8,128)(2,1)} %get-tuple-element.440.rest_1_, ...), custom_call_target="tpu_custom_call" | custom-call | flops 1048576 | bytes 4096 | tf_op jit(solution)/shard_map/cond/branch_1_fun/pallas_call | solution.py:470
  607.9 38.0 %branch_1_fun.32 = (bf16[2560,1024]{1,0:T(8,128)(2,1)}, bf16[2560,512]{1,0:T(8,128)(2,1)}) custom-call(bf16[384,2560]{1,0:T(8,128)(2,1)} %get-tuple-element.441.rest_2_.rest_0_, bf16[384,2560]{1,0:T(8,128)(2,1)} %get-tuple-element.443.rest_4_.rest_1_, bf16[384,2560]{1,0:T(8,128)(2,1)} %get-tuple-element.445.rest_6_.rest_2_, ...), custom_call_target="tpu_custom_call" | custom-call | flops 1048576 | bytes 4096 | tf_op jit(solution)/shard_map/cond/branch_1_fun/pallas_call | solution.py:533
  650.7 136.9 %conditional.11 = (bf16[384,3072]{1,0:T(8,128)(2,1)}, f32[384,2560]{1,0:T(8,128)}, bf16[192,2560]{1,0:T(8,128)(2,1)}, bf16[192,2560]{1,0:T(8,128)(2,1)}, bf16[19...) conditional(s32[]{:T(128)} %bitcast.17, () %tuple.123, ...), branch_computations={%region_11.0_spmd, %region_12.0_spmd} | conditional | flops 19727420 | bytes 144675504 | solution.py:61
  685.0 9.7 branch_1_fun.37.grads
  696.0 35.6 %branch_1_fun.38 = (bf16[384,2560]{1,0:T(8,128)(2,1)}, f32[4,384,512]{2,1,0:T(8,128)}, bf16[4,384,512]{2,1,0:T(8,128)(2,1)}) custom-call(s32[1]{0:T(128)} %bitcast.6.core, s32[1,384]{1,0:T(1,128)S(1)} %get-tuple-element.562.places, bf16[384,2560]{1,0:T(8,128)(2,1)} %get-tuple-element.563.queries, bf16[384,2560]{1,0:T(8,128)(2,1)} %copy-done.2, ...), custom_call_target="tpu_custom_call" | custom-call | flops 1048576 | bytes 4096 | tf_op jit(solution)/shard_map/cond/branch_1_fun/pallas_call | solution.py:229
  751.4 13.2 %branch_1_fun.39 = (bf16[4,4,80,2560]{3,2,1,0:T(8,128)(2,1)}, bf16[4,4,80,2560]{3,2,1,0:T(8,128)(2,1)}) custom-call(s32[8]{0:T(128)S(1)} %gather_fusion, bf16[384,2560]{1,0:T(8,128)(2,1)S(1)} %copy-done.1, bf16[384,2560]{1,0:T(8,128)(2,1)} %get-tuple-element.603.right), custom_call_target="tpu_custom_call" | custom-call | flops 1048576 | bytes 4096 | tf_op jit(solution)/shard_map/cond/branch_1_fun/pallas_call | solution.py:368
  789.2 86.8 %conditional.12 = (bf16[2560,384]{1,0:T(8,128)(2,1)}, bf16[2,80,2560]{2,1,0:T(8,128)(2,1)}, bf16[2,80,2560]{2,1,0:T(8,128)(2,1)}, bf16[4,80,2560]{2,1,0:T(8,128)...) conditional(s32[]{:T(128)} %bitcast.17, () %tuple.122, ...), branch_computations={%region_14.0_spmd, %region_15.17_spmd} | conditional | flops 18743324 | bytes 97153816 | solution.py:61
  800.6 11.9 %branch_1_fun.41 = f32[384,2560]{1,0:T(8,128)S(1)} custom-call(s32[8]{0:T(128)S(1)} %get-tuple-element.1148.slots, bf16[384,3072]{1,0:T(8,128)(2,1)} %get-tuple-element.644.value.left, bf16[4,80,3072]{2,1,0:T(8,128)(2,1)} %get-tuple-element.645.rest_0_, bf16[4,80,3072]{2,1,0:T(8,128)(2,1)} %get-tuple-element.646.rest_1_, ...), custom_call_target="tpu_custom_call" | custom-call | flops 1048576 | bytes 4096 | tf_op jit(solution)/shard_map/cond/branch_1_fun/pallas_call | solution.py:319
  842.5 14.1 %branch_1_fun.43 = bf16[2560,384]{1,0:T(8,128)(2,1)} custom-call(bf16[384,2560]{1,0:T(8,128)(2,1)} %get-tuple-element.681.rest_0_, bf16[384,2560]{1,0:T(8,128)(2,1)} %get-tuple-element.682.rest_1_, bf16[384,2560]{1,0:T(8,128)(2,1)} %get-tuple-element.683.rest_2_, bf16[384,2560]{1,0:T(8,128)(2,1)} %get-tuple-element.684.rest_3_, ...), custom_call_target="tpu_custom_call" | custom-call | flops 1048576 | bytes 4096 | tf_op jit(solution)/shard_map/cond/branch_1_fun/pallas_call | solution.py:568
  859.2 15.7 %collective-permute-done.65 = bf16[2,80,2560]{2,1,0:T(8,128)(2,1)} collective-permute-done((bf16[2,80,2560]{2,1,0:T(8,128)(2,1)S(1)}, bf16[2,80,2560]{2,1,0:T(8,128)(2,1)}, u32[]{:S(2)}, u32[]{:S(2)}) %collective-permute-start.65) | collective-permute-done | bytes 819232 | tf_op jit(solution)/shard_map/cond/branch_1_fun/ppermute | solution.py:29
  877.3 26.2 %conditional.13 = (bf16[320,2560]{1,0:T(8,128)(2,1)}, bf16[640,1536]{1,0:T(8,128)(2,1)S(1)}, f32[1,384,2560]{2,1,0:T(8,128)}) conditional(s32[]{:T(128)} %bitcast.17, () %tuple.121, (bf16[4,80,2560]{2,1,0:T(8,128)(2,1)}, bf16[2,80,2560]{2,1,0:T(8,128)(2,1)}, bf16[2,80,2560]{2,1,0:T(8,128)(2,1)}, bf16[2,80,2560]{2,1,0:T(8,128)(2,1)}, ...), branch_computations={%region_18.0_spmd, %region_19.0_spmd} | conditional | flops 19824640 | bytes 49479812 | solution.py:61
  908.5 15.1 %reduce-scatter.12.cloned.1.call-done = bf16[640,384]{1,0:T(8,128)(2,1)} async-done(((bf16[2560,384]{1,0:T(8,128)(2,1)}), bf16[640,384]{1,0:T(8,128)(2,1)}) %reduce-scatter.12.cloned.1.call-update) | async-done | bytes 491536 | tf_op jit(solution)/shard_map/reduce_scatter | solution.py:1143
  950.3 11.2 %reduce-scatter.14.cloned.1.call-done = bf16[80,2560]{1,0:T(8,128)(2,1)} async-done(((bf16[320,2560]{1,0:T(8,128)(2,1)}), bf16[80,2560]{1,0:T(8,128)(2,1)}) %reduce-scatter.14.cloned.1.call-update) | async-done | bytes 409616 | tf_op jit(solution)/shard_map/reduce_scatter | solution.py:1167
  (377 shorter events, 346.2 us)
Async XLA Ops:
  14.3 51.0 %all-to-all-start = ((bf16[8,80,3072]{2,1,0:T(8,128)(2,1)}), bf16[8,80,3072]{2,1,0:T(8,128)(2,1)}, u32[]{:S(2)}, u32[]{:S(2)}) async-start(bf16[8,80,3072]{2,1,0:T(8,128)(2,1)} %shard_map.249), calls=%async_computation | async-start | bytes 7864320 | tf_op jit(solution)/shard_map/all_to_all | solution.py:875
  19.6 49.9 %all-gather.8.cloned.1.call-start = ((), (), s32[]{:S(2)}) async-start(), calls=%async_computation.8 | async-start | bytes 2457600 | tf_op jit(solution)/shard_map/all_gather | solution.py:865
  20.7 195.5 %all-gather.10.cloned.1.call-start = ((), (), s32[]{:S(2)}) async-start(), calls=%async_computation.9 | async-start | bytes 4915200 | tf_op jit(solution)/shard_map/all_gather | solution.py:882
  67.6 148.6 %all-gather.18.cloned.1.call-start = ((), (), s32[]{:S(2)}) async-start(), calls=%async_computation.18 | async-start | bytes 2048000 | tf_op jit(solution)/shard_map/all_gather | solution.py:866
  68.3 288.7 %all-gather.12.cloned.1.call-start = ((), (), s32[]{:S(2)}) async-start(), calls=%async_computation.10 | async-start | bytes 4915200 | tf_op jit(solution)/shard_map/all_gather | solution.py:882
  69.6 45.0 %collective-permute-start.42 = (bf16[4,80,3072]{2,1,0:T(8,128)(2,1)}, bf16[4,80,3072]{2,1,0:T(8,128)(2,1)}, u32[]{:S(2)}, u32[]{:S(2)}) collective-permute-start(bf16[4,80,3072]{2,1,0:T(8,128)(2,1)} %get-tuple-element.282.rest_0_), channel_id=1, source_target_pairs={{0,4},{4,0},{1,5},{5,1},{2,6},{6,2},{3,7},{7,3},{8,12},{12,8},{9,1... | collective-permute-start | bytes 5898248 | tf_op jit(solution)/shard_map/cond/branch_1_fun/ppermute | solution.py:29
  70.3 47.2 %collective-permute-start.39 = (bf16[4,80,3072]{2,1,0:T(8,128)(2,1)}, bf16[4,80,3072]{2,1,0:T(8,128)(2,1)}, u32[]{:S(2)}, u32[]{:S(2)}) collective-permute-start(bf16[4,80,3072]{2,1,0:T(8,128)(2,1)} %get-tuple-element.282.rest_0_), channel_id=1, source_target_pairs={{0,1},{1,0},{2,3},{3,2},{4,5},{5,4},{6,7},{7,6},{8,9},{9,8},{10,11... | collective-permute-start | bytes 5898248 | tf_op jit(solution)/shard_map/cond/branch_1_fun/ppermute | solution.py:29
  157.6 54.1 %collective-permute-start.52 = (bf16[384,2560]{1,0:T(8,128)(2,1)S(1)}, bf16[384,2560]{1,0:T(8,128)(2,1)}, u32[]{:S(2)}, u32[]{:S(2)}) collective-permute-start(bf16[384,2560]{1,0:T(8,128)(2,1)S(1)} %copy-done.11), channel_id=1, source_target_pairs={{0,1},{1,0},{2,3},{3,2},{4,5},{5,4},{6,7},{7,6},{8,9},{9,8},{10,11... | collective-permute-start | bytes 5898248 | tf_op jit(solution)/shard_map/cond/branch_1_fun/ppermute | solution.py:29
  159.4 52.3 %collective-permute-start.53 = (bf16[384,2560]{1,0:T(8,128)(2,1)S(1)}, bf16[384,2560]{1,0:T(8,128)(2,1)}, u32[]{:S(2)}, u32[]{:S(2)}) collective-permute-start(bf16[384,2560]{1,0:T(8,128)(2,1)S(1)} %copy-done.11), channel_id=1, source_target_pairs={{0,4},{4,0},{1,5},{5,1},{2,6},{6,2},{3,7},{7,3},{8,12},{12,8},{9,1... | collective-permute-start | bytes 5898248 | tf_op jit(solution)/shard_map/cond/branch_1_fun/ppermute | solution.py:29
  161.1 50.5 %collective-permute-start.54 = (bf16[384,2560]{1,0:T(8,128)(2,1)S(1)}, bf16[384,2560]{1,0:T(8,128)(2,1)}, u32[]{:S(2)}, u32[]{:S(2)}) collective-permute-start(bf16[384,2560]{1,0:T(8,128)(2,1)S(1)} %copy-done.11), channel_id=1, source_target_pairs={{0,2},{2,0},{1,3},{3,1},{4,6},{6,4},{5,7},{7,5},{8,10},{10,8},{9,1... | collective-permute-start | bytes 5898248 | tf_op jit(solution)/shard_map/cond/branch_1_fun/ppermute | solution.py:29
  215.0 278.7 %all-gather.14.cloned.1.call-start = ((), (), s32[]{:S(2)}) async-start(), calls=%async_computation.12 | async-start | bytes 4915200 | tf_op jit(solution)/shard_map/all_gather | solution.py:882
  215.5 278.1 %all-gather.16.cloned.1.call-start = ((), (), s32[]{:S(2)}) async-start(), calls=%async_computation.13 | async-start | bytes 4915200 | tf_op jit(solution)/shard_map/all_gather | solution.py:882
  216.1 434.0 %reduce-scatter.6.cloned.1.call-start = ((), (), s32[]{:S(2)}) async-start(), calls=%async_computation.11 | async-start | bytes 9830400 | tf_op jit(solution)/shard_map/reduce_scatter | solution.py:989
  304.6 45.2 %collective-permute-start.32 = (bf16[384,2560]{1,0:T(8,128)(2,1)}, bf16[384,2560]{1,0:T(8,128)(2,1)}, u32[]{:S(2)}, u32[]{:S(2)}) collective-permute-start(bf16[384,2560]{1,0:T(8,128)(2,1)} %multiply_convert_fusion), channel_id=1, source_target_pairs={{0,1},{1,0},{2,3},{3,2},{4,5},{5,4},{6,7},{7,6},{8,9},{9,8},{10,11... | collective-permute-start | bytes 5898248 | tf_op jit(solution)/shard_map/cond/branch_1_fun/ppermute | solution.py:29
  305.0 44.9 %collective-permute-start.33 = (bf16[384,2560]{1,0:T(8,128)(2,1)}, bf16[384,2560]{1,0:T(8,128)(2,1)}, u32[]{:S(2)}, u32[]{:S(2)}) collective-permute-start(bf16[384,2560]{1,0:T(8,128)(2,1)} %multiply_convert_fusion), channel_id=1, source_target_pairs={{0,4},{4,0},{1,5},{5,1},{2,6},{6,2},{3,7},{7,3},{8,12},{12,8},{9,1... | collective-permute-start | bytes 5898248 | tf_op jit(solution)/shard_map/cond/branch_1_fun/ppermute | solution.py:29
  306.7 43.2 %collective-permute-start.34 = (bf16[384,2560]{1,0:T(8,128)(2,1)}, bf16[384,2560]{1,0:T(8,128)(2,1)}, u32[]{:S(2)}, u32[]{:S(2)}) collective-permute-start(bf16[384,2560]{1,0:T(8,128)(2,1)} %multiply_convert_fusion), channel_id=1, source_target_pairs={{0,2},{2,0},{1,3},{3,1},{4,6},{6,4},{5,7},{7,5},{8,10},{10,8},{9,1... | collective-permute-start | bytes 5898248 | tf_op jit(solution)/shard_map/cond/branch_1_fun/ppermute | solution.py:29
  357.0 45.2 %collective-permute-start = (bf16[384,2560]{1,0:T(8,128)(2,1)}, bf16[384,2560]{1,0:T(8,128)(2,1)}, u32[]{:S(2)}, u32[]{:S(2)}) collective-permute-start(bf16[384,2560]{1,0:T(8,128)(2,1)} %get-tuple-element.380.rest_2_.rest_4_), channel_id=1, source_target_pairs={{0,1},{1,0},{2,3},{3,2},{4,5},{5,4},{6,7},{7,6},{8,9},{9,8},{10,11... | collective-permute-start | bytes 5898248 | tf_op jit(solution)/shard_map/cond/branch_1_fun/ppermute | solution.py:29
  358.7 44.9 %collective-permute-start.1 = (bf16[384,2560]{1,0:T(8,128)(2,1)}, bf16[384,2560]{1,0:T(8,128)(2,1)}, u32[]{:S(2)}, u32[]{:S(2)}) collective-permute-start(bf16[384,2560]{1,0:T(8,128)(2,1)} %get-tuple-element.377.rest_5_.rest_9_), channel_id=1, source_target_pairs={{0,4},{4,0},{1,5},{5,1},{2,6},{6,2},{3,7},{7,3},{8,12},{12,8},{9,1... | collective-permute-start | bytes 5898248 | tf_op jit(solution)/shard_map/cond/branch_1_fun/ppermute | solution.py:29
  404.1 45.0 %collective-permute-start.4 = (bf16[384,2560]{1,0:T(8,128)(2,1)}, bf16[384,2560]{1,0:T(8,128)(2,1)}, u32[]{:S(2)}, u32[]{:S(2)}) collective-permute-start(bf16[384,2560]{1,0:T(8,128)(2,1)} %get-tuple-element.402), channel_id=1, source_target_pairs={{0,1},{1,0},{2,3},{3,2},{4,5},{5,4},{6,7},{7,6},{8,9},{9,8},{10,11... | collective-permute-start | bytes 5898248 | tf_op jit(solution)/shard_map/cond/branch_1_fun/ppermute | solution.py:29
  404.5 44.8 %collective-permute-start.5 = (bf16[384,2560]{1,0:T(8,128)(2,1)}, bf16[384,2560]{1,0:T(8,128)(2,1)}, u32[]{:S(2)}, u32[]{:S(2)}) collective-permute-start(bf16[384,2560]{1,0:T(8,128)(2,1)} %get-tuple-element.402), channel_id=1, source_target_pairs={{0,4},{4,0},{1,5},{5,1},{2,6},{6,2},{3,7},{7,3},{8,12},{12,8},{9,1... | collective-permute-start | bytes 5898248 | tf_op jit(solution)/shard_map/cond/branch_1_fun/ppermute | solution.py:29
  449.2 44.1 %collective-permute-start.7 = (bf16[384,2560]{1,0:T(8,128)(2,1)}, bf16[384,2560]{1,0:T(8,128)(2,1)}, u32[]{:S(2)}, u32[]{:S(2)}) collective-permute-start(bf16[384,2560]{1,0:T(8,128)(2,1)} %collective-permute-done.5), channel_id=1, source_target_pairs={{0,1},{1,0},{2,3},{3,2},{4,5},{5,4},{6,7},{7,6},{8,9},{9,8},{10,11... | collective-permute-start | bytes 5898248 | tf_op jit(solution)/shard_map/cond/branch_1_fun/ppermute | solution.py:29
  493.6 294.2 %reduce-scatter.8.cloned.1.call-start = ((), (), s32[]{:S(2)}) async-start(), calls=%async_computation.14 | async-start | bytes 6553600 | tf_op jit(solution)/shard_map/reduce_scatter | solution.py:1036
  547.4 45.6 %collective-permute-start.15 = (bf16[768,2560]{1,0:T(8,128)(2,1)}, bf16[768,2560]{1,0:T(8,128)(2,1)}, u32[]{:S(2)}, u32[]{:S(2)}) collective-permute-start(bf16[768,2560]{1,0:T(8,128)(2,1)} %get-tuple-element.471), channel_id=1, source_target_pairs={{0,2},{2,0},{1,3},{3,1},{4,6},{6,4},{5,7},{7,5},{8,10},{10,8},{9,1... | collective-permute-start | bytes 11796488 | tf_op jit(solution)/shard_map/cond/branch_1_fun/ppermute | solution.py:29
  547.7 44.0 %collective-permute-start.12 = (bf16[192,2560]{1,0:T(8,128)(2,1)}, bf16[192,2560]{1,0:T(8,128)(2,1)}, u32[]{:S(2)}, u32[]{:S(2)}) collective-permute-start(bf16[192,2560]{1,0:T(8,128)(2,1)} %get-tuple-element.468), channel_id=1, source_target_pairs={{0,1},{1,0},{2,3},{3,2},{4,5},{5,4},{6,7},{7,6},{8,9},{9,8},{10,11... | collective-permute-start | bytes 2949128 | tf_op jit(solution)/shard_map/cond/branch_1_fun/ppermute | solution.py:29
  604.3 45.6 %collective-permute-start.20 = (bf16[768,2560]{1,0:T(8,128)(2,1)}, bf16[768,2560]{1,0:T(8,128)(2,1)}, u32[]{:S(2)}, u32[]{:S(2)}) collective-permute-start(bf16[768,2560]{1,0:T(8,128)(2,1)} %get-tuple-element.503), channel_id=1, source_target_pairs={{0,2},{2,0},{1,3},{3,1},{4,6},{6,4},{5,7},{7,5},{8,10},{10,8},{9,1... | collective-permute-start | bytes 11796488 | tf_op jit(solution)/shard_map/cond/branch_1_fun/ppermute | solution.py:29
  650.1 226.0 %reduce-scatter.10.cloned.1.call-start = ((), (), s32[]{:S(2)}) async-start(), calls=%async_computation.15 | async-start | bytes 3276800 | tf_op jit(solution)/shard_map/reduce_scatter | solution.py:1105
  679.4 54.0 %collective-permute-start.70 = (bf16[192,2560]{1,0:T(8,128)(2,1)}, bf16[192,2560]{1,0:T(8,128)(2,1)}, u32[]{:S(2)}, u32[]{:S(2)}) collective-permute-start(bf16[192,2560]{1,0:T(8,128)(2,1)} %get-tuple-element.558), channel_id=1, source_target_pairs={{0,1},{1,0},{2,3},{3,2},{4,5},{5,4},{6,7},{7,6},{8,9},{9,8},{10,11... | collective-permute-start | bytes 2949128 | tf_op jit(solution)/shard_map/cond/branch_1_fun/ppermute | solution.py:29
  680.8 52.6 %collective-permute-start.71 = (bf16[192,2560]{1,0:T(8,128)(2,1)}, bf16[192,2560]{1,0:T(8,128)(2,1)}, u32[]{:S(2)}, u32[]{:S(2)}) collective-permute-start(bf16[192,2560]{1,0:T(8,128)(2,1)} %get-tuple-element.559), channel_id=1, source_target_pairs={{0,4},{4,0},{1,5},{5,1},{2,6},{6,2},{3,7},{7,3},{8,12},{12,8},{9,1... | collective-permute-start | bytes 2949128 | tf_op jit(solution)/shard_map/cond/branch_1_fun/ppermute | solution.py:29
  681.7 51.7 %collective-permute-start.72 = (bf16[192,2560]{1,0:T(8,128)(2,1)}, bf16[192,2560]{1,0:T(8,128)(2,1)}, u32[]{:S(2)}, u32[]{:S(2)}) collective-permute-start(bf16[192,2560]{1,0:T(8,128)(2,1)} %get-tuple-element.560), channel_id=1, source_target_pairs={{0,1},{1,0},{2,3},{3,2},{4,5},{5,4},{6,7},{7,6},{8,9},{9,8},{10,11... | collective-permute-start | bytes 2949128 | tf_op jit(solution)/shard_map/cond/branch_1_fun/ppermute | solution.py:29
  683.0 50.4 %collective-permute-start.73 = (bf16[192,2560]{1,0:T(8,128)(2,1)}, bf16[192,2560]{1,0:T(8,128)(2,1)}, u32[]{:S(2)}, u32[]{:S(2)}) collective-permute-start(bf16[192,2560]{1,0:T(8,128)(2,1)} %get-tuple-element.561), channel_id=1, source_target_pairs={{0,4},{4,0},{1,5},{5,1},{2,6},{6,2},{3,7},{7,3},{8,12},{12,8},{9,1... | collective-permute-start | bytes 2949128 | tf_op jit(solution)/shard_map/cond/branch_1_fun/ppermute | solution.py:29
  787.7 135.9 %reduce-scatter.12.cloned.1.call-start = ((), (), s32[]{:S(2)}) async-start(), calls=%async_computation.16 | async-start | bytes 2457600 | tf_op jit(solution)/shard_map/reduce_scatter | solution.py:1143
  876.0 85.5 %reduce-scatter.14.cloned.1.call-start = ((), (), s32[]{:S(2)}) async-start(), calls=%async_computation.17 | async-start | bytes 2048000 | tf_op jit(solution)/shard_map/reduce_scatter | solution.py:1167
  (118 other events, 2039.3 us)
Sparse Core Ops, SparseCore 0:
  22.6 45.9 all-gather.7
  70.8 75.2 all-gather.9
  147.7 48.2 all-gather.17
  215.1 86.9 all-gather.11
  303.5 74.9 all-gather.13
  380.0 74.9 all-gather.15
  493.7 147.4 reduce-scatter.5
  650.2 106.2 reduce-scatter.7
  787.8 62.4 reduce-scatter.9
  876.1 47.4 reduce-scatter.11
  925.9 35.5 reduce-scatter.13

commit v12 on v11

--- a/solution.py
+++ b/solution.py
@@ -548,11 +548,14 @@
 
 
 def token_grads_kernel(number, *rest):
-    units, (right, out, turned) = rest[:number], rest[number:]
+    units, (*rights, out, turned) = rest[:number], rest[number:]
 
     @pl.when(pl.program_id(0) == 0)
     def _():
-        turned[...] = right[...].T
+        at = 0
+        for right in rights:
+            turned[:, at : at + right.shape[0]] = right[...].T
+            at += right.shape[0]
 
     value, at = 0.0, 0
     for unit in units:
@@ -561,21 +564,21 @@
     out[...] = value.astype(low).T
 
 
-def token_grads(units, right):
+def token_grads(units, rights, sizes):
     wide = units[0].shape[1]
-    count, deep = right.shape
+    count, deep = sum(sizes), rights[0].shape[1]
     rows = 512
     return pl.pallas_call(
         functools.partial(token_grads_kernel, len(units)),
         out_shape=jax.ShapeDtypeStruct((wide, deep), low),
         grid=(wide // rows,),
         in_specs=[pl.BlockSpec((piece.shape[0], rows), lambda s: (0, s)) for piece in units]
-        + [pl.BlockSpec(right.shape, lambda s: (0, 0), pipeline_mode=pl.Buffered(1))],
+        + [pl.BlockSpec((size, deep), lambda s: (0, 0), pipeline_mode=pl.Buffered(1)) for size in sizes],
         out_specs=pl.BlockSpec((rows, deep), lambda s: (s, 0)),
         scratch_shapes=[pltpu.VMEM((deep, count), low)],
         compiler_params=pltpu.CompilerParams(vmem_limit_bytes=56 << 20),
         cost_estimate=NOMINAL,
-    )(*units, right)
+    )(*units, *rights)
 
 
 def spread_kernel(slots, value, *outs):
@@ -1123,8 +1126,8 @@
 
         started, qkv_column = stage(
             [(diag_top, "x"), (diag_bottom, "y"), (x_top, "x"), (y_bottom, "y")],
-            lambda *gathered: token_grads(flat_ones, jnp.concatenate(gathered, 0)),
-            [own, by_x[:count], by_y[:count], by_d[:count], by_c],
+            lambda *gathered: token_grads(flat_ones, gathered, [count] * 4 + [4 * count]),
+            [own, by_x, by_y, by_d, by_c],
         )
         return qkv_column, grad_tokens, x_bottom, y_top, out_sums, started
 

time: 980 us -> 980 us (level)
  no operation moved by 1% of the time
where the time goes in v12:
time: 980 us; the launch traced here: 970 us
  Pallas kernels  418 us (43%)
  waiting for transfers between devices  359 us (37%)
  starting transfers between devices  89.5 us (9%)
  other arithmetic  46 us (5%)
  local copies, waits for them, and re-layouts  40.8 us (4%)
  between operations  15.3 us (2%)
    ppermute x76, waiting for transfers between devices, swap(): return lax.ppermute(value, axis, [(0, 1), (1, 0)])  221 us
    pallas_call x4, Pallas kernels, mlp(): pl.pallas_call(functools.partial(mlp_kernel, each // 3, per, tiles), out_...  153 us
    pallas_call x2, Pallas kernels, mlp_grads(): pl.pallas_call(functools.partial(mlp_grads_kernel, len(units)), out_shape...  75.9 us
    ppermute x76, starting transfers between devices, swap(): return lax.ppermute(value, axis, [(0, 1), (1, 0)])  59 us
    ppermute x6, waiting for transfers between devices, behind(): return lambda value: lax.ppermute(value, ('z', 'y'), pairs)  53.4 us
    pallas_call x4, Pallas kernels, apply_rows(): pl.pallas_call(functools.partial(kernel, layout), out_shape=shape, grid_s...  45.3 us
    all_to_all x1, waiting for transfers between devices, local(): lax.all_to_all(mine, PLANE, split_axis=0, concat_axis=0, tiled=True)  44.6 us
    pallas_call x1, Pallas kernels, attend_back(): pl.pallas_call(functools.partial(attend_back_kernel, size, size ** (-0.5)...  35.6 us
  transfers between devices with their start and end apart: 98, of which 50 were waited for; matrix products, arithmetic and copies ran while one was open for 7% of the time, Pallas kernels for 43%

profile of v12, /device:TPU:0, one launch (start us, length us, event | category | flops | bytes accessed | tf_op | source)
XLA Modules:
  0.0 970.1 jit_solution(3089035369375528071)
XLA Ops:
  20.7 44.6 %all-to-all-done = bf16[8,80,3072]{2,1,0:T(8,128)(2,1)} async-done(((bf16[8,80,3072]{2,1,0:T(8,128)(2,1)}), bf16[8,80,3072]{2,1,0:T(8,128)(2,1)}, u32[]{:S(2)}, u32[]{:S(2)}) %all-to-all-start) | async-done | bytes 3932192 | tf_op jit(solution)/shard_map/all_to_all | solution.py:878
  69.6 145.3 %conditional.7 = (bf16[4,80,3072]{2,1,0:T(8,128)(2,1)}, bf16[4,80,3072]{2,1,0:T(8,128)(2,1)}, bf16[4,80,3072]{2,1,0:T(8,128)(2,1)}, bf16[4,80,3072]{2,1,0:T(8,12...) conditional(s32[]{:T(128)} %bitcast.17, () %tuple.127, ...), branch_computations={%region_0.0_spmd, %region_1.0_spmd} | conditional | flops 6947220 | bytes 125057264 | solution.py:61
  71.6 43.1 %collective-permute-done.51.rest_4_ = bf16[4,80,3072]{2,1,0:T(8,128)(2,1)} collective-permute-done((bf16[4,80,3072]{2,1,0:T(8,128)(2,1)}, bf16[4,80,3072]{2,1,0:T(8,128)(2,1)}, u32[]{:S(2)}, u32[]{:S(2)}) %collective-permute-start.51) | collective-permute-done | bytes 1966112 | tf_op jit(solution)/shard_map/cond/branch_1_fun/ppermute | solution.py:29
  121.9 17.9 %collective-permute-done.52.rest_5_ = bf16[2,80,3072]{2,1,0:T(8,128)(2,1)S(1)} collective-permute-done((bf16[2,80,3072]{2,1,0:T(8,128)(2,1)}, bf16[2,80,3072]{2,1,0:T(8,128)(2,1)S(1)}, u32[]{:S(2)}, u32[]{:S(2)}) %collective-permute-start.52) | collective-permute-done | bytes 983072 | tf_op jit(solution)/shard_map/cond/branch_1_fun/ppermute | solution.py:29
  145.6 11.9 %branch_1_fun.22 = bf16[384,3072]{1,0:T(8,128)(2,1)S(1)} custom-call(s32[8]{0:T(128)S(1)} %iota_xor_fusion.slots, bf16[384,2560]{1,0:T(8,128)(2,1)} %fusion.1.left, bf16[4,80,3072]{2,1,0:T(8,128)(2,1)} %get-tuple-element.282.rest_0_, bf16[4,80,3072]{2,1,0:T(8,128)(2,1)} %collective-permute-done.48.rest_1_, ...), custom_call_target="tpu_custom_call" | custom-call | flops 1048576 | bytes 4096 | tf_op jit(solution)/shard_map/cond/branch_1_fun/pallas_call | solution.py:319
  169.3 13.6 %collective-permute-done.57 = bf16[384,512]{1,0:T(8,128)(2,1)} collective-permute-done((bf16[384,512]{1,0:T(8,128)(2,1)S(1)}, bf16[384,512]{1,0:T(8,128)(2,1)}, u32[]{:S(2)}, u32[]{:S(2)}) %collective-permute-start.57) | collective-permute-done | bytes 393248 | tf_op jit(solution)/shard_map/cond/branch_1_fun/ppermute | solution.py:81
  187.7 9.9 %collective-permute-done.58 = bf16[384,512]{1,0:T(8,128)(2,1)} collective-permute-done((bf16[384,512]{1,0:T(8,128)(2,1)S(1)}, bf16[384,512]{1,0:T(8,128)(2,1)}, u32[]{:S(2)}, u32[]{:S(2)}) %collective-permute-start.58) | collective-permute-done | bytes 393248 | tf_op jit(solution)/shard_map/cond/branch_1_fun/ppermute | solution.py:81
  201.1 10.6 %collective-permute-done.59 = bf16[384,512]{1,0:T(8,128)(2,1)} collective-permute-done((bf16[384,512]{1,0:T(8,128)(2,1)S(1)}, bf16[384,512]{1,0:T(8,128)(2,1)}, u32[]{:S(2)}, u32[]{:S(2)}) %collective-permute-start.59) | collective-permute-done | bytes 393248 | tf_op jit(solution)/shard_map/cond/branch_1_fun/ppermute | solution.py:81
  216.2 140.7 %conditional.8 = (bf16[4,80,2560]{2,1,0:T(8,128)(2,1)}, bf16[4,80,2560]{2,1,0:T(8,128)(2,1)}, bf16[4,80,2560]{2,1,0:T(8,128)(2,1)}, bf16[4,80,2560]{2,1,0:T(8,12...) conditional(s32[]{:T(128)} %bitcast.17, () %tuple.125, ...), branch_computations={%region_3.0_spmd, %region_4.0_spmd} | conditional | flops 7012756 | bytes 129779728 | solution.py:61
  220.0 28.9 %branch_1_fun.23 = (bf16[384,2560]{1,0:T(8,128)(2,1)}, f32[384,2560]{1,0:T(8,128)}, f32[15,1,256]{2,1,0:T(1,128)S(1)}) custom-call(s32[1]{0:T(128)} %bitcast.2.core, s32[1,384]{1,0:T(1,128)S(1)} %get-tuple-element.327.places, bf16[384,2560]{1,0:T(8,128)(2,1)} %get-tuple-element.328.queries, bf16[384,512]{1,0:T(8,128)(2,1)} %get-tuple-element.329.rest_0_, ...), custom_call_target="tpu_custom_call" | custom-call | flops 1048576 | bytes 4096 | tf_op jit(solution)/shard_map/cond/branch_1_fun/pallas_call | solution.py:196
  264.2 17.0 %collective-permute-done.26.rest_6_ = bf16[2,80,2560]{2,1,0:T(8,128)(2,1)S(1)} collective-permute-done((bf16[2,80,2560]{2,1,0:T(8,128)(2,1)}, bf16[2,80,2560]{2,1,0:T(8,128)(2,1)S(1)}, u32[]{:S(2)}, u32[]{:S(2)}) %collective-permute-start.26) | collective-permute-done | bytes 819232 | tf_op jit(solution)/shard_map/cond/branch_1_fun/ppermute | solution.py:29
  286.6 11.9 %branch_1_fun.24 = f32[384,2560]{1,0:T(8,128)} custom-call(s32[8]{0:T(128)S(1)} %iota_xor_fusion.1.slots, bf16[384,2560]{1,0:T(8,128)(2,1)} %get-tuple-element.1244.left, f32[384,2560]{1,0:T(8,128)S(1)} %bitcast_convert_fusion.rest_0_, bf16[4,80,2560]{2,1,0:T(8,128)(2,1)S(1)} %copy-done.20, bf16[4,80,2560]{2,1,0:T(8,128)(2,1)} %collective-permute-done.21.rest_2_, ...), custom_call_target="tpu_custom_call" | custom-call | flops 1048576 | bytes 4096 | tf_op jit(solution)/shard_map/cond/branch_1_fun/pallas_call | solution.py:319
  306.6 43.1 %collective-permute-done.32 = bf16[384,2560]{1,0:T(8,128)(2,1)} collective-permute-done((bf16[384,2560]{1,0:T(8,128)(2,1)}, bf16[384,2560]{1,0:T(8,128)(2,1)}, u32[]{:S(2)}, u32[]{:S(2)}) %collective-permute-start.32) | collective-permute-done | bytes 1966112 | tf_op jit(solution)/shard_map/cond/branch_1_fun/ppermute | solution.py:29
  357.0 136.5 %conditional.9 = (bf16[384,2560]{1,0:T(8,128)(2,1)}, bf16[384,2560]{1,0:T(8,128)(2,1)}, bf16[384,2560]{1,0:T(8,128)(2,1)}, bf16[384,2560]{1,0:T(8,128)(2,1)}, bf...) conditional(s32[]{:T(128)} %bitcast.17, () %tuple.124, ...), branch_computations={%region_6.0_spmd, %region_7.0_spmd} | conditional | flops 3145728 | bytes 86520392 | solution.py:61
  360.3 36.6 %branch_1_fun.25 = (bf16[768,2560]{1,0:T(8,128)(2,1)}, bf16[768,2560]{1,0:T(8,128)(2,1)}, bf16[768,2560]{1,0:T(8,128)(2,1)}, bf16[768,2560]{1,0:T(8,128)(2,1)}, bf16[1536,1536]{1,0:T(8,128)(2,1)}) custom-call(bf16[2560,768]{1,0:T(8,128)(2,1)} %get-tuple-element.403.rest_0_, bf16[2560,768]{1,0:T(8,128)(2,1)} %get-tuple-element.404.rest_1_, ...), custom_call_target="tpu_custom_call" | custom-call | flops 1048576 | bytes 4096 | tf_op jit(solution)/shard_map/cond/branch_1_fun/pallas_call | solution.py:470
  410.7 36.3 %branch_1_fun.26 = (bf16[768,2560]{1,0:T(8,128)(2,1)}, bf16[768,2560]{1,0:T(8,128)(2,1)}, bf16[768,2560]{1,0:T(8,128)(2,1)}, bf16[768,2560]{1,0:T(8,128)(2,1)}, bf16[1536,1536]{1,0:T(8,128)(2,1)}) custom-call(bf16[2560,768]{1,0:T(8,128)(2,1)} %get-tuple-element.403.rest_0_, bf16[2560,768]{1,0:T(8,128)(2,1)} %get-tuple-element.404.rest_1_, ...), custom_call_target="tpu_custom_call" | custom-call | flops 1048576 | bytes 4096 | tf_op jit(solution)/shard_map/cond/branch_1_fun/pallas_call | solution.py:470
  451.3 38.0 %branch_1_fun.27 = bf16[2560,1536]{1,0:T(8,128)(2,1)} custom-call(bf16[384,2560]{1,0:T(8,128)(2,1)} %collective-permute-done.rest_2_.rest_0_, bf16[384,2560]{1,0:T(8,128)(2,1)} %get-tuple-element.405.rest_4_.rest_1_, bf16[384,2560]{1,0:T(8,128)(2,1)} %collective-permute-done.2.rest_6_.rest_2_, bf16[384,2560]{1,0:T(8,128)(2,1)} %get-tuple-element.406.rest_8_.rest_3_, ...), custom_call_target="tpu_custom_call" | custom-call | flops 1048576 | bytes 4096 | tf_op jit(solution)/shard_map/cond/branch_1_fun/pallas_call | solution.py:533
  495.0 154.9 %conditional.10 = (bf16[2560,1024]{1,0:T(8,128)(2,1)}, bf16[2560,512]{1,0:T(8,128)(2,1)}, bf16[768,2560]{1,0:T(8,128)(2,1)}, bf16[768,2560]{1,0:T(8,128)(2,1)}, ...) conditional(s32[]{:T(128)} %bitcast.17, () %tuple.134, ...), branch_computations={%region_9.0_spmd, %region_10.0_spmd} | conditional | flops 5242880 | bytes 94392864 | solution.py:61
  495.0 39.8 %branch_1_fun.28 = (bf16[768,2560]{1,0:T(8,128)(2,1)}, bf16[768,2560]{1,0:T(8,128)(2,1)}, bf16[768,2560]{1,0:T(8,128)(2,1)}, bf16[768,2560]{1,0:T(8,128)(2,1)}, bf16[1536,1536]{1,0:T(8,128)(2,1)}) custom-call(bf16[2560,768]{1,0:T(8,128)(2,1)} %get-tuple-element.439.rest_0_, bf16[2560,768]{1,0:T(8,128)(2,1)} %get-tuple-element.440.rest_1_, ...), custom_call_target="tpu_custom_call" | custom-call | flops 1048576 | bytes 4096 | tf_op jit(solution)/shard_map/cond/branch_1_fun/pallas_call | solution.py:470
  551.5 40.2 %branch_1_fun.30 = (bf16[768,2560]{1,0:T(8,128)(2,1)}, bf16[768,2560]{1,0:T(8,128)(2,1)}, bf16[768,2560]{1,0:T(8,128)(2,1)}, bf16[768,2560]{1,0:T(8,128)(2,1)}, bf16[1536,1536]{1,0:T(8,128)(2,1)}) custom-call(bf16[2560,768]{1,0:T(8,128)(2,1)} %get-tuple-element.439.rest_0_, bf16[2560,768]{1,0:T(8,128)(2,1)} %get-tuple-element.440.rest_1_, ...), custom_call_target="tpu_custom_call" | custom-call | flops 1048576 | bytes 4096 | tf_op jit(solution)/shard_map/cond/branch_1_fun/pallas_call | solution.py:470
  607.8 38.0 %branch_1_fun.32 = (bf16[2560,1024]{1,0:T(8,128)(2,1)}, bf16[2560,512]{1,0:T(8,128)(2,1)}) custom-call(bf16[384,2560]{1,0:T(8,128)(2,1)} %get-tuple-element.441.rest_2_.rest_0_, bf16[384,2560]{1,0:T(8,128)(2,1)} %get-tuple-element.443.rest_4_.rest_1_, bf16[384,2560]{1,0:T(8,128)(2,1)} %get-tuple-element.445.rest_6_.rest_2_, ...), custom_call_target="tpu_custom_call" | custom-call | flops 1048576 | bytes 4096 | tf_op jit(solution)/shard_map/cond/branch_1_fun/pallas_call | solution.py:533
  650.6 136.9 %conditional.11 = (bf16[384,3072]{1,0:T(8,128)(2,1)}, f32[384,2560]{1,0:T(8,128)}, bf16[192,2560]{1,0:T(8,128)(2,1)}, bf16[192,2560]{1,0:T(8,128)(2,1)}, bf16[19...) conditional(s32[]{:T(128)} %bitcast.17, () %tuple.123, ...), branch_computations={%region_11.0_spmd, %region_12.0_spmd} | conditional | flops 19727420 | bytes 144675504 | solution.py:61
  695.9 35.6 %branch_1_fun.38 = (bf16[384,2560]{1,0:T(8,128)(2,1)}, f32[4,384,512]{2,1,0:T(8,128)}, bf16[4,384,512]{2,1,0:T(8,128)(2,1)}) custom-call(s32[1]{0:T(128)} %bitcast.6.core, s32[1,384]{1,0:T(1,128)S(1)} %get-tuple-element.562.places, bf16[384,2560]{1,0:T(8,128)(2,1)} %get-tuple-element.563.queries, bf16[384,2560]{1,0:T(8,128)(2,1)} %copy-done.2, ...), custom_call_target="tpu_custom_call" | custom-call | flops 1048576 | bytes 4096 | tf_op jit(solution)/shard_map/cond/branch_1_fun/pallas_call | solution.py:229
  751.3 13.2 %branch_1_fun.39 = (bf16[4,4,80,2560]{3,2,1,0:T(8,128)(2,1)}, bf16[4,4,80,2560]{3,2,1,0:T(8,128)(2,1)}) custom-call(s32[8]{0:T(128)S(1)} %gather_fusion, bf16[384,2560]{1,0:T(8,128)(2,1)S(1)} %copy-done.1, bf16[384,2560]{1,0:T(8,128)(2,1)} %get-tuple-element.603.right), custom_call_target="tpu_custom_call" | custom-call | flops 1048576 | bytes 4096 | tf_op jit(solution)/shard_map/cond/branch_1_fun/pallas_call | solution.py:368
  789.1 86.8 %conditional.12 = (bf16[2560,384]{1,0:T(8,128)(2,1)}, bf16[2,80,2560]{2,1,0:T(8,128)(2,1)}, bf16[2,80,2560]{2,1,0:T(8,128)(2,1)}, bf16[4,80,2560]{2,1,0:T(8,128)...) conditional(s32[]{:T(128)} %bitcast.17, () %tuple.122, ...), branch_computations={%region_14.0_spmd, %region_15.17_spmd} | conditional | flops 18743324 | bytes 87126792 | solution.py:61
  800.5 11.9 %branch_1_fun.41 = f32[384,2560]{1,0:T(8,128)S(1)} custom-call(s32[8]{0:T(128)S(1)} %get-tuple-element.1142.slots, bf16[384,3072]{1,0:T(8,128)(2,1)} %get-tuple-element.644.value.left, bf16[4,80,3072]{2,1,0:T(8,128)(2,1)} %get-tuple-element.645.rest_0_, bf16[4,80,3072]{2,1,0:T(8,128)(2,1)} %get-tuple-element.646.rest_1_, ...), custom_call_target="tpu_custom_call" | custom-call | flops 1048576 | bytes 4096 | tf_op jit(solution)/shard_map/cond/branch_1_fun/pallas_call | solution.py:319
  840.6 14.1 %branch_1_fun.43 = bf16[2560,384]{1,0:T(8,128)(2,1)} custom-call(bf16[384,2560]{1,0:T(8,128)(2,1)} %get-tuple-element.681.rest_0_, bf16[384,2560]{1,0:T(8,128)(2,1)} %get-tuple-element.682.rest_1_, bf16[384,2560]{1,0:T(8,128)(2,1)} %get-tuple-element.683.rest_2_, bf16[384,2560]{1,0:T(8,128)(2,1)} %get-tuple-element.684.rest_3_, ...), custom_call_target="tpu_custom_call" | custom-call | flops 1048576 | bytes 4096 | tf_op jit(solution)/shard_map/cond/branch_1_fun/pallas_call | solution.py:571
  859.0 15.8 %collective-permute-done.46 = bf16[2,80,2560]{2,1,0:T(8,128)(2,1)} collective-permute-done((bf16[2,80,2560]{2,1,0:T(8,128)(2,1)S(1)}, bf16[2,80,2560]{2,1,0:T(8,128)(2,1)}, u32[]{:S(2)}, u32[]{:S(2)}) %collective-permute-start.46) | collective-permute-done | bytes 819232 | tf_op jit(solution)/shard_map/cond/branch_1_fun/ppermute | solution.py:29
  877.2 26.2 %conditional.13 = (bf16[320,2560]{1,0:T(8,128)(2,1)}, bf16[640,1536]{1,0:T(8,128)(2,1)S(1)}, f32[1,384,2560]{2,1,0:T(8,128)}) conditional(s32[]{:T(128)} %bitcast.17, () %tuple.121, (bf16[4,80,2560]{2,1,0:T(8,128)(2,1)}, bf16[2,80,2560]{2,1,0:T(8,128)(2,1)}, bf16[2,80,2560]{2,1,0:T(8,128)(2,1)}, bf16[2,80,2560]{2,1,0:T(8,128)(2,1)}, ...), branch_computations={%region_18.0_spmd, %region_19.0_spmd} | conditional | flops 19824640 | bytes 49479812 | solution.py:61
  908.4 14.9 %reduce-scatter.12.cloned.1.call-done = bf16[640,384]{1,0:T(8,128)(2,1)} async-done(((bf16[2560,384]{1,0:T(8,128)(2,1)}), bf16[640,384]{1,0:T(8,128)(2,1)}) %reduce-scatter.12.cloned.1.call-update) | async-done | bytes 491536 | tf_op jit(solution)/shard_map/reduce_scatter | solution.py:1146
  923.3 9.8 %all-to-all-done.1.whole = bf16[8,80,1536]{2,1,0:T(8,128)(2,1)S(1)} async-done(((bf16[8,80,1536]{2,1,0:T(8,128)(2,1)}), bf16[8,80,1536]{2,1,0:T(8,128)(2,1)S(1)}, u32[]{:S(2)}, u32[]{:S(2)}) %all-to-all-start.1) | async-done | bytes 1966112 | tf_op jit(solution)/shard_map/all_to_all | solution.py:1172
  950.2 11.0 %reduce-scatter.14.cloned.1.call-done = bf16[80,2560]{1,0:T(8,128)(2,1)} async-done(((bf16[320,2560]{1,0:T(8,128)(2,1)}), bf16[80,2560]{1,0:T(8,128)(2,1)}) %reduce-scatter.14.cloned.1.call-update) | async-done | bytes 409616 | tf_op jit(solution)/shard_map/reduce_scatter | solution.py:1170
  (372 shorter events, 346.0 us)
Async XLA Ops:
  14.3 51.0 %all-to-all-start = ((bf16[8,80,3072]{2,1,0:T(8,128)(2,1)}), bf16[8,80,3072]{2,1,0:T(8,128)(2,1)}, u32[]{:S(2)}, u32[]{:S(2)}) async-start(bf16[8,80,3072]{2,1,0:T(8,128)(2,1)} %shard_map.249), calls=%async_computation | async-start | bytes 7864320 | tf_op jit(solution)/shard_map/all_to_all | solution.py:878
  19.6 49.9 %all-gather.8.cloned.1.call-start = ((), (), s32[]{:S(2)}) async-start(), calls=%async_computation.8 | async-start | bytes 2457600 | tf_op jit(solution)/shard_map/all_gather | solution.py:868
  20.7 195.5 %all-gather.10.cloned.1.call-start = ((), (), s32[]{:S(2)}) async-start(), calls=%async_computation.9 | async-start | bytes 4915200 | tf_op jit(solution)/shard_map/all_gather | solution.py:885
  67.6 148.6 %all-gather.18.cloned.1.call-start = ((), (), s32[]{:S(2)}) async-start(), calls=%async_computation.18 | async-start | bytes 2048000 | tf_op jit(solution)/shard_map/all_gather | solution.py:869
  68.3 288.6 %all-gather.12.cloned.1.call-start = ((), (), s32[]{:S(2)}) async-start(), calls=%async_computation.10 | async-start | bytes 4915200 | tf_op jit(solution)/shard_map/all_gather | solution.py:885
  69.6 45.0 %collective-permute-start.51 = (bf16[4,80,3072]{2,1,0:T(8,128)(2,1)}, bf16[4,80,3072]{2,1,0:T(8,128)(2,1)}, u32[]{:S(2)}, u32[]{:S(2)}) collective-permute-start(bf16[4,80,3072]{2,1,0:T(8,128)(2,1)} %get-tuple-element.282.rest_0_), channel_id=1, source_target_pairs={{0,4},{4,0},{1,5},{5,1},{2,6},{6,2},{3,7},{7,3},{8,12},{12,8},{9,1... | collective-permute-start | bytes 5898248 | tf_op jit(solution)/shard_map/cond/branch_1_fun/ppermute | solution.py:29
  70.3 47.2 %collective-permute-start.48 = (bf16[4,80,3072]{2,1,0:T(8,128)(2,1)}, bf16[4,80,3072]{2,1,0:T(8,128)(2,1)}, u32[]{:S(2)}, u32[]{:S(2)}) collective-permute-start(bf16[4,80,3072]{2,1,0:T(8,128)(2,1)} %get-tuple-element.282.rest_0_), channel_id=1, source_target_pairs={{0,1},{1,0},{2,3},{3,2},{4,5},{5,4},{6,7},{7,6},{8,9},{9,8},{10,11... | collective-permute-start | bytes 5898248 | tf_op jit(solution)/shard_map/cond/branch_1_fun/ppermute | solution.py:29
  157.6 54.1 %collective-permute-start.61 = (bf16[384,2560]{1,0:T(8,128)(2,1)S(1)}, bf16[384,2560]{1,0:T(8,128)(2,1)}, u32[]{:S(2)}, u32[]{:S(2)}) collective-permute-start(bf16[384,2560]{1,0:T(8,128)(2,1)S(1)} %copy-done.11), channel_id=1, source_target_pairs={{0,1},{1,0},{2,3},{3,2},{4,5},{5,4},{6,7},{7,6},{8,9},{9,8},{10,11... | collective-permute-start | bytes 5898248 | tf_op jit(solution)/shard_map/cond/branch_1_fun/ppermute | solution.py:29
  159.4 52.3 %collective-permute-start.62 = (bf16[384,2560]{1,0:T(8,128)(2,1)S(1)}, bf16[384,2560]{1,0:T(8,128)(2,1)}, u32[]{:S(2)}, u32[]{:S(2)}) collective-permute-start(bf16[384,2560]{1,0:T(8,128)(2,1)S(1)} %copy-done.11), channel_id=1, source_target_pairs={{0,4},{4,0},{1,5},{5,1},{2,6},{6,2},{3,7},{7,3},{8,12},{12,8},{9,1... | collective-permute-start | bytes 5898248 | tf_op jit(solution)/shard_map/cond/branch_1_fun/ppermute | solution.py:29
  161.1 50.5 %collective-permute-start.63 = (bf16[384,2560]{1,0:T(8,128)(2,1)S(1)}, bf16[384,2560]{1,0:T(8,128)(2,1)}, u32[]{:S(2)}, u32[]{:S(2)}) collective-permute-start(bf16[384,2560]{1,0:T(8,128)(2,1)S(1)} %copy-done.11), channel_id=1, source_target_pairs={{0,2},{2,0},{1,3},{3,1},{4,6},{6,4},{5,7},{7,5},{8,10},{10,8},{9,1... | collective-permute-start | bytes 5898248 | tf_op jit(solution)/shard_map/cond/branch_1_fun/ppermute | solution.py:29
  214.9 278.6 %all-gather.14.cloned.1.call-start = ((), (), s32[]{:S(2)}) async-start(), calls=%async_computation.12 | async-start | bytes 4915200 | tf_op jit(solution)/shard_map/all_gather | solution.py:885
  215.5 278.1 %all-gather.16.cloned.1.call-start = ((), (), s32[]{:S(2)}) async-start(), calls=%async_computation.13 | async-start | bytes 4915200 | tf_op jit(solution)/shard_map/all_gather | solution.py:885
  216.1 433.9 %reduce-scatter.6.cloned.1.call-start = ((), (), s32[]{:S(2)}) async-start(), calls=%async_computation.11 | async-start | bytes 9830400 | tf_op jit(solution)/shard_map/reduce_scatter | solution.py:992
  304.6 45.2 %collective-permute-start.32 = (bf16[384,2560]{1,0:T(8,128)(2,1)}, bf16[384,2560]{1,0:T(8,128)(2,1)}, u32[]{:S(2)}, u32[]{:S(2)}) collective-permute-start(bf16[384,2560]{1,0:T(8,128)(2,1)} %multiply_convert_fusion), channel_id=1, source_target_pairs={{0,1},{1,0},{2,3},{3,2},{4,5},{5,4},{6,7},{7,6},{8,9},{9,8},{10,11... | collective-permute-start | bytes 5898248 | tf_op jit(solution)/shard_map/cond/branch_1_fun/ppermute | solution.py:29
  304.9 44.9 %collective-permute-start.33 = (bf16[384,2560]{1,0:T(8,128)(2,1)}, bf16[384,2560]{1,0:T(8,128)(2,1)}, u32[]{:S(2)}, u32[]{:S(2)}) collective-permute-start(bf16[384,2560]{1,0:T(8,128)(2,1)} %multiply_convert_fusion), channel_id=1, source_target_pairs={{0,4},{4,0},{1,5},{5,1},{2,6},{6,2},{3,7},{7,3},{8,12},{12,8},{9,1... | collective-permute-start | bytes 5898248 | tf_op jit(solution)/shard_map/cond/branch_1_fun/ppermute | solution.py:29
  306.6 43.2 %collective-permute-start.34 = (bf16[384,2560]{1,0:T(8,128)(2,1)}, bf16[384,2560]{1,0:T(8,128)(2,1)}, u32[]{:S(2)}, u32[]{:S(2)}) collective-permute-start(bf16[384,2560]{1,0:T(8,128)(2,1)} %multiply_convert_fusion), channel_id=1, source_target_pairs={{0,2},{2,0},{1,3},{3,1},{4,6},{6,4},{5,7},{7,5},{8,10},{10,8},{9,1... | collective-permute-start | bytes 5898248 | tf_op jit(solution)/shard_map/cond/branch_1_fun/ppermute | solution.py:29
  357.0 45.2 %collective-permute-start = (bf16[384,2560]{1,0:T(8,128)(2,1)}, bf16[384,2560]{1,0:T(8,128)(2,1)}, u32[]{:S(2)}, u32[]{:S(2)}) collective-permute-start(bf16[384,2560]{1,0:T(8,128)(2,1)} %get-tuple-element.380.rest_2_.rest_4_), channel_id=1, source_target_pairs={{0,1},{1,0},{2,3},{3,2},{4,5},{5,4},{6,7},{7,6},{8,9},{9,8},{10,11... | collective-permute-start | bytes 5898248 | tf_op jit(solution)/shard_map/cond/branch_1_fun/ppermute | solution.py:29
  358.6 44.9 %collective-permute-start.1 = (bf16[384,2560]{1,0:T(8,128)(2,1)}, bf16[384,2560]{1,0:T(8,128)(2,1)}, u32[]{:S(2)}, u32[]{:S(2)}) collective-permute-start(bf16[384,2560]{1,0:T(8,128)(2,1)} %get-tuple-element.377.rest_5_.rest_9_), channel_id=1, source_target_pairs={{0,4},{4,0},{1,5},{5,1},{2,6},{6,2},{3,7},{7,3},{8,12},{12,8},{9,1... | collective-permute-start | bytes 5898248 | tf_op jit(solution)/shard_map/cond/branch_1_fun/ppermute | solution.py:29
  404.0 45.0 %collective-permute-start.4 = (bf16[384,2560]{1,0:T(8,128)(2,1)}, bf16[384,2560]{1,0:T(8,128)(2,1)}, u32[]{:S(2)}, u32[]{:S(2)}) collective-permute-start(bf16[384,2560]{1,0:T(8,128)(2,1)} %get-tuple-element.402), channel_id=1, source_target_pairs={{0,1},{1,0},{2,3},{3,2},{4,5},{5,4},{6,7},{7,6},{8,9},{9,8},{10,11... | collective-permute-start | bytes 5898248 | tf_op jit(solution)/shard_map/cond/branch_1_fun/ppermute | solution.py:29
  404.4 44.8 %collective-permute-start.5 = (bf16[384,2560]{1,0:T(8,128)(2,1)}, bf16[384,2560]{1,0:T(8,128)(2,1)}, u32[]{:S(2)}, u32[]{:S(2)}) collective-permute-start(bf16[384,2560]{1,0:T(8,128)(2,1)} %get-tuple-element.402), channel_id=1, source_target_pairs={{0,4},{4,0},{1,5},{5,1},{2,6},{6,2},{3,7},{7,3},{8,12},{12,8},{9,1... | collective-permute-start | bytes 5898248 | tf_op jit(solution)/shard_map/cond/branch_1_fun/ppermute | solution.py:29
  449.2 44.1 %collective-permute-start.7 = (bf16[384,2560]{1,0:T(8,128)(2,1)}, bf16[384,2560]{1,0:T(8,128)(2,1)}, u32[]{:S(2)}, u32[]{:S(2)}) collective-permute-start(bf16[384,2560]{1,0:T(8,128)(2,1)} %collective-permute-done.5), channel_id=1, source_target_pairs={{0,1},{1,0},{2,3},{3,2},{4,5},{5,4},{6,7},{7,6},{8,9},{9,8},{10,11... | collective-permute-start | bytes 5898248 | tf_op jit(solution)/shard_map/cond/branch_1_fun/ppermute | solution.py:29
  493.5 294.1 %reduce-scatter.8.cloned.1.call-start = ((), (), s32[]{:S(2)}) async-start(), calls=%async_computation.14 | async-start | bytes 6553600 | tf_op jit(solution)/shard_map/reduce_scatter | solution.py:1039
  547.3 45.6 %collective-permute-start.15 = (bf16[768,2560]{1,0:T(8,128)(2,1)}, bf16[768,2560]{1,0:T(8,128)(2,1)}, u32[]{:S(2)}, u32[]{:S(2)}) collective-permute-start(bf16[768,2560]{1,0:T(8,128)(2,1)} %get-tuple-element.471), channel_id=1, source_target_pairs={{0,2},{2,0},{1,3},{3,1},{4,6},{6,4},{5,7},{7,5},{8,10},{10,8},{9,1... | collective-permute-start | bytes 11796488 | tf_op jit(solution)/shard_map/cond/branch_1_fun/ppermute | solution.py:29
  547.7 44.0 %collective-permute-start.12 = (bf16[192,2560]{1,0:T(8,128)(2,1)}, bf16[192,2560]{1,0:T(8,128)(2,1)}, u32[]{:S(2)}, u32[]{:S(2)}) collective-permute-start(bf16[192,2560]{1,0:T(8,128)(2,1)} %get-tuple-element.468), channel_id=1, source_target_pairs={{0,1},{1,0},{2,3},{3,2},{4,5},{5,4},{6,7},{7,6},{8,9},{9,8},{10,11... | collective-permute-start | bytes 2949128 | tf_op jit(solution)/shard_map/cond/branch_1_fun/ppermute | solution.py:29
  604.2 45.6 %collective-permute-start.20 = (bf16[768,2560]{1,0:T(8,128)(2,1)}, bf16[768,2560]{1,0:T(8,128)(2,1)}, u32[]{:S(2)}, u32[]{:S(2)}) collective-permute-start(bf16[768,2560]{1,0:T(8,128)(2,1)} %get-tuple-element.503), channel_id=1, source_target_pairs={{0,2},{2,0},{1,3},{3,1},{4,6},{6,4},{5,7},{7,5},{8,10},{10,8},{9,1... | collective-permute-start | bytes 11796488 | tf_op jit(solution)/shard_map/cond/branch_1_fun/ppermute | solution.py:29
  650.0 226.0 %reduce-scatter.10.cloned.1.call-start = ((), (), s32[]{:S(2)}) async-start(), calls=%async_computation.15 | async-start | bytes 3276800 | tf_op jit(solution)/shard_map/reduce_scatter | solution.py:1108
  679.3 54.1 %collective-permute-start.70 = (bf16[192,2560]{1,0:T(8,128)(2,1)}, bf16[192,2560]{1,0:T(8,128)(2,1)}, u32[]{:S(2)}, u32[]{:S(2)}) collective-permute-start(bf16[192,2560]{1,0:T(8,128)(2,1)} %get-tuple-element.558), channel_id=1, source_target_pairs={{0,1},{1,0},{2,3},{3,2},{4,5},{5,4},{6,7},{7,6},{8,9},{9,8},{10,11... | collective-permute-start | bytes 2949128 | tf_op jit(solution)/shard_map/cond/branch_1_fun/ppermute | solution.py:29
  680.7 52.6 %collective-permute-start.71 = (bf16[192,2560]{1,0:T(8,128)(2,1)}, bf16[192,2560]{1,0:T(8,128)(2,1)}, u32[]{:S(2)}, u32[]{:S(2)}) collective-permute-start(bf16[192,2560]{1,0:T(8,128)(2,1)} %get-tuple-element.559), channel_id=1, source_target_pairs={{0,4},{4,0},{1,5},{5,1},{2,6},{6,2},{3,7},{7,3},{8,12},{12,8},{9,1... | collective-permute-start | bytes 2949128 | tf_op jit(solution)/shard_map/cond/branch_1_fun/ppermute | solution.py:29
  681.5 51.8 %collective-permute-start.72 = (bf16[192,2560]{1,0:T(8,128)(2,1)}, bf16[192,2560]{1,0:T(8,128)(2,1)}, u32[]{:S(2)}, u32[]{:S(2)}) collective-permute-start(bf16[192,2560]{1,0:T(8,128)(2,1)} %get-tuple-element.560), channel_id=1, source_target_pairs={{0,1},{1,0},{2,3},{3,2},{4,5},{5,4},{6,7},{7,6},{8,9},{9,8},{10,11... | collective-permute-start | bytes 2949128 | tf_op jit(solution)/shard_map/cond/branch_1_fun/ppermute | solution.py:29
  682.9 50.4 %collective-permute-start.73 = (bf16[192,2560]{1,0:T(8,128)(2,1)}, bf16[192,2560]{1,0:T(8,128)(2,1)}, u32[]{:S(2)}, u32[]{:S(2)}) collective-permute-start(bf16[192,2560]{1,0:T(8,128)(2,1)} %get-tuple-element.561), channel_id=1, source_target_pairs={{0,4},{4,0},{1,5},{5,1},{2,6},{6,2},{3,7},{7,3},{8,12},{12,8},{9,1... | collective-permute-start | bytes 2949128 | tf_op jit(solution)/shard_map/cond/branch_1_fun/ppermute | solution.py:29
  787.6 135.7 %reduce-scatter.12.cloned.1.call-start = ((), (), s32[]{:S(2)}) async-start(), calls=%async_computation.16 | async-start | bytes 2457600 | tf_op jit(solution)/shard_map/reduce_scatter | solution.py:1146
  875.9 85.3 %reduce-scatter.14.cloned.1.call-start = ((), (), s32[]{:S(2)}) async-start(), calls=%async_computation.17 | async-start | bytes 2048000 | tf_op jit(solution)/shard_map/reduce_scatter | solution.py:1170
  (118 other events, 2042.6 us)
Sparse Core Ops, SparseCore 0:
  22.6 45.9 all-gather.7
  70.8 75.2 all-gather.9
  147.7 48.2 all-gather.17
  215.1 86.9 all-gather.11
  303.5 75.0 all-gather.13
  379.9 74.9 all-gather.15
  493.6 147.3 reduce-scatter.5
  650.1 106.2 reduce-scatter.7
  787.7 62.4 reduce-scatter.9
  876.0 47.2 reduce-scatter.11
  925.6 35.5 reduce-scatter.13
